TPU v7x, 32 devices: a whole 2x2x4 slice. The times are simulated.
32 devices in a mesh: groups: 2 (over x), dp: 8 (over z, y), tensor: 2 (over core).
Axes of the slice: x: 2, y: 2, z: 4, core: 2. Of those that a mesh axis runs over, the one named last changes fastest.
Arguments:
- hidden: bfloat16 [4096, 28672], P(('groups', 'dp'), 'tensor'), parts along dimension 0, may hold values from -6 to 6
- out_grad: bfloat16 [4096, 8192], P(('groups', 'dp'), 'tensor'), parts along dimension 0, may hold values from -6 to 6
- proj_in: bfloat16 [28672, 64], P('tensor'), may hold values from -0.03125 to 0.03125
- proj_out: bfloat16 [8192, 64], P('tensor'), may hold values from -0.0625 to 0.0625
- doc_ids: int32 [4096], P(('groups', 'dp')), parts along dimension 0, may hold values from 0 to 63, as said below
- queries: float32 [32, 4096], P(('groups', 'dp')), parts along dimension 0, may hold values from -6 to 6
Outputs:
- scores: float32 [32, 64], P('groups', 'dp'), parts along dimension 0
There are 2 independent parts, one for each index of `groups`. A program takes and returns all parts, laid end to end along the dimension named above; an argument that names none is the same for every part. Nothing has to cross between parts.
Inputs may be any that keep to these rules, and one draw needn't show every extreme that they name: `doc_ids`: document ids never fall along the window and every id from 0 to 63 occurs; each document has 1 to 512 tokens, one exactly that many.
All inputs are finite; a program needn't handle non-finite values.
Results may differ from a plain program's by a relative error of at most 0.0003.
Values sent between devices are 32-bit elements; how exact they have to be, the bound alone decides.
No kernel may reach another device: no remote copies, remote signals or barrier semaphores. Data moves between devices by JAX's collectives and lax.ppermute only.
A program may use at most 64 MiB of HBM per device.

v0:
```python
import jax
import jax.numpy as jnp
from jax import lax
from jax.sharding import PartitionSpec as P

TOK_DEV = 256
DOC_DEV = 8


def local(hidden, out_grad, proj_in, proj_out, doc_ids, queries):
    rank_out = proj_out.shape[1]
    rank_in = proj_in.shape[1]
    local_proj = jnp.concatenate(
        [
            jnp.dot(out_grad, proj_out, preferred_element_type=jnp.float32),
            jnp.dot(hidden, proj_in, preferred_element_type=jnp.float32),
        ],
        axis=1,
    )
    owned_cols = DOC_DEV
    num_docs = owned_cols * lax.axis_size("dp")
    coeff = jnp.sqrt(jnp.float32(rank_in * rank_out))
    projected = lax.psum(local_proj, "tensor")
    grad_part = projected[:, :rank_out]
    input_part = projected[:, rank_out:]
    outer = (grad_part[:, :, None] * input_part[:, None, :]).reshape(
        grad_part.shape[0], rank_out * rank_in
    )
    member = (doc_ids[None, :] == jnp.arange(num_docs, dtype=jnp.int32)[:, None]).astype(
        jnp.float32
    )
    partial_grads = jnp.dot(member, outer, precision=lax.Precision.HIGHEST) / jnp.sqrt(
        jnp.float32(TOK_DEV)
    )
    doc_grads = lax.psum(partial_grads, "dp")
    kernel = jnp.dot(doc_grads, doc_grads.T, precision=lax.Precision.HIGHEST)
    mean_diag = jnp.trace(kernel) / num_docs
    damping = 0.1 * mean_diag
    identity_mat = jnp.eye(num_docs, dtype=jnp.float32)
    factor = jnp.linalg.cholesky(kernel + damping * identity_mat)
    kernel_inv = jax.scipy.linalg.cho_solve((factor, True), identity_mat)
    mapped = jnp.dot(doc_grads.T, kernel_inv, precision=lax.Precision.HIGHEST) * (mean_diag / coeff)
    owned = lax.dynamic_slice_in_dim(mapped, lax.axis_index("dp") * owned_cols, owned_cols, 1)
    return jnp.dot(
        lax.all_gather(queries, "dp", axis=0, tiled=True), owned, precision=lax.Precision.HIGHEST
    )


def solution(mesh):
    return jax.shard_map(
        local,
        mesh=mesh,
        in_specs=(
            P(("groups", "dp"), "tensor"),
            P(("groups", "dp"), "tensor"),
            P("tensor", None),
            P("tensor", None),
            P(("groups", "dp")),
            P(("groups", "dp"), None),
        ),
        out_specs=P("groups", "dp"),
        check_vma=False,
    )
```

profile of v0, /device:TPU:0, one launch (start us, length us, event | category | flops | bytes accessed | tf_op | source)
XLA Modules:
  0.0 149.9 jit_solution(2579220286411028083)
XLA Ops:
  6.5 0.0 copy-start
  6.5 0.0 all-reduce.3.cloned.1.call-start
  6.5 1.6 %copy-done = bf16[256,4096]{1,0:T(8,128)(2,1)S(1)} copy-done((bf16[256,4096]{1,0:T(8,128)(2,1)S(1)}, bf16[256,4096]{1,0:T(8,128)(2,1)}, u32[]{:S(2)}) %copy-start) | copy-done | bytes 2097176
  8.1 1.8 %fusion.11 = f32[256,64]{0,1:T(8,128)S(1)} fusion(bf16[256,4096]{1,0:T(8,128)(2,1)S(1)} %copy-done, bf16[4096,64]{0,1:T(8,128)(2,1)} %param.9), kind=kOutput, calls=%fused_computation.25 | convolution fusion | flops 134217728 | bytes 2686976 | tf_op jit(solution)/shard_map/dot_general | solution.py:15
  9.9 6.0 %fusion.12 = f32[256,64]{0,1:T(8,128)S(1)} fusion(bf16[256,14336]{1,0:T(8,128)(2,1)} %param.6, bf16[14336,64]{0,1:T(8,128)(2,1)} %param.8), kind=kOutput, calls=%fused_computation.26 | convolution fusion | flops 469762048 | bytes 9240576 | tf_op jit(solution)/shard_map/dot_general | solution.py:16
  15.9 0.0 copy-start.2
  16.0 0.7 pad_maximum_fusion
  16.6 0.0 all-reduce.3.cloned.1.call-update
  16.6 0.0 all-reduce.5.cloned.1.call-start
  16.7 20.7 %all-reduce.3.cloned.1.call-done = f32[256,128]{0,1:T(8,128)} async-done(((f32[256,128]{0,1:T(8,128)}), f32[256,128]{0,1:T(8,128)}) %all-reduce.3.cloned.1.call-update) | async-done | bytes 131088 | tf_op jit(solution)/shard_map/psum | solution.py:23
  37.4 0.9 fusion.10
  38.3 0.5 broadcast_multiply_fusion
  38.8 0.0 copy-start.1
  38.8 0.0 copy-done.2
  38.8 3.3 %convolution_multiply_fusion = f32[64,4096]{1,0:T(8,128)} fusion(f32[256,4096]{0,1:T(8,128)S(1)} %bitcast.28, s32[256]{0:T(256)S(1)} %copy-done.2), kind=kOutput, calls=%fused_computation | convolution fusion | flops 805584896 | bytes 5243904 | tf_op jit(solution)/shard_map/dot_general | solution.py:32
  42.2 0.0 all-reduce.5.cloned.1.call-update
  42.2 0.0 copy-done.1
  42.2 31.7 %all-gather = f32[8,2,4096]{2,1,0:T(2,128)S(1)} all-gather(f32[1,2,4096]{2,1,0:T(2,128)S(1)} %bitcast.29), channel_id=1, replica_groups=mesh['groups'=2,'dp'=8,'tensor'=2] {'dp'}, dimensions={0}, use_global_device_ids=true | all-gather | bytes 294912 | tf_op jit(solution)/shard_map/all_gather | solution.py:45
  73.9 0.2 reshape.21
  74.1 48.5 %all-reduce.5.cloned.1.call-done = f32[64,4096]{1,0:T(8,128)} async-done(((f32[64,4096]{1,0:T(8,128)}), f32[64,4096]{1,0:T(8,128)}) %all-reduce.5.cloned.1.call-update) | async-done | bytes 1048592 | tf_op jit(solution)/shard_map/psum | solution.py:35
  122.7 3.1 %select_reduce_fusion.1 = (f32[]{:T(128)}, f32[64,64]{1,0:T(8,128)S(1)}) fusion(f32[64,4096]{1,0:T(8,128)} %all-reduce.5.cloned.1.call-done), kind=kOutput, calls=%fused_computation.18 | convolution fusion | flops 201338880 | bytes 1064964 | tf_op jit(solution)/shard_map/dot_general | solution.py:36
  125.8 0.1 copy.11
  126.6 5.8 %cholesky.18 = f32[64,64]{1,0:T(8,128)S(1)} custom-call(f32[64,64]{1,0:T(8,128)S(1)} %fusion.7), custom_call_target="Cholesky" | custom-call | tf_op jit(solution)/shard_map/jit(cholesky)/cholesky | solution.py:40
  132.4 0.7 compare_reduce_fusion
  133.2 0.7 fusion.1
  133.9 4.9 %custom-call.10 = f32[1,64,64]{1,2,0:T(8,128)S(1)} custom-call(f32[1,64,64]{2,1,0:T(8,128)S(1)} %fusion.1), custom_call_target="InvertDiagBlocksLowerTriangular" | custom-call | tf_op jit(solution)/shard_map/jit(_cho_solve)/triangular_solve | solution.py:41
  138.8 0.2 fusion.4
  139.0 0.2 fusion.2
  139.8 2.3 %fusion.13 = f32[4096,64]{0,1:T(8,128)S(1)} fusion(f32[64,4096]{1,0:T(8,128)} %all-reduce.5.cloned.1.call-done, f32[64,64]{1,0:T(8,128)S(1)} %fusion.2), kind=kOutput, calls=%fused_computation.27 | convolution fusion | flops 201326592 | bytes 2113536 | tf_op jit(solution)/shard_map/dot_general | solution.py:42
  142.1 1.0 convolution_bitcast_fusion
  (2 shorter events, 0.0 us)
Async XLA Ops:
  6.5 1.6 %copy-start = (bf16[256,4096]{1,0:T(8,128)(2,1)S(1)}, bf16[256,4096]{1,0:T(8,128)(2,1)}, u32[]{:S(2)}) copy-start(bf16[256,4096]{1,0:T(8,128)(2,1)} %param.7) | copy-start | bytes 6291460
  6.5 30.9 %all-reduce.3.cloned.1.call-start = ((), (), s32[]{:S(2)}) async-start(), calls=%async_computation | async-start | bytes 262144 | tf_op jit(solution)/shard_map/psum | solution.py:23
  15.9 22.9 %copy-start.2 = (s32[256]{0:T(256)S(1)}, s32[256]{0:T(256)}, u32[]{:S(2)}) copy-start(s32[256]{0:T(256)} %param.10) | copy-start | bytes 3076
  16.6 106.0 %all-reduce.5.cloned.1.call-start = ((), (), s32[]{:S(2)}) async-start(), calls=%async_computation.1 | async-start | bytes 2097152 | tf_op jit(solution)/shard_map/psum | solution.py:35
  38.8 3.4 %copy-start.1 = (f32[2,4096]{1,0:T(2,128)S(1)}, f32[2,4096]{1,0:T(2,128)}, u32[]{:S(2)}) copy-start(f32[2,4096]{1,0:T(2,128)} %param.11) | copy-start | bytes 98308
Sparse Core Ops, SparseCore 0:
  16.8 20.5 all-reduce.2
  42.3 80.3 all-reduce.4
where the time goes:
time: 150 us
  waiting for transfers between devices  69.3 us (46%)
  blocking collectives  31.7 us (21%)
  matrix products  17.9 us (12%)
  between operations  14.8 us (10%)
  other arithmetic  13.4 us (9%)
  local copies, waits for them, and re-layouts  2.73 us (2%)
    psum x1, waiting for transfers between devices, local(): doc_grads = lax.psum(partial_grads, 'dp')  48.5 us
    all_gather x1, blocking collectives, local(): lax.all_gather(queries, 'dp', axis=0, tiled=True)  31.7 us
    psum x1, waiting for transfers between devices, local(): projected = lax.psum(local_proj, 'tensor')  20.7 us
    another operation x3, other arithmetic, local(): factor = jnp.linalg.cholesky(kernel + damping * identity_mat)  6.6 us
    dot_general x1, matrix products, local(): jnp.dot(hidden, proj_in, preferred_element_type=jnp.float32)  6.02 us
    another operation x2, other arithmetic, local(): kernel_inv = jax.scipy.linalg.cho_solve((factor, True), identity_mat)  5.59 us
    dot_general x1, matrix products, local(): jnp.dot(member, outer, precision=lax.Precision.HIGHEST)  3.33 us
    dot_general x1, matrix products, local(): kernel = jnp.dot(doc_grads, doc_grads.T, precision=lax.Precision.HIGHEST)  3.13 us
  transfers between devices with their start and end apart: 2, of which 2 were waited for; matrix products, arithmetic and copies ran while one was open for 0% of the time, Pallas kernels for 0%

commit v1 on v0

v1 whole, which is shorter than its diff:
```python
import functools

import jax
import jax.numpy as jnp
from jax import lax
from jax.experimental import pallas as pl
from jax.experimental.pallas import tpu as pltpu
from jax.sharding import PartitionSpec as P

TOK_DEV = 256
DOC_DEV = 8
LANES = 128
NT = (((1,), (1,)), ((), ()))
HIGHEST = lax.Precision.HIGHEST
VMEM = pl.BlockSpec(memory_space=pltpu.VMEM)
ANY = pl.BlockSpec(memory_space=pl.ANY)


def vmem_params(mib):
    return pltpu.CompilerParams(vmem_limit_bytes=mib << 20)


def chunks_of(length, most=1024):
    size = most
    while length % size:
        size //= 2
    return size, length // size


def project_kernel(sizes, h_ref, g_ref, pin_ref, pout_ref, keep_ref, send_ref, h_buf, g_buf, pin_buf, pout_buf, sems):
    h_size, h_count, g_size, g_count = sizes
    copies = {}
    slot = 0
    for name, src, dst in (("po", pout_ref, pout_buf), ("pi", pin_ref, pin_buf)):
        copies[name] = pltpu.make_async_copy(src, dst, sems.at[slot])
        slot += 1
    for i in range(g_count):
        at = pl.ds(i * g_size, g_size)
        copies["g", i] = pltpu.make_async_copy(g_ref.at[:, at], g_buf.at[:, at], sems.at[slot])
        slot += 1
    for i in range(h_count):
        at = pl.ds(i * h_size, h_size)
        copies["h", i] = pltpu.make_async_copy(h_ref.at[:, at], h_buf.at[:, at], sems.at[slot])
        slot += 1
    order = ["po"] + [("g", i) for i in range(g_count)] + ["pi"] + [("h", i) for i in range(h_count)]
    for name in order:
        copies[name].start()

    def run(tag, count, size, proj, data):
        total = None
        for i in range(count):
            copies[tag, i].wait()
            at = pl.ds(i * size, size)
            part = lax.dot_general(proj[:, at], data[:, at], NT, preferred_element_type=jnp.float32)
            total = part if total is None else total + part
        return total

    copies["po"].wait()
    grad = run("g", g_count, g_size, pout_buf, g_buf)
    copies["pi"].wait()
    inp = run("h", h_count, h_size, pin_buf, h_buf)
    both = jnp.concatenate([grad, inp], axis=0)
    half = both.shape[1] // 2
    first, second = both[:, :half], both[:, half:]
    lead = lax.axis_index("tensor") == 0
    keep_ref[...] = jnp.where(lead, first, second)
    send_ref[...] = jnp.where(lead, second, first)


def project(hidden, out_grad, pin_t, pout_t):
    tokens, units = hidden.shape
    width = out_grad.shape[1]
    ranks = pin_t.shape[0] + pout_t.shape[0]
    h_size, h_count = chunks_of(units)
    g_size, g_count = chunks_of(width)
    half = jax.ShapeDtypeStruct((ranks, tokens // 2), jnp.float32)
    return pl.pallas_call(
        functools.partial(project_kernel, (h_size, h_count, g_size, g_count)),
        out_shape=(half, half),
        in_specs=[ANY] * 4,
        out_specs=(VMEM, VMEM),
        scratch_shapes=[
            pltpu.VMEM(hidden.shape, hidden.dtype),
            pltpu.VMEM(out_grad.shape, out_grad.dtype),
            pltpu.VMEM(pin_t.shape, pin_t.dtype),
            pltpu.VMEM(pout_t.shape, pout_t.dtype),
            pltpu.SemaphoreType.DMA((2 + g_count + h_count,)),
        ],
        compiler_params=vmem_params(40),
        cost_estimate=pl.CostEstimate(
            flops=2 * tokens * 64 * (units + width),
            bytes_accessed=2 * (tokens + 64) * (units + width),
            transcendentals=0,
        ),
        name="project",
    )(hidden, out_grad, pin_t, pout_t)


def pack_kernel(pa, pb, keep_ref, recv_ref, extra_ref, out_ref):
    total = keep_ref[...] + recv_ref[...]
    ranks = total.shape[0] // 2
    rows_a, rows_b = ranks // pa, ranks // pb
    for s in range(pa * pb):
        p, q = s // pb, s % pb
        out_ref[s, 0:rows_a, :] = total[p * rows_a:(p + 1) * rows_a, :]
        out_ref[s, rows_a:rows_a + rows_b, :] = total[ranks + q * rows_b:ranks + (q + 1) * rows_b, :]
        out_ref[s, rows_a + rows_b:, :] = extra_ref[s]


def pack(keep, recv, extra, pa, pb):
    ranks = keep.shape[0] // 2
    rows = ranks // pa + ranks // pb + extra.shape[1]
    return pl.pallas_call(
        functools.partial(pack_kernel, pa, pb),
        out_shape=jax.ShapeDtypeStruct((pa * pb, rows, keep.shape[1]), jnp.float32),
        in_specs=[VMEM] * 3,
        out_specs=VMEM,
        compiler_params=vmem_params(16),
        name="pack",
    )(keep, recv, extra)


def gram_kernel(rows_a, rows_b, docs, copies, x_ref, out_ref, outer_ref, member_ref):
    n, _, lanes = x_ref.shape
    wide = rows_a * rows_b
    doc = lax.broadcasted_iota(jnp.int32, (docs, lanes), 0)

    def place(s):
        at = pl.ds(pl.multiple_of(s * lanes, lanes), lanes)
        g = x_ref[s, 0:rows_a, :]
        b = x_ref[s, rows_a:rows_a + rows_b, :]
        ids = x_ref[s, rows_a + rows_b:rows_a + rows_b + 1, :].astype(jnp.int32)
        member_ref[:, at] = jnp.where(doc == ids, 1.0, 0.0).astype(jnp.bfloat16)
        outer = (g[:, None, :] * b[None, :, :]).reshape(wide, lanes)
        high = outer.astype(jnp.bfloat16)
        rest = outer - high.astype(jnp.float32)
        mid = rest.astype(jnp.bfloat16)
        outer_ref[0:wide, at] = high
        outer_ref[wide:2 * wide, at] = mid
        outer_ref[2 * wide:, at] = (rest - mid.astype(jnp.float32)).astype(jnp.bfloat16)

    if n <= 16:
        for s in range(n):
            place(s)
    else:
        pl.loop(0, n)(place)
    sums = lax.dot_general(member_ref[...], outer_ref[...], NT, preferred_element_type=jnp.float32)
    grads = (sums[:, 2 * wide:] + sums[:, wide:2 * wide] + sums[:, :wide]) * (TOK_DEV ** -0.5)
    first = rows_a + rows_b + 1
    if wide >= lanes:
        queries = jnp.concatenate([x_ref[:, first + j, :] for j in range(wide // lanes)], axis=1)
    else:
        queries = x_ref[:, first, :][:, :wide]
    both = jnp.concatenate([grads, queries], axis=0)
    share = lax.dot_general(grads, both, NT, precision=HIGHEST, preferred_element_type=jnp.float32)
    for s in range(copies):
        out_ref[s, :, 0:docs + n] = share
        if out_ref.shape[2] > docs + n:
            out_ref[s, :, docs + n:] = jnp.zeros((docs, out_ref.shape[2] - docs - n), jnp.float32)


def gram(x, rows_a, rows_b, docs, copies):
    n, _, lanes = x.shape
    wide = rows_a * rows_b
    cols = -(-(docs + n) // LANES) * LANES
    return pl.pallas_call(
        functools.partial(gram_kernel, rows_a, rows_b, docs, copies),
        out_shape=jax.ShapeDtypeStruct((copies, docs, cols), jnp.float32),
        in_specs=[VMEM],
        out_specs=VMEM,
        scratch_shapes=[
            pltpu.VMEM((3 * wide, n * lanes), jnp.bfloat16),
            pltpu.VMEM((docs, n * lanes), jnp.bfloat16),
        ],
        compiler_params=vmem_params(40),
        name="gram",
    )(x)


def solve_kernel(docs, queries, scale, x_ref, out_ref, done_ref):
    total = x_ref[0]
    for s in range(1, x_ref.shape[0]):
        total = total + x_ref[s]
    rows, cols = total.shape
    row = lax.broadcasted_iota(jnp.int32, (rows, cols), 0)
    col = lax.broadcasted_iota(jnp.int32, (rows, cols), 1)
    mean_diag = jnp.sum(jnp.where(row == col, total, 0.0)) * (1.0 / docs)
    work = total + jnp.where(row == col, 0.1 * mean_diag, 0.0)
    here = lax.broadcasted_iota(jnp.int32, (rows, 1), 0)
    for k in range(docs):
        line = work[k:k + 1, :]
        inverse = 1.0 / line[:, k:k + 1]
        factor = jnp.where(here == k, 1.0 - inverse, work[:, k:k + 1] * inverse)
        work = work - factor * line
    done_ref[...] = work * (mean_diag * scale)
    mine = pl.ds(pl.multiple_of(lax.axis_index("dp") * DOC_DEV, DOC_DEV), DOC_DEV)
    out_ref[...] = done_ref[mine, :][:, docs:docs + queries]


def solve(x, docs, queries, scale):
    return pl.pallas_call(
        functools.partial(solve_kernel, docs, queries, scale),
        out_shape=jax.ShapeDtypeStruct((DOC_DEV, queries), jnp.float32),
        in_specs=[VMEM],
        out_specs=VMEM,
        scratch_shapes=[pltpu.VMEM(x.shape[1:], jnp.float32)],
        compiler_params=vmem_params(16),
        name="solve",
    )(x)


def solve_large(total, docs, queries, scale):
    kernel = total[:, :docs]
    mean_diag = jnp.trace(kernel) / docs
    factor = jnp.linalg.cholesky(kernel + 0.1 * mean_diag * jnp.eye(docs, dtype=jnp.float32))
    solved = jax.scipy.linalg.cho_solve((factor, True), total[:, docs:docs + queries]) * (mean_diag * scale)
    return lax.dynamic_slice_in_dim(solved, lax.axis_index("dp") * DOC_DEV, DOC_DEV, 0)


def local(hidden, out_grad, proj_in, proj_out, doc_ids, queries):
    dp, tensor = lax.axis_size("dp"), lax.axis_size("tensor")
    n = dp * tensor
    docs = DOC_DEV * dp
    ranks = proj_in.shape[1]
    pa = 1
    while pa * pa < n:
        pa *= 2
    pb = n // pa
    rows_a, rows_b = ranks // pa, ranks // pb
    wide = rows_a * rows_b
    core = lax.axis_index("tensor")
    all_axes = ("dp", "tensor")

    keep, send = project(hidden, out_grad, proj_in.T, proj_out.T)
    recv = lax.ppermute(send, "tensor", [(i, tensor - 1 - i) for i in range(tensor)])

    lanes = keep.shape[1]
    ids = lax.dynamic_slice_in_dim(doc_ids, core * lanes, lanes).astype(jnp.float32)
    query = lax.dynamic_slice_in_dim(queries, core, 1, 0).reshape(pa, rows_a, pb, rows_b)
    query = query.transpose(0, 2, 1, 3).reshape(n, wide)
    q_rows = -(-wide // lanes)
    query = jnp.pad(query, ((0, 0), (0, q_rows * lanes - wide))).reshape(n, q_rows, lanes)
    extra = jnp.concatenate([jnp.broadcast_to(ids, (n, 1, lanes)), query], axis=1)
    extra = jnp.pad(extra, ((0, 0), (0, -(1 + q_rows) % 8), (0, 0)))

    block = pack(keep, recv, extra, pa, pb)
    block = lax.all_to_all(block, all_axes, 0, 0, tiled=True)
    scale = float(ranks * ranks) ** -0.5
    if docs <= 64:
        share = gram(block, rows_a, rows_b, docs, n)
        share = lax.all_to_all(share, all_axes, 0, 0, tiled=True)
        return solve(share, docs, n, scale).T
    share = gram(block, rows_a, rows_b, docs, 1)[0]
    return solve_large(lax.psum(share, all_axes), docs, n, scale).T


def solution(mesh):
    return jax.shard_map(
        local,
        mesh=mesh,
        in_specs=(
            P(("groups", "dp"), "tensor"),
            P(("groups", "dp"), "tensor"),
            P("tensor", None),
            P("tensor", None),
            P(("groups", "dp")),
            P(("groups", "dp"), None),
        ),
        out_specs=P("groups", "dp"),
        check_vma=False,
    )
```

time: 150 us -> 59.8 us (0.40)
  waiting for transfers between devices: 69.3 us -> 0.45 us
  matrix products: 17.9 us -> 0 us
  Pallas kernels: 0 us -> 15.1 us
  between operations: 14.8 us -> 0.07 us
  other arithmetic: 13.4 us -> 0.1 us
  local copies, waits for them, and re-layouts: 2.73 us -> 7.54 us
  blocking collectives: 31.7 us -> 35.7 us
    psum x2 -> x0, waiting for transfers between devices: 69.3 us -> none  [the longest x1 48.5 us: local(): doc_grads = lax.psum(partial_grads, 'dp')]
    all_to_all x0 -> x2, blocking collectives: none -> 35.7 us  [the longest x1 18.2 us: local(): block = lax.all_to_all(block, all_axes, 0, 0, tiled=True)]
    all_gather x1 -> x0, blocking collectives: 31.7 us -> none  [local(): lax.all_gather(queries, 'dp', axis=0, tiled=True)]
    dot_general x6 -> x0, matrix products: 17.5 us -> none  [the longest x1 6.02 us: local(): jnp.dot(hidden, proj_in, preferred_element_type=jnp.float32)]
    pallas_call x0 -> x4, Pallas kernels: none -> 15.1 us  [the longest x1 7.02 us: project(): pl.pallas_call(functools.partial(project_kernel, (h_size, h_count, g_size...]
    another operation x5 -> x0, other arithmetic: 12.2 us -> none  [the longest x3 6.6 us: local(): factor = jnp.linalg.cholesky(kernel + damping * identity_mat)]
    unnamed x7 -> x12, local copies, waits for them, and re-layouts: 1.78 us -> 7.23 us
  transfers between devices with their start and end apart: 2 -> 1, of which waited for: 2 -> 1; matrix products, arithmetic and copies ran while one was open for 0% -> 1% of each run, Pallas kernels for 0% -> 0%
where the time goes in v1:
time: 59.8 us; the launch traced here: 59.5 us
  blocking collectives  35.7 us (60%)
  Pallas kernels  15.1 us (25%)
  local copies, waits for them, and re-layouts  7.54 us (13%)
    all_to_all x1, blocking collectives, local(): block = lax.all_to_all(block, all_axes, 0, 0, tiled=True)  18.2 us
    all_to_all x1, blocking collectives, local(): share = lax.all_to_all(share, all_axes, 0, 0, tiled=True)  17.5 us
    unnamed x12, local copies, waits for them, and re-layouts  7.23 us
    pallas_call x1, Pallas kernels, project(): pl.pallas_call(functools.partial(project_kernel, (h_size, h_count, g_size...  7.02 us
    pallas_call x1, Pallas kernels, solve(): pl.pallas_call(functools.partial(solve_kernel, docs, queries, scale), out...  6.18 us
    pallas_call x1, Pallas kernels, gram(): pl.pallas_call(functools.partial(gram_kernel, rows_a, rows_b, docs, copie...  1.89 us
  transfers between devices with their start and end apart: 1, of which 1 were waited for; matrix products, arithmetic and copies ran while one was open for 1% of the time, Pallas kernels for 0%

profile of v1, /device:TPU:0, one launch (start us, length us, event | category | flops | bytes accessed | tf_op | source)
XLA Modules:
  0.0 59.5 jit_solution(5507870938192817668)
XLA Ops:
  0.0 0.0 copy-start
  0.0 0.0 copy-start.1
  0.0 3.1 %copy-done.1 = bf16[256,14336]{1,0:T(8,128)(2,1)S(1)} copy-done((bf16[256,14336]{1,0:T(8,128)(2,1)S(1)}, bf16[256,14336]{1,0:T(8,128)(2,1)}, u32[]{:S(2)}) %copy-start.1) | copy-done | bytes 7340056
  3.1 0.0 copy-start.2
  3.1 1.6 %copy-done.2 = bf16[256,4096]{1,0:T(8,128)(2,1)S(1)} copy-done((bf16[256,4096]{1,0:T(8,128)(2,1)S(1)}, bf16[256,4096]{1,0:T(8,128)(2,1)}, u32[]{:S(2)}) %copy-start.2) | copy-done | bytes 2097176
  4.7 0.0 copy-start.3
  4.7 1.5 %copy-done.3 = bf16[14336,64]{0,1:T(8,128)(2,1)S(1)} copy-done((bf16[14336,64]{0,1:T(8,128)(2,1)S(1)}, bf16[14336,64]{0,1:T(8,128)(2,1)}, u32[]{:S(2)}) %copy-start.3) | copy-done | bytes 1835032
  6.2 0.0 copy-start.4
  6.2 1.0 %copy-done.4 = bf16[4096,64]{0,1:T(8,128)(2,1)S(1)} copy-done((bf16[4096,64]{0,1:T(8,128)(2,1)S(1)}, bf16[4096,64]{0,1:T(8,128)(2,1)}, u32[]{:S(2)}) %copy-start.4) | copy-done | bytes 524312
  7.2 0.0 copy-start.5
  7.2 7.0 %project.1 = (f32[128,128]{1,0:T(8,128)S(1)}, f32[128,128]{1,0:T(8,128)S(1)}) custom-call(bf16[256,14336]{1,0:T(8,128)(2,1)S(1)} %copy-done.1, bf16[256,4096]{1,0:T(8,128)(2,1)S(1)} %copy-done.2, bf16[64,14336]{1,0:T(8,128)(2,1)S(1)} %bitcast.6, bf16[64,4096]{1,0:T(8,128)(2,1)S(1)} %bitcast.7), custom_call_target="tpu_custom_call" | custom-call | flops 603979776 | bytes 11796480 | tf_op jit(solution)/shard_map/project/pallas_call | solution.py:77
  14.3 0.5 collective-permute-start
  14.8 0.0 copy-done
  14.8 0.1 reshape.8
  15.0 0.1 reshape.9
  15.1 0.0 copy-done.5
  15.1 0.1 dynamic-slice_convert_fusion
  15.2 0.5 collective-permute-done.recv_ref
  15.7 18.2 %all_to_all.10.x_ref = f32[16,40,128]{2,1,0:T(8,128)S(1)} all-to-all(f32[16,40,128]{2,1,0:T(8,128)S(1)} %pack.1), channel_id=1, replica_groups=mesh['groups'=2,'dp'=8,'tensor'=2] {'dp','tensor'}, dimensions={0} | all-to-all | bytes 655360 | tf_op jit(solution)/shard_map/all_to_all | solution.py:247
  33.9 1.9 %gram.1 = f32[16,64,128]{2,1,0:T(8,128)S(1)} custom-call(f32[16,40,128]{2,1,0:T(8,128)S(1)} %all_to_all.10.x_ref), custom_call_target="tpu_custom_call" | custom-call | tf_op jit(solution)/shard_map/gram/pallas_call | solution.py:166
  35.8 17.5 %all_to_all.11.x_ref = f32[16,64,128]{2,1,0:T(8,128)S(1)} all-to-all(f32[16,64,128]{2,1,0:T(8,128)S(1)} %gram.1), channel_id=1, replica_groups=mesh['groups'=2,'dp'=8,'tensor'=2] {'dp','tensor'}, dimensions={0} | all-to-all | bytes 1048576 | tf_op jit(solution)/shard_map/all_to_all | solution.py:251
  53.3 6.2 %solve.1 = f32[8,16]{1,0:T(8,128)} custom-call(f32[16,64,128]{2,1,0:T(8,128)S(1)} %all_to_all.11.x_ref), custom_call_target="tpu_custom_call" | custom-call | tf_op jit(solution)/shard_map/solve/pallas_call | solution.py:201
  (5 shorter events, 0.1 us)
Async XLA Ops:
  0.0 14.8 %copy-start = (f32[2,4096]{1,0:T(2,128)S(1)}, f32[2,4096]{1,0:T(2,128)}, u32[]{:S(2)}) copy-start(f32[2,4096]{1,0:T(2,128)} %param.11) | copy-start | bytes 98308
  0.0 3.1 %copy-start.1 = (bf16[256,14336]{1,0:T(8,128)(2,1)S(1)}, bf16[256,14336]{1,0:T(8,128)(2,1)}, u32[]{:S(2)}) copy-start(bf16[256,14336]{1,0:T(8,128)(2,1)} %h_ref.1) | copy-start | bytes 22020100
  3.1 1.6 %copy-start.2 = (bf16[256,4096]{1,0:T(8,128)(2,1)S(1)}, bf16[256,4096]{1,0:T(8,128)(2,1)}, u32[]{:S(2)}) copy-start(bf16[256,4096]{1,0:T(8,128)(2,1)} %g_ref.1) | copy-start | bytes 6291460
  4.7 1.5 %copy-start.3 = (bf16[14336,64]{0,1:T(8,128)(2,1)S(1)}, bf16[14336,64]{0,1:T(8,128)(2,1)}, u32[]{:S(2)}) copy-start(bf16[14336,64]{0,1:T(8,128)(2,1)} %param.8) | copy-start | bytes 5505028
  6.2 1.0 %copy-start.4 = (bf16[4096,64]{0,1:T(8,128)(2,1)S(1)}, bf16[4096,64]{0,1:T(8,128)(2,1)}, u32[]{:S(2)}) copy-start(bf16[4096,64]{0,1:T(8,128)(2,1)} %param.9) | copy-start | bytes 1572868
  7.2 7.9 %copy-start.5 = (s32[256]{0:T(256)S(1)}, s32[256]{0:T(256)}, u32[]{:S(2)}) copy-start(s32[256]{0:T(256)} %param.10) | copy-start | bytes 3076
  14.3 1.4 %collective-permute-start = (f32[128,128]{1,0:T(8,128)S(1)}, f32[128,128]{1,0:T(8,128)S(1)}, u32[]{:S(2)}, u32[]{:S(2)}) collective-permute-start(f32[128,128]{1,0:T(8,128)S(1)} %get-tuple-element.8), channel_id=1, source_target_pairs={{0,1},{1,0},{2,3},{3,2},{4,5},{5,4},{6,7},{7,6},{8,9},{9,8},{10,11... | collective-permute-start | bytes 196616 | tf_op jit(solution)/shard_map/ppermute | solution.py:235

commit v2 on v1

v2 whole, which is shorter than its diff:
```python
import functools

import jax
import jax.numpy as jnp
from jax import lax
from jax.experimental import pallas as pl
from jax.experimental.pallas import tpu as pltpu
from jax.sharding import PartitionSpec as P

TOK_DEV = 256
DOC_DEV = 8
LANES = 128
NT = (((1,), (1,)), ((), ()))
HIGHEST = lax.Precision.HIGHEST
VMEM = pl.BlockSpec(memory_space=pltpu.VMEM)
HBM = pl.BlockSpec(memory_space=pltpu.HBM)


def vmem_params(mib):
    return pltpu.CompilerParams(vmem_limit_bytes=mib << 20)


def chunks_of(length, most=1024):
    size = most
    while length % size:
        size //= 2
    return size, length // size


def project_kernel(sizes, h_ref, g_ref, pin_ref, pout_ref, keep_ref, send_ref, h_buf, g_buf, pin_buf, pout_buf, sems):
    h_size, h_count, g_size, g_count = sizes
    copies = {}
    slot = 0
    for name, src, dst in (("po", pout_ref, pout_buf), ("pi", pin_ref, pin_buf)):
        copies[name] = pltpu.make_async_copy(src, dst, sems.at[slot])
        slot += 1
    for i in range(g_count):
        at = pl.ds(i * g_size, g_size)
        copies["g", i] = pltpu.make_async_copy(g_ref.at[:, at], g_buf.at[:, at], sems.at[slot])
        slot += 1
    for i in range(h_count):
        at = pl.ds(i * h_size, h_size)
        copies["h", i] = pltpu.make_async_copy(h_ref.at[:, at], h_buf.at[:, at], sems.at[slot])
        slot += 1
    order = ["po"] + [("g", i) for i in range(g_count)] + ["pi"] + [("h", i) for i in range(h_count)]
    for name in order:
        copies[name].start()

    def run(tag, count, size, proj, data):
        total = None
        for i in range(count):
            copies[tag, i].wait()
            at = pl.ds(i * size, size)
            part = lax.dot_general(proj[:, at], data[:, at], NT, preferred_element_type=jnp.float32)
            total = part if total is None else total + part
        return total

    copies["po"].wait()
    grad = run("g", g_count, g_size, pout_buf, g_buf)
    copies["pi"].wait()
    inp = run("h", h_count, h_size, pin_buf, h_buf)
    both = jnp.concatenate([grad, inp], axis=0)
    half = both.shape[1] // 2
    first, second = both[:, :half], both[:, half:]
    lead = lax.axis_index("tensor") == 0
    keep_ref[...] = jnp.where(lead, first, second)
    send_ref[...] = jnp.where(lead, second, first)


def project(hidden, out_grad, pin_t, pout_t):
    tokens, units = hidden.shape
    width = out_grad.shape[1]
    ranks = pin_t.shape[0] + pout_t.shape[0]
    h_size, h_count = chunks_of(units)
    g_size, g_count = chunks_of(width)
    half = jax.ShapeDtypeStruct((ranks, tokens // 2), jnp.float32)
    return pl.pallas_call(
        functools.partial(project_kernel, (h_size, h_count, g_size, g_count)),
        out_shape=(half, half),
        in_specs=[HBM] * 4,
        out_specs=(VMEM, VMEM),
        scratch_shapes=[
            pltpu.VMEM(hidden.shape, hidden.dtype),
            pltpu.VMEM(out_grad.shape, out_grad.dtype),
            pltpu.VMEM(pin_t.shape, pin_t.dtype),
            pltpu.VMEM(pout_t.shape, pout_t.dtype),
            pltpu.SemaphoreType.DMA((2 + g_count + h_count,)),
        ],
        compiler_params=vmem_params(56),
        cost_estimate=pl.CostEstimate(
            flops=2 * tokens * 64 * (units + width),
            bytes_accessed=2 * (tokens + 64) * (units + width),
            transcendentals=0,
        ),
        name="project",
    )(hidden, out_grad, pin_t, pout_t)


def pack_kernel(pa, pb, keep_ref, recv_ref, extra_ref, *refs):
    outs, total_ref = refs[:-1], refs[-1]
    total_ref[...] = keep_ref[...] + recv_ref[...]
    ranks = total_ref.shape[0] // 2
    rows_a, rows_b = ranks // pa, ranks // pb
    me = lax.axis_index("dp")
    for m, out_ref in enumerate(outs):
        owner = me ^ m
        p, q = owner // pb, owner % pb
        out_ref[0:rows_a, :] = total_ref[pl.ds(pl.multiple_of(p * rows_a, rows_a), rows_a), :]
        out_ref[rows_a:rows_a + rows_b, :] = total_ref[pl.ds(pl.multiple_of(ranks + q * rows_b, rows_b), rows_b), :]
        out_ref[rows_a + rows_b:, :] = extra_ref[owner]


def pack(keep, recv, extra, pa, pb):
    ranks = keep.shape[0] // 2
    rows = ranks // pa + ranks // pb + extra.shape[1]
    out = jax.ShapeDtypeStruct((rows, keep.shape[1]), jnp.float32)
    return pl.pallas_call(
        functools.partial(pack_kernel, pa, pb),
        out_shape=(out,) * (pa * pb),
        in_specs=[VMEM] * 3,
        out_specs=(VMEM,) * (pa * pb),
        scratch_shapes=[pltpu.VMEM(keep.shape, jnp.float32)],
        compiler_params=vmem_params(16),
        name="pack",
    )(keep, recv, extra)


def grads_kernel(rows_a, rows_b, docs, *refs):
    xs, (keep_ref, send_ref, outer_ref, member_ref) = refs[:-4], refs[-4:]
    lanes = xs[0].shape[1]
    wide = rows_a * rows_b
    doc = lax.broadcasted_iota(jnp.int32, (docs, lanes), 0)
    source = lax.broadcasted_iota(jnp.int32, (len(xs), lanes), 0)
    queries = [jnp.zeros((len(xs), lanes), jnp.float32)] * (wide // lanes)
    first = rows_a + rows_b
    me = lax.axis_index("dp")
    for m, x_ref in enumerate(xs):
        at = slice(m * lanes, (m + 1) * lanes)
        g, b = x_ref[0:rows_a, :], x_ref[rows_a:first, :]
        ids = x_ref[first:first + 1, :].astype(jnp.int32)
        member_ref[:, at] = jnp.where(doc == ids, 1.0, 0.0).astype(jnp.bfloat16)
        outer = (g[:, None, :] * b[None, :, :]).reshape(wide, lanes)
        high = outer.astype(jnp.bfloat16)
        outer_ref[0:wide, at] = high
        outer_ref[wide:, at] = (outer - high.astype(jnp.float32)).astype(jnp.bfloat16)
        for j in range(wide // lanes):
            line = x_ref[first + 1 + j:first + 2 + j, :]
            queries[j] = jnp.where(source == (me ^ m), line, queries[j])
    sums = lax.dot_general(member_ref[...], outer_ref[...], NT, preferred_element_type=jnp.float32)
    grads = (sums[:, wide:] + sums[:, :wide]) * (TOK_DEV ** -0.5)
    lead = lax.axis_index("tensor") == 0
    half = wide // 2
    for part, at in ((grads, slice(0, docs)), (jnp.concatenate(queries, axis=1), slice(docs, docs + len(xs)))):
        keep_ref[at, :] = jnp.where(lead, part[:, :half], part[:, half:])
        send_ref[at, :] = jnp.where(lead, part[:, half:], part[:, :half])


def grads_of(xs, rows_a, rows_b, docs):
    lanes = xs[0].shape[1]
    wide = rows_a * rows_b
    out = jax.ShapeDtypeStruct((docs + len(xs), wide // 2), jnp.float32)
    return pl.pallas_call(
        functools.partial(grads_kernel, rows_a, rows_b, docs),
        out_shape=(out, out),
        in_specs=[VMEM] * len(xs),
        out_specs=(VMEM, VMEM),
        scratch_shapes=[
            pltpu.VMEM((2 * wide, len(xs) * lanes), jnp.bfloat16),
            pltpu.VMEM((docs, len(xs) * lanes), jnp.bfloat16),
        ],
        compiler_params=vmem_params(40),
        name="grads",
    )(*xs)


def gram_kernel(docs, keep_ref, recv_ref, out_ref):
    pairs = keep_ref.shape[0] - docs
    grads = keep_ref[0:docs, :] + recv_ref[0:docs, :]
    lead = lax.axis_index("tensor") == 0
    mine, other = keep_ref[docs:, :], recv_ref[docs:, :]
    even, odd = jnp.where(lead, mine, other), jnp.where(lead, other, mine)
    lines = [x[i:i + 1, :] for i in range(pairs) for x in (even, odd)]
    both = jnp.concatenate([grads] + lines, axis=0)
    share = lax.dot_general(both, grads, NT, precision=HIGHEST, preferred_element_type=jnp.float32)
    half = share.shape[0] // 2
    out_ref[...] = jnp.concatenate([share[:half], share[half:]], axis=1)


def gram(keep, recv, docs):
    rows = docs + 2 * (keep.shape[0] - docs)
    return pl.pallas_call(
        functools.partial(gram_kernel, docs),
        out_shape=jax.ShapeDtypeStruct((rows // 2, 2 * docs), jnp.float32),
        in_specs=[VMEM] * 2,
        out_specs=VMEM,
        compiler_params=vmem_params(16),
        name="gram",
    )(keep, recv)


def solve_kernel(docs, queries, scale, *refs):
    xs, out_ref, done_ref = refs[:-2], refs[-2], refs[-1]
    total = xs[0][...]
    for x_ref in xs[1:]:
        total = total + x_ref[...]
    stack = jnp.concatenate([total[:, :docs], total[:, docs:]], axis=0)
    cols = done_ref.shape[1]
    stack = jnp.concatenate([stack, jnp.zeros((cols - stack.shape[0], docs), jnp.float32)], axis=0)
    total = stack.T
    rows = docs
    row = lax.broadcasted_iota(jnp.int32, (rows, cols), 0)
    col = lax.broadcasted_iota(jnp.int32, (rows, cols), 1)
    mean_diag = jnp.sum(jnp.where(row == col, total, 0.0)) * (1.0 / docs)
    work = total + jnp.where(row == col, 0.1 * mean_diag, 0.0)
    here = lax.broadcasted_iota(jnp.int32, (rows, 1), 0)
    for k in range(docs):
        line = work[k:k + 1, :]
        inverse = 1.0 / line[:, k:k + 1]
        factor = jnp.where(here == k, 1.0 - inverse, work[:, k:k + 1] * inverse)
        work = work - factor * line
    done_ref[...] = work * (mean_diag * scale)
    mine = pl.ds(pl.multiple_of(lax.axis_index("dp") * DOC_DEV, DOC_DEV), DOC_DEV)
    out_ref[...] = done_ref[mine, :][:, docs:docs + queries]


def solve(xs, docs, queries, scale):
    return pl.pallas_call(
        functools.partial(solve_kernel, docs, queries, scale),
        out_shape=jax.ShapeDtypeStruct((DOC_DEV, queries), jnp.float32),
        in_specs=[VMEM] * len(xs),
        out_specs=VMEM,
        scratch_shapes=[pltpu.VMEM((docs, -(-(docs + queries) // LANES) * LANES), jnp.float32)],
        compiler_params=vmem_params(16),
        name="solve",
    )(*xs)


def solve_large(total, docs, queries, scale):
    kernel = total[:, :docs]
    mean_diag = jnp.trace(kernel) / docs
    factor = jnp.linalg.cholesky(kernel + 0.1 * mean_diag * jnp.eye(docs, dtype=jnp.float32))
    solved = jax.scipy.linalg.cho_solve((factor, True), total[:, docs:docs + queries]) * (mean_diag * scale)
    return lax.dynamic_slice_in_dim(solved, lax.axis_index("dp") * DOC_DEV, DOC_DEV, 0)


def swap_cores(x):
    cores = lax.axis_size("tensor")
    return lax.ppermute(x, "tensor", [(i, cores - 1 - i) for i in range(cores)])


def trade(xs):
    dp = lax.axis_size("dp")
    return [xs[0]] + [lax.ppermute(xs[m], "dp", [(i, i ^ m) for i in range(dp)]) for m in range(1, dp)]


def local(hidden, out_grad, proj_in, proj_out, doc_ids, queries):
    dp, tensor = lax.axis_size("dp"), lax.axis_size("tensor")
    docs, num_queries = DOC_DEV * dp, queries.shape[0] * dp
    ranks = proj_in.shape[1]
    pa = 1
    while pa * pa < dp:
        pa *= 2
    pb = dp // pa
    rows_a, rows_b = ranks // pa, ranks // pb
    wide = rows_a * rows_b
    core = lax.axis_index("tensor")

    keep, send = project(hidden, out_grad, proj_in.T, proj_out.T)
    recv = swap_cores(send)

    lanes = keep.shape[1]
    ids = lax.dynamic_slice_in_dim(doc_ids, core * lanes, lanes).astype(jnp.float32)
    query = lax.dynamic_slice_in_dim(queries, core, 1, 0).reshape(pa, rows_a, pb, rows_b)
    query = query.transpose(0, 2, 1, 3).reshape(dp, wide // lanes, lanes)
    extra = jnp.concatenate([jnp.broadcast_to(ids, (dp, 1, lanes)), query], axis=1)
    extra = jnp.pad(extra, ((0, 0), (0, -extra.shape[1] % 8), (0, 0)))

    blocks = trade(pack(keep, recv, extra, pa, pb))
    keep, send = grads_of(blocks, rows_a, rows_b, docs)
    share = gram(keep, swap_cores(send), docs)
    scale = float(ranks * ranks) ** -0.5
    if docs <= 64:
        share = share + swap_cores(share)
        return solve(trade([share] * dp), docs, num_queries, scale).T
    share = lax.psum(share, ("dp", "tensor"))
    return solve_large(jnp.concatenate([share[:, :docs], share[:, docs:]], axis=0).T, docs, num_queries, scale).T


def solution(mesh):
    return jax.shard_map(
        local,
        mesh=mesh,
        in_specs=(
            P(("groups", "dp"), "tensor"),
            P(("groups", "dp"), "tensor"),
            P("tensor", None),
            P("tensor", None),
            P(("groups", "dp")),
            P(("groups", "dp"), None),
        ),
        out_specs=P("groups", "dp"),
        check_vma=False,
    )
```

time: 59.8 us -> 52.9 us (0.88)
  blocking collectives: 35.7 us -> 0 us
  starting transfers between devices: 0.52 us -> 24.3 us
  waiting for transfers between devices: 0.45 us -> 11.8 us
  local copies, waits for them, and re-layouts: 7.54 us -> 1.1 us
    all_to_all x2 -> x0, blocking collectives: 35.7 us -> none  [the longest x1 18.2 us: local(): block = lax.all_to_all(block, all_axes, 0, 0, tiled=True)]
    ppermute x1 -> x17, starting transfers between devices: 0.52 us -> 24.3 us  [the longest x14 23.5 us: trade(): lax.ppermute(xs[m], 'dp', [(i, i ^ m) for i in range(dp)])]
    ppermute x1 -> x17, waiting for transfers between devices: 0.45 us -> 11.8 us  [the longest x14 8.82 us: trade(): lax.ppermute(xs[m], 'dp', [(i, i ^ m) for i in range(dp)])]
    unnamed x12 -> x6, local copies, waits for them, and re-layouts: 7.23 us -> 0.85 us
    pallas_call x1, Pallas kernels: 7.02 us -> 7.82 us  [project(): pl.pallas_call(functools.partial(project_kernel, (h_size, h_count, g_size...]
    pallas_call x2 -> x3, Pallas kernels: 1.92 us -> 1.24 us  [the longest x1 0.9 us: grads_of(): pl.pallas_call(functools.partial(grads_kernel, rows_a, rows_b, docs), out...]
  transfers between devices with their start and end apart: 1 -> 17, of which waited for: 1 -> 8; matrix products, arithmetic and copies ran while one was open for 1% -> 1% of each run, Pallas kernels for 0% -> 0%
where the time goes in v2:
time: 52.9 us; the launch traced here: 52.8 us
  starting transfers between devices  24.3 us (46%)
  Pallas kernels  15.3 us (29%)
  waiting for transfers between devices  11.8 us (22%)
  local copies, waits for them, and re-layouts  1.1 us (2%)
    ppermute x14, starting transfers between devices, trade(): lax.ppermute(xs[m], 'dp', [(i, i ^ m) for i in range(dp)])  23.5 us
    ppermute x14, waiting for transfers between devices, trade(): lax.ppermute(xs[m], 'dp', [(i, i ^ m) for i in range(dp)])  8.82 us
    pallas_call x1, Pallas kernels, project(): pl.pallas_call(functools.partial(project_kernel, (h_size, h_count, g_size...  7.82 us
    pallas_call x1, Pallas kernels, solve(): pl.pallas_call(functools.partial(solve_kernel, docs, queries, scale), out...  6.29 us
    ppermute x3, waiting for transfers between devices, swap_cores(): return lax.ppermute(x, 'tensor', [(i, cores - 1 - i) for i in range(cores)])  3.01 us
  transfers between devices with their start and end apart: 17, of which 8 were waited for; matrix products, arithmetic and copies ran while one was open for 1% of the time, Pallas kernels for 0%

profile of v2, /device:TPU:0, one launch (start us, length us, event | category | flops | bytes accessed | tf_op | source)
XLA Modules:
  0.0 52.8 jit_solution(15600656590187751886)
XLA Ops:
  0.0 0.0 copy-start
  0.0 0.0 copy-start.2
  0.0 7.8 %project.1 = (f32[128,128]{1,0:T(8,128)}, f32[128,128]{1,0:T(8,128)}) custom-call(bf16[256,14336]{1,0:T(8,128)(2,1)} %h_ref.1, bf16[256,4096]{1,0:T(8,128)(2,1)} %g_ref.1, bf16[64,14336]{1,0:T(8,128)(2,1)} %bitcast.6, bf16[64,4096]{1,0:T(8,128)(2,1)} %bitcast.7), custom_call_target="tpu_custom_call" | custom-call | flops 603979776 | bytes 11796480 | tf_op jit(solution)/shard_map/project/pallas_call | solution.py:77
  7.8 0.5 collective-permute-start
  8.3 0.0 copy-done
  8.4 0.1 reshape.6
  8.5 0.1 reshape.7
  8.6 0.0 copy-done.2
  8.6 0.1 dynamic-slice_convert_fusion
  8.7 0.7 %collective-permute-done.recv_ref = f32[128,128]{1,0:T(8,128)S(1)} collective-permute-done((f32[128,128]{1,0:T(8,128)}, f32[128,128]{1,0:T(8,128)S(1)}, u32[]{:S(2)}, u32[]{:S(2)}) %collective-permute-start) | collective-permute-done | bytes 65568 | tf_op jit(solution)/shard_map/ppermute | solution.py:248
  9.5 0.0 copy-start.1
  9.5 0.8 %copy-done.1 = f32[128,128]{1,0:T(8,128)S(1)} copy-done((f32[128,128]{1,0:T(8,128)S(1)}, f32[128,128]{1,0:T(8,128)}, u32[]{:S(2)}) %copy-start.1) | copy-done | bytes 65560
  10.3 0.1 pack.1
  10.4 2.9 %collective-permute-start.1 = (f32[56,128]{1,0:T(8,128)S(1)}, f32[56,128]{1,0:T(8,128)S(1)}, u32[]{:S(2)}, u32[]{:S(2)}) collective-permute-start(f32[56,128]{1,0:T(8,128)S(1)} %get-tuple-element.20), channel_id=1, source_target_pairs={{0,2},{2,0},{4,6},{6,4},{8,10},{10,8},{12,14},{14,12},{1,3},{3,1},... | collective-permute-start | bytes 86024 | tf_op jit(solution)/shard_map/ppermute | solution.py:253
  13.3 1.6 %collective-permute-start.2 = (f32[56,128]{1,0:T(8,128)S(1)}, f32[56,128]{1,0:T(8,128)S(1)}, u32[]{:S(2)}, u32[]{:S(2)}) collective-permute-start(f32[56,128]{1,0:T(8,128)S(1)} %get-tuple-element.21), channel_id=1, source_target_pairs={{0,4},{2,6},{4,0},{6,2},{8,12},{10,14},{12,8},{14,10},{1,5},{3,7},... | collective-permute-start | bytes 86024 | tf_op jit(solution)/shard_map/ppermute | solution.py:253
  14.9 0.0 collective-permute-start.3
  14.9 3.0 %collective-permute-start.4 = (f32[56,128]{1,0:T(8,128)S(1)}, f32[56,128]{1,0:T(8,128)S(1)}, u32[]{:S(2)}, u32[]{:S(2)}) collective-permute-start(f32[56,128]{1,0:T(8,128)S(1)} %get-tuple-element.23), channel_id=1, source_target_pairs={{0,8},{2,10},{4,12},{6,14},{8,0},{10,2},{12,4},{14,6},{1,9},{3,11}... | collective-permute-start | bytes 86024 | tf_op jit(solution)/shard_map/ppermute | solution.py:253
  17.9 1.3 %collective-permute-start.5 = (f32[56,128]{1,0:T(8,128)S(1)}, f32[56,128]{1,0:T(8,128)S(1)}, u32[]{:S(2)}, u32[]{:S(2)}) collective-permute-start(f32[56,128]{1,0:T(8,128)S(1)} %get-tuple-element.24), channel_id=1, source_target_pairs={{0,10},{2,8},{4,14},{6,12},{8,2},{10,0},{12,6},{14,4},{1,11},{3,9}... | collective-permute-start | bytes 86024 | tf_op jit(solution)/shard_map/ppermute | solution.py:253
  19.2 0.0 collective-permute-done.1.refs_1_
  19.2 3.6 %collective-permute-start.6 = (f32[56,128]{1,0:T(8,128)S(1)}, f32[56,128]{1,0:T(8,128)S(1)}, u32[]{:S(2)}, u32[]{:S(2)}) collective-permute-start(f32[56,128]{1,0:T(8,128)S(1)} %get-tuple-element.25), channel_id=1, source_target_pairs={{0,12},{2,14},{4,8},{6,10},{8,4},{10,6},{12,0},{14,2},{1,13},{3,15... | collective-permute-start | bytes 86024 | tf_op jit(solution)/shard_map/ppermute | solution.py:253
  22.8 0.0 collective-permute-done.2.refs_2_
  22.8 0.0 collective-permute-start.7
  22.8 0.0 collective-permute-done.3.refs_3_
  22.8 0.0 collective-permute-done.4.refs_4_
  22.8 0.7 %collective-permute-done.5.refs_5_ = f32[56,128]{1,0:T(8,128)S(1)} collective-permute-done((f32[56,128]{1,0:T(8,128)S(1)}, f32[56,128]{1,0:T(8,128)S(1)}, u32[]{:S(2)}, u32[]{:S(2)}) %collective-permute-start.5) | collective-permute-done | bytes 28704 | tf_op jit(solution)/shard_map/ppermute | solution.py:253
  23.5 1.4 %collective-permute-done.6.refs_6_ = f32[56,128]{1,0:T(8,128)S(1)} collective-permute-done((f32[56,128]{1,0:T(8,128)S(1)}, f32[56,128]{1,0:T(8,128)S(1)}, u32[]{:S(2)}, u32[]{:S(2)}) %collective-permute-start.6) | collective-permute-done | bytes 28704 | tf_op jit(solution)/shard_map/ppermute | solution.py:253
  24.9 4.4 %collective-permute-done.7.refs_7_ = f32[56,128]{1,0:T(8,128)S(1)} collective-permute-done((f32[56,128]{1,0:T(8,128)S(1)}, f32[56,128]{1,0:T(8,128)S(1)}, u32[]{:S(2)}, u32[]{:S(2)}) %collective-permute-start.7) | collective-permute-done | bytes 28704 | tf_op jit(solution)/shard_map/ppermute | solution.py:253
  29.3 0.9 %grads.1 = (f32[72,256]{1,0:T(8,128)S(1)}, f32[72,256]{1,0:T(8,128)S(1)}) custom-call(f32[56,128]{1,0:T(8,128)S(1)} %get-tuple-element.19.refs_0_, f32[56,128]{1,0:T(8,128)S(1)} %collective-permute-done.1.refs_1_, f32[56,128]{1,0:T(8,128)S(1)} %collective-permute-done.2.refs_2_, f32[56,128]{1,0:T(8,128)S(1)} %collective-permute-done.3.refs_3_, ...), custom_call_target="tpu_custom_call" | custom-call | tf_op jit(solution)/shard_map/grads/pallas_call | solution.py:162
  30.2 0.1 collective-permute-start.8
  30.3 1.3 %collective-permute-done.8.recv_ref = f32[72,256]{1,0:T(8,128)S(1)} collective-permute-done((f32[72,256]{1,0:T(8,128)S(1)}, f32[72,256]{1,0:T(8,128)S(1)}, u32[]{:S(2)}, u32[]{:S(2)}) %collective-permute-start.8) | collective-permute-done | bytes 73760 | tf_op jit(solution)/shard_map/ppermute | solution.py:248
  31.6 0.3 gram.1
  31.8 0.2 collective-permute-start.9
  32.0 1.0 %collective-permute-done.9 = f32[40,128]{1,0:T(8,128)S(1)} collective-permute-done((f32[40,128]{1,0:T(8,128)S(1)}, f32[40,128]{1,0:T(8,128)S(1)}, u32[]{:S(2)}, u32[]{:S(2)}) %collective-permute-start.9) | collective-permute-done | bytes 20512 | tf_op jit(solution)/shard_map/ppermute | solution.py:248
  33.1 0.3 collective-permute-start.16
  33.4 3.5 %collective-permute-start.15 = (f32[40,128]{1,0:T(8,128)S(1)}, f32[40,128]{1,0:T(8,128)S(1)}, u32[]{:S(2)}, u32[]{:S(2)}) collective-permute-start(f32[40,128]{1,0:T(8,128)S(1)} %add.13.refs_0_), channel_id=1, source_target_pairs={{0,12},{2,14},{4,8},{6,10},{8,4},{10,6},{12,0},{14,2},{1,13},{3,15... | collective-permute-start | bytes 61448 | tf_op jit(solution)/shard_map/ppermute | solution.py:253
  36.8 0.0 collective-permute-start.14
  36.8 3.9 %collective-permute-start.13 = (f32[40,128]{1,0:T(8,128)S(1)}, f32[40,128]{1,0:T(8,128)S(1)}, u32[]{:S(2)}, u32[]{:S(2)}) collective-permute-start(f32[40,128]{1,0:T(8,128)S(1)} %add.13.refs_0_), channel_id=1, source_target_pairs={{0,8},{2,10},{4,12},{6,14},{8,0},{10,2},{12,4},{14,6},{1,9},{3,11}... | collective-permute-start | bytes 61448 | tf_op jit(solution)/shard_map/ppermute | solution.py:253
  40.7 0.0 collective-permute-start.12
  40.7 0.0 collective-permute-done.16.refs_7_
  40.7 2.0 %collective-permute-start.11 = (f32[40,128]{1,0:T(8,128)S(1)}, f32[40,128]{1,0:T(8,128)S(1)}, u32[]{:S(2)}, u32[]{:S(2)}) collective-permute-start(f32[40,128]{1,0:T(8,128)S(1)} %add.13.refs_0_), channel_id=1, source_target_pairs={{0,4},{2,6},{4,0},{6,2},{8,12},{10,14},{12,8},{14,10},{1,5},{3,7},... | collective-permute-start | bytes 61448 | tf_op jit(solution)/shard_map/ppermute | solution.py:253
  42.7 0.0 collective-permute-done.15.refs_6_
  42.7 1.5 %collective-permute-start.10 = (f32[40,128]{1,0:T(8,128)S(1)}, f32[40,128]{1,0:T(8,128)S(1)}, u32[]{:S(2)}, u32[]{:S(2)}) collective-permute-start(f32[40,128]{1,0:T(8,128)S(1)} %add.13.refs_0_), channel_id=1, source_target_pairs={{0,2},{2,0},{4,6},{6,4},{8,10},{10,8},{12,14},{14,12},{1,3},{3,1},... | collective-permute-start | bytes 61448 | tf_op jit(solution)/shard_map/ppermute | solution.py:253
  44.2 0.0 collective-permute-done.14.refs_5_
  44.2 0.0 collective-permute-done.13.refs_4_
  44.2 1.2 %collective-permute-done.12.refs_3_ = f32[40,128]{1,0:T(8,128)S(1)} collective-permute-done((f32[40,128]{1,0:T(8,128)S(1)}, f32[40,128]{1,0:T(8,128)S(1)}, u32[]{:S(2)}, u32[]{:S(2)}) %collective-permute-start.12) | collective-permute-done | bytes 20512 | tf_op jit(solution)/shard_map/ppermute | solution.py:253
  45.4 0.0 collective-permute-done.11.refs_2_
  45.4 1.1 %collective-permute-done.10.refs_1_ = f32[40,128]{1,0:T(8,128)S(1)} collective-permute-done((f32[40,128]{1,0:T(8,128)S(1)}, f32[40,128]{1,0:T(8,128)S(1)}, u32[]{:S(2)}, u32[]{:S(2)}) %collective-permute-start.10) | collective-permute-done | bytes 20512 | tf_op jit(solution)/shard_map/ppermute | solution.py:253
  46.5 6.3 %solve.1 = f32[8,16]{1,0:T(8,128)} custom-call(f32[40,128]{1,0:T(8,128)S(1)} %add.13.refs_0_, f32[40,128]{1,0:T(8,128)S(1)} %collective-permute-done.10.refs_1_, f32[40,128]{1,0:T(8,128)S(1)} %collective-permute-done.11.refs_2_, f32[40,128]{1,0:T(8,128)S(1)} %collective-permute-done.12.refs_3_, f32[40,128]{1,0:T(8,128)S(1)} %collective-permute-done.13.refs_4_, ...), custom_call_target="tpu_custom_call" | custom-call | tf_op jit(solution)/shard_map/solve/pallas_call | solution.py:227
  (5 shorter events, 0.1 us)
Async XLA Ops:
  0.0 8.4 %copy-start = (f32[2,4096]{1,0:T(2,128)S(1)}, f32[2,4096]{1,0:T(2,128)}, u32[]{:S(2)}) copy-start(f32[2,4096]{1,0:T(2,128)} %param.11) | copy-start | bytes 98308
  0.0 8.6 %copy-start.2 = (s32[256]{0:T(256)S(1)}, s32[256]{0:T(256)}, u32[]{:S(2)}) copy-start(s32[256]{0:T(256)} %param.10) | copy-start | bytes 3076
  7.8 1.6 %collective-permute-start = (f32[128,128]{1,0:T(8,128)}, f32[128,128]{1,0:T(8,128)S(1)}, u32[]{:S(2)}, u32[]{:S(2)}) collective-permute-start(f32[128,128]{1,0:T(8,128)} %get-tuple-element.18), channel_id=1, source_target_pairs={{0,1},{1,0},{2,3},{3,2},{4,5},{5,4},{6,7},{7,6},{8,9},{9,8},{10,11... | collective-permute-start | bytes 196616 | tf_op jit(solution)/shard_map/ppermute | solution.py:248
  9.5 0.8 %copy-start.1 = (f32[128,128]{1,0:T(8,128)S(1)}, f32[128,128]{1,0:T(8,128)}, u32[]{:S(2)}) copy-start(f32[128,128]{1,0:T(8,128)} %get-tuple-element.17.keep_ref) | copy-start | bytes 196612
  10.4 8.8 %collective-permute-start.1 = (f32[56,128]{1,0:T(8,128)S(1)}, f32[56,128]{1,0:T(8,128)S(1)}, u32[]{:S(2)}, u32[]{:S(2)}) collective-permute-start(f32[56,128]{1,0:T(8,128)S(1)} %get-tuple-element.20), channel_id=1, source_target_pairs={{0,2},{2,0},{4,6},{6,4},{8,10},{10,8},{12,14},{14,12},{1,3},{3,1},... | collective-permute-start | bytes 86024 | tf_op jit(solution)/shard_map/ppermute | solution.py:253
  13.3 9.5 %collective-permute-start.2 = (f32[56,128]{1,0:T(8,128)S(1)}, f32[56,128]{1,0:T(8,128)S(1)}, u32[]{:S(2)}, u32[]{:S(2)}) collective-permute-start(f32[56,128]{1,0:T(8,128)S(1)} %get-tuple-element.21), channel_id=1, source_target_pairs={{0,4},{2,6},{4,0},{6,2},{8,12},{10,14},{12,8},{14,10},{1,5},{3,7},... | collective-permute-start | bytes 86024 | tf_op jit(solution)/shard_map/ppermute | solution.py:253
  14.9 7.9 %collective-permute-start.3 = (f32[56,128]{1,0:T(8,128)S(1)}, f32[56,128]{1,0:T(8,128)S(1)}, u32[]{:S(2)}, u32[]{:S(2)}) collective-permute-start(f32[56,128]{1,0:T(8,128)S(1)} %get-tuple-element.22), channel_id=1, source_target_pairs={{0,6},{2,4},{4,2},{6,0},{8,14},{10,12},{12,10},{14,8},{1,7},{3,5},... | collective-permute-start | bytes 86024 | tf_op jit(solution)/shard_map/ppermute | solution.py:253
  14.9 7.9 %collective-permute-start.4 = (f32[56,128]{1,0:T(8,128)S(1)}, f32[56,128]{1,0:T(8,128)S(1)}, u32[]{:S(2)}, u32[]{:S(2)}) collective-permute-start(f32[56,128]{1,0:T(8,128)S(1)} %get-tuple-element.23), channel_id=1, source_target_pairs={{0,8},{2,10},{4,12},{6,14},{8,0},{10,2},{12,4},{14,6},{1,9},{3,11}... | collective-permute-start | bytes 86024 | tf_op jit(solution)/shard_map/ppermute | solution.py:253
  17.9 5.7 %collective-permute-start.5 = (f32[56,128]{1,0:T(8,128)S(1)}, f32[56,128]{1,0:T(8,128)S(1)}, u32[]{:S(2)}, u32[]{:S(2)}) collective-permute-start(f32[56,128]{1,0:T(8,128)S(1)} %get-tuple-element.24), channel_id=1, source_target_pairs={{0,10},{2,8},{4,14},{6,12},{8,2},{10,0},{12,6},{14,4},{1,11},{3,9}... | collective-permute-start | bytes 86024 | tf_op jit(solution)/shard_map/ppermute | solution.py:253
  19.2 5.7 %collective-permute-start.6 = (f32[56,128]{1,0:T(8,128)S(1)}, f32[56,128]{1,0:T(8,128)S(1)}, u32[]{:S(2)}, u32[]{:S(2)}) collective-permute-start(f32[56,128]{1,0:T(8,128)S(1)} %get-tuple-element.25), channel_id=1, source_target_pairs={{0,12},{2,14},{4,8},{6,10},{8,4},{10,6},{12,0},{14,2},{1,13},{3,15... | collective-permute-start | bytes 86024 | tf_op jit(solution)/shard_map/ppermute | solution.py:253
  22.8 6.6 %collective-permute-start.7 = (f32[56,128]{1,0:T(8,128)S(1)}, f32[56,128]{1,0:T(8,128)S(1)}, u32[]{:S(2)}, u32[]{:S(2)}) collective-permute-start(f32[56,128]{1,0:T(8,128)S(1)} %get-tuple-element.26), channel_id=1, source_target_pairs={{0,14},{2,12},{4,10},{6,8},{8,6},{10,4},{12,2},{14,0},{1,15},{3,13... | collective-permute-start | bytes 86024 | tf_op jit(solution)/shard_map/ppermute | solution.py:253
  30.2 1.3 %collective-permute-start.8 = (f32[72,256]{1,0:T(8,128)S(1)}, f32[72,256]{1,0:T(8,128)S(1)}, u32[]{:S(2)}, u32[]{:S(2)}) collective-permute-start(f32[72,256]{1,0:T(8,128)S(1)} %get-tuple-element.28), channel_id=1, source_target_pairs={{0,1},{1,0},{2,3},{3,2},{4,5},{5,4},{6,7},{7,6},{8,9},{9,8},{10,11... | collective-permute-start | bytes 221192 | tf_op jit(solution)/shard_map/ppermute | solution.py:248
  31.8 1.2 %collective-permute-start.9 = (f32[40,128]{1,0:T(8,128)S(1)}, f32[40,128]{1,0:T(8,128)S(1)}, u32[]{:S(2)}, u32[]{:S(2)}) collective-permute-start(f32[40,128]{1,0:T(8,128)S(1)} %gram.1), channel_id=1, source_target_pairs={{0,1},{1,0},{2,3},{3,2},{4,5},{5,4},{6,7},{7,6},{8,9},{9,8},{10,11... | collective-permute-start | bytes 61448 | tf_op jit(solution)/shard_map/ppermute | solution.py:248
  33.1 7.7 %collective-permute-start.16 = (f32[40,128]{1,0:T(8,128)S(1)}, f32[40,128]{1,0:T(8,128)S(1)}, u32[]{:S(2)}, u32[]{:S(2)}) collective-permute-start(f32[40,128]{1,0:T(8,128)S(1)} %add.13.refs_0_), channel_id=1, source_target_pairs={{0,14},{2,12},{4,10},{6,8},{8,6},{10,4},{12,2},{14,0},{1,15},{3,13... | collective-permute-start | bytes 61448 | tf_op jit(solution)/shard_map/ppermute | solution.py:253
  33.4 9.3 %collective-permute-start.15 = (f32[40,128]{1,0:T(8,128)S(1)}, f32[40,128]{1,0:T(8,128)S(1)}, u32[]{:S(2)}, u32[]{:S(2)}) collective-permute-start(f32[40,128]{1,0:T(8,128)S(1)} %add.13.refs_0_), channel_id=1, source_target_pairs={{0,12},{2,14},{4,8},{6,10},{8,4},{10,6},{12,0},{14,2},{1,13},{3,15... | collective-permute-start | bytes 61448 | tf_op jit(solution)/shard_map/ppermute | solution.py:253
  36.8 7.4 %collective-permute-start.14 = (f32[40,128]{1,0:T(8,128)S(1)}, f32[40,128]{1,0:T(8,128)S(1)}, u32[]{:S(2)}, u32[]{:S(2)}) collective-permute-start(f32[40,128]{1,0:T(8,128)S(1)} %add.13.refs_0_), channel_id=1, source_target_pairs={{0,10},{2,8},{4,14},{6,12},{8,2},{10,0},{12,6},{14,4},{1,11},{3,9}... | collective-permute-start | bytes 61448 | tf_op jit(solution)/shard_map/ppermute | solution.py:253
  36.8 7.4 %collective-permute-start.13 = (f32[40,128]{1,0:T(8,128)S(1)}, f32[40,128]{1,0:T(8,128)S(1)}, u32[]{:S(2)}, u32[]{:S(2)}) collective-permute-start(f32[40,128]{1,0:T(8,128)S(1)} %add.13.refs_0_), channel_id=1, source_target_pairs={{0,8},{2,10},{4,12},{6,14},{8,0},{10,2},{12,4},{14,6},{1,9},{3,11}... | collective-permute-start | bytes 61448 | tf_op jit(solution)/shard_map/ppermute | solution.py:253
  40.7 4.7 %collective-permute-start.12 = (f32[40,128]{1,0:T(8,128)S(1)}, f32[40,128]{1,0:T(8,128)S(1)}, u32[]{:S(2)}, u32[]{:S(2)}) collective-permute-start(f32[40,128]{1,0:T(8,128)S(1)} %add.13.refs_0_), channel_id=1, source_target_pairs={{0,6},{2,4},{4,2},{6,0},{8,14},{10,12},{12,10},{14,8},{1,7},{3,5},... | collective-permute-start | bytes 61448 | tf_op jit(solution)/shard_map/ppermute | solution.py:253
  40.7 4.7 %collective-permute-start.11 = (f32[40,128]{1,0:T(8,128)S(1)}, f32[40,128]{1,0:T(8,128)S(1)}, u32[]{:S(2)}, u32[]{:S(2)}) collective-permute-start(f32[40,128]{1,0:T(8,128)S(1)} %add.13.refs_0_), channel_id=1, source_target_pairs={{0,4},{2,6},{4,0},{6,2},{8,12},{10,14},{12,8},{14,10},{1,5},{3,7},... | collective-permute-start | bytes 61448 | tf_op jit(solution)/shard_map/ppermute | solution.py:253
  42.7 3.8 %collective-permute-start.10 = (f32[40,128]{1,0:T(8,128)S(1)}, f32[40,128]{1,0:T(8,128)S(1)}, u32[]{:S(2)}, u32[]{:S(2)}) collective-permute-start(f32[40,128]{1,0:T(8,128)S(1)} %add.13.refs_0_), channel_id=1, source_target_pairs={{0,2},{2,0},{4,6},{6,4},{8,10},{10,8},{12,14},{14,12},{1,3},{3,1},... | collective-permute-start | bytes 61448 | tf_op jit(solution)/shard_map/ppermute | solution.py:253

commit v3 on v2

--- a/solution.py
+++ b/solution.py
@@ -51,7 +51,7 @@
         for i in range(count):
             copies[tag, i].wait()
             at = pl.ds(i * size, size)
-            part = lax.dot_general(proj[:, at], data[:, at], NT, preferred_element_type=jnp.float32)
+            part = lax.dot_general(data[:, at], proj[:, at], NT, preferred_element_type=jnp.float32)
             total = part if total is None else total + part
         return total
 
@@ -59,7 +59,7 @@
     grad = run("g", g_count, g_size, pout_buf, g_buf)
     copies["pi"].wait()
     inp = run("h", h_count, h_size, pin_buf, h_buf)
-    both = jnp.concatenate([grad, inp], axis=0)
+    both = jnp.concatenate([grad, inp], axis=1).T
     half = both.shape[1] // 2
     first, second = both[:, :half], both[:, half:]
     lead = lax.axis_index("tensor") == 0
@@ -96,81 +96,70 @@
     )(hidden, out_grad, pin_t, pout_t)
 
 
-def pack_kernel(pa, pb, keep_ref, recv_ref, extra_ref, *refs):
-    outs, total_ref = refs[:-1], refs[-1]
-    total_ref[...] = keep_ref[...] + recv_ref[...]
-    ranks = total_ref.shape[0] // 2
-    rows_a, rows_b = ranks // pa, ranks // pb
-    me = lax.axis_index("dp")
-    for m, out_ref in enumerate(outs):
-        owner = me ^ m
+def pack_kernel(pb, rows_a, rows_b, keep_ref, recv_ref, extra_ref, out_ref):
+    total = keep_ref[...] + recv_ref[...]
+    ranks = total.shape[0] // 2
+    for owner in range(out_ref.shape[0]):
         p, q = owner // pb, owner % pb
-        out_ref[0:rows_a, :] = total_ref[pl.ds(pl.multiple_of(p * rows_a, rows_a), rows_a), :]
-        out_ref[rows_a:rows_a + rows_b, :] = total_ref[pl.ds(pl.multiple_of(ranks + q * rows_b, rows_b), rows_b), :]
-        out_ref[rows_a + rows_b:, :] = extra_ref[owner]
+        out_ref[owner, 0:rows_a, :] = total[p * rows_a:(p + 1) * rows_a, :]
+        out_ref[owner, rows_a:rows_a + rows_b, :] = total[ranks + q * rows_b:ranks + (q + 1) * rows_b, :]
+        out_ref[owner, rows_a + rows_b:, :] = extra_ref[owner]
 
 
 def pack(keep, recv, extra, pa, pb):
     ranks = keep.shape[0] // 2
-    rows = ranks // pa + ranks // pb + extra.shape[1]
-    out = jax.ShapeDtypeStruct((rows, keep.shape[1]), jnp.float32)
-    return pl.pallas_call(
-        functools.partial(pack_kernel, pa, pb),
-        out_shape=(out,) * (pa * pb),
+    rows_a, rows_b = ranks // pa, ranks // pb
+    rows = rows_a + rows_b + extra.shape[1]
+    return pl.pallas_call(
+        functools.partial(pack_kernel, pb, rows_a, rows_b),
+        out_shape=jax.ShapeDtypeStruct((pa * pb, rows, keep.shape[1]), jnp.float32),
         in_specs=[VMEM] * 3,
-        out_specs=(VMEM,) * (pa * pb),
-        scratch_shapes=[pltpu.VMEM(keep.shape, jnp.float32)],
+        out_specs=VMEM,
         compiler_params=vmem_params(16),
         name="pack",
     )(keep, recv, extra)
 
 
-def grads_kernel(rows_a, rows_b, docs, *refs):
-    xs, (keep_ref, send_ref, outer_ref, member_ref) = refs[:-4], refs[-4:]
-    lanes = xs[0].shape[1]
+def grads_kernel(rows_a, rows_b, docs, x_ref, keep_ref, send_ref, outer_ref, member_ref):
+    sources, _, lanes = x_ref.shape
     wide = rows_a * rows_b
     doc = lax.broadcasted_iota(jnp.int32, (docs, lanes), 0)
-    source = lax.broadcasted_iota(jnp.int32, (len(xs), lanes), 0)
-    queries = [jnp.zeros((len(xs), lanes), jnp.float32)] * (wide // lanes)
     first = rows_a + rows_b
-    me = lax.axis_index("dp")
-    for m, x_ref in enumerate(xs):
-        at = slice(m * lanes, (m + 1) * lanes)
-        g, b = x_ref[0:rows_a, :], x_ref[rows_a:first, :]
-        ids = x_ref[first:first + 1, :].astype(jnp.int32)
+    for s in range(sources):
+        at = slice(s * lanes, (s + 1) * lanes)
+        g, b = x_ref[s, 0:rows_a, :], x_ref[s, rows_a:first, :]
+        ids = x_ref[s, first:first + 1, :].astype(jnp.int32)
         member_ref[:, at] = jnp.where(doc == ids, 1.0, 0.0).astype(jnp.bfloat16)
         outer = (g[:, None, :] * b[None, :, :]).reshape(wide, lanes)
         high = outer.astype(jnp.bfloat16)
         outer_ref[0:wide, at] = high
         outer_ref[wide:, at] = (outer - high.astype(jnp.float32)).astype(jnp.bfloat16)
-        for j in range(wide // lanes):
-            line = x_ref[first + 1 + j:first + 2 + j, :]
-            queries[j] = jnp.where(source == (me ^ m), line, queries[j])
+    queries = [x_ref[:, first + 1 + j, :] for j in range(wide // lanes)]
     sums = lax.dot_general(member_ref[...], outer_ref[...], NT, preferred_element_type=jnp.float32)
     grads = (sums[:, wide:] + sums[:, :wide]) * (TOK_DEV ** -0.5)
     lead = lax.axis_index("tensor") == 0
     half = wide // 2
-    for part, at in ((grads, slice(0, docs)), (jnp.concatenate(queries, axis=1), slice(docs, docs + len(xs)))):
+    for part, at in ((grads, slice(0, docs)), (jnp.concatenate(queries, axis=1), slice(docs, docs + sources))):
         keep_ref[at, :] = jnp.where(lead, part[:, :half], part[:, half:])
         send_ref[at, :] = jnp.where(lead, part[:, half:], part[:, :half])
 
 
-def grads_of(xs, rows_a, rows_b, docs):
-    lanes = xs[0].shape[1]
+def grads_of(x, rows_a, rows_b, docs):
+    sources, _, lanes = x.shape
     wide = rows_a * rows_b
-    out = jax.ShapeDtypeStruct((docs + len(xs), wide // 2), jnp.float32)
+    out = jax.ShapeDtypeStruct((docs + sources, wide // 2), jnp.float32)
     return pl.pallas_call(
         functools.partial(grads_kernel, rows_a, rows_b, docs),
         out_shape=(out, out),
-        in_specs=[VMEM] * len(xs),
+        in_specs=[VMEM],
         out_specs=(VMEM, VMEM),
         scratch_shapes=[
-            pltpu.VMEM((2 * wide, len(xs) * lanes), jnp.bfloat16),
-            pltpu.VMEM((docs, len(xs) * lanes), jnp.bfloat16),
+            pltpu.VMEM((2 * wide, sources * lanes), jnp.bfloat16),
+            pltpu.VMEM((docs, sources * lanes), jnp.bfloat16),
         ],
         compiler_params=vmem_params(40),
         name="grads",
-    )(*xs)
+    )(x)
 
 
 def gram_kernel(docs, keep_ref, recv_ref, out_ref):
@@ -198,11 +187,8 @@
     )(keep, recv)
 
 
-def solve_kernel(docs, queries, scale, *refs):
-    xs, out_ref, done_ref = refs[:-2], refs[-2], refs[-1]
-    total = xs[0][...]
-    for x_ref in xs[1:]:
-        total = total + x_ref[...]
+def solve_kernel(docs, queries, scale, x_ref, recv_ref, out_ref, done_ref):
+    total = x_ref[...] + recv_ref[...]
     stack = jnp.concatenate([total[:, :docs], total[:, docs:]], axis=0)
     cols = done_ref.shape[1]
     stack = jnp.concatenate([stack, jnp.zeros((cols - stack.shape[0], docs), jnp.float32)], axis=0)
@@ -223,16 +209,16 @@
     out_ref[...] = done_ref[mine, :][:, docs:docs + queries]
 
 
-def solve(xs, docs, queries, scale):
+def solve(x, recv, docs, queries, scale):
     return pl.pallas_call(
         functools.partial(solve_kernel, docs, queries, scale),
         out_shape=jax.ShapeDtypeStruct((DOC_DEV, queries), jnp.float32),
-        in_specs=[VMEM] * len(xs),
+        in_specs=[VMEM] * 2,
         out_specs=VMEM,
         scratch_shapes=[pltpu.VMEM((docs, -(-(docs + queries) // LANES) * LANES), jnp.float32)],
         compiler_params=vmem_params(16),
         name="solve",
-    )(*xs)
+    )(x, recv)
 
 
 def solve_large(total, docs, queries, scale):
@@ -248,9 +234,8 @@
     return lax.ppermute(x, "tensor", [(i, cores - 1 - i) for i in range(cores)])
 
 
-def trade(xs):
-    dp = lax.axis_size("dp")
-    return [xs[0]] + [lax.ppermute(xs[m], "dp", [(i, i ^ m) for i in range(dp)]) for m in range(1, dp)]
+def swap_dp(x, m):
+    return lax.ppermute(x, "dp", [(i, i ^ m) for i in range(lax.axis_size("dp"))])
 
 
 def local(hidden, out_grad, proj_in, proj_out, doc_ids, queries):
@@ -275,13 +260,17 @@
     extra = jnp.concatenate([jnp.broadcast_to(ids, (dp, 1, lanes)), query], axis=1)
     extra = jnp.pad(extra, ((0, 0), (0, -extra.shape[1] % 8), (0, 0)))
 
-    blocks = trade(pack(keep, recv, extra, pa, pb))
+    blocks = lax.all_to_all(pack(keep, recv, extra, pa, pb), "dp", 0, 0, tiled=True)
     keep, send = grads_of(blocks, rows_a, rows_b, docs)
     share = gram(keep, swap_cores(send), docs)
     scale = float(ranks * ranks) ** -0.5
     if docs <= 64:
         share = share + swap_cores(share)
-        return solve(trade([share] * dp), docs, num_queries, scale).T
+        m = 1
+        while 2 * m < dp:
+            share = share + swap_dp(share, m)
+            m *= 2
+        return solve(share, swap_dp(share, m), docs, num_queries, scale).T
     share = lax.psum(share, ("dp", "tensor"))
     return solve_large(jnp.concatenate([share[:, :docs], share[:, docs:]], axis=0).T, docs, num_queries, scale).T
 

time: 52.9 us -> 48.6 us (0.919)
  starting transfers between devices: 24.3 us -> 3.72 us
  blocking collectives: 0 us -> 15.7 us
    ppermute x14 -> x3, starting transfers between devices: 23.5 us -> 2.96 us  [swap_dp(): lax.ppermute(x, 'dp', [(i, i ^ m) for i in range(lax.axis_size('dp'))])]
    all_to_all x0 -> x1, blocking collectives: none -> 15.7 us  [local(): lax.all_to_all(pack(keep, recv, extra, pa, pb), 'dp', 0, 0, tiled=True)]
    ppermute x14 -> x3, waiting for transfers between devices: 8.82 us -> 9.29 us  [swap_dp(): lax.ppermute(x, 'dp', [(i, i ^ m) for i in range(lax.axis_size('dp'))])]
  transfers between devices with their start and end apart: 17 -> 6, of which waited for: 8 -> 6; matrix products, arithmetic and copies ran while one was open for 1% -> 1% of each run, Pallas kernels for 0% -> 0%
where the time goes in v3:
time: 48.6 us; the launch traced here: 48.4 us
  blocking collectives  15.7 us (32%)
  Pallas kernels  15.3 us (31%)
  waiting for transfers between devices  12.3 us (25%)
  starting transfers between devices  3.72 us (8%)
  local copies, waits for them, and re-layouts  1.1 us (2%)
    all_to_all x1, blocking collectives, local(): lax.all_to_all(pack(keep, recv, extra, pa, pb), 'dp', 0, 0, tiled=True)  15.7 us
    ppermute x3, waiting for transfers between devices, swap_dp(): lax.ppermute(x, 'dp', [(i, i ^ m) for i in range(lax.axis_size('dp'))])  9.29 us
    pallas_call x1, Pallas kernels, project(): pl.pallas_call(functools.partial(project_kernel, (h_size, h_count, g_size...  7.85 us
    pallas_call x1, Pallas kernels, solve(): pl.pallas_call(functools.partial(solve_kernel, docs, queries, scale), out...  6.28 us
    ppermute x3, waiting for transfers between devices, swap_cores(): return lax.ppermute(x, 'tensor', [(i, cores - 1 - i) for i in range(cores)])  3.01 us
    ppermute x3, starting transfers between devices, swap_dp(): lax.ppermute(x, 'dp', [(i, i ^ m) for i in range(lax.axis_size('dp'))])  2.96 us
  transfers between devices with their start and end apart: 6, of which 6 were waited for; matrix products, arithmetic and copies ran while one was open for 1% of the time, Pallas kernels for 0%

profile of v3, /device:TPU:0, one launch (start us, length us, event | category | flops | bytes accessed | tf_op | source)
XLA Modules:
  0.0 48.4 jit_solution(11349276362456639753)
XLA Ops:
  0.0 0.0 copy-start
  0.0 0.0 copy-start.2
  0.0 7.8 %project.1 = (f32[128,128]{1,0:T(8,128)}, f32[128,128]{1,0:T(8,128)}) custom-call(bf16[256,14336]{1,0:T(8,128)(2,1)} %h_ref.1, bf16[256,4096]{1,0:T(8,128)(2,1)} %g_ref.1, bf16[64,14336]{1,0:T(8,128)(2,1)} %bitcast.6, bf16[64,4096]{1,0:T(8,128)(2,1)} %bitcast.7), custom_call_target="tpu_custom_call" | custom-call | flops 603979776 | bytes 11796480 | tf_op jit(solution)/shard_map/project/pallas_call | solution.py:77
  7.9 0.5 %collective-permute-start = (f32[128,128]{1,0:T(8,128)}, f32[128,128]{1,0:T(8,128)S(1)}, u32[]{:S(2)}, u32[]{:S(2)}) collective-permute-start(f32[128,128]{1,0:T(8,128)} %get-tuple-element.10), channel_id=1, source_target_pairs={{0,1},{1,0},{2,3},{3,2},{4,5},{5,4},{6,7},{7,6},{8,9},{9,8},{10,11... | collective-permute-start | bytes 196616 | tf_op jit(solution)/shard_map/ppermute | solution.py:234
  8.4 0.0 copy-done
  8.4 0.1 reshape.6
  8.6 0.1 reshape.7
  8.7 0.0 copy-done.2
  8.7 0.1 dynamic-slice_convert_fusion
  8.8 0.7 %collective-permute-done.recv_ref = f32[128,128]{1,0:T(8,128)S(1)} collective-permute-done((f32[128,128]{1,0:T(8,128)}, f32[128,128]{1,0:T(8,128)S(1)}, u32[]{:S(2)}, u32[]{:S(2)}) %collective-permute-start) | collective-permute-done | bytes 65568 | tf_op jit(solution)/shard_map/ppermute | solution.py:234
  9.5 0.0 copy-start.1
  9.5 0.8 %copy-done.1 = f32[128,128]{1,0:T(8,128)S(1)} copy-done((f32[128,128]{1,0:T(8,128)S(1)}, f32[128,128]{1,0:T(8,128)}, u32[]{:S(2)}) %copy-start.1) | copy-done | bytes 65560
  10.4 15.7 %all_to_all.5.x_ref = f32[8,56,128]{2,1,0:T(8,128)S(1)} all-to-all(f32[8,56,128]{2,1,0:T(8,128)S(1)} %pack.1), channel_id=1, replica_groups=mesh['groups'=2,'dp'=8,'tensor'=2] {'dp'}, dimensions={0} | all-to-all | bytes 458752 | tf_op jit(solution)/shard_map/all_to_all | solution.py:263
  26.1 0.9 %grads.1 = (f32[72,256]{1,0:T(8,128)S(1)}, f32[72,256]{1,0:T(8,128)S(1)}) custom-call(f32[8,56,128]{2,1,0:T(8,128)S(1)} %all_to_all.5.x_ref), custom_call_target="tpu_custom_call" | custom-call | tf_op jit(solution)/shard_map/grads/pallas_call | solution.py:151
  27.0 0.1 collective-permute-start.1
  27.1 1.3 %collective-permute-done.1.recv_ref = f32[72,256]{1,0:T(8,128)S(1)} collective-permute-done((f32[72,256]{1,0:T(8,128)S(1)}, f32[72,256]{1,0:T(8,128)S(1)}, u32[]{:S(2)}, u32[]{:S(2)}) %collective-permute-start.1) | collective-permute-done | bytes 73760 | tf_op jit(solution)/shard_map/ppermute | solution.py:234
  28.3 0.3 gram.1
  28.6 0.2 collective-permute-start.2
  28.8 1.0 %collective-permute-done.2 = f32[40,128]{1,0:T(8,128)S(1)} collective-permute-done((f32[40,128]{1,0:T(8,128)S(1)}, f32[40,128]{1,0:T(8,128)S(1)}, u32[]{:S(2)}, u32[]{:S(2)}) %collective-permute-start.2) | collective-permute-done | bytes 20512 | tf_op jit(solution)/shard_map/ppermute | solution.py:234
  29.8 1.2 %collective-permute-start.3 = (f32[40,128]{1,0:T(8,128)S(1)}, f32[40,128]{1,0:T(8,128)S(1)}, u32[]{:S(2)}, u32[]{:S(2)}) collective-permute-start(f32[40,128]{1,0:T(8,128)S(1)} %add.19), channel_id=1, source_target_pairs={{0,2},{2,0},{4,6},{6,4},{8,10},{10,8},{12,14},{14,12},{1,3},{3,1},... | collective-permute-start | bytes 61448 | tf_op jit(solution)/shard_map/ppermute | solution.py:238
  31.0 2.6 %collective-permute-done.3 = f32[40,128]{1,0:T(8,128)S(1)} collective-permute-done((f32[40,128]{1,0:T(8,128)S(1)}, f32[40,128]{1,0:T(8,128)S(1)}, u32[]{:S(2)}, u32[]{:S(2)}) %collective-permute-start.3) | collective-permute-done | bytes 20512 | tf_op jit(solution)/shard_map/ppermute | solution.py:238
  33.6 0.9 %collective-permute-start.4 = (f32[40,128]{1,0:T(8,128)S(1)}, f32[40,128]{1,0:T(8,128)S(1)}, u32[]{:S(2)}, u32[]{:S(2)}) collective-permute-start(f32[40,128]{1,0:T(8,128)S(1)} %add.20), channel_id=1, source_target_pairs={{0,4},{2,6},{4,0},{6,2},{8,12},{10,14},{12,8},{14,10},{1,5},{3,7},... | collective-permute-start | bytes 61448 | tf_op jit(solution)/shard_map/ppermute | solution.py:238
  34.5 2.9 %collective-permute-done.4 = f32[40,128]{1,0:T(8,128)S(1)} collective-permute-done((f32[40,128]{1,0:T(8,128)S(1)}, f32[40,128]{1,0:T(8,128)S(1)}, u32[]{:S(2)}, u32[]{:S(2)}) %collective-permute-start.4) | collective-permute-done | bytes 20512 | tf_op jit(solution)/shard_map/ppermute | solution.py:238
  37.4 0.9 %collective-permute-start.5 = (f32[40,128]{1,0:T(8,128)S(1)}, f32[40,128]{1,0:T(8,128)S(1)}, u32[]{:S(2)}, u32[]{:S(2)}) collective-permute-start(f32[40,128]{1,0:T(8,128)S(1)} %add.21.x_ref), channel_id=1, source_target_pairs={{0,8},{2,10},{4,12},{6,14},{8,0},{10,2},{12,4},{14,6},{1,9},{3,11}... | collective-permute-start | bytes 61448 | tf_op jit(solution)/shard_map/ppermute | solution.py:238
  38.3 3.8 %collective-permute-done.5.recv_ref = f32[40,128]{1,0:T(8,128)S(1)} collective-permute-done((f32[40,128]{1,0:T(8,128)S(1)}, f32[40,128]{1,0:T(8,128)S(1)}, u32[]{:S(2)}, u32[]{:S(2)}) %collective-permute-start.5) | collective-permute-done | bytes 20512 | tf_op jit(solution)/shard_map/ppermute | solution.py:238
  42.1 6.3 %solve.1 = f32[8,16]{1,0:T(8,128)} custom-call(f32[40,128]{1,0:T(8,128)S(1)} %add.21.x_ref, f32[40,128]{1,0:T(8,128)S(1)} %collective-permute-done.5.recv_ref), custom_call_target="tpu_custom_call" | custom-call | tf_op jit(solution)/shard_map/solve/pallas_call | solution.py:213
  (8 shorter events, 0.1 us)
Async XLA Ops:
  0.0 8.4 %copy-start = (f32[2,4096]{1,0:T(2,128)S(1)}, f32[2,4096]{1,0:T(2,128)}, u32[]{:S(2)}) copy-start(f32[2,4096]{1,0:T(2,128)} %param.11) | copy-start | bytes 98308
  0.0 8.6 %copy-start.2 = (s32[256]{0:T(256)S(1)}, s32[256]{0:T(256)}, u32[]{:S(2)}) copy-start(s32[256]{0:T(256)} %param.10) | copy-start | bytes 3076
  7.9 1.6 %collective-permute-start = (f32[128,128]{1,0:T(8,128)}, f32[128,128]{1,0:T(8,128)S(1)}, u32[]{:S(2)}, u32[]{:S(2)}) collective-permute-start(f32[128,128]{1,0:T(8,128)} %get-tuple-element.10), channel_id=1, source_target_pairs={{0,1},{1,0},{2,3},{3,2},{4,5},{5,4},{6,7},{7,6},{8,9},{9,8},{10,11... | collective-permute-start | bytes 196616 | tf_op jit(solution)/shard_map/ppermute | solution.py:234
  9.5 0.8 %copy-start.1 = (f32[128,128]{1,0:T(8,128)S(1)}, f32[128,128]{1,0:T(8,128)}, u32[]{:S(2)}) copy-start(f32[128,128]{1,0:T(8,128)} %get-tuple-element.9.keep_ref) | copy-start | bytes 196612
  27.0 1.3 %collective-permute-start.1 = (f32[72,256]{1,0:T(8,128)S(1)}, f32[72,256]{1,0:T(8,128)S(1)}, u32[]{:S(2)}, u32[]{:S(2)}) collective-permute-start(f32[72,256]{1,0:T(8,128)S(1)} %get-tuple-element.12), channel_id=1, source_target_pairs={{0,1},{1,0},{2,3},{3,2},{4,5},{5,4},{6,7},{7,6},{8,9},{9,8},{10,11... | collective-permute-start | bytes 221192 | tf_op jit(solution)/shard_map/ppermute | solution.py:234
  28.6 1.2 %collective-permute-start.2 = (f32[40,128]{1,0:T(8,128)S(1)}, f32[40,128]{1,0:T(8,128)S(1)}, u32[]{:S(2)}, u32[]{:S(2)}) collective-permute-start(f32[40,128]{1,0:T(8,128)S(1)} %gram.1), channel_id=1, source_target_pairs={{0,1},{1,0},{2,3},{3,2},{4,5},{5,4},{6,7},{7,6},{8,9},{9,8},{10,11... | collective-permute-start | bytes 61448 | tf_op jit(solution)/shard_map/ppermute | solution.py:234
  29.8 3.8 %collective-permute-start.3 = (f32[40,128]{1,0:T(8,128)S(1)}, f32[40,128]{1,0:T(8,128)S(1)}, u32[]{:S(2)}, u32[]{:S(2)}) collective-permute-start(f32[40,128]{1,0:T(8,128)S(1)} %add.19), channel_id=1, source_target_pairs={{0,2},{2,0},{4,6},{6,4},{8,10},{10,8},{12,14},{14,12},{1,3},{3,1},... | collective-permute-start | bytes 61448 | tf_op jit(solution)/shard_map/ppermute | solution.py:238
  33.6 3.8 %collective-permute-start.4 = (f32[40,128]{1,0:T(8,128)S(1)}, f32[40,128]{1,0:T(8,128)S(1)}, u32[]{:S(2)}, u32[]{:S(2)}) collective-permute-start(f32[40,128]{1,0:T(8,128)S(1)} %add.20), channel_id=1, source_target_pairs={{0,4},{2,6},{4,0},{6,2},{8,12},{10,14},{12,8},{14,10},{1,5},{3,7},... | collective-permute-start | bytes 61448 | tf_op jit(solution)/shard_map/ppermute | solution.py:238
  37.4 4.7 %collective-permute-start.5 = (f32[40,128]{1,0:T(8,128)S(1)}, f32[40,128]{1,0:T(8,128)S(1)}, u32[]{:S(2)}, u32[]{:S(2)}) collective-permute-start(f32[40,128]{1,0:T(8,128)S(1)} %add.21.x_ref), channel_id=1, source_target_pairs={{0,8},{2,10},{4,12},{6,14},{8,0},{10,2},{12,4},{14,6},{1,9},{3,11}... | collective-permute-start | bytes 61448 | tf_op jit(solution)/shard_map/ppermute | solution.py:238

commit v4 on v2

v4 whole, which is shorter than its diff:
```python
import functools

import jax
import jax.numpy as jnp
from jax import lax
from jax.experimental import pallas as pl
from jax.experimental.pallas import tpu as pltpu
from jax.sharding import PartitionSpec as P

TOK_DEV = 256
DOC_DEV = 8
LANES = 128
DEPTH = 256
NT = (((1,), (1,)), ((), ()))
HIGHEST = lax.Precision.HIGHEST
VMEM = pl.BlockSpec(memory_space=pltpu.VMEM)
HBM = pl.BlockSpec(memory_space=pltpu.HBM)


def vmem_params(mib):
    return pltpu.CompilerParams(vmem_limit_bytes=int(mib * (1 << 20)))


def chunks_of(length, most=1024):
    size = most
    while length % size:
        size //= 2
    return size, length // size


def project_kernel(sizes, h_ref, g_ref, pin_ref, pout_ref, out_ref, h_buf, g_buf, pin_buf, pout_buf, sems):
    h_size, h_count, g_size, g_count = sizes
    copies = {}

    def copy(name, src, dst):
        copies[name] = pltpu.make_async_copy(src, dst, sems.at[len(copies)])
        copies[name].start()

    copy("po", pout_ref, pout_buf)
    for i in range(g_count):
        at = pl.ds(i * g_size, g_size)
        copy(("g", i), g_ref.at[:, at], g_buf.at[:, at])
    copy("pi", pin_ref, pin_buf)
    for i in range(h_count):
        at = pl.ds(i * h_size, h_size)
        copy(("h", i), h_ref.at[:, at], h_buf.at[:, at])

    def run(tag, count, size, proj, data):
        total = None
        depth = min(size, DEPTH)
        for i in range(count):
            copies[tag, i].wait()
            parts = []
            for j in range(size // depth):
                at = pl.ds(i * size + j * depth, depth)
                parts.append(lax.dot_general(data[:, at], proj[:, at], NT, preferred_element_type=jnp.float32))
            part = sum(parts[1:], parts[0])
            total = part if total is None else total + part
        return total

    copies["po"].wait()
    grad = run("g", g_count, g_size, pout_buf, g_buf)
    copies["pi"].wait()
    inp = run("h", h_count, h_size, pin_buf, h_buf)
    out_ref[...] = jnp.concatenate([grad, inp], axis=1).T


def project(hidden, out_grad, pin_t, pout_t):
    tokens, units = hidden.shape
    width = out_grad.shape[1]
    ranks = pin_t.shape[0] + pout_t.shape[0]
    h_size, h_count = chunks_of(units)
    g_size, g_count = chunks_of(width)
    return pl.pallas_call(
        functools.partial(project_kernel, (h_size, h_count, g_size, g_count)),
        out_shape=jax.ShapeDtypeStruct((ranks, tokens), jnp.float32),
        in_specs=[HBM] * 4,
        out_specs=VMEM,
        scratch_shapes=[
            pltpu.VMEM(hidden.shape, hidden.dtype),
            pltpu.VMEM(out_grad.shape, out_grad.dtype),
            pltpu.VMEM(pin_t.shape, pin_t.dtype),
            pltpu.VMEM(pout_t.shape, pout_t.dtype),
            pltpu.SemaphoreType.DMA((2 + g_count + h_count,)),
        ],
        compiler_params=vmem_params(53.5),
        cost_estimate=pl.CostEstimate(
            flops=2 * tokens * 64 * (units + width),
            bytes_accessed=2 * (tokens + 64) * (units + width),
            transcendentals=0,
        ),
        name="project",
    )(hidden, out_grad, pin_t, pout_t)


def pack_kernel(pb, rows_a, rows_b, part_ref, recv_ref, extra_ref, *refs):
    outs, total_ref = refs[:-1], refs[-1]
    total_ref[...] = part_ref[...] + recv_ref[...]
    ranks = total_ref.shape[0] // 2
    first = lax.axis_index("tensor") * len(outs)
    me = lax.axis_index("dp")
    for t, out_ref in enumerate(outs):
        owner = me ^ (first + t)
        p, q = owner // pb, owner % pb
        out_ref[0:rows_a, :] = total_ref[pl.ds(pl.multiple_of(p * rows_a, rows_a), rows_a), :]
        out_ref[rows_a:rows_a + rows_b, :] = total_ref[pl.ds(pl.multiple_of(ranks + q * rows_b, rows_b), rows_b), :]
        out_ref[rows_a + rows_b:, :] = extra_ref[owner]


def pack(part, recv, extra, pa, pb):
    ranks, lanes = part.shape[0] // 2, part.shape[1]
    rows_a, rows_b = ranks // pa, ranks // pb
    rows = rows_a + rows_b + extra.shape[1]
    count = pa * pb // 2
    return pl.pallas_call(
        functools.partial(pack_kernel, pb, rows_a, rows_b),
        out_shape=(jax.ShapeDtypeStruct((rows, lanes), jnp.float32),) * count,
        in_specs=[VMEM] * 3,
        out_specs=(VMEM,) * count,
        scratch_shapes=[pltpu.VMEM(part.shape, jnp.float32)],
        compiler_params=vmem_params(16),
        name="pack",
    )(part, recv, extra)


def grads_kernel(rows_a, rows_b, docs, *refs):
    xs, (out_ref, outer_ref, member_ref) = refs[:-3], refs[-3:]
    lanes = xs[0].shape[1]
    wide = rows_a * rows_b
    first = rows_a + rows_b
    queries = out_ref.shape[0] - docs
    per = queries // (2 * len(xs))
    doc = lax.broadcasted_iota(jnp.int32, (docs, lanes), 0)
    place = lax.broadcasted_iota(jnp.int32, (queries, wide), 0)
    begin = lax.axis_index("tensor") * len(xs)
    me = lax.axis_index("dp")
    asked = jnp.zeros((queries, wide), jnp.float32)
    for t, x_ref in enumerate(xs):
        at = slice(t * lanes, (t + 1) * lanes)
        g, b = x_ref[0:rows_a, :], x_ref[rows_a:first, :]
        ids = x_ref[first:first + 1, :].astype(jnp.int32)
        member_ref[:, at] = jnp.where(doc == ids, 1.0, 0.0).astype(jnp.bfloat16)
        outer = (g[:, None, :] * b[None, :, :]).reshape(wide, lanes)
        high = outer.astype(jnp.bfloat16)
        outer_ref[0:wide, at] = high
        outer_ref[wide:, at] = (outer - high.astype(jnp.float32)).astype(jnp.bfloat16)
        source = me ^ (begin + t)
        for q in range(per):
            if wide >= lanes:
                span = wide // lanes
                row = first + 1 + q * span
                line = jnp.concatenate([x_ref[row + j:row + j + 1, :] for j in range(span)], axis=1)
            else:
                line = x_ref[first + 1:first + 2, q * wide:(q + 1) * wide]
            asked = jnp.where(place == source * per + q, line, asked)
    sums = lax.dot_general(member_ref[...], outer_ref[...], NT, preferred_element_type=jnp.float32)
    out_ref[0:docs, :] = (sums[:, wide:] + sums[:, :wide]) * (TOK_DEV ** -0.5)
    out_ref[docs:, :] = asked


def grads_of(xs, rows_a, rows_b, docs, queries):
    lanes = xs[0].shape[1]
    wide = rows_a * rows_b
    return pl.pallas_call(
        functools.partial(grads_kernel, rows_a, rows_b, docs),
        out_shape=jax.ShapeDtypeStruct((docs + queries, wide), jnp.float32),
        in_specs=[VMEM] * len(xs),
        out_specs=VMEM,
        scratch_shapes=[
            pltpu.VMEM((2 * wide, len(xs) * lanes), jnp.bfloat16),
            pltpu.VMEM((docs, len(xs) * lanes), jnp.bfloat16),
        ],
        compiler_params=vmem_params(40),
        name="grads",
    )(*xs)


def gram_kernel(docs, part_ref, recv_ref, out_ref):
    both = part_ref[...] + recv_ref[...]
    share = lax.dot_general(both, both[:docs], NT, precision=HIGHEST, preferred_element_type=jnp.float32)
    half = share.shape[0] // 2
    out_ref[...] = jnp.concatenate([share[:half], share[half:]], axis=1)


def gram(part, recv, docs):
    return pl.pallas_call(
        functools.partial(gram_kernel, docs),
        out_shape=jax.ShapeDtypeStruct((part.shape[0] // 2, 2 * docs), jnp.float32),
        in_specs=[VMEM] * 2,
        out_specs=VMEM,
        compiler_params=vmem_params(16),
        name="gram",
    )(part, recv)


def solve_kernel(docs, queries, scale, x_ref, recv_ref, out_ref, done_ref):
    total = x_ref[...] + recv_ref[...]
    stack = jnp.concatenate([total[:, :docs], total[:, docs:]], axis=0)
    cols = done_ref.shape[1]
    stack = jnp.concatenate([stack, jnp.zeros((cols - stack.shape[0], docs), jnp.float32)], axis=0)
    total = stack.T
    row = lax.broadcasted_iota(jnp.int32, (docs, cols), 0)
    col = lax.broadcasted_iota(jnp.int32, (docs, cols), 1)
    mean_diag = jnp.sum(jnp.where(row == col, total, 0.0)) * (1.0 / docs)
    work = total + jnp.where(row == col, 0.1 * mean_diag, 0.0)
    size = 8
    here = lax.broadcasted_iota(jnp.int32, (size, cols), 0)
    rows = [work[i:i + size] for i in range(0, docs, size)]
    for r in range(len(rows)):
        wide = [[jnp.broadcast_to(x[:, c:c + 1], (size, cols)) for c in range(r * size, (r + 1) * size)] for x in rows]
        pivot, line = wide[r], rows[r]
        for j in range(size):
            inverse = 1.0 / pivot[j][j:j + 1]
            factor = jnp.where(here == j, 1.0 - inverse, pivot[j] * inverse)
            pivot = [x if i <= j else x - factor * x[j:j + 1] for i, x in enumerate(pivot)]
            line = line - factor * line[j:j + 1]
        for s in range(len(rows)):
            if s == r:
                rows[s] = line
            else:
                terms = [wide[s][j] * line[j:j + 1] for j in range(size)]
                rows[s] = rows[s] - (((terms[0] + terms[1]) + (terms[2] + terms[3]))
                                     + ((terms[4] + terms[5]) + (terms[6] + terms[7])))
    for r, x in enumerate(rows):
        done_ref[r * size:(r + 1) * size, :] = x * (mean_diag * scale)
    mine = pl.ds(pl.multiple_of(lax.axis_index("dp") * DOC_DEV, DOC_DEV), DOC_DEV)
    out_ref[...] = done_ref[mine, :][:, docs:docs + queries]


def solve(x, recv, docs, queries, scale):
    return pl.pallas_call(
        functools.partial(solve_kernel, docs, queries, scale),
        out_shape=jax.ShapeDtypeStruct((DOC_DEV, queries), jnp.float32),
        in_specs=[VMEM] * 2,
        out_specs=VMEM,
        scratch_shapes=[pltpu.VMEM((docs, -(-(docs + queries) // LANES) * LANES), jnp.float32)],
        compiler_params=vmem_params(16),
        name="solve",
    )(x, recv)


def solve_large(total, docs, queries, scale):
    kernel = total[:, :docs]
    mean_diag = jnp.trace(kernel) / docs
    factor = jnp.linalg.cholesky(kernel + 0.1 * mean_diag * jnp.eye(docs, dtype=jnp.float32))
    solved = jax.scipy.linalg.cho_solve((factor, True), total[:, docs:docs + queries]) * (mean_diag * scale)
    return lax.dynamic_slice_in_dim(solved, lax.axis_index("dp") * DOC_DEV, DOC_DEV, 0)


def swap_cores(x):
    cores = lax.axis_size("tensor")
    return lax.ppermute(x, "tensor", [(i, cores - 1 - i) for i in range(cores)])


def trade(xs):
    dp, count = lax.axis_size("dp"), len(xs)
    got = []
    for t, x in enumerate(xs):
        pairs = [(i * 2 + k, (i ^ (k * count + t)) * 2 + k) for i in range(dp) for k in range(2)]
        got.append(lax.ppermute(x, ("dp", "tensor"), pairs))
    return got


def local(hidden, out_grad, proj_in, proj_out, doc_ids, queries):
    dp = lax.axis_size("dp")
    docs, num_queries = DOC_DEV * dp, queries.shape[0] * dp
    ranks = proj_in.shape[1]
    pa = 1
    while pa * pa < dp:
        pa *= 2
    pb = dp // pa
    rows_a, rows_b = ranks // pa, ranks // pb

    part = project(hidden, out_grad, proj_in.T, proj_out.T)
    recv = swap_cores(part)

    lanes = part.shape[1]
    ids = doc_ids.astype(jnp.float32)
    asked = queries.reshape(-1, pa, rows_a, pb, rows_b).transpose(1, 3, 0, 2, 4).reshape(dp, -1, lanes)
    extra = jnp.concatenate([jnp.broadcast_to(ids, (dp, 1, lanes)), asked], axis=1)
    extra = jnp.pad(extra, ((0, 0), (0, -extra.shape[1] % 8), (0, 0)))

    blocks = trade(pack(part, recv, extra, pa, pb))
    grads = grads_of(blocks, rows_a, rows_b, docs, num_queries)
    share = gram(grads, swap_cores(grads), docs)
    scale = float(ranks * ranks) ** -0.5
    if docs <= 64:
        share = sum(trade([share] * (dp // 2)))
        return solve(share, swap_cores(share), docs, num_queries, scale).T
    share = lax.psum(share, "dp")
    return solve_large(jnp.concatenate([share[:, :docs], share[:, docs:]], axis=0).T, docs, num_queries, scale).T


def solution(mesh):
    return jax.shard_map(
        local,
        mesh=mesh,
        in_specs=(
            P(("groups", "dp"), "tensor"),
            P(("groups", "dp"), "tensor"),
            P("tensor", None),
            P("tensor", None),
            P(("groups", "dp")),
            P(("groups", "dp"), None),
        ),
        out_specs=P("groups", "dp"),
        check_vma=False,
    )
```

time: 52.9 us -> 40.6 us (0.77)
  Pallas kernels: 15.3 us -> 10.8 us
  starting transfers between devices: 24.3 us -> 20 us
  waiting for transfers between devices: 11.8 us -> 9.21 us
  local copies, waits for them, and re-layouts: 1.1 us -> 0.29 us
    ppermute x14 -> x8, starting transfers between devices: 23.5 us -> 9.34 us  [trade(): got.append(lax.ppermute(x, ('dp', 'tensor'), pairs))]
    ppermute x3, starting transfers between devices: 0.77 us -> 10.6 us  [swap_cores(): return lax.ppermute(x, 'tensor', [(i, cores - 1 - i) for i in range(cores)])]
    pallas_call x1, Pallas kernels: 6.29 us -> 2.61 us  [solve(): pl.pallas_call(functools.partial(solve_kernel, docs, queries, scale), out...]
    ppermute x14 -> x8, waiting for transfers between devices: 8.82 us -> 6.69 us  [trade(): got.append(lax.ppermute(x, ('dp', 'tensor'), pairs))]
    unnamed x6 -> x4, local copies, waits for them, and re-layouts: 0.85 us -> 0.01 us
    pallas_call x1, Pallas kernels: 7.82 us -> 7.05 us  [project(): pl.pallas_call(functools.partial(project_kernel, (h_size, h_count, g_size...]
  transfers between devices with their start and end apart: 17 -> 11, of which waited for: 8 -> 8; matrix products, arithmetic and copies ran while one was open for 1% -> 1% of each run, Pallas kernels for 0% -> 0%
where the time goes in v4:
time: 40.6 us; the launch traced here: 40.4 us
  starting transfers between devices  20 us (49%)
  Pallas kernels  10.8 us (27%)
  waiting for transfers between devices  9.21 us (23%)
    ppermute x3, starting transfers between devices, swap_cores(): return lax.ppermute(x, 'tensor', [(i, cores - 1 - i) for i in range(cores)])  10.6 us
    ppermute x8, starting transfers between devices, trade(): got.append(lax.ppermute(x, ('dp', 'tensor'), pairs))  9.34 us
    pallas_call x1, Pallas kernels, project(): pl.pallas_call(functools.partial(project_kernel, (h_size, h_count, g_size...  7.05 us
    ppermute x8, waiting for transfers between devices, trade(): got.append(lax.ppermute(x, ('dp', 'tensor'), pairs))  6.69 us
    pallas_call x1, Pallas kernels, solve(): pl.pallas_call(functools.partial(solve_kernel, docs, queries, scale), out...  2.61 us
    ppermute x3, waiting for transfers between devices, swap_cores(): return lax.ppermute(x, 'tensor', [(i, cores - 1 - i) for i in range(cores)])  2.51 us
  transfers between devices with their start and end apart: 11, of which 8 were waited for; matrix products, arithmetic and copies ran while one was open for 1% of the time, Pallas kernels for 0%

profile of v4, /device:TPU:0, one launch (start us, length us, event | category | flops | bytes accessed | tf_op | source)
XLA Modules:
  0.0 40.4 jit_solution(8421580382828474359)
XLA Ops:
  0.0 0.0 copy-start.1
  0.0 0.0 copy-start
  0.0 7.0 %project.1.part_ref = f32[128,256]{1,0:T(8,128)S(1)} custom-call(bf16[256,14336]{1,0:T(8,128)(2,1)} %h_ref.1, bf16[256,4096]{1,0:T(8,128)(2,1)} %g_ref.1, bf16[64,14336]{1,0:T(8,128)(2,1)} %bitcast.8, bf16[64,4096]{1,0:T(8,128)(2,1)} %bitcast.9), custom_call_target="tpu_custom_call" | custom-call | flops 603979776 | bytes 11796480 | tf_op jit(solution)/shard_map/project/pallas_call | solution.py:74
  7.1 0.5 %collective-permute-start = (f32[128,256]{1,0:T(8,128)S(1)}, f32[128,256]{1,0:T(8,128)S(1)}, u32[]{:S(2)}, u32[]{:S(2)}) collective-permute-start(f32[128,256]{1,0:T(8,128)S(1)} %project.1.part_ref), channel_id=1, source_target_pairs={{0,1},{1,0},{2,3},{3,2},{4,5},{5,4},{6,7},{7,6},{8,9},{9,8},{10,11... | collective-permute-start | bytes 393224 | tf_op jit(solution)/shard_map/ppermute | solution.py:252
  7.6 0.0 copy-done.1
  7.6 0.0 copy-done
  7.6 0.2 reshape.6
  7.8 0.1 reshape.7
  7.9 0.6 %collective-permute-done.recv_ref = f32[128,256]{1,0:T(8,128)S(1)} collective-permute-done((f32[128,256]{1,0:T(8,128)S(1)}, f32[128,256]{1,0:T(8,128)S(1)}, u32[]{:S(2)}, u32[]{:S(2)}) %collective-permute-start) | collective-permute-done | bytes 131104 | tf_op jit(solution)/shard_map/ppermute | solution.py:252
  8.6 0.7 %collective-permute-start.1 = (f32[56,256]{1,0:T(8,128)S(1)}, f32[56,256]{1,0:T(8,128)S(1)}, u32[]{:S(2)}, u32[]{:S(2)}) collective-permute-start(f32[56,256]{1,0:T(8,128)S(1)} %get-tuple-element.9), channel_id=1, source_target_pairs={{0,0},{1,9},{2,2},{3,11},{4,4},{5,13},{6,6},{7,15},{8,8},{9,1},{10... | collective-permute-start | bytes 172040 | tf_op jit(solution)/shard_map/ppermute | solution.py:260
  9.3 2.9 %collective-permute-start.2 = (f32[56,256]{1,0:T(8,128)S(1)}, f32[56,256]{1,0:T(8,128)S(1)}, u32[]{:S(2)}, u32[]{:S(2)}) collective-permute-start(f32[56,256]{1,0:T(8,128)S(1)} %get-tuple-element.10), channel_id=1, source_target_pairs={{0,2},{1,11},{2,0},{3,9},{4,6},{5,15},{6,4},{7,13},{8,10},{9,3},{1... | collective-permute-start | bytes 172040 | tf_op jit(solution)/shard_map/ppermute | solution.py:260
  12.2 1.6 %collective-permute-start.3 = (f32[56,256]{1,0:T(8,128)S(1)}, f32[56,256]{1,0:T(8,128)S(1)}, u32[]{:S(2)}, u32[]{:S(2)}) collective-permute-start(f32[56,256]{1,0:T(8,128)S(1)} %get-tuple-element.11), channel_id=1, source_target_pairs={{0,4},{1,13},{2,6},{3,15},{4,0},{5,9},{6,2},{7,11},{8,12},{9,5},{1... | collective-permute-start | bytes 172040 | tf_op jit(solution)/shard_map/ppermute | solution.py:260
  13.8 0.0 collective-permute-start.4
  13.8 0.0 collective-permute-done.1.refs_0_
  13.8 0.6 %collective-permute-done.2.refs_1_ = f32[56,256]{1,0:T(8,128)S(1)} collective-permute-done((f32[56,256]{1,0:T(8,128)S(1)}, f32[56,256]{1,0:T(8,128)S(1)}, u32[]{:S(2)}, u32[]{:S(2)}) %collective-permute-start.2) | collective-permute-done | bytes 57376 | tf_op jit(solution)/shard_map/ppermute | solution.py:260
  14.4 2.3 %collective-permute-done.3.refs_2_ = f32[56,256]{1,0:T(8,128)S(1)} collective-permute-done((f32[56,256]{1,0:T(8,128)S(1)}, f32[56,256]{1,0:T(8,128)S(1)}, u32[]{:S(2)}, u32[]{:S(2)}) %collective-permute-start.3) | collective-permute-done | bytes 57376 | tf_op jit(solution)/shard_map/ppermute | solution.py:260
  16.7 2.2 %collective-permute-done.4.refs_3_ = f32[56,256]{1,0:T(8,128)S(1)} collective-permute-done((f32[56,256]{1,0:T(8,128)S(1)}, f32[56,256]{1,0:T(8,128)S(1)}, u32[]{:S(2)}, u32[]{:S(2)}) %collective-permute-start.4) | collective-permute-done | bytes 57376 | tf_op jit(solution)/shard_map/ppermute | solution.py:260
  18.9 0.8 %grads.1.part_ref = f32[80,512]{1,0:T(8,128)S(1)} custom-call(f32[56,256]{1,0:T(8,128)S(1)} %collective-permute-done.1.refs_0_, f32[56,256]{1,0:T(8,128)S(1)} %collective-permute-done.2.refs_1_, f32[56,256]{1,0:T(8,128)S(1)} %collective-permute-done.3.refs_2_, f32[56,256]{1,0:T(8,128)S(1)} %collective-permute-done.4.refs_3_), custom_call_target="tpu_custom_call" | custom-call | tf_op jit(solution)/shard_map/grads/pallas_call | solution.py:164
  19.7 5.6 %collective-permute-start.5 = (f32[80,512]{1,0:T(8,128)S(1)}, f32[80,512]{1,0:T(8,128)S(1)}, u32[]{:S(2)}, u32[]{:S(2)}) collective-permute-start(f32[80,512]{1,0:T(8,128)S(1)} %grads.1.part_ref), channel_id=1, source_target_pairs={{0,1},{1,0},{2,3},{3,2},{4,5},{5,4},{6,7},{7,6},{8,9},{9,8},{10,11... | collective-permute-start | bytes 491528 | tf_op jit(solution)/shard_map/ppermute | solution.py:252
  25.3 1.0 %collective-permute-done.5.recv_ref = f32[80,512]{1,0:T(8,128)S(1)} collective-permute-done((f32[80,512]{1,0:T(8,128)S(1)}, f32[80,512]{1,0:T(8,128)S(1)}, u32[]{:S(2)}, u32[]{:S(2)}) %collective-permute-start.5) | collective-permute-done | bytes 163872 | tf_op jit(solution)/shard_map/ppermute | solution.py:252
  26.3 0.4 gram.1
  26.7 0.0 collective-permute-start.9
  26.7 1.9 %collective-permute-start.8 = (f32[40,128]{1,0:T(8,128)S(1)}, f32[40,128]{1,0:T(8,128)S(1)}, u32[]{:S(2)}, u32[]{:S(2)}) collective-permute-start(f32[40,128]{1,0:T(8,128)S(1)} %gram.1), channel_id=1, source_target_pairs={{0,4},{1,13},{2,6},{3,15},{4,0},{5,9},{6,2},{7,11},{8,12},{9,5},{1... | collective-permute-start | bytes 61448 | tf_op jit(solution)/shard_map/ppermute | solution.py:260
  28.7 1.5 %collective-permute-start.7 = (f32[40,128]{1,0:T(8,128)S(1)}, f32[40,128]{1,0:T(8,128)S(1)}, u32[]{:S(2)}, u32[]{:S(2)}) collective-permute-start(f32[40,128]{1,0:T(8,128)S(1)} %gram.1), channel_id=1, source_target_pairs={{0,2},{1,11},{2,0},{3,9},{4,6},{5,15},{6,4},{7,13},{8,10},{9,3},{1... | collective-permute-start | bytes 61448 | tf_op jit(solution)/shard_map/ppermute | solution.py:260
  30.2 0.7 %collective-permute-start.6 = (f32[40,128]{1,0:T(8,128)S(1)}, f32[40,128]{1,0:T(8,128)S(1)}, u32[]{:S(2)}, u32[]{:S(2)}) collective-permute-start(f32[40,128]{1,0:T(8,128)S(1)} %gram.1), channel_id=1, source_target_pairs={{0,0},{1,9},{2,2},{3,11},{4,4},{5,13},{6,6},{7,15},{8,8},{9,1},{10... | collective-permute-start | bytes 61448 | tf_op jit(solution)/shard_map/ppermute | solution.py:260
  30.9 0.5 %collective-permute-done.9 = f32[40,128]{1,0:T(8,128)S(1)} collective-permute-done((f32[40,128]{1,0:T(8,128)S(1)}, f32[40,128]{1,0:T(8,128)S(1)}, u32[]{:S(2)}, u32[]{:S(2)}) %collective-permute-start.9) | collective-permute-done | bytes 20512 | tf_op jit(solution)/shard_map/ppermute | solution.py:260
  31.4 0.0 collective-permute-done.8
  31.4 1.1 %collective-permute-done.7 = f32[40,128]{1,0:T(8,128)S(1)} collective-permute-done((f32[40,128]{1,0:T(8,128)S(1)}, f32[40,128]{1,0:T(8,128)S(1)}, u32[]{:S(2)}, u32[]{:S(2)}) %collective-permute-start.7) | collective-permute-done | bytes 20512 | tf_op jit(solution)/shard_map/ppermute | solution.py:260
  32.5 0.0 collective-permute-done.6
  32.5 4.5 %collective-permute-start.10 = (f32[40,128]{1,0:T(8,128)S(1)}, f32[40,128]{1,0:T(8,128)S(1)}, u32[]{:S(2)}, u32[]{:S(2)}) collective-permute-start(f32[40,128]{1,0:T(8,128)S(1)} %add_add_fusion.x_ref), channel_id=1, source_target_pairs={{0,1},{1,0},{2,3},{3,2},{4,5},{5,4},{6,7},{7,6},{8,9},{9,8},{10,11... | collective-permute-start | bytes 61448 | tf_op jit(solution)/shard_map/ppermute | solution.py:252
  37.0 0.8 %collective-permute-done.10.recv_ref = f32[40,128]{1,0:T(8,128)S(1)} collective-permute-done((f32[40,128]{1,0:T(8,128)S(1)}, f32[40,128]{1,0:T(8,128)S(1)}, u32[]{:S(2)}, u32[]{:S(2)}) %collective-permute-start.10) | collective-permute-done | bytes 20512 | tf_op jit(solution)/shard_map/ppermute | solution.py:252
  37.8 2.6 %solve.1 = f32[8,16]{1,0:T(8,128)} custom-call(f32[40,128]{1,0:T(8,128)S(1)} %add_add_fusion.x_ref, f32[40,128]{1,0:T(8,128)S(1)} %collective-permute-done.10.recv_ref), custom_call_target="tpu_custom_call" | custom-call | tf_op jit(solution)/shard_map/solve/pallas_call | solution.py:231
  (6 shorter events, 0.1 us)
Async XLA Ops:
  0.0 7.6 %copy-start.1 = (s32[256]{0:T(256)S(1)}, s32[256]{0:T(256)}, u32[]{:S(2)}) copy-start(s32[256]{0:T(256)} %param.10) | copy-start | bytes 3076
  0.0 7.6 %copy-start = (f32[2,4096]{1,0:T(2,128)S(1)}, f32[2,4096]{1,0:T(2,128)}, u32[]{:S(2)}) copy-start(f32[2,4096]{1,0:T(2,128)} %param.11) | copy-start | bytes 98308
  7.1 1.5 %collective-permute-start = (f32[128,256]{1,0:T(8,128)S(1)}, f32[128,256]{1,0:T(8,128)S(1)}, u32[]{:S(2)}, u32[]{:S(2)}) collective-permute-start(f32[128,256]{1,0:T(8,128)S(1)} %project.1.part_ref), channel_id=1, source_target_pairs={{0,1},{1,0},{2,3},{3,2},{4,5},{5,4},{6,7},{7,6},{8,9},{9,8},{10,11... | collective-permute-start | bytes 393224 | tf_op jit(solution)/shard_map/ppermute | solution.py:252
  8.6 5.2 %collective-permute-start.1 = (f32[56,256]{1,0:T(8,128)S(1)}, f32[56,256]{1,0:T(8,128)S(1)}, u32[]{:S(2)}, u32[]{:S(2)}) collective-permute-start(f32[56,256]{1,0:T(8,128)S(1)} %get-tuple-element.9), channel_id=1, source_target_pairs={{0,0},{1,9},{2,2},{3,11},{4,4},{5,13},{6,6},{7,15},{8,8},{9,1},{10... | collective-permute-start | bytes 172040 | tf_op jit(solution)/shard_map/ppermute | solution.py:260
  9.3 5.1 %collective-permute-start.2 = (f32[56,256]{1,0:T(8,128)S(1)}, f32[56,256]{1,0:T(8,128)S(1)}, u32[]{:S(2)}, u32[]{:S(2)}) collective-permute-start(f32[56,256]{1,0:T(8,128)S(1)} %get-tuple-element.10), channel_id=1, source_target_pairs={{0,2},{1,11},{2,0},{3,9},{4,6},{5,15},{6,4},{7,13},{8,10},{9,3},{1... | collective-permute-start | bytes 172040 | tf_op jit(solution)/shard_map/ppermute | solution.py:260
  12.2 4.5 %collective-permute-start.3 = (f32[56,256]{1,0:T(8,128)S(1)}, f32[56,256]{1,0:T(8,128)S(1)}, u32[]{:S(2)}, u32[]{:S(2)}) collective-permute-start(f32[56,256]{1,0:T(8,128)S(1)} %get-tuple-element.11), channel_id=1, source_target_pairs={{0,4},{1,13},{2,6},{3,15},{4,0},{5,9},{6,2},{7,11},{8,12},{9,5},{1... | collective-permute-start | bytes 172040 | tf_op jit(solution)/shard_map/ppermute | solution.py:260
  13.8 5.1 %collective-permute-start.4 = (f32[56,256]{1,0:T(8,128)S(1)}, f32[56,256]{1,0:T(8,128)S(1)}, u32[]{:S(2)}, u32[]{:S(2)}) collective-permute-start(f32[56,256]{1,0:T(8,128)S(1)} %get-tuple-element.12), channel_id=1, source_target_pairs={{0,6},{1,15},{2,4},{3,13},{4,2},{5,11},{6,0},{7,9},{8,14},{9,7},{1... | collective-permute-start | bytes 172040 | tf_op jit(solution)/shard_map/ppermute | solution.py:260
  19.7 6.7 %collective-permute-start.5 = (f32[80,512]{1,0:T(8,128)S(1)}, f32[80,512]{1,0:T(8,128)S(1)}, u32[]{:S(2)}, u32[]{:S(2)}) collective-permute-start(f32[80,512]{1,0:T(8,128)S(1)} %grads.1.part_ref), channel_id=1, source_target_pairs={{0,1},{1,0},{2,3},{3,2},{4,5},{5,4},{6,7},{7,6},{8,9},{9,8},{10,11... | collective-permute-start | bytes 491528 | tf_op jit(solution)/shard_map/ppermute | solution.py:252
  26.7 4.7 %collective-permute-start.9 = (f32[40,128]{1,0:T(8,128)S(1)}, f32[40,128]{1,0:T(8,128)S(1)}, u32[]{:S(2)}, u32[]{:S(2)}) collective-permute-start(f32[40,128]{1,0:T(8,128)S(1)} %gram.1), channel_id=1, source_target_pairs={{0,6},{1,15},{2,4},{3,13},{4,2},{5,11},{6,0},{7,9},{8,14},{9,7},{1... | collective-permute-start | bytes 61448 | tf_op jit(solution)/shard_map/ppermute | solution.py:260
  26.7 4.7 %collective-permute-start.8 = (f32[40,128]{1,0:T(8,128)S(1)}, f32[40,128]{1,0:T(8,128)S(1)}, u32[]{:S(2)}, u32[]{:S(2)}) collective-permute-start(f32[40,128]{1,0:T(8,128)S(1)} %gram.1), channel_id=1, source_target_pairs={{0,4},{1,13},{2,6},{3,15},{4,0},{5,9},{6,2},{7,11},{8,12},{9,5},{1... | collective-permute-start | bytes 61448 | tf_op jit(solution)/shard_map/ppermute | solution.py:260
  28.7 3.8 %collective-permute-start.7 = (f32[40,128]{1,0:T(8,128)S(1)}, f32[40,128]{1,0:T(8,128)S(1)}, u32[]{:S(2)}, u32[]{:S(2)}) collective-permute-start(f32[40,128]{1,0:T(8,128)S(1)} %gram.1), channel_id=1, source_target_pairs={{0,2},{1,11},{2,0},{3,9},{4,6},{5,15},{6,4},{7,13},{8,10},{9,3},{1... | collective-permute-start | bytes 61448 | tf_op jit(solution)/shard_map/ppermute | solution.py:260
  30.2 2.3 %collective-permute-start.6 = (f32[40,128]{1,0:T(8,128)S(1)}, f32[40,128]{1,0:T(8,128)S(1)}, u32[]{:S(2)}, u32[]{:S(2)}) collective-permute-start(f32[40,128]{1,0:T(8,128)S(1)} %gram.1), channel_id=1, source_target_pairs={{0,0},{1,9},{2,2},{3,11},{4,4},{5,13},{6,6},{7,15},{8,8},{9,1},{10... | collective-permute-start | bytes 61448 | tf_op jit(solution)/shard_map/ppermute | solution.py:260
  32.5 5.3 %collective-permute-start.10 = (f32[40,128]{1,0:T(8,128)S(1)}, f32[40,128]{1,0:T(8,128)S(1)}, u32[]{:S(2)}, u32[]{:S(2)}) collective-permute-start(f32[40,128]{1,0:T(8,128)S(1)} %add_add_fusion.x_ref), channel_id=1, source_target_pairs={{0,1},{1,0},{2,3},{3,2},{4,5},{5,4},{6,7},{7,6},{8,9},{9,8},{10,11... | collective-permute-start | bytes 61448 | tf_op jit(solution)/shard_map/ppermute | solution.py:252

commit v5 on v4

--- a/solution.py
+++ b/solution.py
@@ -11,6 +11,7 @@
 DOC_DEV = 8
 LANES = 128
 DEPTH = 256
+FLIGHT = 8
 NT = (((1,), (1,)), ((), ()))
 HIGHEST = lax.Precision.HIGHEST
 VMEM = pl.BlockSpec(memory_space=pltpu.VMEM)
@@ -30,11 +31,19 @@
 
 def project_kernel(sizes, h_ref, g_ref, pin_ref, pout_ref, out_ref, h_buf, g_buf, pin_buf, pout_buf, sems):
     h_size, h_count, g_size, g_count = sizes
-    copies = {}
+    copies, order = {}, []
 
     def copy(name, src, dst):
         copies[name] = pltpu.make_async_copy(src, dst, sems.at[len(copies)])
-        copies[name].start()
+        order.append(name)
+        if len(order) <= FLIGHT:
+            copies[name].start()
+
+    def arrive(name):
+        copies[name].wait()
+        ahead = order.index(name) + FLIGHT
+        if ahead < len(order):
+            copies[order[ahead]].start()
 
     copy("po", pout_ref, pout_buf)
     for i in range(g_count):
@@ -49,7 +58,7 @@
         total = None
         depth = min(size, DEPTH)
         for i in range(count):
-            copies[tag, i].wait()
+            arrive((tag, i))
             parts = []
             for j in range(size // depth):
                 at = pl.ds(i * size + j * depth, depth)
@@ -58,9 +67,9 @@
             total = part if total is None else total + part
         return total
 
-    copies["po"].wait()
+    arrive("po")
     grad = run("g", g_count, g_size, pout_buf, g_buf)
-    copies["pi"].wait()
+    arrive("pi")
     inp = run("h", h_count, h_size, pin_buf, h_buf)
     out_ref[...] = jnp.concatenate([grad, inp], axis=1).T
 
@@ -93,82 +102,112 @@
     )(hidden, out_grad, pin_t, pout_t)
 
 
+def partners(dp):
+    order = [m for far in (True, False) for m in range(1, dp - 1) if (2 * m >= dp) == far]
+    return order[0::2], order[1::2]
+
+
+def partner(dp, t):
+    first, second = partners(dp)
+    return jnp.where(lax.axis_index("tensor") == 0, first[t], second[t])
+
+
 def pack_kernel(pb, rows_a, rows_b, part_ref, recv_ref, extra_ref, *refs):
     outs, total_ref = refs[:-1], refs[-1]
     total_ref[...] = part_ref[...] + recv_ref[...]
-    ranks = total_ref.shape[0] // 2
-    first = lax.axis_index("tensor") * len(outs)
+    ranks, lanes = total_ref.shape[0] // 2, total_ref.shape[1]
+    dp = extra_ref.shape[0]
     me = lax.axis_index("dp")
-    for t, out_ref in enumerate(outs):
-        owner = me ^ (first + t)
+    lead = lax.axis_index("tensor") == 0
+
+    def rows(out_ref, owner, pick):
         p, q = owner // pb, owner % pb
-        out_ref[0:rows_a, :] = total_ref[pl.ds(pl.multiple_of(p * rows_a, rows_a), rows_a), :]
-        out_ref[rows_a:rows_a + rows_b, :] = total_ref[pl.ds(pl.multiple_of(ranks + q * rows_b, rows_b), rows_b), :]
-        out_ref[rows_a + rows_b:, :] = extra_ref[owner]
+        out_ref[0:rows_a, :] = pick(total_ref[pl.ds(pl.multiple_of(p * rows_a, rows_a), rows_a), :])
+        out_ref[rows_a:rows_a + rows_b, :] = pick(total_ref[pl.ds(pl.multiple_of(ranks + q * rows_b, rows_b), rows_b), :])
+        out_ref[rows_a + rows_b:, :] = pick(extra_ref[owner])
+
+    def half(x):
+        return jnp.where(lead, x[:, :lanes // 2], x[:, lanes // 2:])
+
+    for t, out_ref in enumerate(outs[:-2]):
+        rows(out_ref, me ^ partner(dp, t), lambda x: x)
+    rows(outs[-2], me ^ (dp - 1), half)
+    rows(outs[-1], me, half)
 
 
 def pack(part, recv, extra, pa, pb):
     ranks, lanes = part.shape[0] // 2, part.shape[1]
     rows_a, rows_b = ranks // pa, ranks // pb
     rows = rows_a + rows_b + extra.shape[1]
-    count = pa * pb // 2
+    count = pa * pb // 2 - 1
+    whole, half = (jax.ShapeDtypeStruct((rows, n), jnp.float32) for n in (lanes, lanes // 2))
     return pl.pallas_call(
         functools.partial(pack_kernel, pb, rows_a, rows_b),
-        out_shape=(jax.ShapeDtypeStruct((rows, lanes), jnp.float32),) * count,
+        out_shape=(whole,) * count + (half, half),
         in_specs=[VMEM] * 3,
-        out_specs=(VMEM,) * count,
+        out_specs=(VMEM,) * (count + 2),
         scratch_shapes=[pltpu.VMEM(part.shape, jnp.float32)],
         compiler_params=vmem_params(16),
         name="pack",
     )(part, recv, extra)
 
 
-def grads_kernel(rows_a, rows_b, docs, *refs):
+def grads_kernel(rows_a, rows_b, docs, dp, *refs):
     xs, (out_ref, outer_ref, member_ref) = refs[:-3], refs[-3:]
-    lanes = xs[0].shape[1]
+    whole = xs[0].shape[1]
     wide = rows_a * rows_b
     first = rows_a + rows_b
     queries = out_ref.shape[0] - docs
-    per = queries // (2 * len(xs))
-    doc = lax.broadcasted_iota(jnp.int32, (docs, lanes), 0)
-    place = lax.broadcasted_iota(jnp.int32, (queries, wide), 0)
-    begin = lax.axis_index("tensor") * len(xs)
+    per = queries // dp
+    place = lax.broadcasted_iota(jnp.int32, (queries, whole), 0)
+    lane = lax.broadcasted_iota(jnp.int32, (queries, whole), 1)
     me = lax.axis_index("dp")
-    asked = jnp.zeros((queries, wide), jnp.float32)
+    core = lax.axis_index("tensor")
+    mine = lane // (whole // 2) == core
+    flat = [jnp.zeros((queries, whole), jnp.float32)] * (per * wide // whole)
+    start = 0
     for t, x_ref in enumerate(xs):
-        at = slice(t * lanes, (t + 1) * lanes)
+        lanes = x_ref.shape[1]
+        at = slice(start, start + lanes)
+        start += lanes
         g, b = x_ref[0:rows_a, :], x_ref[rows_a:first, :]
         ids = x_ref[first:first + 1, :].astype(jnp.int32)
+        doc = lax.broadcasted_iota(jnp.int32, (docs, lanes), 0)
         member_ref[:, at] = jnp.where(doc == ids, 1.0, 0.0).astype(jnp.bfloat16)
         outer = (g[:, None, :] * b[None, :, :]).reshape(wide, lanes)
         high = outer.astype(jnp.bfloat16)
         outer_ref[0:wide, at] = high
         outer_ref[wide:, at] = (outer - high.astype(jnp.float32)).astype(jnp.bfloat16)
-        source = me ^ (begin + t)
-        for q in range(per):
-            if wide >= lanes:
-                span = wide // lanes
-                row = first + 1 + q * span
-                line = jnp.concatenate([x_ref[row + j:row + j + 1, :] for j in range(span)], axis=1)
-            else:
-                line = x_ref[first + 1:first + 2, q * wide:(q + 1) * wide]
-            asked = jnp.where(place == source * per + q, line, asked)
+        gap = partner(dp, t) if t < len(xs) - 2 else dp - 1 if t == len(xs) - 2 else 0
+        held = place // per == me ^ gap
+        if lanes < whole:
+            held = jnp.logical_and(held, mine)
+        for j in range(len(flat)):
+            line = x_ref[first + 1 + j:first + 2 + j, :]
+            if lanes < whole:
+                line = jnp.concatenate([line, line], axis=1)
+            flat[j] = jnp.where(held, line, flat[j])
     sums = lax.dot_general(member_ref[...], outer_ref[...], NT, preferred_element_type=jnp.float32)
     out_ref[0:docs, :] = (sums[:, wide:] + sums[:, :wide]) * (TOK_DEV ** -0.5)
+    flat = jnp.concatenate(flat, axis=1)
+    asked = jnp.zeros((queries, wide), jnp.float32)
+    which = lax.broadcasted_iota(jnp.int32, (queries, wide), 0) % per
+    for q in range(per):
+        asked = jnp.where(which == q, flat[:, q * wide:(q + 1) * wide], asked)
     out_ref[docs:, :] = asked
 
 
-def grads_of(xs, rows_a, rows_b, docs, queries):
-    lanes = xs[0].shape[1]
+def grads_of(xs, rows_a, rows_b, docs, queries, dp):
+    tokens = sum(x.shape[1] for x in xs)
     wide = rows_a * rows_b
     return pl.pallas_call(
-        functools.partial(grads_kernel, rows_a, rows_b, docs),
+        functools.partial(grads_kernel, rows_a, rows_b, docs, dp),
         out_shape=jax.ShapeDtypeStruct((docs + queries, wide), jnp.float32),
         in_specs=[VMEM] * len(xs),
         out_specs=VMEM,
         scratch_shapes=[
-            pltpu.VMEM((2 * wide, len(xs) * lanes), jnp.bfloat16),
-            pltpu.VMEM((docs, len(xs) * lanes), jnp.bfloat16),
+            pltpu.VMEM((2 * wide, tokens), jnp.bfloat16),
+            pltpu.VMEM((docs, tokens), jnp.bfloat16),
         ],
         compiler_params=vmem_params(40),
         name="grads",
@@ -253,12 +292,17 @@
 
 
 def trade(xs):
-    dp, count = lax.axis_size("dp"), len(xs)
+    dp = lax.axis_size("dp")
     got = []
-    for t, x in enumerate(xs):
-        pairs = [(i * 2 + k, (i ^ (k * count + t)) * 2 + k) for i in range(dp) for k in range(2)]
+    for x, ms in zip(xs, zip(*partners(dp))):
+        pairs = [(i * 2 + k, (i ^ m) * 2 + k) for i in range(dp) for k, m in enumerate(ms)]
         got.append(lax.ppermute(x, ("dp", "tensor"), pairs))
     return got
+
+
+def trade_last(x):
+    dp = lax.axis_size("dp")
+    return lax.ppermute(x, "dp", [(i, i ^ (dp - 1)) for i in range(dp)])
 
 
 def local(hidden, out_grad, proj_in, proj_out, doc_ids, queries):
@@ -280,12 +324,14 @@
     extra = jnp.concatenate([jnp.broadcast_to(ids, (dp, 1, lanes)), asked], axis=1)
     extra = jnp.pad(extra, ((0, 0), (0, -extra.shape[1] % 8), (0, 0)))
 
-    blocks = trade(pack(part, recv, extra, pa, pb))
-    grads = grads_of(blocks, rows_a, rows_b, docs, num_queries)
+    *blocks, last, own = pack(part, recv, extra, pa, pb)
+    blocks = trade(blocks) + [trade_last(last), own]
+    grads = grads_of(blocks, rows_a, rows_b, docs, num_queries, dp)
     share = gram(grads, swap_cores(grads), docs)
     scale = float(ranks * ranks) ** -0.5
     if docs <= 64:
-        share = sum(trade([share] * (dp // 2)))
+        halves = jnp.where(lax.axis_index("tensor") == 0, share, trade_last(share))
+        share = sum(trade([share] * (dp // 2 - 1)), halves)
         return solve(share, swap_cores(share), docs, num_queries, scale).T
     share = lax.psum(share, "dp")
     return solve_large(jnp.concatenate([share[:, :docs], share[:, docs:]], axis=0).T, docs, num_queries, scale).T

time: 40.6 us -> 36.9 us (0.909)
  starting transfers between devices: 20 us -> 17.9 us
  waiting for transfers between devices: 9.21 us -> 7.63 us
    ppermute x3, starting transfers between devices: 10.6 us -> 1.22 us  [swap_cores(): return lax.ppermute(x, 'tensor', [(i, cores - 1 - i) for i in range(cores)])]
    ppermute x0 -> x2, starting transfers between devices: none -> 7.57 us  [trade_last(): return lax.ppermute(x, 'dp', [(i, i ^ dp - 1) for i in range(dp)])]
    ppermute x8 -> x6, waiting for transfers between devices: 6.69 us -> 2.1 us  [trade(): got.append(lax.ppermute(x, ('dp', 'tensor'), pairs))]
    ppermute x0 -> x2, waiting for transfers between devices: none -> 2.69 us  [trade_last(): return lax.ppermute(x, 'dp', [(i, i ^ dp - 1) for i in range(dp)])]
    ppermute x8 -> x6, starting transfers between devices: 9.34 us -> 9.08 us  [trade(): got.append(lax.ppermute(x, ('dp', 'tensor'), pairs))]
  transfers between devices with their start and end apart: 11 -> 11, of which waited for: 8 -> 6; matrix products, arithmetic and copies ran while one was open for 1% -> 1% of each run, Pallas kernels for 0% -> 0%
where the time goes in v5:
time: 36.9 us; the launch traced here: 36.8 us
  starting transfers between devices  17.9 us (49%)
  Pallas kernels  10.9 us (30%)
  waiting for transfers between devices  7.63 us (21%)
    ppermute x6, starting transfers between devices, trade(): got.append(lax.ppermute(x, ('dp', 'tensor'), pairs))  9.08 us
    ppermute x2, starting transfers between devices, trade_last(): return lax.ppermute(x, 'dp', [(i, i ^ dp - 1) for i in range(dp)])  7.57 us
    pallas_call x1, Pallas kernels, project(): pl.pallas_call(functools.partial(project_kernel, (h_size, h_count, g_size...  7.02 us
    ppermute x3, waiting for transfers between devices, swap_cores(): return lax.ppermute(x, 'tensor', [(i, cores - 1 - i) for i in range(cores)])  2.83 us
    ppermute x2, waiting for transfers between devices, trade_last(): return lax.ppermute(x, 'dp', [(i, i ^ dp - 1) for i in range(dp)])  2.69 us
    pallas_call x1, Pallas kernels, solve(): pl.pallas_call(functools.partial(solve_kernel, docs, queries, scale), out...  2.61 us
    ppermute x6, waiting for transfers between devices, trade(): got.append(lax.ppermute(x, ('dp', 'tensor'), pairs))  2.1 us
    ppermute x3, starting transfers between devices, swap_cores(): return lax.ppermute(x, 'tensor', [(i, cores - 1 - i) for i in range(cores)])  1.22 us
  transfers between devices with their start and end apart: 11, of which 6 were waited for; matrix products, arithmetic and copies ran while one was open for 1% of the time, Pallas kernels for 0%

profile of v5, /device:TPU:0, one launch (start us, length us, event | category | flops | bytes accessed | tf_op | source)
XLA Modules:
  0.0 36.8 jit_solution(18371197698301641948)
XLA Ops:
  0.0 0.0 copy-start
  0.0 0.0 copy-start.1
  0.0 7.0 %project.1.part_ref = f32[128,256]{1,0:T(8,128)S(1)} custom-call(bf16[256,14336]{1,0:T(8,128)(2,1)} %h_ref.1, bf16[256,4096]{1,0:T(8,128)(2,1)} %g_ref.1, bf16[64,14336]{1,0:T(8,128)(2,1)} %bitcast.8, bf16[64,4096]{1,0:T(8,128)(2,1)} %bitcast.9), custom_call_target="tpu_custom_call" | custom-call | flops 603979776 | bytes 11796480 | tf_op jit(solution)/shard_map/project/pallas_call | solution.py:83
  7.0 0.5 %collective-permute-start = (f32[128,256]{1,0:T(8,128)S(1)}, f32[128,256]{1,0:T(8,128)S(1)}, u32[]{:S(2)}, u32[]{:S(2)}) collective-permute-start(f32[128,256]{1,0:T(8,128)S(1)} %project.1.part_ref), channel_id=1, source_target_pairs={{0,1},{1,0},{2,3},{3,2},{4,5},{5,4},{6,7},{7,6},{8,9},{9,8},{10,11... | collective-permute-start | bytes 393224 | tf_op jit(solution)/shard_map/ppermute | solution.py:291
  7.6 0.0 copy-done
  7.6 0.2 reshape.6
  7.7 0.1 reshape.7
  7.8 0.0 copy-done.1
  7.9 0.6 %collective-permute-done.recv_ref = f32[128,256]{1,0:T(8,128)S(1)} collective-permute-done((f32[128,256]{1,0:T(8,128)S(1)}, f32[128,256]{1,0:T(8,128)S(1)}, u32[]{:S(2)}, u32[]{:S(2)}) %collective-permute-start) | collective-permute-done | bytes 131104 | tf_op jit(solution)/shard_map/ppermute | solution.py:291
  8.5 0.1 pack.1
  8.6 4.0 %collective-permute-start.1 = (f32[56,256]{1,0:T(8,128)S(1)}, f32[56,256]{1,0:T(8,128)S(1)}, u32[]{:S(2)}, u32[]{:S(2)}) collective-permute-start(f32[56,256]{1,0:T(8,128)S(1)} %get-tuple-element.10), channel_id=1, source_target_pairs={{0,8},{1,11},{2,10},{3,9},{4,12},{5,15},{6,14},{7,13},{8,0},{9,3},... | collective-permute-start | bytes 172040 | tf_op jit(solution)/shard_map/ppermute | solution.py:299
  12.6 1.3 %collective-permute-start.2 = (f32[56,256]{1,0:T(8,128)S(1)}, f32[56,256]{1,0:T(8,128)S(1)}, u32[]{:S(2)}, u32[]{:S(2)}) collective-permute-start(f32[56,256]{1,0:T(8,128)S(1)} %get-tuple-element.11), channel_id=1, source_target_pairs={{0,12},{1,3},{2,14},{3,1},{4,8},{5,7},{6,10},{7,5},{8,4},{9,11},{1... | collective-permute-start | bytes 172040 | tf_op jit(solution)/shard_map/ppermute | solution.py:299
  14.0 0.2 collective-permute-start.3
  14.2 3.9 %collective-permute-start.4 = (f32[56,128]{1,0:T(8,128)S(1)}, f32[56,128]{1,0:T(8,128)S(1)}, u32[]{:S(2)}, u32[]{:S(2)}) collective-permute-start(f32[56,128]{1,0:T(8,128)S(1)} %get-tuple-element.13), channel_id=1, source_target_pairs={{0,14},{2,12},{4,10},{6,8},{8,6},{10,4},{12,2},{14,0},{1,15},{3,13... | collective-permute-start | bytes 86024 | tf_op jit(solution)/shard_map/ppermute | solution.py:305
  18.1 2.7 %collective-permute-done.4.refs_3_ = f32[56,128]{1,0:T(8,128)S(1)} collective-permute-done((f32[56,128]{1,0:T(8,128)S(1)}, f32[56,128]{1,0:T(8,128)S(1)}, u32[]{:S(2)}, u32[]{:S(2)}) %collective-permute-start.4) | collective-permute-done | bytes 28704 | tf_op jit(solution)/shard_map/ppermute | solution.py:305
  20.8 0.0 collective-permute-done.1.refs_0_
  20.8 0.0 collective-permute-done.2.refs_1_
  20.8 0.0 collective-permute-done.3.refs_2_
  20.8 0.8 %grads.1.part_ref = f32[80,512]{1,0:T(8,128)S(1)} custom-call(f32[56,256]{1,0:T(8,128)S(1)} %collective-permute-done.1.refs_0_, f32[56,256]{1,0:T(8,128)S(1)} %collective-permute-done.2.refs_1_, f32[56,256]{1,0:T(8,128)S(1)} %collective-permute-done.3.refs_2_, f32[56,128]{1,0:T(8,128)S(1)} %collective-permute-done.4.refs_3_, ...), custom_call_target="tpu_custom_call" | custom-call | tf_op jit(solution)/shard_map/grads/pallas_call | solution.py:203
  21.6 0.6 %collective-permute-start.5 = (f32[80,512]{1,0:T(8,128)S(1)}, f32[80,512]{1,0:T(8,128)S(1)}, u32[]{:S(2)}, u32[]{:S(2)}) collective-permute-start(f32[80,512]{1,0:T(8,128)S(1)} %grads.1.part_ref), channel_id=1, source_target_pairs={{0,1},{1,0},{2,3},{3,2},{4,5},{5,4},{6,7},{7,6},{8,9},{9,8},{10,11... | collective-permute-start | bytes 491528 | tf_op jit(solution)/shard_map/ppermute | solution.py:291
  22.3 1.0 %collective-permute-done.5.recv_ref = f32[80,512]{1,0:T(8,128)S(1)} collective-permute-done((f32[80,512]{1,0:T(8,128)S(1)}, f32[80,512]{1,0:T(8,128)S(1)}, u32[]{:S(2)}, u32[]{:S(2)}) %collective-permute-start.5) | collective-permute-done | bytes 163872 | tf_op jit(solution)/shard_map/ppermute | solution.py:291
  23.3 0.4 gram.1
  23.6 3.7 %collective-permute-start.6 = (f32[40,128]{1,0:T(8,128)S(1)}, f32[40,128]{1,0:T(8,128)S(1)}, u32[]{:S(2)}, u32[]{:S(2)}) collective-permute-start(f32[40,128]{1,0:T(8,128)S(1)} %gram.1), channel_id=1, source_target_pairs={{0,14},{2,12},{4,10},{6,8},{8,6},{10,4},{12,2},{14,0},{1,15},{3,13... | collective-permute-start | bytes 61448 | tf_op jit(solution)/shard_map/ppermute | solution.py:305
  27.3 0.0 collective-permute-start.7
  27.3 1.0 %collective-permute-start.8 = (f32[40,128]{1,0:T(8,128)S(1)}, f32[40,128]{1,0:T(8,128)S(1)}, u32[]{:S(2)}, u32[]{:S(2)}) collective-permute-start(f32[40,128]{1,0:T(8,128)S(1)} %gram.1), channel_id=1, source_target_pairs={{0,12},{1,3},{2,14},{3,1},{4,8},{5,7},{6,10},{7,5},{8,4},{9,11},{1... | collective-permute-start | bytes 61448 | tf_op jit(solution)/shard_map/ppermute | solution.py:299
  28.3 2.5 %collective-permute-start.9 = (f32[40,128]{1,0:T(8,128)S(1)}, f32[40,128]{1,0:T(8,128)S(1)}, u32[]{:S(2)}, u32[]{:S(2)}) collective-permute-start(f32[40,128]{1,0:T(8,128)S(1)} %gram.1), channel_id=1, source_target_pairs={{0,4},{1,7},{2,6},{3,5},{4,0},{5,3},{6,2},{7,1},{8,12},{9,15},{10,... | collective-permute-start | bytes 61448 | tf_op jit(solution)/shard_map/ppermute | solution.py:299
  30.8 0.0 collective-permute-done.6
  30.8 1.2 %collective-permute-done.7 = f32[40,128]{1,0:T(8,128)S(1)} collective-permute-done((f32[40,128]{1,0:T(8,128)S(1)}, f32[40,128]{1,0:T(8,128)S(1)}, u32[]{:S(2)}, u32[]{:S(2)}) %collective-permute-start.7) | collective-permute-done | bytes 20512 | tf_op jit(solution)/shard_map/ppermute | solution.py:299
  32.0 0.9 %collective-permute-done.8 = f32[40,128]{1,0:T(8,128)S(1)} collective-permute-done((f32[40,128]{1,0:T(8,128)S(1)}, f32[40,128]{1,0:T(8,128)S(1)}, u32[]{:S(2)}, u32[]{:S(2)}) %collective-permute-start.8) | collective-permute-done | bytes 20512 | tf_op jit(solution)/shard_map/ppermute | solution.py:299
  32.9 0.0 collective-permute-done.9
  32.9 0.1 collective-permute-start.10
  33.0 1.2 %collective-permute-done.10.recv_ref = f32[40,128]{1,0:T(8,128)S(1)} collective-permute-done((f32[40,128]{1,0:T(8,128)S(1)}, f32[40,128]{1,0:T(8,128)S(1)}, u32[]{:S(2)}, u32[]{:S(2)}) %collective-permute-start.10) | collective-permute-done | bytes 20512 | tf_op jit(solution)/shard_map/ppermute | solution.py:291
  34.2 2.6 %solve.1 = f32[8,16]{1,0:T(8,128)} custom-call(f32[40,128]{1,0:T(8,128)S(1)} %add_add_fusion.x_ref, f32[40,128]{1,0:T(8,128)S(1)} %collective-permute-done.10.recv_ref), custom_call_target="tpu_custom_call" | custom-call | tf_op jit(solution)/shard_map/solve/pallas_call | solution.py:270
  (5 shorter events, 0.1 us)
Async XLA Ops:
  0.0 7.6 %copy-start = (f32[2,4096]{1,0:T(2,128)S(1)}, f32[2,4096]{1,0:T(2,128)}, u32[]{:S(2)}) copy-start(f32[2,4096]{1,0:T(2,128)} %param.11) | copy-start | bytes 98308
  0.0 7.8 %copy-start.1 = (s32[256]{0:T(256)S(1)}, s32[256]{0:T(256)}, u32[]{:S(2)}) copy-start(s32[256]{0:T(256)} %param.10) | copy-start | bytes 3076
  7.0 1.5 %collective-permute-start = (f32[128,256]{1,0:T(8,128)S(1)}, f32[128,256]{1,0:T(8,128)S(1)}, u32[]{:S(2)}, u32[]{:S(2)}) collective-permute-start(f32[128,256]{1,0:T(8,128)S(1)} %project.1.part_ref), channel_id=1, source_target_pairs={{0,1},{1,0},{2,3},{3,2},{4,5},{5,4},{6,7},{7,6},{8,9},{9,8},{10,11... | collective-permute-start | bytes 393224 | tf_op jit(solution)/shard_map/ppermute | solution.py:291
  8.6 12.2 %collective-permute-start.1 = (f32[56,256]{1,0:T(8,128)S(1)}, f32[56,256]{1,0:T(8,128)S(1)}, u32[]{:S(2)}, u32[]{:S(2)}) collective-permute-start(f32[56,256]{1,0:T(8,128)S(1)} %get-tuple-element.10), channel_id=1, source_target_pairs={{0,8},{1,11},{2,10},{3,9},{4,12},{5,15},{6,14},{7,13},{8,0},{9,3},... | collective-permute-start | bytes 172040 | tf_op jit(solution)/shard_map/ppermute | solution.py:299
  12.6 8.2 %collective-permute-start.2 = (f32[56,256]{1,0:T(8,128)S(1)}, f32[56,256]{1,0:T(8,128)S(1)}, u32[]{:S(2)}, u32[]{:S(2)}) collective-permute-start(f32[56,256]{1,0:T(8,128)S(1)} %get-tuple-element.11), channel_id=1, source_target_pairs={{0,12},{1,3},{2,14},{3,1},{4,8},{5,7},{6,10},{7,5},{8,4},{9,11},{1... | collective-permute-start | bytes 172040 | tf_op jit(solution)/shard_map/ppermute | solution.py:299
  14.0 6.8 %collective-permute-start.3 = (f32[56,256]{1,0:T(8,128)S(1)}, f32[56,256]{1,0:T(8,128)S(1)}, u32[]{:S(2)}, u32[]{:S(2)}) collective-permute-start(f32[56,256]{1,0:T(8,128)S(1)} %get-tuple-element.12), channel_id=1, source_target_pairs={{0,4},{1,7},{2,6},{3,5},{4,0},{5,3},{6,2},{7,1},{8,12},{9,15},{10,... | collective-permute-start | bytes 172040 | tf_op jit(solution)/shard_map/ppermute | solution.py:299
  14.2 6.6 %collective-permute-start.4 = (f32[56,128]{1,0:T(8,128)S(1)}, f32[56,128]{1,0:T(8,128)S(1)}, u32[]{:S(2)}, u32[]{:S(2)}) collective-permute-start(f32[56,128]{1,0:T(8,128)S(1)} %get-tuple-element.13), channel_id=1, source_target_pairs={{0,14},{2,12},{4,10},{6,8},{8,6},{10,4},{12,2},{14,0},{1,15},{3,13... | collective-permute-start | bytes 86024 | tf_op jit(solution)/shard_map/ppermute | solution.py:305
  21.6 1.7 %collective-permute-start.5 = (f32[80,512]{1,0:T(8,128)S(1)}, f32[80,512]{1,0:T(8,128)S(1)}, u32[]{:S(2)}, u32[]{:S(2)}) collective-permute-start(f32[80,512]{1,0:T(8,128)S(1)} %grads.1.part_ref), channel_id=1, source_target_pairs={{0,1},{1,0},{2,3},{3,2},{4,5},{5,4},{6,7},{7,6},{8,9},{9,8},{10,11... | collective-permute-start | bytes 491528 | tf_op jit(solution)/shard_map/ppermute | solution.py:291
  23.6 7.2 %collective-permute-start.6 = (f32[40,128]{1,0:T(8,128)S(1)}, f32[40,128]{1,0:T(8,128)S(1)}, u32[]{:S(2)}, u32[]{:S(2)}) collective-permute-start(f32[40,128]{1,0:T(8,128)S(1)} %gram.1), channel_id=1, source_target_pairs={{0,14},{2,12},{4,10},{6,8},{8,6},{10,4},{12,2},{14,0},{1,15},{3,13... | collective-permute-start | bytes 61448 | tf_op jit(solution)/shard_map/ppermute | solution.py:305
  27.3 4.7 %collective-permute-start.7 = (f32[40,128]{1,0:T(8,128)S(1)}, f32[40,128]{1,0:T(8,128)S(1)}, u32[]{:S(2)}, u32[]{:S(2)}) collective-permute-start(f32[40,128]{1,0:T(8,128)S(1)} %gram.1), channel_id=1, source_target_pairs={{0,8},{1,11},{2,10},{3,9},{4,12},{5,15},{6,14},{7,13},{8,0},{9,3},... | collective-permute-start | bytes 61448 | tf_op jit(solution)/shard_map/ppermute | solution.py:299
  27.3 5.6 %collective-permute-start.8 = (f32[40,128]{1,0:T(8,128)S(1)}, f32[40,128]{1,0:T(8,128)S(1)}, u32[]{:S(2)}, u32[]{:S(2)}) collective-permute-start(f32[40,128]{1,0:T(8,128)S(1)} %gram.1), channel_id=1, source_target_pairs={{0,12},{1,3},{2,14},{3,1},{4,8},{5,7},{6,10},{7,5},{8,4},{9,11},{1... | collective-permute-start | bytes 61448 | tf_op jit(solution)/shard_map/ppermute | solution.py:299
  28.3 4.6 %collective-permute-start.9 = (f32[40,128]{1,0:T(8,128)S(1)}, f32[40,128]{1,0:T(8,128)S(1)}, u32[]{:S(2)}, u32[]{:S(2)}) collective-permute-start(f32[40,128]{1,0:T(8,128)S(1)} %gram.1), channel_id=1, source_target_pairs={{0,4},{1,7},{2,6},{3,5},{4,0},{5,3},{6,2},{7,1},{8,12},{9,15},{10,... | collective-permute-start | bytes 61448 | tf_op jit(solution)/shard_map/ppermute | solution.py:299
  32.9 1.3 %collective-permute-start.10 = (f32[40,128]{1,0:T(8,128)S(1)}, f32[40,128]{1,0:T(8,128)S(1)}, u32[]{:S(2)}, u32[]{:S(2)}) collective-permute-start(f32[40,128]{1,0:T(8,128)S(1)} %add_add_fusion.x_ref), channel_id=1, source_target_pairs={{0,1},{1,0},{2,3},{3,2},{4,5},{5,4},{6,7},{7,6},{8,9},{9,8},{10,11... | collective-permute-start | bytes 61448 | tf_op jit(solution)/shard_map/ppermute | solution.py:291

commit v6 on v5

--- a/solution.py
+++ b/solution.py
@@ -10,8 +10,9 @@
 TOK_DEV = 256
 DOC_DEV = 8
 LANES = 128
-DEPTH = 256
-FLIGHT = 8
+ROWS = 64
+PIECES = 4
+FLIGHT = 5
 NT = (((1,), (1,)), ((), ()))
 HIGHEST = lax.Precision.HIGHEST
 VMEM = pl.BlockSpec(memory_space=pltpu.VMEM)
@@ -22,15 +23,7 @@
     return pltpu.CompilerParams(vmem_limit_bytes=int(mib * (1 << 20)))
 
 
-def chunks_of(length, most=1024):
-    size = most
-    while length % size:
-        size //= 2
-    return size, length // size
-
-
-def project_kernel(sizes, h_ref, g_ref, pin_ref, pout_ref, out_ref, h_buf, g_buf, pin_buf, pout_buf, sems):
-    h_size, h_count, g_size, g_count = sizes
+def project_kernel(h_ref, g_ref, pin_ref, pout_ref, out_ref, h_buf, g_buf, pin_buf, pout_buf, sems):
     copies, order = {}, []
 
     def copy(name, src, dst):
@@ -45,43 +38,39 @@
         if ahead < len(order):
             copies[order[ahead]].start()
 
+    chunks = [pl.ds(i, ROWS) for i in range(0, h_ref.shape[0], ROWS)]
     copy("po", pout_ref, pout_buf)
-    for i in range(g_count):
-        at = pl.ds(i * g_size, g_size)
-        copy(("g", i), g_ref.at[:, at], g_buf.at[:, at])
+    for i, at in enumerate(chunks):
+        copy(("g", i), g_ref.at[at], g_buf.at[at])
     copy("pi", pin_ref, pin_buf)
-    for i in range(h_count):
-        at = pl.ds(i * h_size, h_size)
-        copy(("h", i), h_ref.at[:, at], h_buf.at[:, at])
-
-    def run(tag, count, size, proj, data):
-        total = None
-        depth = min(size, DEPTH)
-        for i in range(count):
+    for i, at in enumerate(chunks):
+        copy(("h", i), h_ref.at[at], h_buf.at[at])
+
+    def run(tag, proj, data):
+        depth = data.shape[1] // PIECES
+        done = []
+        for i, at in enumerate(chunks):
             arrive((tag, i))
             parts = []
-            for j in range(size // depth):
-                at = pl.ds(i * size + j * depth, depth)
-                parts.append(lax.dot_general(data[:, at], proj[:, at], NT, preferred_element_type=jnp.float32))
-            part = sum(parts[1:], parts[0])
-            total = part if total is None else total + part
-        return total
-
+            for j in range(PIECES):
+                units = pl.ds(j * depth, depth)
+                parts.append(lax.dot_general(proj[:, units], data[at, units], NT, preferred_element_type=jnp.float32))
+            done.append(sum(parts[1:], parts[0]))
+        return jnp.concatenate(done, axis=1)
+
+    ranks = pout_ref.shape[0]
     arrive("po")
-    grad = run("g", g_count, g_size, pout_buf, g_buf)
+    out_ref[0:ranks, :] = run("g", pout_buf, g_buf)
     arrive("pi")
-    inp = run("h", h_count, h_size, pin_buf, h_buf)
-    out_ref[...] = jnp.concatenate([grad, inp], axis=1).T
+    out_ref[ranks:, :] = run("h", pin_buf, h_buf)
 
 
 def project(hidden, out_grad, pin_t, pout_t):
     tokens, units = hidden.shape
     width = out_grad.shape[1]
     ranks = pin_t.shape[0] + pout_t.shape[0]
-    h_size, h_count = chunks_of(units)
-    g_size, g_count = chunks_of(width)
-    return pl.pallas_call(
-        functools.partial(project_kernel, (h_size, h_count, g_size, g_count)),
+    return pl.pallas_call(
+        project_kernel,
         out_shape=jax.ShapeDtypeStruct((ranks, tokens), jnp.float32),
         in_specs=[HBM] * 4,
         out_specs=VMEM,
@@ -90,7 +79,7 @@
             pltpu.VMEM(out_grad.shape, out_grad.dtype),
             pltpu.VMEM(pin_t.shape, pin_t.dtype),
             pltpu.VMEM(pout_t.shape, pout_t.dtype),
-            pltpu.SemaphoreType.DMA((2 + g_count + h_count,)),
+            pltpu.SemaphoreType.DMA((2 + 2 * tokens // ROWS,)),
         ],
         compiler_params=vmem_params(53.5),
         cost_estimate=pl.CostEstimate(

time: 36.9 us -> 37.6 us (1.019)
  Pallas kernels: 10.9 us -> 11.5 us
    pallas_call x1, Pallas kernels: 7.02 us -> 7.68 us  [project(): pl.pallas_call(project_kernel, out_shape=jax.ShapeDtypeStruct((ranks, tok...]
where the time goes in v6:
time: 37.6 us; the launch traced here: 37.4 us
  starting transfers between devices  17.9 us (48%)
  Pallas kernels  11.5 us (31%)
  waiting for transfers between devices  7.62 us (20%)
    ppermute x6, starting transfers between devices, trade(): got.append(lax.ppermute(x, ('dp', 'tensor'), pairs))  9.08 us
    pallas_call x1, Pallas kernels, project(): pl.pallas_call(project_kernel, out_shape=jax.ShapeDtypeStruct((ranks, tok...  7.68 us
    ppermute x2, starting transfers between devices, trade_last(): return lax.ppermute(x, 'dp', [(i, i ^ dp - 1) for i in range(dp)])  7.57 us
    ppermute x3, waiting for transfers between devices, swap_cores(): return lax.ppermute(x, 'tensor', [(i, cores - 1 - i) for i in range(cores)])  2.83 us
    ppermute x2, waiting for transfers between devices, trade_last(): return lax.ppermute(x, 'dp', [(i, i ^ dp - 1) for i in range(dp)])  2.69 us
    pallas_call x1, Pallas kernels, solve(): pl.pallas_call(functools.partial(solve_kernel, docs, queries, scale), out...  2.61 us
    ppermute x6, waiting for transfers between devices, trade(): got.append(lax.ppermute(x, ('dp', 'tensor'), pairs))  2.1 us
    ppermute x3, starting transfers between devices, swap_cores(): return lax.ppermute(x, 'tensor', [(i, cores - 1 - i) for i in range(cores)])  1.23 us
  transfers between devices with their start and end apart: 11, of which 6 were waited for; matrix products, arithmetic and copies ran while one was open for 1% of the time, Pallas kernels for 0%

profile of v6, /device:TPU:0, one launch (start us, length us, event | category | flops | bytes accessed | tf_op | source)
XLA Modules:
  0.0 37.4 jit_solution(17973368039939608042)
XLA Ops:
  0.0 0.0 copy-start
  0.0 0.0 copy-start.1
  0.0 7.7 %project.1.part_ref = f32[128,256]{1,0:T(8,128)S(1)} custom-call(bf16[256,14336]{1,0:T(8,128)(2,1)} %h_ref.1, bf16[256,4096]{1,0:T(8,128)(2,1)} %g_ref.1, bf16[64,14336]{1,0:T(8,128)(2,1)} %bitcast.8, bf16[64,4096]{1,0:T(8,128)(2,1)} %bitcast.9), custom_call_target="tpu_custom_call" | custom-call | flops 603979776 | bytes 11796480 | tf_op jit(solution)/shard_map/project/pallas_call | solution.py:72
  7.7 0.5 %collective-permute-start = (f32[128,256]{1,0:T(8,128)S(1)}, f32[128,256]{1,0:T(8,128)S(1)}, u32[]{:S(2)}, u32[]{:S(2)}) collective-permute-start(f32[128,256]{1,0:T(8,128)S(1)} %project.1.part_ref), channel_id=1, source_target_pairs={{0,1},{1,0},{2,3},{3,2},{4,5},{5,4},{6,7},{7,6},{8,9},{9,8},{10,11... | collective-permute-start | bytes 393224 | tf_op jit(solution)/shard_map/ppermute | solution.py:280
  8.2 0.0 copy-done
  8.2 0.2 reshape.6
  8.4 0.1 reshape.7
  8.5 0.0 copy-done.1
  8.6 0.6 %collective-permute-done.recv_ref = f32[128,256]{1,0:T(8,128)S(1)} collective-permute-done((f32[128,256]{1,0:T(8,128)S(1)}, f32[128,256]{1,0:T(8,128)S(1)}, u32[]{:S(2)}, u32[]{:S(2)}) %collective-permute-start) | collective-permute-done | bytes 131104 | tf_op jit(solution)/shard_map/ppermute | solution.py:280
  9.2 0.1 pack.1
  9.3 4.0 %collective-permute-start.1 = (f32[56,256]{1,0:T(8,128)S(1)}, f32[56,256]{1,0:T(8,128)S(1)}, u32[]{:S(2)}, u32[]{:S(2)}) collective-permute-start(f32[56,256]{1,0:T(8,128)S(1)} %get-tuple-element.10), channel_id=1, source_target_pairs={{0,8},{1,11},{2,10},{3,9},{4,12},{5,15},{6,14},{7,13},{8,0},{9,3},... | collective-permute-start | bytes 172040 | tf_op jit(solution)/shard_map/ppermute | solution.py:288
  13.3 1.3 %collective-permute-start.2 = (f32[56,256]{1,0:T(8,128)S(1)}, f32[56,256]{1,0:T(8,128)S(1)}, u32[]{:S(2)}, u32[]{:S(2)}) collective-permute-start(f32[56,256]{1,0:T(8,128)S(1)} %get-tuple-element.11), channel_id=1, source_target_pairs={{0,12},{1,3},{2,14},{3,1},{4,8},{5,7},{6,10},{7,5},{8,4},{9,11},{1... | collective-permute-start | bytes 172040 | tf_op jit(solution)/shard_map/ppermute | solution.py:288
  14.6 0.2 collective-permute-start.3
  14.8 3.9 %collective-permute-start.4 = (f32[56,128]{1,0:T(8,128)S(1)}, f32[56,128]{1,0:T(8,128)S(1)}, u32[]{:S(2)}, u32[]{:S(2)}) collective-permute-start(f32[56,128]{1,0:T(8,128)S(1)} %get-tuple-element.13), channel_id=1, source_target_pairs={{0,14},{2,12},{4,10},{6,8},{8,6},{10,4},{12,2},{14,0},{1,15},{3,13... | collective-permute-start | bytes 86024 | tf_op jit(solution)/shard_map/ppermute | solution.py:294
  18.7 2.7 %collective-permute-done.4.refs_3_ = f32[56,128]{1,0:T(8,128)S(1)} collective-permute-done((f32[56,128]{1,0:T(8,128)S(1)}, f32[56,128]{1,0:T(8,128)S(1)}, u32[]{:S(2)}, u32[]{:S(2)}) %collective-permute-start.4) | collective-permute-done | bytes 28704 | tf_op jit(solution)/shard_map/ppermute | solution.py:294
  21.4 0.0 collective-permute-done.1.refs_0_
  21.4 0.0 collective-permute-done.2.refs_1_
  21.4 0.0 collective-permute-done.3.refs_2_
  21.4 0.8 %grads.1.part_ref = f32[80,512]{1,0:T(8,128)S(1)} custom-call(f32[56,256]{1,0:T(8,128)S(1)} %collective-permute-done.1.refs_0_, f32[56,256]{1,0:T(8,128)S(1)} %collective-permute-done.2.refs_1_, f32[56,256]{1,0:T(8,128)S(1)} %collective-permute-done.3.refs_2_, f32[56,128]{1,0:T(8,128)S(1)} %collective-permute-done.4.refs_3_, ...), custom_call_target="tpu_custom_call" | custom-call | tf_op jit(solution)/shard_map/grads/pallas_call | solution.py:192
  22.3 0.6 %collective-permute-start.5 = (f32[80,512]{1,0:T(8,128)S(1)}, f32[80,512]{1,0:T(8,128)S(1)}, u32[]{:S(2)}, u32[]{:S(2)}) collective-permute-start(f32[80,512]{1,0:T(8,128)S(1)} %grads.1.part_ref), channel_id=1, source_target_pairs={{0,1},{1,0},{2,3},{3,2},{4,5},{5,4},{6,7},{7,6},{8,9},{9,8},{10,11... | collective-permute-start | bytes 491528 | tf_op jit(solution)/shard_map/ppermute | solution.py:280
  22.9 1.0 %collective-permute-done.5.recv_ref = f32[80,512]{1,0:T(8,128)S(1)} collective-permute-done((f32[80,512]{1,0:T(8,128)S(1)}, f32[80,512]{1,0:T(8,128)S(1)}, u32[]{:S(2)}, u32[]{:S(2)}) %collective-permute-start.5) | collective-permute-done | bytes 163872 | tf_op jit(solution)/shard_map/ppermute | solution.py:280
  23.9 0.4 gram.1
  24.3 3.7 %collective-permute-start.6 = (f32[40,128]{1,0:T(8,128)S(1)}, f32[40,128]{1,0:T(8,128)S(1)}, u32[]{:S(2)}, u32[]{:S(2)}) collective-permute-start(f32[40,128]{1,0:T(8,128)S(1)} %gram.1), channel_id=1, source_target_pairs={{0,14},{2,12},{4,10},{6,8},{8,6},{10,4},{12,2},{14,0},{1,15},{3,13... | collective-permute-start | bytes 61448 | tf_op jit(solution)/shard_map/ppermute | solution.py:294
  28.0 0.0 collective-permute-start.7
  28.0 1.0 %collective-permute-start.8 = (f32[40,128]{1,0:T(8,128)S(1)}, f32[40,128]{1,0:T(8,128)S(1)}, u32[]{:S(2)}, u32[]{:S(2)}) collective-permute-start(f32[40,128]{1,0:T(8,128)S(1)} %gram.1), channel_id=1, source_target_pairs={{0,12},{1,3},{2,14},{3,1},{4,8},{5,7},{6,10},{7,5},{8,4},{9,11},{1... | collective-permute-start | bytes 61448 | tf_op jit(solution)/shard_map/ppermute | solution.py:288
  29.0 2.5 %collective-permute-start.9 = (f32[40,128]{1,0:T(8,128)S(1)}, f32[40,128]{1,0:T(8,128)S(1)}, u32[]{:S(2)}, u32[]{:S(2)}) collective-permute-start(f32[40,128]{1,0:T(8,128)S(1)} %gram.1), channel_id=1, source_target_pairs={{0,4},{1,7},{2,6},{3,5},{4,0},{5,3},{6,2},{7,1},{8,12},{9,15},{10,... | collective-permute-start | bytes 61448 | tf_op jit(solution)/shard_map/ppermute | solution.py:288
  31.5 0.0 collective-permute-done.6
  31.5 1.2 %collective-permute-done.7 = f32[40,128]{1,0:T(8,128)S(1)} collective-permute-done((f32[40,128]{1,0:T(8,128)S(1)}, f32[40,128]{1,0:T(8,128)S(1)}, u32[]{:S(2)}, u32[]{:S(2)}) %collective-permute-start.7) | collective-permute-done | bytes 20512 | tf_op jit(solution)/shard_map/ppermute | solution.py:288
  32.7 0.9 %collective-permute-done.8 = f32[40,128]{1,0:T(8,128)S(1)} collective-permute-done((f32[40,128]{1,0:T(8,128)S(1)}, f32[40,128]{1,0:T(8,128)S(1)}, u32[]{:S(2)}, u32[]{:S(2)}) %collective-permute-start.8) | collective-permute-done | bytes 20512 | tf_op jit(solution)/shard_map/ppermute | solution.py:288
  33.6 0.0 collective-permute-done.9
  33.6 0.1 collective-permute-start.10
  33.7 1.2 %collective-permute-done.10.recv_ref = f32[40,128]{1,0:T(8,128)S(1)} collective-permute-done((f32[40,128]{1,0:T(8,128)S(1)}, f32[40,128]{1,0:T(8,128)S(1)}, u32[]{:S(2)}, u32[]{:S(2)}) %collective-permute-start.10) | collective-permute-done | bytes 20512 | tf_op jit(solution)/shard_map/ppermute | solution.py:280
  34.8 2.6 %solve.1 = f32[8,16]{1,0:T(8,128)} custom-call(f32[40,128]{1,0:T(8,128)S(1)} %add_add_fusion.x_ref, f32[40,128]{1,0:T(8,128)S(1)} %collective-permute-done.10.recv_ref), custom_call_target="tpu_custom_call" | custom-call | tf_op jit(solution)/shard_map/solve/pallas_call | solution.py:259
  (5 shorter events, 0.1 us)
Async XLA Ops:
  0.0 8.2 %copy-start = (f32[2,4096]{1,0:T(2,128)S(1)}, f32[2,4096]{1,0:T(2,128)}, u32[]{:S(2)}) copy-start(f32[2,4096]{1,0:T(2,128)} %param.11) | copy-start | bytes 98308
  0.0 8.5 %copy-start.1 = (s32[256]{0:T(256)S(1)}, s32[256]{0:T(256)}, u32[]{:S(2)}) copy-start(s32[256]{0:T(256)} %param.10) | copy-start | bytes 3076
  7.7 1.5 %collective-permute-start = (f32[128,256]{1,0:T(8,128)S(1)}, f32[128,256]{1,0:T(8,128)S(1)}, u32[]{:S(2)}, u32[]{:S(2)}) collective-permute-start(f32[128,256]{1,0:T(8,128)S(1)} %project.1.part_ref), channel_id=1, source_target_pairs={{0,1},{1,0},{2,3},{3,2},{4,5},{5,4},{6,7},{7,6},{8,9},{9,8},{10,11... | collective-permute-start | bytes 393224 | tf_op jit(solution)/shard_map/ppermute | solution.py:280
  9.3 12.2 %collective-permute-start.1 = (f32[56,256]{1,0:T(8,128)S(1)}, f32[56,256]{1,0:T(8,128)S(1)}, u32[]{:S(2)}, u32[]{:S(2)}) collective-permute-start(f32[56,256]{1,0:T(8,128)S(1)} %get-tuple-element.10), channel_id=1, source_target_pairs={{0,8},{1,11},{2,10},{3,9},{4,12},{5,15},{6,14},{7,13},{8,0},{9,3},... | collective-permute-start | bytes 172040 | tf_op jit(solution)/shard_map/ppermute | solution.py:288
  13.3 8.2 %collective-permute-start.2 = (f32[56,256]{1,0:T(8,128)S(1)}, f32[56,256]{1,0:T(8,128)S(1)}, u32[]{:S(2)}, u32[]{:S(2)}) collective-permute-start(f32[56,256]{1,0:T(8,128)S(1)} %get-tuple-element.11), channel_id=1, source_target_pairs={{0,12},{1,3},{2,14},{3,1},{4,8},{5,7},{6,10},{7,5},{8,4},{9,11},{1... | collective-permute-start | bytes 172040 | tf_op jit(solution)/shard_map/ppermute | solution.py:288
  14.6 6.8 %collective-permute-start.3 = (f32[56,256]{1,0:T(8,128)S(1)}, f32[56,256]{1,0:T(8,128)S(1)}, u32[]{:S(2)}, u32[]{:S(2)}) collective-permute-start(f32[56,256]{1,0:T(8,128)S(1)} %get-tuple-element.12), channel_id=1, source_target_pairs={{0,4},{1,7},{2,6},{3,5},{4,0},{5,3},{6,2},{7,1},{8,12},{9,15},{10,... | collective-permute-start | bytes 172040 | tf_op jit(solution)/shard_map/ppermute | solution.py:288
  14.8 6.6 %collective-permute-start.4 = (f32[56,128]{1,0:T(8,128)S(1)}, f32[56,128]{1,0:T(8,128)S(1)}, u32[]{:S(2)}, u32[]{:S(2)}) collective-permute-start(f32[56,128]{1,0:T(8,128)S(1)} %get-tuple-element.13), channel_id=1, source_target_pairs={{0,14},{2,12},{4,10},{6,8},{8,6},{10,4},{12,2},{14,0},{1,15},{3,13... | collective-permute-start | bytes 86024 | tf_op jit(solution)/shard_map/ppermute | solution.py:294
  22.3 1.7 %collective-permute-start.5 = (f32[80,512]{1,0:T(8,128)S(1)}, f32[80,512]{1,0:T(8,128)S(1)}, u32[]{:S(2)}, u32[]{:S(2)}) collective-permute-start(f32[80,512]{1,0:T(8,128)S(1)} %grads.1.part_ref), channel_id=1, source_target_pairs={{0,1},{1,0},{2,3},{3,2},{4,5},{5,4},{6,7},{7,6},{8,9},{9,8},{10,11... | collective-permute-start | bytes 491528 | tf_op jit(solution)/shard_map/ppermute | solution.py:280
  24.3 7.2 %collective-permute-start.6 = (f32[40,128]{1,0:T(8,128)S(1)}, f32[40,128]{1,0:T(8,128)S(1)}, u32[]{:S(2)}, u32[]{:S(2)}) collective-permute-start(f32[40,128]{1,0:T(8,128)S(1)} %gram.1), channel_id=1, source_target_pairs={{0,14},{2,12},{4,10},{6,8},{8,6},{10,4},{12,2},{14,0},{1,15},{3,13... | collective-permute-start | bytes 61448 | tf_op jit(solution)/shard_map/ppermute | solution.py:294
  28.0 4.7 %collective-permute-start.7 = (f32[40,128]{1,0:T(8,128)S(1)}, f32[40,128]{1,0:T(8,128)S(1)}, u32[]{:S(2)}, u32[]{:S(2)}) collective-permute-start(f32[40,128]{1,0:T(8,128)S(1)} %gram.1), channel_id=1, source_target_pairs={{0,8},{1,11},{2,10},{3,9},{4,12},{5,15},{6,14},{7,13},{8,0},{9,3},... | collective-permute-start | bytes 61448 | tf_op jit(solution)/shard_map/ppermute | solution.py:288
  28.0 5.6 %collective-permute-start.8 = (f32[40,128]{1,0:T(8,128)S(1)}, f32[40,128]{1,0:T(8,128)S(1)}, u32[]{:S(2)}, u32[]{:S(2)}) collective-permute-start(f32[40,128]{1,0:T(8,128)S(1)} %gram.1), channel_id=1, source_target_pairs={{0,12},{1,3},{2,14},{3,1},{4,8},{5,7},{6,10},{7,5},{8,4},{9,11},{1... | collective-permute-start | bytes 61448 | tf_op jit(solution)/shard_map/ppermute | solution.py:288
  29.0 4.6 %collective-permute-start.9 = (f32[40,128]{1,0:T(8,128)S(1)}, f32[40,128]{1,0:T(8,128)S(1)}, u32[]{:S(2)}, u32[]{:S(2)}) collective-permute-start(f32[40,128]{1,0:T(8,128)S(1)} %gram.1), channel_id=1, source_target_pairs={{0,4},{1,7},{2,6},{3,5},{4,0},{5,3},{6,2},{7,1},{8,12},{9,15},{10,... | collective-permute-start | bytes 61448 | tf_op jit(solution)/shard_map/ppermute | solution.py:288
  33.6 1.3 %collective-permute-start.10 = (f32[40,128]{1,0:T(8,128)S(1)}, f32[40,128]{1,0:T(8,128)S(1)}, u32[]{:S(2)}, u32[]{:S(2)}) collective-permute-start(f32[40,128]{1,0:T(8,128)S(1)} %add_add_fusion.x_ref), channel_id=1, source_target_pairs={{0,1},{1,0},{2,3},{3,2},{4,5},{5,4},{6,7},{7,6},{8,9},{9,8},{10,11... | collective-permute-start | bytes 61448 | tf_op jit(solution)/shard_map/ppermute | solution.py:280

commit v7 on v6

--- a/solution.py
+++ b/solution.py
@@ -10,9 +10,8 @@
 TOK_DEV = 256
 DOC_DEV = 8
 LANES = 128
-ROWS = 64
-PIECES = 4
-FLIGHT = 5
+STACK = 2
+FLIGHT = 10
 NT = (((1,), (1,)), ((), ()))
 HIGHEST = lax.Precision.HIGHEST
 VMEM = pl.BlockSpec(memory_space=pltpu.VMEM)
@@ -21,6 +20,13 @@
 
 def vmem_params(mib):
     return pltpu.CompilerParams(vmem_limit_bytes=int(mib * (1 << 20)))
+
+
+def chunks_of(length, most=1024):
+    size = most
+    while length % size:
+        size //= 2
+    return size, length // size
 
 
 def project_kernel(h_ref, g_ref, pin_ref, pout_ref, out_ref, h_buf, g_buf, pin_buf, pout_buf, sems):
@@ -38,30 +44,40 @@
         if ahead < len(order):
             copies[order[ahead]].start()
 
-    chunks = [pl.ds(i, ROWS) for i in range(0, h_ref.shape[0], ROWS)]
-    copy("po", pout_ref, pout_buf)
-    for i, at in enumerate(chunks):
-        copy(("g", i), g_ref.at[at], g_buf.at[at])
-    copy("pi", pin_ref, pin_buf)
-    for i, at in enumerate(chunks):
-        copy(("h", i), h_ref.at[at], h_buf.at[at])
-
-    def run(tag, proj, data):
-        depth = data.shape[1] // PIECES
-        done = []
-        for i, at in enumerate(chunks):
-            arrive((tag, i))
-            parts = []
-            for j in range(PIECES):
-                units = pl.ds(j * depth, depth)
-                parts.append(lax.dot_general(proj[:, units], data[at, units], NT, preferred_element_type=jnp.float32))
-            done.append(sum(parts[1:], parts[0]))
-        return jnp.concatenate(done, axis=1)
-
+    def plan(tag, proj, proj_buf, data, data_buf):
+        depth = data_buf.shape[1]
+        ranks, tokens = proj.shape[0], data.shape[0]
+        size, count = chunks_of(depth)
+        for s in range(STACK):
+            copy((tag, s), proj.at[:, pl.ds(s * depth, depth)], proj_buf.at[pl.ds(s * ranks, ranks)])
+        for i in range(count):
+            for s in range(STACK):
+                copy(
+                    (tag, s, i),
+                    data.at[:, pl.ds(s * depth + i * size, size)],
+                    data_buf.at[pl.ds(s * tokens, tokens), pl.ds(i * size, size)],
+                )
+
+    def run(tag, proj_buf, data_buf):
+        ranks, tokens = proj_buf.shape[0] // STACK, data_buf.shape[0] // STACK
+        size, count = chunks_of(data_buf.shape[1])
+        for s in range(STACK):
+            arrive((tag, s))
+        total = None
+        for i in range(count):
+            for s in range(STACK):
+                arrive((tag, s, i))
+            at = pl.ds(i * size, size)
+            part = lax.dot_general(proj_buf[:, at], data_buf[:, at], NT, preferred_element_type=jnp.float32)
+            for s in range(STACK):
+                block = part[s * ranks:(s + 1) * ranks, s * tokens:(s + 1) * tokens]
+                total = block if total is None else total + block
+        return total
+
+    plan("g", pout_ref, pout_buf, g_ref, g_buf)
+    plan("h", pin_ref, pin_buf, h_ref, h_buf)
     ranks = pout_ref.shape[0]
-    arrive("po")
     out_ref[0:ranks, :] = run("g", pout_buf, g_buf)
-    arrive("pi")
     out_ref[ranks:, :] = run("h", pin_buf, h_buf)
 
 
@@ -69,18 +85,15 @@
     tokens, units = hidden.shape
     width = out_grad.shape[1]
     ranks = pin_t.shape[0] + pout_t.shape[0]
+    operands = (hidden, out_grad, pin_t, pout_t)
+    copies = sum(STACK * (1 + chunks_of(x.shape[1] // STACK)[1]) for x in operands[:2])
     return pl.pallas_call(
         project_kernel,
         out_shape=jax.ShapeDtypeStruct((ranks, tokens), jnp.float32),
         in_specs=[HBM] * 4,
         out_specs=VMEM,
-        scratch_shapes=[
-            pltpu.VMEM(hidden.shape, hidden.dtype),
-            pltpu.VMEM(out_grad.shape, out_grad.dtype),
-            pltpu.VMEM(pin_t.shape, pin_t.dtype),
-            pltpu.VMEM(pout_t.shape, pout_t.dtype),
-            pltpu.SemaphoreType.DMA((2 + 2 * tokens // ROWS,)),
-        ],
+        scratch_shapes=[pltpu.VMEM((x.shape[0] * STACK, x.shape[1] // STACK), x.dtype) for x in operands]
+        + [pltpu.SemaphoreType.DMA((copies,))],
         compiler_params=vmem_params(53.5),
         cost_estimate=pl.CostEstimate(
             flops=2 * tokens * 64 * (units + width),
@@ -88,7 +101,7 @@
             transcendentals=0,
         ),
         name="project",
-    )(hidden, out_grad, pin_t, pout_t)
+    )(*operands)
 
 
 def partners(dp):

time: 37.6 us -> 37.5 us (level)
  no operation moved by 1% of the time
where the time goes in v7:
time: 37.5 us; the launch traced here: 37.4 us
  starting transfers between devices  17.9 us (48%)
  Pallas kernels  11.4 us (30%)
  waiting for transfers between devices  7.62 us (20%)
    ppermute x6, starting transfers between devices, trade(): got.append(lax.ppermute(x, ('dp', 'tensor'), pairs))  9.08 us
    pallas_call x1, Pallas kernels, project(): pl.pallas_call(project_kernel, out_shape=jax.ShapeDtypeStruct((ranks, tok...  7.59 us
    ppermute x2, starting transfers between devices, trade_last(): return lax.ppermute(x, 'dp', [(i, i ^ dp - 1) for i in range(dp)])  7.58 us
    ppermute x3, waiting for transfers between devices, swap_cores(): return lax.ppermute(x, 'tensor', [(i, cores - 1 - i) for i in range(cores)])  2.83 us
    ppermute x2, waiting for transfers between devices, trade_last(): return lax.ppermute(x, 'dp', [(i, i ^ dp - 1) for i in range(dp)])  2.69 us
    pallas_call x1, Pallas kernels, solve(): pl.pallas_call(functools.partial(solve_kernel, docs, queries, scale), out...  2.61 us
    ppermute x6, waiting for transfers between devices, trade(): got.append(lax.ppermute(x, ('dp', 'tensor'), pairs))  2.1 us
    ppermute x3, starting transfers between devices, swap_cores(): return lax.ppermute(x, 'tensor', [(i, cores - 1 - i) for i in range(cores)])  1.23 us
  transfers between devices with their start and end apart: 11, of which 6 were waited for; matrix products, arithmetic and copies ran while one was open for 1% of the time, Pallas kernels for 0%

profile of v7, /device:TPU:0, one launch (start us, length us, event | category | flops | bytes accessed | tf_op | source)
XLA Modules:
  0.0 37.4 jit_solution(5554009445187620459)
XLA Ops:
  0.0 0.0 copy-start
  0.0 0.0 copy-start.1
  0.0 7.6 %project.1.part_ref = f32[128,256]{1,0:T(8,128)S(1)} custom-call(bf16[256,14336]{1,0:T(8,128)(2,1)} %h_ref.1, bf16[256,4096]{1,0:T(8,128)(2,1)} %g_ref.1, bf16[64,14336]{1,0:T(8,128)(2,1)} %bitcast.8, bf16[64,4096]{1,0:T(8,128)(2,1)} %bitcast.9), custom_call_target="tpu_custom_call" | custom-call | flops 603979776 | bytes 11796480 | tf_op jit(solution)/shard_map/project/pallas_call | solution.py:90
  7.6 0.5 %collective-permute-start = (f32[128,256]{1,0:T(8,128)S(1)}, f32[128,256]{1,0:T(8,128)S(1)}, u32[]{:S(2)}, u32[]{:S(2)}) collective-permute-start(f32[128,256]{1,0:T(8,128)S(1)} %project.1.part_ref), channel_id=1, source_target_pairs={{0,1},{1,0},{2,3},{3,2},{4,5},{5,4},{6,7},{7,6},{8,9},{9,8},{10,11... | collective-permute-start | bytes 393224 | tf_op jit(solution)/shard_map/ppermute | solution.py:293
  8.1 0.0 copy-done
  8.1 0.2 reshape.6
  8.3 0.1 reshape.7
  8.4 0.0 copy-done.1
  8.5 0.6 %collective-permute-done.recv_ref = f32[128,256]{1,0:T(8,128)S(1)} collective-permute-done((f32[128,256]{1,0:T(8,128)S(1)}, f32[128,256]{1,0:T(8,128)S(1)}, u32[]{:S(2)}, u32[]{:S(2)}) %collective-permute-start) | collective-permute-done | bytes 131104 | tf_op jit(solution)/shard_map/ppermute | solution.py:293
  9.1 0.1 pack.1
  9.2 4.0 %collective-permute-start.1 = (f32[56,256]{1,0:T(8,128)S(1)}, f32[56,256]{1,0:T(8,128)S(1)}, u32[]{:S(2)}, u32[]{:S(2)}) collective-permute-start(f32[56,256]{1,0:T(8,128)S(1)} %get-tuple-element.10), channel_id=1, source_target_pairs={{0,8},{1,11},{2,10},{3,9},{4,12},{5,15},{6,14},{7,13},{8,0},{9,3},... | collective-permute-start | bytes 172040 | tf_op jit(solution)/shard_map/ppermute | solution.py:301
  13.2 1.3 %collective-permute-start.2 = (f32[56,256]{1,0:T(8,128)S(1)}, f32[56,256]{1,0:T(8,128)S(1)}, u32[]{:S(2)}, u32[]{:S(2)}) collective-permute-start(f32[56,256]{1,0:T(8,128)S(1)} %get-tuple-element.11), channel_id=1, source_target_pairs={{0,12},{1,3},{2,14},{3,1},{4,8},{5,7},{6,10},{7,5},{8,4},{9,11},{1... | collective-permute-start | bytes 172040 | tf_op jit(solution)/shard_map/ppermute | solution.py:301
  14.5 0.2 collective-permute-start.3
  14.8 3.9 %collective-permute-start.4 = (f32[56,128]{1,0:T(8,128)S(1)}, f32[56,128]{1,0:T(8,128)S(1)}, u32[]{:S(2)}, u32[]{:S(2)}) collective-permute-start(f32[56,128]{1,0:T(8,128)S(1)} %get-tuple-element.13), channel_id=1, source_target_pairs={{0,14},{2,12},{4,10},{6,8},{8,6},{10,4},{12,2},{14,0},{1,15},{3,13... | collective-permute-start | bytes 86024 | tf_op jit(solution)/shard_map/ppermute | solution.py:307
  18.6 2.7 %collective-permute-done.4.refs_3_ = f32[56,128]{1,0:T(8,128)S(1)} collective-permute-done((f32[56,128]{1,0:T(8,128)S(1)}, f32[56,128]{1,0:T(8,128)S(1)}, u32[]{:S(2)}, u32[]{:S(2)}) %collective-permute-start.4) | collective-permute-done | bytes 28704 | tf_op jit(solution)/shard_map/ppermute | solution.py:307
  21.3 0.0 collective-permute-done.1.refs_0_
  21.3 0.0 collective-permute-done.2.refs_1_
  21.3 0.0 collective-permute-done.3.refs_2_
  21.3 0.8 %grads.1.part_ref = f32[80,512]{1,0:T(8,128)S(1)} custom-call(f32[56,256]{1,0:T(8,128)S(1)} %collective-permute-done.1.refs_0_, f32[56,256]{1,0:T(8,128)S(1)} %collective-permute-done.2.refs_1_, f32[56,256]{1,0:T(8,128)S(1)} %collective-permute-done.3.refs_2_, f32[56,128]{1,0:T(8,128)S(1)} %collective-permute-done.4.refs_3_, ...), custom_call_target="tpu_custom_call" | custom-call | tf_op jit(solution)/shard_map/grads/pallas_call | solution.py:205
  22.2 0.6 %collective-permute-start.5 = (f32[80,512]{1,0:T(8,128)S(1)}, f32[80,512]{1,0:T(8,128)S(1)}, u32[]{:S(2)}, u32[]{:S(2)}) collective-permute-start(f32[80,512]{1,0:T(8,128)S(1)} %grads.1.part_ref), channel_id=1, source_target_pairs={{0,1},{1,0},{2,3},{3,2},{4,5},{5,4},{6,7},{7,6},{8,9},{9,8},{10,11... | collective-permute-start | bytes 491528 | tf_op jit(solution)/shard_map/ppermute | solution.py:293
  22.8 1.0 %collective-permute-done.5.recv_ref = f32[80,512]{1,0:T(8,128)S(1)} collective-permute-done((f32[80,512]{1,0:T(8,128)S(1)}, f32[80,512]{1,0:T(8,128)S(1)}, u32[]{:S(2)}, u32[]{:S(2)}) %collective-permute-start.5) | collective-permute-done | bytes 163872 | tf_op jit(solution)/shard_map/ppermute | solution.py:293
  23.9 0.3 gram.1
  24.2 3.7 %collective-permute-start.6 = (f32[40,128]{1,0:T(8,128)S(1)}, f32[40,128]{1,0:T(8,128)S(1)}, u32[]{:S(2)}, u32[]{:S(2)}) collective-permute-start(f32[40,128]{1,0:T(8,128)S(1)} %gram.1), channel_id=1, source_target_pairs={{0,14},{2,12},{4,10},{6,8},{8,6},{10,4},{12,2},{14,0},{1,15},{3,13... | collective-permute-start | bytes 61448 | tf_op jit(solution)/shard_map/ppermute | solution.py:307
  27.9 0.0 collective-permute-start.7
  27.9 1.0 %collective-permute-start.8 = (f32[40,128]{1,0:T(8,128)S(1)}, f32[40,128]{1,0:T(8,128)S(1)}, u32[]{:S(2)}, u32[]{:S(2)}) collective-permute-start(f32[40,128]{1,0:T(8,128)S(1)} %gram.1), channel_id=1, source_target_pairs={{0,12},{1,3},{2,14},{3,1},{4,8},{5,7},{6,10},{7,5},{8,4},{9,11},{1... | collective-permute-start | bytes 61448 | tf_op jit(solution)/shard_map/ppermute | solution.py:301
  28.9 2.5 %collective-permute-start.9 = (f32[40,128]{1,0:T(8,128)S(1)}, f32[40,128]{1,0:T(8,128)S(1)}, u32[]{:S(2)}, u32[]{:S(2)}) collective-permute-start(f32[40,128]{1,0:T(8,128)S(1)} %gram.1), channel_id=1, source_target_pairs={{0,4},{1,7},{2,6},{3,5},{4,0},{5,3},{6,2},{7,1},{8,12},{9,15},{10,... | collective-permute-start | bytes 61448 | tf_op jit(solution)/shard_map/ppermute | solution.py:301
  31.4 0.0 collective-permute-done.6
  31.4 1.2 %collective-permute-done.7 = f32[40,128]{1,0:T(8,128)S(1)} collective-permute-done((f32[40,128]{1,0:T(8,128)S(1)}, f32[40,128]{1,0:T(8,128)S(1)}, u32[]{:S(2)}, u32[]{:S(2)}) %collective-permute-start.7) | collective-permute-done | bytes 20512 | tf_op jit(solution)/shard_map/ppermute | solution.py:301
  32.6 0.9 %collective-permute-done.8 = f32[40,128]{1,0:T(8,128)S(1)} collective-permute-done((f32[40,128]{1,0:T(8,128)S(1)}, f32[40,128]{1,0:T(8,128)S(1)}, u32[]{:S(2)}, u32[]{:S(2)}) %collective-permute-start.8) | collective-permute-done | bytes 20512 | tf_op jit(solution)/shard_map/ppermute | solution.py:301
  33.5 0.0 collective-permute-done.9
  33.5 0.1 collective-permute-start.10
  33.6 1.2 %collective-permute-done.10.recv_ref = f32[40,128]{1,0:T(8,128)S(1)} collective-permute-done((f32[40,128]{1,0:T(8,128)S(1)}, f32[40,128]{1,0:T(8,128)S(1)}, u32[]{:S(2)}, u32[]{:S(2)}) %collective-permute-start.10) | collective-permute-done | bytes 20512 | tf_op jit(solution)/shard_map/ppermute | solution.py:293
  34.8 2.6 %solve.1 = f32[8,16]{1,0:T(8,128)} custom-call(f32[40,128]{1,0:T(8,128)S(1)} %add_add_fusion.x_ref, f32[40,128]{1,0:T(8,128)S(1)} %collective-permute-done.10.recv_ref), custom_call_target="tpu_custom_call" | custom-call | tf_op jit(solution)/shard_map/solve/pallas_call | solution.py:272
  (5 shorter events, 0.1 us)
Async XLA Ops:
  0.0 8.1 %copy-start = (f32[2,4096]{1,0:T(2,128)S(1)}, f32[2,4096]{1,0:T(2,128)}, u32[]{:S(2)}) copy-start(f32[2,4096]{1,0:T(2,128)} %param.11) | copy-start | bytes 98308
  0.0 8.4 %copy-start.1 = (s32[256]{0:T(256)S(1)}, s32[256]{0:T(256)}, u32[]{:S(2)}) copy-start(s32[256]{0:T(256)} %param.10) | copy-start | bytes 3076
  7.6 1.5 %collective-permute-start = (f32[128,256]{1,0:T(8,128)S(1)}, f32[128,256]{1,0:T(8,128)S(1)}, u32[]{:S(2)}, u32[]{:S(2)}) collective-permute-start(f32[128,256]{1,0:T(8,128)S(1)} %project.1.part_ref), channel_id=1, source_target_pairs={{0,1},{1,0},{2,3},{3,2},{4,5},{5,4},{6,7},{7,6},{8,9},{9,8},{10,11... | collective-permute-start | bytes 393224 | tf_op jit(solution)/shard_map/ppermute | solution.py:293
  9.2 12.2 %collective-permute-start.1 = (f32[56,256]{1,0:T(8,128)S(1)}, f32[56,256]{1,0:T(8,128)S(1)}, u32[]{:S(2)}, u32[]{:S(2)}) collective-permute-start(f32[56,256]{1,0:T(8,128)S(1)} %get-tuple-element.10), channel_id=1, source_target_pairs={{0,8},{1,11},{2,10},{3,9},{4,12},{5,15},{6,14},{7,13},{8,0},{9,3},... | collective-permute-start | bytes 172040 | tf_op jit(solution)/shard_map/ppermute | solution.py:301
  13.2 8.1 %collective-permute-start.2 = (f32[56,256]{1,0:T(8,128)S(1)}, f32[56,256]{1,0:T(8,128)S(1)}, u32[]{:S(2)}, u32[]{:S(2)}) collective-permute-start(f32[56,256]{1,0:T(8,128)S(1)} %get-tuple-element.11), channel_id=1, source_target_pairs={{0,12},{1,3},{2,14},{3,1},{4,8},{5,7},{6,10},{7,5},{8,4},{9,11},{1... | collective-permute-start | bytes 172040 | tf_op jit(solution)/shard_map/ppermute | solution.py:301
  14.5 6.8 %collective-permute-start.3 = (f32[56,256]{1,0:T(8,128)S(1)}, f32[56,256]{1,0:T(8,128)S(1)}, u32[]{:S(2)}, u32[]{:S(2)}) collective-permute-start(f32[56,256]{1,0:T(8,128)S(1)} %get-tuple-element.12), channel_id=1, source_target_pairs={{0,4},{1,7},{2,6},{3,5},{4,0},{5,3},{6,2},{7,1},{8,12},{9,15},{10,... | collective-permute-start | bytes 172040 | tf_op jit(solution)/shard_map/ppermute | solution.py:301
  14.8 6.6 %collective-permute-start.4 = (f32[56,128]{1,0:T(8,128)S(1)}, f32[56,128]{1,0:T(8,128)S(1)}, u32[]{:S(2)}, u32[]{:S(2)}) collective-permute-start(f32[56,128]{1,0:T(8,128)S(1)} %get-tuple-element.13), channel_id=1, source_target_pairs={{0,14},{2,12},{4,10},{6,8},{8,6},{10,4},{12,2},{14,0},{1,15},{3,13... | collective-permute-start | bytes 86024 | tf_op jit(solution)/shard_map/ppermute | solution.py:307
  22.2 1.7 %collective-permute-start.5 = (f32[80,512]{1,0:T(8,128)S(1)}, f32[80,512]{1,0:T(8,128)S(1)}, u32[]{:S(2)}, u32[]{:S(2)}) collective-permute-start(f32[80,512]{1,0:T(8,128)S(1)} %grads.1.part_ref), channel_id=1, source_target_pairs={{0,1},{1,0},{2,3},{3,2},{4,5},{5,4},{6,7},{7,6},{8,9},{9,8},{10,11... | collective-permute-start | bytes 491528 | tf_op jit(solution)/shard_map/ppermute | solution.py:293
  24.2 7.2 %collective-permute-start.6 = (f32[40,128]{1,0:T(8,128)S(1)}, f32[40,128]{1,0:T(8,128)S(1)}, u32[]{:S(2)}, u32[]{:S(2)}) collective-permute-start(f32[40,128]{1,0:T(8,128)S(1)} %gram.1), channel_id=1, source_target_pairs={{0,14},{2,12},{4,10},{6,8},{8,6},{10,4},{12,2},{14,0},{1,15},{3,13... | collective-permute-start | bytes 61448 | tf_op jit(solution)/shard_map/ppermute | solution.py:307
  27.9 4.7 %collective-permute-start.7 = (f32[40,128]{1,0:T(8,128)S(1)}, f32[40,128]{1,0:T(8,128)S(1)}, u32[]{:S(2)}, u32[]{:S(2)}) collective-permute-start(f32[40,128]{1,0:T(8,128)S(1)} %gram.1), channel_id=1, source_target_pairs={{0,8},{1,11},{2,10},{3,9},{4,12},{5,15},{6,14},{7,13},{8,0},{9,3},... | collective-permute-start | bytes 61448 | tf_op jit(solution)/shard_map/ppermute | solution.py:301
  27.9 5.6 %collective-permute-start.8 = (f32[40,128]{1,0:T(8,128)S(1)}, f32[40,128]{1,0:T(8,128)S(1)}, u32[]{:S(2)}, u32[]{:S(2)}) collective-permute-start(f32[40,128]{1,0:T(8,128)S(1)} %gram.1), channel_id=1, source_target_pairs={{0,12},{1,3},{2,14},{3,1},{4,8},{5,7},{6,10},{7,5},{8,4},{9,11},{1... | collective-permute-start | bytes 61448 | tf_op jit(solution)/shard_map/ppermute | solution.py:301
  28.9 4.6 %collective-permute-start.9 = (f32[40,128]{1,0:T(8,128)S(1)}, f32[40,128]{1,0:T(8,128)S(1)}, u32[]{:S(2)}, u32[]{:S(2)}) collective-permute-start(f32[40,128]{1,0:T(8,128)S(1)} %gram.1), channel_id=1, source_target_pairs={{0,4},{1,7},{2,6},{3,5},{4,0},{5,3},{6,2},{7,1},{8,12},{9,15},{10,... | collective-permute-start | bytes 61448 | tf_op jit(solution)/shard_map/ppermute | solution.py:301
  33.5 1.3 %collective-permute-start.10 = (f32[40,128]{1,0:T(8,128)S(1)}, f32[40,128]{1,0:T(8,128)S(1)}, u32[]{:S(2)}, u32[]{:S(2)}) collective-permute-start(f32[40,128]{1,0:T(8,128)S(1)} %add_add_fusion.x_ref), channel_id=1, source_target_pairs={{0,1},{1,0},{2,3},{3,2},{4,5},{5,4},{6,7},{7,6},{8,9},{9,8},{10,11... | collective-permute-start | bytes 61448 | tf_op jit(solution)/shard_map/ppermute | solution.py:293

commit v8 on v5

--- a/solution.py
+++ b/solution.py
@@ -37,13 +37,13 @@
         copies[name] = pltpu.make_async_copy(src, dst, sems.at[len(copies)])
         order.append(name)
         if len(order) <= FLIGHT:
-            copies[name].start()
+            copies[name].start(priority=(len(order) - 1) % 2)
 
     def arrive(name):
         copies[name].wait()
         ahead = order.index(name) + FLIGHT
         if ahead < len(order):
-            copies[order[ahead]].start()
+            copies[order[ahead]].start(priority=ahead % 2)
 
     copy("po", pout_ref, pout_buf)
     for i in range(g_count):
@@ -152,9 +152,8 @@
     )(part, recv, extra)
 
 
-def grads_kernel(rows_a, rows_b, docs, dp, *refs):
-    xs, (out_ref, outer_ref, member_ref) = refs[:-3], refs[-3:]
-    whole = xs[0].shape[1]
+def grads_kernel(rows_a, rows_b, docs, dp, whole, gaps, *refs):
+    xs, before, (out_ref, outer_ref, member_ref) = refs[:len(gaps)], refs[len(gaps):-3], refs[-3:]
     wide = rows_a * rows_b
     first = rows_a + rows_b
     queries = out_ref.shape[0] - docs
@@ -166,7 +165,7 @@
     mine = lane // (whole // 2) == core
     flat = [jnp.zeros((queries, whole), jnp.float32)] * (per * wide // whole)
     start = 0
-    for t, x_ref in enumerate(xs):
+    for x_ref, gap in zip(xs, gaps):
         lanes = x_ref.shape[1]
         at = slice(start, start + lanes)
         start += lanes
@@ -178,8 +177,7 @@
         high = outer.astype(jnp.bfloat16)
         outer_ref[0:wide, at] = high
         outer_ref[wide:, at] = (outer - high.astype(jnp.float32)).astype(jnp.bfloat16)
-        gap = partner(dp, t) if t < len(xs) - 2 else dp - 1 if t == len(xs) - 2 else 0
-        held = place // per == me ^ gap
+        held = place // per == me ^ jnp.where(core == 0, gap[0], gap[1])
         if lanes < whole:
             held = jnp.logical_and(held, mine)
         for j in range(len(flat)):
@@ -188,30 +186,37 @@
                 line = jnp.concatenate([line, line], axis=1)
             flat[j] = jnp.where(held, line, flat[j])
     sums = lax.dot_general(member_ref[...], outer_ref[...], NT, preferred_element_type=jnp.float32)
-    out_ref[0:docs, :] = (sums[:, wide:] + sums[:, :wide]) * (TOK_DEV ** -0.5)
+    sums = (sums[:, wide:] + sums[:, :wide]) * (TOK_DEV ** -0.5)
     flat = jnp.concatenate(flat, axis=1)
     asked = jnp.zeros((queries, wide), jnp.float32)
     which = lax.broadcasted_iota(jnp.int32, (queries, wide), 0) % per
     for q in range(per):
         asked = jnp.where(which == q, flat[:, q * wide:(q + 1) * wide], asked)
+    if before:
+        sums, asked = sums + before[0][0:docs, :], asked + before[0][docs:, :]
+    out_ref[0:docs, :] = sums
     out_ref[docs:, :] = asked
 
 
-def grads_of(xs, rows_a, rows_b, docs, queries, dp):
+def grads_of(xs, gaps, before, rows_a, rows_b, docs, queries, dp, whole):
     tokens = sum(x.shape[1] for x in xs)
     wide = rows_a * rows_b
-    return pl.pallas_call(
-        functools.partial(grads_kernel, rows_a, rows_b, docs, dp),
+    operands = (*xs, *before)
+    return pl.pallas_call(
+        functools.partial(grads_kernel, rows_a, rows_b, docs, dp, whole, gaps),
         out_shape=jax.ShapeDtypeStruct((docs + queries, wide), jnp.float32),
-        in_specs=[VMEM] * len(xs),
+        in_specs=[VMEM] * len(operands),
         out_specs=VMEM,
         scratch_shapes=[
             pltpu.VMEM((2 * wide, tokens), jnp.bfloat16),
             pltpu.VMEM((docs, tokens), jnp.bfloat16),
         ],
         compiler_params=vmem_params(40),
+        cost_estimate=pl.CostEstimate(
+            flops=4 * docs * wide * tokens, bytes_accessed=4 * (rows_a + rows_b) * tokens, transcendentals=0
+        ),
         name="grads",
-    )(*xs)
+    )(*operands)
 
 
 def gram_kernel(docs, part_ref, recv_ref, out_ref):
@@ -325,8 +330,11 @@
     extra = jnp.pad(extra, ((0, 0), (0, -extra.shape[1] % 8), (0, 0)))
 
     *blocks, last, own = pack(part, recv, extra, pa, pb)
-    blocks = trade(blocks) + [trade_last(last), own]
-    grads = grads_of(blocks, rows_a, rows_b, docs, num_queries, dp)
+    gaps = list(zip(*partners(dp)))
+    sizes = (rows_a, rows_b, docs, num_queries, dp, lanes)
+    last = trade_last(last)
+    grads = grads_of(trade(blocks) + [own], gaps + [(0, 0)], (), *sizes)
+    grads = grads_of([last], [(dp - 1, dp - 1)], (grads,), *sizes)
     share = gram(grads, swap_cores(grads), docs)
     scale = float(ranks * ranks) ** -0.5
     if docs <= 64:

time: 36.9 us -> 36.8 us (level)
  waiting for transfers between devices: 7.63 us -> 6.88 us
  Pallas kernels: 10.9 us -> 11.5 us
    ppermute x2, waiting for transfers between devices: 2.69 us -> 0.97 us  [trade_last(): return lax.ppermute(x, 'dp', [(i, i ^ dp - 1) for i in range(dp)])]
    ppermute x6, waiting for transfers between devices: 2.1 us -> 3.08 us  [trade(): got.append(lax.ppermute(x, ('dp', 'tensor'), pairs))]
    pallas_call x1, Pallas kernels: 7.02 us -> 7.5 us  [project(): pl.pallas_call(functools.partial(project_kernel, (h_size, h_count, g_size...]
    pallas_call x1 -> x2, Pallas kernels: 0.84 us -> 0.96 us  [grads_of(): pl.pallas_call(functools.partial(grads_kernel, rows_a, rows_b, docs, dp,...]
  transfers between devices with their start and end apart: 11 -> 11, of which waited for: 6 -> 8; matrix products, arithmetic and copies ran while one was open for 1% -> 1% of each run, Pallas kernels for 0% -> 2%
where the time goes in v8:
time: 36.8 us; the launch traced here: 36.7 us
  starting transfers between devices  17.9 us (49%)
  Pallas kernels  11.5 us (31%)
  waiting for transfers between devices  6.88 us (19%)
    ppermute x6, starting transfers between devices, trade(): got.append(lax.ppermute(x, ('dp', 'tensor'), pairs))  9.08 us
    ppermute x2, starting transfers between devices, trade_last(): return lax.ppermute(x, 'dp', [(i, i ^ dp - 1) for i in range(dp)])  7.57 us
    pallas_call x1, Pallas kernels, project(): pl.pallas_call(functools.partial(project_kernel, (h_size, h_count, g_size...  7.5 us
    ppermute x6, waiting for transfers between devices, trade(): got.append(lax.ppermute(x, ('dp', 'tensor'), pairs))  3.08 us
    ppermute x3, waiting for transfers between devices, swap_cores(): return lax.ppermute(x, 'tensor', [(i, cores - 1 - i) for i in range(cores)])  2.83 us
    pallas_call x1, Pallas kernels, solve(): pl.pallas_call(functools.partial(solve_kernel, docs, queries, scale), out...  2.61 us
    ppermute x3, starting transfers between devices, swap_cores(): return lax.ppermute(x, 'tensor', [(i, cores - 1 - i) for i in range(cores)])  1.23 us
    ppermute x2, waiting for transfers between devices, trade_last(): return lax.ppermute(x, 'dp', [(i, i ^ dp - 1) for i in range(dp)])  0.97 us
  transfers between devices with their start and end apart: 11, of which 8 were waited for; matrix products, arithmetic and copies ran while one was open for 1% of the time, Pallas kernels for 2%

profile of v8, /device:TPU:0, one launch (start us, length us, event | category | flops | bytes accessed | tf_op | source)
XLA Modules:
  0.0 36.7 jit_solution(16620341530752465401)
XLA Ops:
  0.0 0.0 copy-start
  0.0 0.0 copy-start.1
  0.0 7.5 %project.1.part_ref = f32[128,256]{1,0:T(8,128)S(1)} custom-call(bf16[256,14336]{1,0:T(8,128)(2,1)} %h_ref.1, bf16[256,4096]{1,0:T(8,128)(2,1)} %g_ref.1, bf16[64,14336]{1,0:T(8,128)(2,1)} %bitcast.8, bf16[64,4096]{1,0:T(8,128)(2,1)} %bitcast.9), custom_call_target="tpu_custom_call" | custom-call | flops 603979776 | bytes 11796480 | tf_op jit(solution)/shard_map/project/pallas_call | solution.py:83
  7.5 0.5 %collective-permute-start = (f32[128,256]{1,0:T(8,128)S(1)}, f32[128,256]{1,0:T(8,128)S(1)}, u32[]{:S(2)}, u32[]{:S(2)}) collective-permute-start(f32[128,256]{1,0:T(8,128)S(1)} %project.1.part_ref), channel_id=1, source_target_pairs={{0,1},{1,0},{2,3},{3,2},{4,5},{5,4},{6,7},{7,6},{8,9},{9,8},{10,11... | collective-permute-start | bytes 393224 | tf_op jit(solution)/shard_map/ppermute | solution.py:296
  8.0 0.0 copy-done
  8.0 0.2 reshape.6
  8.2 0.1 reshape.7
  8.3 0.0 copy-done.1
  8.4 0.6 %collective-permute-done.recv_ref = f32[128,256]{1,0:T(8,128)S(1)} collective-permute-done((f32[128,256]{1,0:T(8,128)S(1)}, f32[128,256]{1,0:T(8,128)S(1)}, u32[]{:S(2)}, u32[]{:S(2)}) %collective-permute-start) | collective-permute-done | bytes 131104 | tf_op jit(solution)/shard_map/ppermute | solution.py:296
  9.0 0.1 pack.1
  9.1 4.0 %collective-permute-start.2 = (f32[56,256]{1,0:T(8,128)S(1)}, f32[56,256]{1,0:T(8,128)S(1)}, u32[]{:S(2)}, u32[]{:S(2)}) collective-permute-start(f32[56,256]{1,0:T(8,128)S(1)} %get-tuple-element.11), channel_id=1, source_target_pairs={{0,8},{1,11},{2,10},{3,9},{4,12},{5,15},{6,14},{7,13},{8,0},{9,3},... | collective-permute-start | bytes 172040 | tf_op jit(solution)/shard_map/ppermute | solution.py:304
  13.1 1.3 %collective-permute-start.3 = (f32[56,256]{1,0:T(8,128)S(1)}, f32[56,256]{1,0:T(8,128)S(1)}, u32[]{:S(2)}, u32[]{:S(2)}) collective-permute-start(f32[56,256]{1,0:T(8,128)S(1)} %get-tuple-element.12), channel_id=1, source_target_pairs={{0,12},{1,3},{2,14},{3,1},{4,8},{5,7},{6,10},{7,5},{8,4},{9,11},{1... | collective-permute-start | bytes 172040 | tf_op jit(solution)/shard_map/ppermute | solution.py:304
  14.4 0.2 collective-permute-start.4
  14.7 3.9 %collective-permute-start.1 = (f32[56,128]{1,0:T(8,128)S(1)}, f32[56,128]{1,0:T(8,128)S(1)}, u32[]{:S(2)}, u32[]{:S(2)}) collective-permute-start(f32[56,128]{1,0:T(8,128)S(1)} %get-tuple-element.10), channel_id=1, source_target_pairs={{0,14},{2,12},{4,10},{6,8},{8,6},{10,4},{12,2},{14,0},{1,15},{3,13... | collective-permute-start | bytes 86024 | tf_op jit(solution)/shard_map/ppermute | solution.py:310
  18.6 0.0 collective-permute-done.2.refs_0_
  18.6 0.6 %collective-permute-done.3.refs_1_ = f32[56,256]{1,0:T(8,128)S(1)} collective-permute-done((f32[56,256]{1,0:T(8,128)S(1)}, f32[56,256]{1,0:T(8,128)S(1)}, u32[]{:S(2)}, u32[]{:S(2)}) %collective-permute-start.3) | collective-permute-done | bytes 57376 | tf_op jit(solution)/shard_map/ppermute | solution.py:304
  19.2 0.4 collective-permute-done.4.refs_2_
  19.5 0.7 %grads.2.refs_1_ = f32[80,512]{1,0:T(8,128)S(1)} custom-call(f32[56,256]{1,0:T(8,128)S(1)} %collective-permute-done.2.refs_0_, f32[56,256]{1,0:T(8,128)S(1)} %collective-permute-done.3.refs_1_, f32[56,256]{1,0:T(8,128)S(1)} %collective-permute-done.4.refs_2_, f32[56,128]{1,0:T(8,128)S(1)} %get-tuple-element.14.refs_3_), custom_call_target="tpu_custom_call" | custom-call | flops 117440512 | bytes 172032 | tf_op jit(solution)/shard_map/grads/pallas_call | solution.py:205
  20.3 1.0 %collective-permute-done.1.refs_0_ = f32[56,128]{1,0:T(8,128)S(1)} collective-permute-done((f32[56,128]{1,0:T(8,128)S(1)}, f32[56,128]{1,0:T(8,128)S(1)}, u32[]{:S(2)}, u32[]{:S(2)}) %collective-permute-start.1) | collective-permute-done | bytes 28704 | tf_op jit(solution)/shard_map/ppermute | solution.py:310
  21.2 0.2 grads.3.part_ref
  21.5 0.6 %collective-permute-start.5 = (f32[80,512]{1,0:T(8,128)S(1)}, f32[80,512]{1,0:T(8,128)S(1)}, u32[]{:S(2)}, u32[]{:S(2)}) collective-permute-start(f32[80,512]{1,0:T(8,128)S(1)} %grads.3.part_ref), channel_id=1, source_target_pairs={{0,1},{1,0},{2,3},{3,2},{4,5},{5,4},{6,7},{7,6},{8,9},{9,8},{10,11... | collective-permute-start | bytes 491528 | tf_op jit(solution)/shard_map/ppermute | solution.py:296
  22.1 1.0 %collective-permute-done.5.recv_ref = f32[80,512]{1,0:T(8,128)S(1)} collective-permute-done((f32[80,512]{1,0:T(8,128)S(1)}, f32[80,512]{1,0:T(8,128)S(1)}, u32[]{:S(2)}, u32[]{:S(2)}) %collective-permute-start.5) | collective-permute-done | bytes 163872 | tf_op jit(solution)/shard_map/ppermute | solution.py:296
  23.2 0.3 gram.1
  23.5 3.7 %collective-permute-start.6 = (f32[40,128]{1,0:T(8,128)S(1)}, f32[40,128]{1,0:T(8,128)S(1)}, u32[]{:S(2)}, u32[]{:S(2)}) collective-permute-start(f32[40,128]{1,0:T(8,128)S(1)} %gram.1), channel_id=1, source_target_pairs={{0,14},{2,12},{4,10},{6,8},{8,6},{10,4},{12,2},{14,0},{1,15},{3,13... | collective-permute-start | bytes 61448 | tf_op jit(solution)/shard_map/ppermute | solution.py:310
  27.2 0.0 collective-permute-start.7
  27.2 1.0 %collective-permute-start.8 = (f32[40,128]{1,0:T(8,128)S(1)}, f32[40,128]{1,0:T(8,128)S(1)}, u32[]{:S(2)}, u32[]{:S(2)}) collective-permute-start(f32[40,128]{1,0:T(8,128)S(1)} %gram.1), channel_id=1, source_target_pairs={{0,12},{1,3},{2,14},{3,1},{4,8},{5,7},{6,10},{7,5},{8,4},{9,11},{1... | collective-permute-start | bytes 61448 | tf_op jit(solution)/shard_map/ppermute | solution.py:304
  28.2 2.5 %collective-permute-start.9 = (f32[40,128]{1,0:T(8,128)S(1)}, f32[40,128]{1,0:T(8,128)S(1)}, u32[]{:S(2)}, u32[]{:S(2)}) collective-permute-start(f32[40,128]{1,0:T(8,128)S(1)} %gram.1), channel_id=1, source_target_pairs={{0,4},{1,7},{2,6},{3,5},{4,0},{5,3},{6,2},{7,1},{8,12},{9,15},{10,... | collective-permute-start | bytes 61448 | tf_op jit(solution)/shard_map/ppermute | solution.py:304
  30.7 0.0 collective-permute-done.6
  30.7 1.2 %collective-permute-done.7 = f32[40,128]{1,0:T(8,128)S(1)} collective-permute-done((f32[40,128]{1,0:T(8,128)S(1)}, f32[40,128]{1,0:T(8,128)S(1)}, u32[]{:S(2)}, u32[]{:S(2)}) %collective-permute-start.7) | collective-permute-done | bytes 20512 | tf_op jit(solution)/shard_map/ppermute | solution.py:304
  31.9 0.9 %collective-permute-done.8 = f32[40,128]{1,0:T(8,128)S(1)} collective-permute-done((f32[40,128]{1,0:T(8,128)S(1)}, f32[40,128]{1,0:T(8,128)S(1)}, u32[]{:S(2)}, u32[]{:S(2)}) %collective-permute-start.8) | collective-permute-done | bytes 20512 | tf_op jit(solution)/shard_map/ppermute | solution.py:304
  32.8 0.0 collective-permute-done.9
  32.8 0.1 collective-permute-start.10
  32.9 1.2 %collective-permute-done.10.recv_ref = f32[40,128]{1,0:T(8,128)S(1)} collective-permute-done((f32[40,128]{1,0:T(8,128)S(1)}, f32[40,128]{1,0:T(8,128)S(1)}, u32[]{:S(2)}, u32[]{:S(2)}) %collective-permute-start.10) | collective-permute-done | bytes 20512 | tf_op jit(solution)/shard_map/ppermute | solution.py:296
  34.1 2.6 %solve.1 = f32[8,16]{1,0:T(8,128)} custom-call(f32[40,128]{1,0:T(8,128)S(1)} %add_add_fusion.x_ref, f32[40,128]{1,0:T(8,128)S(1)} %collective-permute-done.10.recv_ref), custom_call_target="tpu_custom_call" | custom-call | tf_op jit(solution)/shard_map/solve/pallas_call | solution.py:275
  (5 shorter events, 0.1 us)
Async XLA Ops:
  0.0 8.0 %copy-start = (f32[2,4096]{1,0:T(2,128)S(1)}, f32[2,4096]{1,0:T(2,128)}, u32[]{:S(2)}) copy-start(f32[2,4096]{1,0:T(2,128)} %param.11) | copy-start | bytes 98308
  0.0 8.3 %copy-start.1 = (s32[256]{0:T(256)S(1)}, s32[256]{0:T(256)}, u32[]{:S(2)}) copy-start(s32[256]{0:T(256)} %param.10) | copy-start | bytes 3076
  7.5 1.5 %collective-permute-start = (f32[128,256]{1,0:T(8,128)S(1)}, f32[128,256]{1,0:T(8,128)S(1)}, u32[]{:S(2)}, u32[]{:S(2)}) collective-permute-start(f32[128,256]{1,0:T(8,128)S(1)} %project.1.part_ref), channel_id=1, source_target_pairs={{0,1},{1,0},{2,3},{3,2},{4,5},{5,4},{6,7},{7,6},{8,9},{9,8},{10,11... | collective-permute-start | bytes 393224 | tf_op jit(solution)/shard_map/ppermute | solution.py:296
  9.1 9.5 %collective-permute-start.2 = (f32[56,256]{1,0:T(8,128)S(1)}, f32[56,256]{1,0:T(8,128)S(1)}, u32[]{:S(2)}, u32[]{:S(2)}) collective-permute-start(f32[56,256]{1,0:T(8,128)S(1)} %get-tuple-element.11), channel_id=1, source_target_pairs={{0,8},{1,11},{2,10},{3,9},{4,12},{5,15},{6,14},{7,13},{8,0},{9,3},... | collective-permute-start | bytes 172040 | tf_op jit(solution)/shard_map/ppermute | solution.py:304
  13.1 6.1 %collective-permute-start.3 = (f32[56,256]{1,0:T(8,128)S(1)}, f32[56,256]{1,0:T(8,128)S(1)}, u32[]{:S(2)}, u32[]{:S(2)}) collective-permute-start(f32[56,256]{1,0:T(8,128)S(1)} %get-tuple-element.12), channel_id=1, source_target_pairs={{0,12},{1,3},{2,14},{3,1},{4,8},{5,7},{6,10},{7,5},{8,4},{9,11},{1... | collective-permute-start | bytes 172040 | tf_op jit(solution)/shard_map/ppermute | solution.py:304
  14.4 5.1 %collective-permute-start.4 = (f32[56,256]{1,0:T(8,128)S(1)}, f32[56,256]{1,0:T(8,128)S(1)}, u32[]{:S(2)}, u32[]{:S(2)}) collective-permute-start(f32[56,256]{1,0:T(8,128)S(1)} %get-tuple-element.13), channel_id=1, source_target_pairs={{0,4},{1,7},{2,6},{3,5},{4,0},{5,3},{6,2},{7,1},{8,12},{9,15},{10,... | collective-permute-start | bytes 172040 | tf_op jit(solution)/shard_map/ppermute | solution.py:304
  14.7 6.6 %collective-permute-start.1 = (f32[56,128]{1,0:T(8,128)S(1)}, f32[56,128]{1,0:T(8,128)S(1)}, u32[]{:S(2)}, u32[]{:S(2)}) collective-permute-start(f32[56,128]{1,0:T(8,128)S(1)} %get-tuple-element.10), channel_id=1, source_target_pairs={{0,14},{2,12},{4,10},{6,8},{8,6},{10,4},{12,2},{14,0},{1,15},{3,13... | collective-permute-start | bytes 86024 | tf_op jit(solution)/shard_map/ppermute | solution.py:310
  21.5 1.7 %collective-permute-start.5 = (f32[80,512]{1,0:T(8,128)S(1)}, f32[80,512]{1,0:T(8,128)S(1)}, u32[]{:S(2)}, u32[]{:S(2)}) collective-permute-start(f32[80,512]{1,0:T(8,128)S(1)} %grads.3.part_ref), channel_id=1, source_target_pairs={{0,1},{1,0},{2,3},{3,2},{4,5},{5,4},{6,7},{7,6},{8,9},{9,8},{10,11... | collective-permute-start | bytes 491528 | tf_op jit(solution)/shard_map/ppermute | solution.py:296
  23.5 7.2 %collective-permute-start.6 = (f32[40,128]{1,0:T(8,128)S(1)}, f32[40,128]{1,0:T(8,128)S(1)}, u32[]{:S(2)}, u32[]{:S(2)}) collective-permute-start(f32[40,128]{1,0:T(8,128)S(1)} %gram.1), channel_id=1, source_target_pairs={{0,14},{2,12},{4,10},{6,8},{8,6},{10,4},{12,2},{14,0},{1,15},{3,13... | collective-permute-start | bytes 61448 | tf_op jit(solution)/shard_map/ppermute | solution.py:310
  27.2 4.7 %collective-permute-start.7 = (f32[40,128]{1,0:T(8,128)S(1)}, f32[40,128]{1,0:T(8,128)S(1)}, u32[]{:S(2)}, u32[]{:S(2)}) collective-permute-start(f32[40,128]{1,0:T(8,128)S(1)} %gram.1), channel_id=1, source_target_pairs={{0,8},{1,11},{2,10},{3,9},{4,12},{5,15},{6,14},{7,13},{8,0},{9,3},... | collective-permute-start | bytes 61448 | tf_op jit(solution)/shard_map/ppermute | solution.py:304
  27.2 5.6 %collective-permute-start.8 = (f32[40,128]{1,0:T(8,128)S(1)}, f32[40,128]{1,0:T(8,128)S(1)}, u32[]{:S(2)}, u32[]{:S(2)}) collective-permute-start(f32[40,128]{1,0:T(8,128)S(1)} %gram.1), channel_id=1, source_target_pairs={{0,12},{1,3},{2,14},{3,1},{4,8},{5,7},{6,10},{7,5},{8,4},{9,11},{1... | collective-permute-start | bytes 61448 | tf_op jit(solution)/shard_map/ppermute | solution.py:304
  28.2 4.6 %collective-permute-start.9 = (f32[40,128]{1,0:T(8,128)S(1)}, f32[40,128]{1,0:T(8,128)S(1)}, u32[]{:S(2)}, u32[]{:S(2)}) collective-permute-start(f32[40,128]{1,0:T(8,128)S(1)} %gram.1), channel_id=1, source_target_pairs={{0,4},{1,7},{2,6},{3,5},{4,0},{5,3},{6,2},{7,1},{8,12},{9,15},{10,... | collective-permute-start | bytes 61448 | tf_op jit(solution)/shard_map/ppermute | solution.py:304
  32.8 1.3 %collective-permute-start.10 = (f32[40,128]{1,0:T(8,128)S(1)}, f32[40,128]{1,0:T(8,128)S(1)}, u32[]{:S(2)}, u32[]{:S(2)}) collective-permute-start(f32[40,128]{1,0:T(8,128)S(1)} %add_add_fusion.x_ref), channel_id=1, source_target_pairs={{0,1},{1,0},{2,3},{3,2},{4,5},{5,4},{6,7},{7,6},{8,9},{9,8},{10,11... | collective-permute-start | bytes 61448 | tf_op jit(solution)/shard_map/ppermute | solution.py:296

commit v9 on v8

--- a/solution.py
+++ b/solution.py
@@ -11,7 +11,7 @@
 DOC_DEV = 8
 LANES = 128
 DEPTH = 256
-FLIGHT = 8
+FLIGHT = 7
 NT = (((1,), (1,)), ((), ()))
 HIGHEST = lax.Precision.HIGHEST
 VMEM = pl.BlockSpec(memory_space=pltpu.VMEM)
@@ -22,76 +22,59 @@
     return pltpu.CompilerParams(vmem_limit_bytes=int(mib * (1 << 20)))
 
 
-def chunks_of(length, most=1024):
-    size = most
-    while length % size:
-        size //= 2
-    return size, length // size
-
-
-def project_kernel(sizes, h_ref, g_ref, pin_ref, pout_ref, out_ref, h_buf, g_buf, pin_buf, pout_buf, sems):
-    h_size, h_count, g_size, g_count = sizes
-    copies, order = {}, []
-
-    def copy(name, src, dst):
-        copies[name] = pltpu.make_async_copy(src, dst, sems.at[len(copies)])
-        order.append(name)
-        if len(order) <= FLIGHT:
-            copies[name].start(priority=(len(order) - 1) % 2)
-
-    def arrive(name):
-        copies[name].wait()
-        ahead = order.index(name) + FLIGHT
-        if ahead < len(order):
-            copies[order[ahead]].start(priority=ahead % 2)
-
-    copy("po", pout_ref, pout_buf)
-    for i in range(g_count):
-        at = pl.ds(i * g_size, g_size)
-        copy(("g", i), g_ref.at[:, at], g_buf.at[:, at])
-    copy("pi", pin_ref, pin_buf)
-    for i in range(h_count):
-        at = pl.ds(i * h_size, h_size)
-        copy(("h", i), h_ref.at[:, at], h_buf.at[:, at])
-
-    def run(tag, count, size, proj, data):
-        total = None
-        depth = min(size, DEPTH)
-        for i in range(count):
-            arrive((tag, i))
-            parts = []
-            for j in range(size // depth):
-                at = pl.ds(i * size + j * depth, depth)
-                parts.append(lax.dot_general(data[:, at], proj[:, at], NT, preferred_element_type=jnp.float32))
-            part = sum(parts[1:], parts[0])
-            total = part if total is None else total + part
-        return total
-
-    arrive("po")
-    grad = run("g", g_count, g_size, pout_buf, g_buf)
-    arrive("pi")
-    inp = run("h", h_count, h_size, pin_buf, h_buf)
-    out_ref[...] = jnp.concatenate([grad, inp], axis=1).T
+def chunks_of(length, ramp, tail):
+    left = length // DEPTH - sum(ramp) - sum(tail)
+    sizes = [*ramp, *([4] * (left // 4)), *([left % 4] if left % 4 else []), *tail]
+    starts = [sum(sizes[:i]) for i in range(len(sizes))]
+    return [(start * DEPTH, size * DEPTH) for start, size in zip(starts, sizes)]
+
+
+def project_kernel(g_chunks, h_chunks, h_ref, g_ref, pin_ref, pout_ref, out_ref, h_buf, g_buf, pin_buf, pout_buf, sems):
+    plan = [(pout_ref, pout_buf, g_ref, g_buf, at) for at in g_chunks] + [(pin_ref, pin_buf, h_ref, h_buf, at) for at in h_chunks]
+    copies = []
+    for i, (proj, proj_buf, data, data_buf, (start, size)) in enumerate(plan):
+        at = pl.ds(start, size)
+        copies.append((
+            pltpu.make_async_copy(proj.at[:, at], proj_buf.at[:, at], sems.at[2 * i]),
+            pltpu.make_async_copy(data.at[:, at], data_buf.at[:, at], sems.at[2 * i + 1]),
+        ))
+
+    def start(i):
+        if i < len(copies):
+            for copy in copies[i]:
+                copy.start()
+
+    for i in range(FLIGHT):
+        start(i)
+    totals = [None, None]
+    for i, (_, proj_buf, _, data_buf, (first, size)) in enumerate(plan):
+        for copy in copies[i]:
+            copy.wait()
+        start(i + FLIGHT)
+        which = 0 if i < len(g_chunks) else 1
+        for j in range(first, first + size, DEPTH):
+            at = pl.ds(j, DEPTH)
+            part = lax.dot_general(proj_buf[:, at], data_buf[:, at], NT, preferred_element_type=jnp.float32)
+            totals[which] = part if totals[which] is None else totals[which] + part
+    ranks = totals[0].shape[0]
+    out_ref[0:ranks, :] = totals[0]
+    out_ref[ranks:, :] = totals[1]
 
 
 def project(hidden, out_grad, pin_t, pout_t):
     tokens, units = hidden.shape
     width = out_grad.shape[1]
     ranks = pin_t.shape[0] + pout_t.shape[0]
-    h_size, h_count = chunks_of(units)
-    g_size, g_count = chunks_of(width)
-    return pl.pallas_call(
-        functools.partial(project_kernel, (h_size, h_count, g_size, g_count)),
+    operands = (hidden, out_grad, pin_t, pout_t)
+    g_chunks = chunks_of(width, (1, 2, 3), ())
+    h_chunks = chunks_of(units, (), (3, 1))
+    return pl.pallas_call(
+        functools.partial(project_kernel, g_chunks, h_chunks),
         out_shape=jax.ShapeDtypeStruct((ranks, tokens), jnp.float32),
         in_specs=[HBM] * 4,
         out_specs=VMEM,
-        scratch_shapes=[
-            pltpu.VMEM(hidden.shape, hidden.dtype),
-            pltpu.VMEM(out_grad.shape, out_grad.dtype),
-            pltpu.VMEM(pin_t.shape, pin_t.dtype),
-            pltpu.VMEM(pout_t.shape, pout_t.dtype),
-            pltpu.SemaphoreType.DMA((2 + g_count + h_count,)),
-        ],
+        scratch_shapes=[pltpu.VMEM(x.shape, x.dtype) for x in operands]
+        + [pltpu.SemaphoreType.DMA((2 * len(g_chunks + h_chunks),))],
         compiler_params=vmem_params(53.5),
         cost_estimate=pl.CostEstimate(
             flops=2 * tokens * 64 * (units + width),
@@ -99,7 +82,7 @@
             transcendentals=0,
         ),
         name="project",
-    )(hidden, out_grad, pin_t, pout_t)
+    )(*operands)
 
 
 def partners(dp):
@@ -253,11 +236,14 @@
     for r in range(len(rows)):
         wide = [[jnp.broadcast_to(x[:, c:c + 1], (size, cols)) for c in range(r * size, (r + 1) * size)] for x in rows]
         pivot, line = wide[r], rows[r]
+        scale_rows = jnp.ones((size, cols), jnp.float32)
         for j in range(size):
             inverse = 1.0 / pivot[j][j:j + 1]
-            factor = jnp.where(here == j, 1.0 - inverse, pivot[j] * inverse)
+            factor = jnp.where(here == j, 0.0, pivot[j]) * inverse
             pivot = [x if i <= j else x - factor * x[j:j + 1] for i, x in enumerate(pivot)]
             line = line - factor * line[j:j + 1]
+            scale_rows = jnp.where(here == j, inverse, scale_rows)
+        line = line * scale_rows
         for s in range(len(rows)):
             if s == r:
                 rows[s] = line

time: 36.8 us -> 36.4 us (0.989)
  Pallas kernels: 11.5 us -> 11.1 us
    pallas_call x1, Pallas kernels: 7.5 us -> 7.13 us  [project(): pl.pallas_call(functools.partial(project_kernel, g_chunks, h_chunks), out...]
where the time goes in v9:
time: 36.4 us; the launch traced here: 36.2 us
  starting transfers between devices  17.9 us (49%)
  Pallas kernels  11.1 us (30%)
  waiting for transfers between devices  6.88 us (19%)
    ppermute x6, starting transfers between devices, trade(): got.append(lax.ppermute(x, ('dp', 'tensor'), pairs))  9.08 us
    ppermute x2, starting transfers between devices, trade_last(): return lax.ppermute(x, 'dp', [(i, i ^ dp - 1) for i in range(dp)])  7.57 us
    pallas_call x1, Pallas kernels, project(): pl.pallas_call(functools.partial(project_kernel, g_chunks, h_chunks), out...  7.13 us
    ppermute x6, waiting for transfers between devices, trade(): got.append(lax.ppermute(x, ('dp', 'tensor'), pairs))  3.08 us
    ppermute x3, waiting for transfers between devices, swap_cores(): return lax.ppermute(x, 'tensor', [(i, cores - 1 - i) for i in range(cores)])  2.83 us
    pallas_call x1, Pallas kernels, solve(): pl.pallas_call(functools.partial(solve_kernel, docs, queries, scale), out...  2.56 us
    ppermute x3, starting transfers between devices, swap_cores(): return lax.ppermute(x, 'tensor', [(i, cores - 1 - i) for i in range(cores)])  1.22 us
    ppermute x2, waiting for transfers between devices, trade_last(): return lax.ppermute(x, 'dp', [(i, i ^ dp - 1) for i in range(dp)])  0.97 us
  transfers between devices with their start and end apart: 11, of which 8 were waited for; matrix products, arithmetic and copies ran while one was open for 1% of the time, Pallas kernels for 2%

profile of v9, /device:TPU:0, one launch (start us, length us, event | category | flops | bytes accessed | tf_op | source)
XLA Modules:
  0.0 36.2 jit_solution(3845632067197817914)
XLA Ops:
  0.0 0.0 copy-start
  0.0 0.0 copy-start.1
  0.0 7.1 %project.1.part_ref = f32[128,256]{1,0:T(8,128)S(1)} custom-call(bf16[256,14336]{1,0:T(8,128)(2,1)} %h_ref.1, bf16[256,4096]{1,0:T(8,128)(2,1)} %g_ref.1, bf16[64,14336]{1,0:T(8,128)(2,1)} %bitcast.8, bf16[64,4096]{1,0:T(8,128)(2,1)} %bitcast.9), custom_call_target="tpu_custom_call" | custom-call | flops 603979776 | bytes 11796480 | tf_op jit(solution)/shard_map/project/pallas_call | solution.py:71
  7.1 0.5 %collective-permute-start = (f32[128,256]{1,0:T(8,128)S(1)}, f32[128,256]{1,0:T(8,128)S(1)}, u32[]{:S(2)}, u32[]{:S(2)}) collective-permute-start(f32[128,256]{1,0:T(8,128)S(1)} %project.1.part_ref), channel_id=1, source_target_pairs={{0,1},{1,0},{2,3},{3,2},{4,5},{5,4},{6,7},{7,6},{8,9},{9,8},{10,11... | collective-permute-start | bytes 393224 | tf_op jit(solution)/shard_map/ppermute | solution.py:282
  7.7 0.0 copy-done
  7.7 0.2 reshape.6
  7.8 0.1 reshape.7
  8.0 0.0 copy-done.1
  8.0 0.6 %collective-permute-done.recv_ref = f32[128,256]{1,0:T(8,128)S(1)} collective-permute-done((f32[128,256]{1,0:T(8,128)S(1)}, f32[128,256]{1,0:T(8,128)S(1)}, u32[]{:S(2)}, u32[]{:S(2)}) %collective-permute-start) | collective-permute-done | bytes 131104 | tf_op jit(solution)/shard_map/ppermute | solution.py:282
  8.6 0.1 pack.1
  8.7 4.0 %collective-permute-start.2 = (f32[56,256]{1,0:T(8,128)S(1)}, f32[56,256]{1,0:T(8,128)S(1)}, u32[]{:S(2)}, u32[]{:S(2)}) collective-permute-start(f32[56,256]{1,0:T(8,128)S(1)} %get-tuple-element.11), channel_id=1, source_target_pairs={{0,8},{1,11},{2,10},{3,9},{4,12},{5,15},{6,14},{7,13},{8,0},{9,3},... | collective-permute-start | bytes 172040 | tf_op jit(solution)/shard_map/ppermute | solution.py:290
  12.7 1.3 %collective-permute-start.3 = (f32[56,256]{1,0:T(8,128)S(1)}, f32[56,256]{1,0:T(8,128)S(1)}, u32[]{:S(2)}, u32[]{:S(2)}) collective-permute-start(f32[56,256]{1,0:T(8,128)S(1)} %get-tuple-element.12), channel_id=1, source_target_pairs={{0,12},{1,3},{2,14},{3,1},{4,8},{5,7},{6,10},{7,5},{8,4},{9,11},{1... | collective-permute-start | bytes 172040 | tf_op jit(solution)/shard_map/ppermute | solution.py:290
  14.1 0.2 collective-permute-start.4
  14.3 3.9 %collective-permute-start.1 = (f32[56,128]{1,0:T(8,128)S(1)}, f32[56,128]{1,0:T(8,128)S(1)}, u32[]{:S(2)}, u32[]{:S(2)}) collective-permute-start(f32[56,128]{1,0:T(8,128)S(1)} %get-tuple-element.10), channel_id=1, source_target_pairs={{0,14},{2,12},{4,10},{6,8},{8,6},{10,4},{12,2},{14,0},{1,15},{3,13... | collective-permute-start | bytes 86024 | tf_op jit(solution)/shard_map/ppermute | solution.py:296
  18.2 0.0 collective-permute-done.2.refs_0_
  18.2 0.6 %collective-permute-done.3.refs_1_ = f32[56,256]{1,0:T(8,128)S(1)} collective-permute-done((f32[56,256]{1,0:T(8,128)S(1)}, f32[56,256]{1,0:T(8,128)S(1)}, u32[]{:S(2)}, u32[]{:S(2)}) %collective-permute-start.3) | collective-permute-done | bytes 57376 | tf_op jit(solution)/shard_map/ppermute | solution.py:290
  18.8 0.4 collective-permute-done.4.refs_2_
  19.2 0.7 %grads.2.refs_1_ = f32[80,512]{1,0:T(8,128)S(1)} custom-call(f32[56,256]{1,0:T(8,128)S(1)} %collective-permute-done.2.refs_0_, f32[56,256]{1,0:T(8,128)S(1)} %collective-permute-done.3.refs_1_, f32[56,256]{1,0:T(8,128)S(1)} %collective-permute-done.4.refs_2_, f32[56,128]{1,0:T(8,128)S(1)} %get-tuple-element.14.refs_3_), custom_call_target="tpu_custom_call" | custom-call | flops 117440512 | bytes 172032 | tf_op jit(solution)/shard_map/grads/pallas_call | solution.py:188
  19.9 1.0 %collective-permute-done.1.refs_0_ = f32[56,128]{1,0:T(8,128)S(1)} collective-permute-done((f32[56,128]{1,0:T(8,128)S(1)}, f32[56,128]{1,0:T(8,128)S(1)}, u32[]{:S(2)}, u32[]{:S(2)}) %collective-permute-start.1) | collective-permute-done | bytes 28704 | tf_op jit(solution)/shard_map/ppermute | solution.py:296
  20.9 0.2 grads.3.part_ref
  21.1 0.6 %collective-permute-start.5 = (f32[80,512]{1,0:T(8,128)S(1)}, f32[80,512]{1,0:T(8,128)S(1)}, u32[]{:S(2)}, u32[]{:S(2)}) collective-permute-start(f32[80,512]{1,0:T(8,128)S(1)} %grads.3.part_ref), channel_id=1, source_target_pairs={{0,1},{1,0},{2,3},{3,2},{4,5},{5,4},{6,7},{7,6},{8,9},{9,8},{10,11... | collective-permute-start | bytes 491528 | tf_op jit(solution)/shard_map/ppermute | solution.py:282
  21.7 1.0 %collective-permute-done.5.recv_ref = f32[80,512]{1,0:T(8,128)S(1)} collective-permute-done((f32[80,512]{1,0:T(8,128)S(1)}, f32[80,512]{1,0:T(8,128)S(1)}, u32[]{:S(2)}, u32[]{:S(2)}) %collective-permute-start.5) | collective-permute-done | bytes 163872 | tf_op jit(solution)/shard_map/ppermute | solution.py:282
  22.8 0.4 gram.1
  23.1 3.7 %collective-permute-start.6 = (f32[40,128]{1,0:T(8,128)S(1)}, f32[40,128]{1,0:T(8,128)S(1)}, u32[]{:S(2)}, u32[]{:S(2)}) collective-permute-start(f32[40,128]{1,0:T(8,128)S(1)} %gram.1), channel_id=1, source_target_pairs={{0,14},{2,12},{4,10},{6,8},{8,6},{10,4},{12,2},{14,0},{1,15},{3,13... | collective-permute-start | bytes 61448 | tf_op jit(solution)/shard_map/ppermute | solution.py:296
  26.8 0.0 collective-permute-start.7
  26.8 1.0 %collective-permute-start.8 = (f32[40,128]{1,0:T(8,128)S(1)}, f32[40,128]{1,0:T(8,128)S(1)}, u32[]{:S(2)}, u32[]{:S(2)}) collective-permute-start(f32[40,128]{1,0:T(8,128)S(1)} %gram.1), channel_id=1, source_target_pairs={{0,12},{1,3},{2,14},{3,1},{4,8},{5,7},{6,10},{7,5},{8,4},{9,11},{1... | collective-permute-start | bytes 61448 | tf_op jit(solution)/shard_map/ppermute | solution.py:290
  27.8 2.5 %collective-permute-start.9 = (f32[40,128]{1,0:T(8,128)S(1)}, f32[40,128]{1,0:T(8,128)S(1)}, u32[]{:S(2)}, u32[]{:S(2)}) collective-permute-start(f32[40,128]{1,0:T(8,128)S(1)} %gram.1), channel_id=1, source_target_pairs={{0,4},{1,7},{2,6},{3,5},{4,0},{5,3},{6,2},{7,1},{8,12},{9,15},{10,... | collective-permute-start | bytes 61448 | tf_op jit(solution)/shard_map/ppermute | solution.py:290
  30.3 0.0 collective-permute-done.6
  30.3 1.2 %collective-permute-done.7 = f32[40,128]{1,0:T(8,128)S(1)} collective-permute-done((f32[40,128]{1,0:T(8,128)S(1)}, f32[40,128]{1,0:T(8,128)S(1)}, u32[]{:S(2)}, u32[]{:S(2)}) %collective-permute-start.7) | collective-permute-done | bytes 20512 | tf_op jit(solution)/shard_map/ppermute | solution.py:290
  31.5 0.9 %collective-permute-done.8 = f32[40,128]{1,0:T(8,128)S(1)} collective-permute-done((f32[40,128]{1,0:T(8,128)S(1)}, f32[40,128]{1,0:T(8,128)S(1)}, u32[]{:S(2)}, u32[]{:S(2)}) %collective-permute-start.8) | collective-permute-done | bytes 20512 | tf_op jit(solution)/shard_map/ppermute | solution.py:290
  32.4 0.0 collective-permute-done.9
  32.4 0.1 collective-permute-start.10
  32.5 1.2 %collective-permute-done.10.recv_ref = f32[40,128]{1,0:T(8,128)S(1)} collective-permute-done((f32[40,128]{1,0:T(8,128)S(1)}, f32[40,128]{1,0:T(8,128)S(1)}, u32[]{:S(2)}, u32[]{:S(2)}) %collective-permute-start.10) | collective-permute-done | bytes 20512 | tf_op jit(solution)/shard_map/ppermute | solution.py:282
  33.7 2.6 %solve.1 = f32[8,16]{1,0:T(8,128)} custom-call(f32[40,128]{1,0:T(8,128)S(1)} %add_add_fusion.x_ref, f32[40,128]{1,0:T(8,128)S(1)} %collective-permute-done.10.recv_ref), custom_call_target="tpu_custom_call" | custom-call | tf_op jit(solution)/shard_map/solve/pallas_call | solution.py:261
  (5 shorter events, 0.1 us)
Async XLA Ops:
  0.0 7.7 %copy-start = (f32[2,4096]{1,0:T(2,128)S(1)}, f32[2,4096]{1,0:T(2,128)}, u32[]{:S(2)}) copy-start(f32[2,4096]{1,0:T(2,128)} %param.11) | copy-start | bytes 98308
  0.0 8.0 %copy-start.1 = (s32[256]{0:T(256)S(1)}, s32[256]{0:T(256)}, u32[]{:S(2)}) copy-start(s32[256]{0:T(256)} %param.10) | copy-start | bytes 3076
  7.1 1.5 %collective-permute-start = (f32[128,256]{1,0:T(8,128)S(1)}, f32[128,256]{1,0:T(8,128)S(1)}, u32[]{:S(2)}, u32[]{:S(2)}) collective-permute-start(f32[128,256]{1,0:T(8,128)S(1)} %project.1.part_ref), channel_id=1, source_target_pairs={{0,1},{1,0},{2,3},{3,2},{4,5},{5,4},{6,7},{7,6},{8,9},{9,8},{10,11... | collective-permute-start | bytes 393224 | tf_op jit(solution)/shard_map/ppermute | solution.py:282
  8.7 9.5 %collective-permute-start.2 = (f32[56,256]{1,0:T(8,128)S(1)}, f32[56,256]{1,0:T(8,128)S(1)}, u32[]{:S(2)}, u32[]{:S(2)}) collective-permute-start(f32[56,256]{1,0:T(8,128)S(1)} %get-tuple-element.11), channel_id=1, source_target_pairs={{0,8},{1,11},{2,10},{3,9},{4,12},{5,15},{6,14},{7,13},{8,0},{9,3},... | collective-permute-start | bytes 172040 | tf_op jit(solution)/shard_map/ppermute | solution.py:290
  12.7 6.1 %collective-permute-start.3 = (f32[56,256]{1,0:T(8,128)S(1)}, f32[56,256]{1,0:T(8,128)S(1)}, u32[]{:S(2)}, u32[]{:S(2)}) collective-permute-start(f32[56,256]{1,0:T(8,128)S(1)} %get-tuple-element.12), channel_id=1, source_target_pairs={{0,12},{1,3},{2,14},{3,1},{4,8},{5,7},{6,10},{7,5},{8,4},{9,11},{1... | collective-permute-start | bytes 172040 | tf_op jit(solution)/shard_map/ppermute | solution.py:290
  14.1 5.1 %collective-permute-start.4 = (f32[56,256]{1,0:T(8,128)S(1)}, f32[56,256]{1,0:T(8,128)S(1)}, u32[]{:S(2)}, u32[]{:S(2)}) collective-permute-start(f32[56,256]{1,0:T(8,128)S(1)} %get-tuple-element.13), channel_id=1, source_target_pairs={{0,4},{1,7},{2,6},{3,5},{4,0},{5,3},{6,2},{7,1},{8,12},{9,15},{10,... | collective-permute-start | bytes 172040 | tf_op jit(solution)/shard_map/ppermute | solution.py:290
  14.3 6.6 %collective-permute-start.1 = (f32[56,128]{1,0:T(8,128)S(1)}, f32[56,128]{1,0:T(8,128)S(1)}, u32[]{:S(2)}, u32[]{:S(2)}) collective-permute-start(f32[56,128]{1,0:T(8,128)S(1)} %get-tuple-element.10), channel_id=1, source_target_pairs={{0,14},{2,12},{4,10},{6,8},{8,6},{10,4},{12,2},{14,0},{1,15},{3,13... | collective-permute-start | bytes 86024 | tf_op jit(solution)/shard_map/ppermute | solution.py:296
  21.1 1.7 %collective-permute-start.5 = (f32[80,512]{1,0:T(8,128)S(1)}, f32[80,512]{1,0:T(8,128)S(1)}, u32[]{:S(2)}, u32[]{:S(2)}) collective-permute-start(f32[80,512]{1,0:T(8,128)S(1)} %grads.3.part_ref), channel_id=1, source_target_pairs={{0,1},{1,0},{2,3},{3,2},{4,5},{5,4},{6,7},{7,6},{8,9},{9,8},{10,11... | collective-permute-start | bytes 491528 | tf_op jit(solution)/shard_map/ppermute | solution.py:282
  23.1 7.2 %collective-permute-start.6 = (f32[40,128]{1,0:T(8,128)S(1)}, f32[40,128]{1,0:T(8,128)S(1)}, u32[]{:S(2)}, u32[]{:S(2)}) collective-permute-start(f32[40,128]{1,0:T(8,128)S(1)} %gram.1), channel_id=1, source_target_pairs={{0,14},{2,12},{4,10},{6,8},{8,6},{10,4},{12,2},{14,0},{1,15},{3,13... | collective-permute-start | bytes 61448 | tf_op jit(solution)/shard_map/ppermute | solution.py:296
  26.8 4.7 %collective-permute-start.7 = (f32[40,128]{1,0:T(8,128)S(1)}, f32[40,128]{1,0:T(8,128)S(1)}, u32[]{:S(2)}, u32[]{:S(2)}) collective-permute-start(f32[40,128]{1,0:T(8,128)S(1)} %gram.1), channel_id=1, source_target_pairs={{0,8},{1,11},{2,10},{3,9},{4,12},{5,15},{6,14},{7,13},{8,0},{9,3},... | collective-permute-start | bytes 61448 | tf_op jit(solution)/shard_map/ppermute | solution.py:290
  26.8 5.6 %collective-permute-start.8 = (f32[40,128]{1,0:T(8,128)S(1)}, f32[40,128]{1,0:T(8,128)S(1)}, u32[]{:S(2)}, u32[]{:S(2)}) collective-permute-start(f32[40,128]{1,0:T(8,128)S(1)} %gram.1), channel_id=1, source_target_pairs={{0,12},{1,3},{2,14},{3,1},{4,8},{5,7},{6,10},{7,5},{8,4},{9,11},{1... | collective-permute-start | bytes 61448 | tf_op jit(solution)/shard_map/ppermute | solution.py:290
  27.8 4.6 %collective-permute-start.9 = (f32[40,128]{1,0:T(8,128)S(1)}, f32[40,128]{1,0:T(8,128)S(1)}, u32[]{:S(2)}, u32[]{:S(2)}) collective-permute-start(f32[40,128]{1,0:T(8,128)S(1)} %gram.1), channel_id=1, source_target_pairs={{0,4},{1,7},{2,6},{3,5},{4,0},{5,3},{6,2},{7,1},{8,12},{9,15},{10,... | collective-permute-start | bytes 61448 | tf_op jit(solution)/shard_map/ppermute | solution.py:290
  32.4 1.3 %collective-permute-start.10 = (f32[40,128]{1,0:T(8,128)S(1)}, f32[40,128]{1,0:T(8,128)S(1)}, u32[]{:S(2)}, u32[]{:S(2)}) collective-permute-start(f32[40,128]{1,0:T(8,128)S(1)} %add_add_fusion.x_ref), channel_id=1, source_target_pairs={{0,1},{1,0},{2,3},{3,2},{4,5},{5,4},{6,7},{7,6},{8,9},{9,8},{10,11... | collective-permute-start | bytes 61448 | tf_op jit(solution)/shard_map/ppermute | solution.py:282

commit v10 on v9

--- a/solution.py
+++ b/solution.py
@@ -10,7 +10,6 @@
 TOK_DEV = 256
 DOC_DEV = 8
 LANES = 128
-DEPTH = 256
 FLIGHT = 7
 NT = (((1,), (1,)), ((), ()))
 HIGHEST = lax.Precision.HIGHEST
@@ -22,11 +21,16 @@
     return pltpu.CompilerParams(vmem_limit_bytes=int(mib * (1 << 20)))
 
 
+def pieces(x):
+    rows, units = x.shape
+    split = x.reshape(rows // 8, 8, units // (2 * LANES), 2, LANES).transpose(0, 2, 3, 1, 4)
+    return split.reshape(rows // 8, units // (2 * LANES), 16, LANES)
+
+
 def chunks_of(length, ramp, tail):
-    left = length // DEPTH - sum(ramp) - sum(tail)
+    left = length - sum(ramp) - sum(tail)
     sizes = [*ramp, *([4] * (left // 4)), *([left % 4] if left % 4 else []), *tail]
-    starts = [sum(sizes[:i]) for i in range(len(sizes))]
-    return [(start * DEPTH, size * DEPTH) for start, size in zip(starts, sizes)]
+    return [(sum(sizes[:i]), size) for i, size in enumerate(sizes)]
 
 
 def project_kernel(g_chunks, h_chunks, h_ref, g_ref, pin_ref, pout_ref, out_ref, h_buf, g_buf, pin_buf, pout_buf, sems):
@@ -46,28 +50,45 @@
 
     for i in range(FLIGHT):
         start(i)
+
+    def line_up(ref, first, size):
+        blocks = [ref[:, j].reshape(ref.shape[0] * 16, LANES) for j in range(first, first + size)]
+        return jnp.concatenate(blocks, axis=1)
+
     totals = [None, None]
     for i, (_, proj_buf, _, data_buf, (first, size)) in enumerate(plan):
         for copy in copies[i]:
             copy.wait()
         start(i + FLIGHT)
         which = 0 if i < len(g_chunks) else 1
-        for j in range(first, first + size, DEPTH):
-            at = pl.ds(j, DEPTH)
-            part = lax.dot_general(proj_buf[:, at], data_buf[:, at], NT, preferred_element_type=jnp.float32)
+        for j in range(first, first + size, 2):
+            n = min(2, first + size - j)
+            part = lax.dot_general(
+                line_up(proj_buf, j, n), line_up(data_buf, j, n), NT, preferred_element_type=jnp.float32
+            )
             totals[which] = part if totals[which] is None else totals[which] + part
-    ranks = totals[0].shape[0]
-    out_ref[0:ranks, :] = totals[0]
-    out_ref[ranks:, :] = totals[1]
+
+    spread = totals[0].shape[1]
+    even = lax.broadcasted_iota(jnp.int32, (8, spread), 1) % 16 < 8
+    lines = []
+    for total in totals:
+        for g in range(total.shape[0] // 16):
+            lines.append(jnp.where(even, total[16 * g:16 * g + 8], total[16 * g + 8:16 * g + 16]))
+    lane = lax.broadcasted_iota(jnp.int32, (spread, spread // 2), 0)
+    token = lax.broadcasted_iota(jnp.int32, (spread, spread // 2), 1)
+    fold = jnp.where(lane // 16 * 8 + lane % 8 == token, 1.0, 0.0)
+    out_ref[...] = jnp.dot(
+        jnp.concatenate(lines, axis=0), fold, precision=HIGHEST, preferred_element_type=jnp.float32
+    )
 
 
 def project(hidden, out_grad, pin_t, pout_t):
     tokens, units = hidden.shape
     width = out_grad.shape[1]
     ranks = pin_t.shape[0] + pout_t.shape[0]
-    operands = (hidden, out_grad, pin_t, pout_t)
-    g_chunks = chunks_of(width, (1, 2, 3), ())
-    h_chunks = chunks_of(units, (), (3, 1))
+    operands = [pieces(x) for x in (hidden, out_grad, pin_t, pout_t)]
+    g_chunks = chunks_of(operands[1].shape[1], (2,), ())
+    h_chunks = chunks_of(operands[0].shape[1], (), (2, 2))
     return pl.pallas_call(
         functools.partial(project_kernel, g_chunks, h_chunks),
         out_shape=jax.ShapeDtypeStruct((ranks, tokens), jnp.float32),

time: 36.4 us -> 35.4 us (0.973)
  Pallas kernels: 11.1 us -> 10.1 us
    pallas_call x1, Pallas kernels: 7.13 us -> 6.2 us  [project(): pl.pallas_call(functools.partial(project_kernel, g_chunks, h_chunks), out...]
where the time goes in v10:
time: 35.4 us; the launch traced here: 35.3 us
  starting transfers between devices  17.9 us (51%)
  Pallas kernels  10.1 us (29%)
  waiting for transfers between devices  6.87 us (19%)
    ppermute x6, starting transfers between devices, trade(): got.append(lax.ppermute(x, ('dp', 'tensor'), pairs))  9.08 us
    ppermute x2, starting transfers between devices, trade_last(): return lax.ppermute(x, 'dp', [(i, i ^ dp - 1) for i in range(dp)])  7.58 us
    pallas_call x1, Pallas kernels, project(): pl.pallas_call(functools.partial(project_kernel, g_chunks, h_chunks), out...  6.2 us
    ppermute x6, waiting for transfers between devices, trade(): got.append(lax.ppermute(x, ('dp', 'tensor'), pairs))  3.08 us
    ppermute x3, waiting for transfers between devices, swap_cores(): return lax.ppermute(x, 'tensor', [(i, cores - 1 - i) for i in range(cores)])  2.83 us
    pallas_call x1, Pallas kernels, solve(): pl.pallas_call(functools.partial(solve_kernel, docs, queries, scale), out...  2.56 us
    ppermute x3, starting transfers between devices, swap_cores(): return lax.ppermute(x, 'tensor', [(i, cores - 1 - i) for i in range(cores)])  1.23 us
    ppermute x2, waiting for transfers between devices, trade_last(): return lax.ppermute(x, 'dp', [(i, i ^ dp - 1) for i in range(dp)])  0.96 us
  transfers between devices with their start and end apart: 11, of which 8 were waited for; matrix products, arithmetic and copies ran while one was open for 1% of the time, Pallas kernels for 2%

profile of v10, /device:TPU:0, one launch (start us, length us, event | category | flops | bytes accessed | tf_op | source)
XLA Modules:
  0.0 35.3 jit_solution(1147837966624483720)
XLA Ops:
  0.0 0.0 copy-start
  0.0 0.0 copy-start.1
  0.0 6.2 %project.1.part_ref = f32[128,256]{1,0:T(8,128)S(1)} custom-call(bf16[32,56,16,128]{3,2,1,0:T(8,128)(2,1)} %bitcast.30, bf16[32,16,16,128]{3,2,1,0:T(8,128)(2,1)} %bitcast.31, bf16[8,56,16,128]{3,2,1,0:T(8,128)(2,1)} %bitcast.32, bf16[8,16,16,128]{3,2,1,0:T(8,128)(2,1)} %bitcast.33), custom_call_target="tpu_custom_call" | custom-call | flops 603979776 | bytes 11796480 | tf_op jit(solution)/shard_map/project/pallas_call | solution.py:92
  6.2 0.5 %collective-permute-start = (f32[128,256]{1,0:T(8,128)S(1)}, f32[128,256]{1,0:T(8,128)S(1)}, u32[]{:S(2)}, u32[]{:S(2)}) collective-permute-start(f32[128,256]{1,0:T(8,128)S(1)} %project.1.part_ref), channel_id=1, source_target_pairs={{0,1},{1,0},{2,3},{3,2},{4,5},{5,4},{6,7},{7,6},{8,9},{9,8},{10,11... | collective-permute-start | bytes 393224 | tf_op jit(solution)/shard_map/ppermute | solution.py:303
  6.7 0.0 copy-done
  6.7 0.2 reshape.38
  6.9 0.1 reshape.39
  7.0 0.0 copy-done.1
  7.1 0.6 %collective-permute-done.recv_ref = f32[128,256]{1,0:T(8,128)S(1)} collective-permute-done((f32[128,256]{1,0:T(8,128)S(1)}, f32[128,256]{1,0:T(8,128)S(1)}, u32[]{:S(2)}, u32[]{:S(2)}) %collective-permute-start) | collective-permute-done | bytes 131104 | tf_op jit(solution)/shard_map/ppermute | solution.py:303
  7.7 0.1 pack.1
  7.8 4.0 %collective-permute-start.2 = (f32[56,256]{1,0:T(8,128)S(1)}, f32[56,256]{1,0:T(8,128)S(1)}, u32[]{:S(2)}, u32[]{:S(2)}) collective-permute-start(f32[56,256]{1,0:T(8,128)S(1)} %get-tuple-element.11), channel_id=1, source_target_pairs={{0,8},{1,11},{2,10},{3,9},{4,12},{5,15},{6,14},{7,13},{8,0},{9,3},... | collective-permute-start | bytes 172040 | tf_op jit(solution)/shard_map/ppermute | solution.py:311
  11.8 1.3 %collective-permute-start.3 = (f32[56,256]{1,0:T(8,128)S(1)}, f32[56,256]{1,0:T(8,128)S(1)}, u32[]{:S(2)}, u32[]{:S(2)}) collective-permute-start(f32[56,256]{1,0:T(8,128)S(1)} %get-tuple-element.12), channel_id=1, source_target_pairs={{0,12},{1,3},{2,14},{3,1},{4,8},{5,7},{6,10},{7,5},{8,4},{9,11},{1... | collective-permute-start | bytes 172040 | tf_op jit(solution)/shard_map/ppermute | solution.py:311
  13.1 0.2 collective-permute-start.4
  13.4 3.9 %collective-permute-start.1 = (f32[56,128]{1,0:T(8,128)S(1)}, f32[56,128]{1,0:T(8,128)S(1)}, u32[]{:S(2)}, u32[]{:S(2)}) collective-permute-start(f32[56,128]{1,0:T(8,128)S(1)} %get-tuple-element.10), channel_id=1, source_target_pairs={{0,14},{2,12},{4,10},{6,8},{8,6},{10,4},{12,2},{14,0},{1,15},{3,13... | collective-permute-start | bytes 86024 | tf_op jit(solution)/shard_map/ppermute | solution.py:317
  17.2 0.0 collective-permute-done.2.refs_0_
  17.2 0.6 %collective-permute-done.3.refs_1_ = f32[56,256]{1,0:T(8,128)S(1)} collective-permute-done((f32[56,256]{1,0:T(8,128)S(1)}, f32[56,256]{1,0:T(8,128)S(1)}, u32[]{:S(2)}, u32[]{:S(2)}) %collective-permute-start.3) | collective-permute-done | bytes 57376 | tf_op jit(solution)/shard_map/ppermute | solution.py:311
  17.9 0.4 %collective-permute-done.4.refs_2_ = f32[56,256]{1,0:T(8,128)S(1)} collective-permute-done((f32[56,256]{1,0:T(8,128)S(1)}, f32[56,256]{1,0:T(8,128)S(1)}, u32[]{:S(2)}, u32[]{:S(2)}) %collective-permute-start.4) | collective-permute-done | bytes 57376 | tf_op jit(solution)/shard_map/ppermute | solution.py:311
  18.2 0.7 %grads.2.refs_1_ = f32[80,512]{1,0:T(8,128)S(1)} custom-call(f32[56,256]{1,0:T(8,128)S(1)} %collective-permute-done.2.refs_0_, f32[56,256]{1,0:T(8,128)S(1)} %collective-permute-done.3.refs_1_, f32[56,256]{1,0:T(8,128)S(1)} %collective-permute-done.4.refs_2_, f32[56,128]{1,0:T(8,128)S(1)} %get-tuple-element.14.refs_3_), custom_call_target="tpu_custom_call" | custom-call | flops 117440512 | bytes 172032 | tf_op jit(solution)/shard_map/grads/pallas_call | solution.py:209
  19.0 1.0 %collective-permute-done.1.refs_0_ = f32[56,128]{1,0:T(8,128)S(1)} collective-permute-done((f32[56,128]{1,0:T(8,128)S(1)}, f32[56,128]{1,0:T(8,128)S(1)}, u32[]{:S(2)}, u32[]{:S(2)}) %collective-permute-start.1) | collective-permute-done | bytes 28704 | tf_op jit(solution)/shard_map/ppermute | solution.py:317
  19.9 0.2 grads.3.part_ref
  20.2 0.6 %collective-permute-start.5 = (f32[80,512]{1,0:T(8,128)S(1)}, f32[80,512]{1,0:T(8,128)S(1)}, u32[]{:S(2)}, u32[]{:S(2)}) collective-permute-start(f32[80,512]{1,0:T(8,128)S(1)} %grads.3.part_ref), channel_id=1, source_target_pairs={{0,1},{1,0},{2,3},{3,2},{4,5},{5,4},{6,7},{7,6},{8,9},{9,8},{10,11... | collective-permute-start | bytes 491528 | tf_op jit(solution)/shard_map/ppermute | solution.py:303
  20.8 1.0 %collective-permute-done.5.recv_ref = f32[80,512]{1,0:T(8,128)S(1)} collective-permute-done((f32[80,512]{1,0:T(8,128)S(1)}, f32[80,512]{1,0:T(8,128)S(1)}, u32[]{:S(2)}, u32[]{:S(2)}) %collective-permute-start.5) | collective-permute-done | bytes 163872 | tf_op jit(solution)/shard_map/ppermute | solution.py:303
  21.8 0.4 gram.1
  22.2 3.7 %collective-permute-start.6 = (f32[40,128]{1,0:T(8,128)S(1)}, f32[40,128]{1,0:T(8,128)S(1)}, u32[]{:S(2)}, u32[]{:S(2)}) collective-permute-start(f32[40,128]{1,0:T(8,128)S(1)} %gram.1), channel_id=1, source_target_pairs={{0,14},{2,12},{4,10},{6,8},{8,6},{10,4},{12,2},{14,0},{1,15},{3,13... | collective-permute-start | bytes 61448 | tf_op jit(solution)/shard_map/ppermute | solution.py:317
  25.9 0.0 collective-permute-start.7
  25.9 1.0 %collective-permute-start.8 = (f32[40,128]{1,0:T(8,128)S(1)}, f32[40,128]{1,0:T(8,128)S(1)}, u32[]{:S(2)}, u32[]{:S(2)}) collective-permute-start(f32[40,128]{1,0:T(8,128)S(1)} %gram.1), channel_id=1, source_target_pairs={{0,12},{1,3},{2,14},{3,1},{4,8},{5,7},{6,10},{7,5},{8,4},{9,11},{1... | collective-permute-start | bytes 61448 | tf_op jit(solution)/shard_map/ppermute | solution.py:311
  26.9 2.5 %collective-permute-start.9 = (f32[40,128]{1,0:T(8,128)S(1)}, f32[40,128]{1,0:T(8,128)S(1)}, u32[]{:S(2)}, u32[]{:S(2)}) collective-permute-start(f32[40,128]{1,0:T(8,128)S(1)} %gram.1), channel_id=1, source_target_pairs={{0,4},{1,7},{2,6},{3,5},{4,0},{5,3},{6,2},{7,1},{8,12},{9,15},{10,... | collective-permute-start | bytes 61448 | tf_op jit(solution)/shard_map/ppermute | solution.py:311
  29.4 0.0 collective-permute-done.6
  29.4 1.2 %collective-permute-done.7 = f32[40,128]{1,0:T(8,128)S(1)} collective-permute-done((f32[40,128]{1,0:T(8,128)S(1)}, f32[40,128]{1,0:T(8,128)S(1)}, u32[]{:S(2)}, u32[]{:S(2)}) %collective-permute-start.7) | collective-permute-done | bytes 20512 | tf_op jit(solution)/shard_map/ppermute | solution.py:311
  30.6 0.9 %collective-permute-done.8 = f32[40,128]{1,0:T(8,128)S(1)} collective-permute-done((f32[40,128]{1,0:T(8,128)S(1)}, f32[40,128]{1,0:T(8,128)S(1)}, u32[]{:S(2)}, u32[]{:S(2)}) %collective-permute-start.8) | collective-permute-done | bytes 20512 | tf_op jit(solution)/shard_map/ppermute | solution.py:311
  31.5 0.0 collective-permute-done.9
  31.5 0.1 collective-permute-start.10
  31.6 1.2 %collective-permute-done.10.recv_ref = f32[40,128]{1,0:T(8,128)S(1)} collective-permute-done((f32[40,128]{1,0:T(8,128)S(1)}, f32[40,128]{1,0:T(8,128)S(1)}, u32[]{:S(2)}, u32[]{:S(2)}) %collective-permute-start.10) | collective-permute-done | bytes 20512 | tf_op jit(solution)/shard_map/ppermute | solution.py:303
  32.8 2.6 %solve.1 = f32[8,16]{1,0:T(8,128)} custom-call(f32[40,128]{1,0:T(8,128)S(1)} %add_add_fusion.x_ref, f32[40,128]{1,0:T(8,128)S(1)} %collective-permute-done.10.recv_ref), custom_call_target="tpu_custom_call" | custom-call | tf_op jit(solution)/shard_map/solve/pallas_call | solution.py:282
  (5 shorter events, 0.1 us)
Async XLA Ops:
  0.0 6.7 %copy-start = (f32[2,4096]{1,0:T(2,128)S(1)}, f32[2,4096]{1,0:T(2,128)}, u32[]{:S(2)}) copy-start(f32[2,4096]{1,0:T(2,128)} %param.11) | copy-start | bytes 98308
  0.0 7.0 %copy-start.1 = (s32[256]{0:T(256)S(1)}, s32[256]{0:T(256)}, u32[]{:S(2)}) copy-start(s32[256]{0:T(256)} %param.10) | copy-start | bytes 3076
  6.2 1.5 %collective-permute-start = (f32[128,256]{1,0:T(8,128)S(1)}, f32[128,256]{1,0:T(8,128)S(1)}, u32[]{:S(2)}, u32[]{:S(2)}) collective-permute-start(f32[128,256]{1,0:T(8,128)S(1)} %project.1.part_ref), channel_id=1, source_target_pairs={{0,1},{1,0},{2,3},{3,2},{4,5},{5,4},{6,7},{7,6},{8,9},{9,8},{10,11... | collective-permute-start | bytes 393224 | tf_op jit(solution)/shard_map/ppermute | solution.py:303
  7.8 9.5 %collective-permute-start.2 = (f32[56,256]{1,0:T(8,128)S(1)}, f32[56,256]{1,0:T(8,128)S(1)}, u32[]{:S(2)}, u32[]{:S(2)}) collective-permute-start(f32[56,256]{1,0:T(8,128)S(1)} %get-tuple-element.11), channel_id=1, source_target_pairs={{0,8},{1,11},{2,10},{3,9},{4,12},{5,15},{6,14},{7,13},{8,0},{9,3},... | collective-permute-start | bytes 172040 | tf_op jit(solution)/shard_map/ppermute | solution.py:311
  11.8 6.1 %collective-permute-start.3 = (f32[56,256]{1,0:T(8,128)S(1)}, f32[56,256]{1,0:T(8,128)S(1)}, u32[]{:S(2)}, u32[]{:S(2)}) collective-permute-start(f32[56,256]{1,0:T(8,128)S(1)} %get-tuple-element.12), channel_id=1, source_target_pairs={{0,12},{1,3},{2,14},{3,1},{4,8},{5,7},{6,10},{7,5},{8,4},{9,11},{1... | collective-permute-start | bytes 172040 | tf_op jit(solution)/shard_map/ppermute | solution.py:311
  13.1 5.1 %collective-permute-start.4 = (f32[56,256]{1,0:T(8,128)S(1)}, f32[56,256]{1,0:T(8,128)S(1)}, u32[]{:S(2)}, u32[]{:S(2)}) collective-permute-start(f32[56,256]{1,0:T(8,128)S(1)} %get-tuple-element.13), channel_id=1, source_target_pairs={{0,4},{1,7},{2,6},{3,5},{4,0},{5,3},{6,2},{7,1},{8,12},{9,15},{10,... | collective-permute-start | bytes 172040 | tf_op jit(solution)/shard_map/ppermute | solution.py:311
  13.4 6.6 %collective-permute-start.1 = (f32[56,128]{1,0:T(8,128)S(1)}, f32[56,128]{1,0:T(8,128)S(1)}, u32[]{:S(2)}, u32[]{:S(2)}) collective-permute-start(f32[56,128]{1,0:T(8,128)S(1)} %get-tuple-element.10), channel_id=1, source_target_pairs={{0,14},{2,12},{4,10},{6,8},{8,6},{10,4},{12,2},{14,0},{1,15},{3,13... | collective-permute-start | bytes 86024 | tf_op jit(solution)/shard_map/ppermute | solution.py:317
  20.2 1.7 %collective-permute-start.5 = (f32[80,512]{1,0:T(8,128)S(1)}, f32[80,512]{1,0:T(8,128)S(1)}, u32[]{:S(2)}, u32[]{:S(2)}) collective-permute-start(f32[80,512]{1,0:T(8,128)S(1)} %grads.3.part_ref), channel_id=1, source_target_pairs={{0,1},{1,0},{2,3},{3,2},{4,5},{5,4},{6,7},{7,6},{8,9},{9,8},{10,11... | collective-permute-start | bytes 491528 | tf_op jit(solution)/shard_map/ppermute | solution.py:303
  22.2 7.2 %collective-permute-start.6 = (f32[40,128]{1,0:T(8,128)S(1)}, f32[40,128]{1,0:T(8,128)S(1)}, u32[]{:S(2)}, u32[]{:S(2)}) collective-permute-start(f32[40,128]{1,0:T(8,128)S(1)} %gram.1), channel_id=1, source_target_pairs={{0,14},{2,12},{4,10},{6,8},{8,6},{10,4},{12,2},{14,0},{1,15},{3,13... | collective-permute-start | bytes 61448 | tf_op jit(solution)/shard_map/ppermute | solution.py:317
  25.9 4.7 %collective-permute-start.7 = (f32[40,128]{1,0:T(8,128)S(1)}, f32[40,128]{1,0:T(8,128)S(1)}, u32[]{:S(2)}, u32[]{:S(2)}) collective-permute-start(f32[40,128]{1,0:T(8,128)S(1)} %gram.1), channel_id=1, source_target_pairs={{0,8},{1,11},{2,10},{3,9},{4,12},{5,15},{6,14},{7,13},{8,0},{9,3},... | collective-permute-start | bytes 61448 | tf_op jit(solution)/shard_map/ppermute | solution.py:311
  25.9 5.6 %collective-permute-start.8 = (f32[40,128]{1,0:T(8,128)S(1)}, f32[40,128]{1,0:T(8,128)S(1)}, u32[]{:S(2)}, u32[]{:S(2)}) collective-permute-start(f32[40,128]{1,0:T(8,128)S(1)} %gram.1), channel_id=1, source_target_pairs={{0,12},{1,3},{2,14},{3,1},{4,8},{5,7},{6,10},{7,5},{8,4},{9,11},{1... | collective-permute-start | bytes 61448 | tf_op jit(solution)/shard_map/ppermute | solution.py:311
  26.9 4.6 %collective-permute-start.9 = (f32[40,128]{1,0:T(8,128)S(1)}, f32[40,128]{1,0:T(8,128)S(1)}, u32[]{:S(2)}, u32[]{:S(2)}) collective-permute-start(f32[40,128]{1,0:T(8,128)S(1)} %gram.1), channel_id=1, source_target_pairs={{0,4},{1,7},{2,6},{3,5},{4,0},{5,3},{6,2},{7,1},{8,12},{9,15},{10,... | collective-permute-start | bytes 61448 | tf_op jit(solution)/shard_map/ppermute | solution.py:311
  31.5 1.3 %collective-permute-start.10 = (f32[40,128]{1,0:T(8,128)S(1)}, f32[40,128]{1,0:T(8,128)S(1)}, u32[]{:S(2)}, u32[]{:S(2)}) collective-permute-start(f32[40,128]{1,0:T(8,128)S(1)} %add_add_fusion.x_ref), channel_id=1, source_target_pairs={{0,1},{1,0},{2,3},{3,2},{4,5},{5,4},{6,7},{7,6},{8,9},{9,8},{10,11... | collective-permute-start | bytes 61448 | tf_op jit(solution)/shard_map/ppermute | solution.py:303

commit v11 on v10

--- a/solution.py
+++ b/solution.py
@@ -11,6 +11,7 @@
 DOC_DEV = 8
 LANES = 128
 FLIGHT = 7
+SHARED = 1
 NT = (((1,), (1,)), ((), ()))
 HIGHEST = lax.Precision.HIGHEST
 VMEM = pl.BlockSpec(memory_space=pltpu.VMEM)
@@ -33,7 +34,7 @@
     return [(sum(sizes[:i]), size) for i, size in enumerate(sizes)]
 
 
-def project_kernel(g_chunks, h_chunks, h_ref, g_ref, pin_ref, pout_ref, out_ref, h_buf, g_buf, pin_buf, pout_buf, sems):
+def project_kernel(g_chunks, h_chunks, h_ref, g_ref, pin_ref, pout_ref, out_ref, h_buf, g_buf, pin_buf, pout_buf, fold_ref, sems):
     plan = [(pout_ref, pout_buf, g_ref, g_buf, at) for at in g_chunks] + [(pin_ref, pin_buf, h_ref, h_buf, at) for at in h_chunks]
     copies = []
     for i, (proj, proj_buf, data, data_buf, (start, size)) in enumerate(plan):
@@ -50,6 +51,9 @@
 
     for i in range(FLIGHT):
         start(i)
+    lane = lax.broadcasted_iota(jnp.int32, fold_ref.shape, 0)
+    token = lax.broadcasted_iota(jnp.int32, fold_ref.shape, 1)
+    fold_ref[...] = jnp.where(lane // 16 * 8 + lane % 8 == token, 1.0, 0.0).astype(jnp.bfloat16)
 
     def line_up(ref, first, size):
         blocks = [ref[:, j].reshape(ref.shape[0] * 16, LANES) for j in range(first, first + size)]
@@ -61,12 +65,10 @@
             copy.wait()
         start(i + FLIGHT)
         which = 0 if i < len(g_chunks) else 1
-        for j in range(first, first + size, 2):
-            n = min(2, first + size - j)
-            part = lax.dot_general(
-                line_up(proj_buf, j, n), line_up(data_buf, j, n), NT, preferred_element_type=jnp.float32
-            )
-            totals[which] = part if totals[which] is None else totals[which] + part
+        part = lax.dot_general(
+            line_up(proj_buf, first, size), line_up(data_buf, first, size), NT, preferred_element_type=jnp.float32
+        )
+        totals[which] = part if totals[which] is None else totals[which] + part
 
     spread = totals[0].shape[1]
     even = lax.broadcasted_iota(jnp.int32, (8, spread), 1) % 16 < 8
@@ -74,12 +76,14 @@
     for total in totals:
         for g in range(total.shape[0] // 16):
             lines.append(jnp.where(even, total[16 * g:16 * g + 8], total[16 * g + 8:16 * g + 16]))
-    lane = lax.broadcasted_iota(jnp.int32, (spread, spread // 2), 0)
-    token = lax.broadcasted_iota(jnp.int32, (spread, spread // 2), 1)
-    fold = jnp.where(lane // 16 * 8 + lane % 8 == token, 1.0, 0.0)
-    out_ref[...] = jnp.dot(
-        jnp.concatenate(lines, axis=0), fold, precision=HIGHEST, preferred_element_type=jnp.float32
-    )
+    lines = jnp.concatenate(lines, axis=0)
+    split = []
+    for _ in range(3):
+        split.append(lines.astype(jnp.bfloat16))
+        lines = lines - split[-1].astype(jnp.float32)
+    rows = out_ref.shape[0]
+    sums = jnp.dot(jnp.concatenate(split, axis=0), fold_ref[...], preferred_element_type=jnp.float32)
+    out_ref[...] = sums[2 * rows:] + sums[rows:2 * rows] + sums[:rows]
 
 
 def project(hidden, out_grad, pin_t, pout_t):
@@ -95,7 +99,7 @@
         in_specs=[HBM] * 4,
         out_specs=VMEM,
         scratch_shapes=[pltpu.VMEM(x.shape, x.dtype) for x in operands]
-        + [pltpu.SemaphoreType.DMA((2 * len(g_chunks + h_chunks),))],
+        + [pltpu.VMEM((2 * tokens, tokens), jnp.bfloat16), pltpu.SemaphoreType.DMA((2 * len(g_chunks + h_chunks),))],
         compiler_params=vmem_params(53.5),
         cost_estimate=pl.CostEstimate(
             flops=2 * tokens * 64 * (units + width),
@@ -107,7 +111,7 @@
 
 
 def partners(dp):
-    order = [m for far in (True, False) for m in range(1, dp - 1) if (2 * m >= dp) == far]
+    order = [m for far in (True, False) for m in range(1, dp) if m != SHARED and (2 * m >= dp) == far]
     return order[0::2], order[1::2]
 
 
@@ -135,7 +139,7 @@
 
     for t, out_ref in enumerate(outs[:-2]):
         rows(out_ref, me ^ partner(dp, t), lambda x: x)
-    rows(outs[-2], me ^ (dp - 1), half)
+    rows(outs[-2], me ^ SHARED, half)
     rows(outs[-1], me, half)
 
 
@@ -257,19 +261,25 @@
     for r in range(len(rows)):
         wide = [[jnp.broadcast_to(x[:, c:c + 1], (size, cols)) for c in range(r * size, (r + 1) * size)] for x in rows]
         pivot, line = wide[r], rows[r]
-        scale_rows = jnp.ones((size, cols), jnp.float32)
-        for j in range(size):
-            inverse = 1.0 / pivot[j][j:j + 1]
-            factor = jnp.where(here == j, 0.0, pivot[j]) * inverse
-            pivot = [x if i <= j else x - factor * x[j:j + 1] for i, x in enumerate(pivot)]
-            line = line - factor * line[j:j + 1]
-            scale_rows = jnp.where(here == j, inverse, scale_rows)
-        line = line * scale_rows
+        pairs = []
+        for j in range(0, size, 2):
+            left, right = pivot[j], pivot[j + 1]
+            a, b, c, d = left[j:j + 1], right[j:j + 1], left[j + 1:j + 2], right[j + 1:j + 2]
+            inverse = 1.0 / (a * d - b * c)
+            left, right = (jnp.where(here // 2 == j // 2, 0.0, x) for x in (left, right))
+            first, second = (left * d - right * c) * inverse, (right * a - left * b) * inverse
+            pairs.append((a * inverse, b * inverse, c * inverse, d * inverse))
+            pivot = [x if i <= j + 1 else x - (first * x[j:j + 1] + second * x[j + 1:j + 2]) for i, x in enumerate(pivot)]
+            line = line - (first * line[j:j + 1] + second * line[j + 1:j + 2])
+        lines = []
+        for j, (a, b, c, d) in zip(range(0, size, 2), pairs):
+            upper, lower = line[j:j + 1], line[j + 1:j + 2]
+            lines += [upper * d - lower * b, lower * a - upper * c]
         for s in range(len(rows)):
             if s == r:
-                rows[s] = line
+                rows[s] = jnp.concatenate(lines, axis=0)
             else:
-                terms = [wide[s][j] * line[j:j + 1] for j in range(size)]
+                terms = [wide[s][j] * lines[j] for j in range(size)]
                 rows[s] = rows[s] - (((terms[0] + terms[1]) + (terms[2] + terms[3]))
                                      + ((terms[4] + terms[5]) + (terms[6] + terms[7])))
     for r, x in enumerate(rows):
@@ -312,9 +322,9 @@
     return got
 
 
-def trade_last(x):
+def trade_shared(x):
     dp = lax.axis_size("dp")
-    return lax.ppermute(x, "dp", [(i, i ^ (dp - 1)) for i in range(dp)])
+    return lax.ppermute(x, "dp", [(i, i ^ SHARED) for i in range(dp)])
 
 
 def local(hidden, out_grad, proj_in, proj_out, doc_ids, queries):
@@ -339,13 +349,13 @@
     *blocks, last, own = pack(part, recv, extra, pa, pb)
     gaps = list(zip(*partners(dp)))
     sizes = (rows_a, rows_b, docs, num_queries, dp, lanes)
-    last = trade_last(last)
+    last = trade_shared(last)
     grads = grads_of(trade(blocks) + [own], gaps + [(0, 0)], (), *sizes)
-    grads = grads_of([last], [(dp - 1, dp - 1)], (grads,), *sizes)
+    grads = grads_of([last], [(SHARED, SHARED)], (grads,), *sizes)
     share = gram(grads, swap_cores(grads), docs)
     scale = float(ranks * ranks) ** -0.5
     if docs <= 64:
-        halves = jnp.where(lax.axis_index("tensor") == 0, share, trade_last(share))
+        halves = jnp.where(lax.axis_index("tensor") == 0, share, trade_shared(share))
         share = sum(trade([share] * (dp // 2 - 1)), halves)
         return solve(share, swap_cores(share), docs, num_queries, scale).T
     share = lax.psum(share, "dp")

time: 35.4 us -> 34.3 us (0.969)
  starting transfers between devices: 17.9 us -> 12.7 us
  waiting for transfers between devices: 6.87 us -> 11.1 us
    ppermute x6, waiting for transfers between devices: 3.08 us -> 7.99 us  [trade(): got.append(lax.ppermute(x, ('dp', 'tensor'), pairs))]
    ppermute x2, starting transfers between devices: 7.58 us -> 2.87 us  [trade_shared(): return lax.ppermute(x, 'dp', [(i, i ^ SHARED) for i in range(dp)])]
    ppermute x2, waiting for transfers between devices: 0.96 us -> 0.01 us  [trade_shared(): return lax.ppermute(x, 'dp', [(i, i ^ SHARED) for i in range(dp)])]
    ppermute x3, starting transfers between devices: 1.23 us -> 0.7 us  [swap_cores(): return lax.ppermute(x, 'tensor', [(i, cores - 1 - i) for i in range(cores)])]
    pallas_call x1, Pallas kernels: 6.2 us -> 5.67 us  [project(): pl.pallas_call(functools.partial(project_kernel, g_chunks, h_chunks), out...]
  transfers between devices with their start and end apart: 11 -> 11, of which waited for: 8 -> 7; matrix products, arithmetic and copies ran while one was open for 1% -> 1% of each run, Pallas kernels for 2% -> 2%
where the time goes in v11:
time: 34.3 us; the launch traced here: 34.2 us
  starting transfers between devices  12.7 us (37%)
  waiting for transfers between devices  11.1 us (32%)
  Pallas kernels  9.93 us (29%)
    ppermute x6, starting transfers between devices, trade(): got.append(lax.ppermute(x, ('dp', 'tensor'), pairs))  9.08 us
    ppermute x6, waiting for transfers between devices, trade(): got.append(lax.ppermute(x, ('dp', 'tensor'), pairs))  7.99 us
    pallas_call x1, Pallas kernels, project(): pl.pallas_call(functools.partial(project_kernel, g_chunks, h_chunks), out...  5.67 us
    ppermute x3, waiting for transfers between devices, swap_cores(): return lax.ppermute(x, 'tensor', [(i, cores - 1 - i) for i in range(cores)])  3.14 us
    pallas_call x1, Pallas kernels, solve(): pl.pallas_call(functools.partial(solve_kernel, docs, queries, scale), out...  2.89 us
    ppermute x2, starting transfers between devices, trade_shared(): return lax.ppermute(x, 'dp', [(i, i ^ SHARED) for i in range(dp)])  2.87 us
    pallas_call x2, Pallas kernels, grads_of(): pl.pallas_call(functools.partial(grads_kernel, rows_a, rows_b, docs, dp,...  0.97 us
    ppermute x3, starting transfers between devices, swap_cores(): return lax.ppermute(x, 'tensor', [(i, cores - 1 - i) for i in range(cores)])  0.7 us
  transfers between devices with their start and end apart: 11, of which 7 were waited for; matrix products, arithmetic and copies ran while one was open for 1% of the time, Pallas kernels for 2%

profile of v11, /device:TPU:0, one launch (start us, length us, event | category | flops | bytes accessed | tf_op | source)
XLA Modules:
  0.0 34.2 jit_solution(7511342037581575918)
XLA Ops:
  0.0 0.0 copy-start
  0.0 0.0 copy-start.1
  0.0 5.7 %project.1.part_ref = f32[128,256]{1,0:T(8,128)S(1)} custom-call(bf16[32,56,16,128]{3,2,1,0:T(8,128)(2,1)} %bitcast.30, bf16[32,16,16,128]{3,2,1,0:T(8,128)(2,1)} %bitcast.31, bf16[8,56,16,128]{3,2,1,0:T(8,128)(2,1)} %bitcast.32, bf16[8,16,16,128]{3,2,1,0:T(8,128)(2,1)} %bitcast.33), custom_call_target="tpu_custom_call" | custom-call | flops 603979776 | bytes 11796480 | tf_op jit(solution)/shard_map/project/pallas_call | solution.py:96
  5.7 0.5 %collective-permute-start = (f32[128,256]{1,0:T(8,128)S(1)}, f32[128,256]{1,0:T(8,128)S(1)}, u32[]{:S(2)}, u32[]{:S(2)}) collective-permute-start(f32[128,256]{1,0:T(8,128)S(1)} %project.1.part_ref), channel_id=1, source_target_pairs={{0,1},{1,0},{2,3},{3,2},{4,5},{5,4},{6,7},{7,6},{8,9},{9,8},{10,11... | collective-permute-start | bytes 393224 | tf_op jit(solution)/shard_map/ppermute | solution.py:313
  6.2 0.0 copy-done
  6.2 0.2 reshape.38
  6.4 0.1 reshape.39
  6.5 0.0 copy-done.1
  6.6 0.6 %collective-permute-done.recv_ref = f32[128,256]{1,0:T(8,128)S(1)} collective-permute-done((f32[128,256]{1,0:T(8,128)S(1)}, f32[128,256]{1,0:T(8,128)S(1)}, u32[]{:S(2)}, u32[]{:S(2)}) %collective-permute-start) | collective-permute-done | bytes 131104 | tf_op jit(solution)/shard_map/ppermute | solution.py:313
  7.2 0.1 pack.1
  7.2 4.0 %collective-permute-start.2 = (f32[56,256]{1,0:T(8,128)S(1)}, f32[56,256]{1,0:T(8,128)S(1)}, u32[]{:S(2)}, u32[]{:S(2)}) collective-permute-start(f32[56,256]{1,0:T(8,128)S(1)} %get-tuple-element.11), channel_id=1, source_target_pairs={{0,8},{1,11},{2,10},{3,9},{4,12},{5,15},{6,14},{7,13},{8,0},{9,3},... | collective-permute-start | bytes 172040 | tf_op jit(solution)/shard_map/ppermute | solution.py:321
  11.3 1.4 %collective-permute-start.3 = (f32[56,256]{1,0:T(8,128)S(1)}, f32[56,256]{1,0:T(8,128)S(1)}, u32[]{:S(2)}, u32[]{:S(2)}) collective-permute-start(f32[56,256]{1,0:T(8,128)S(1)} %get-tuple-element.12), channel_id=1, source_target_pairs={{0,12},{1,15},{2,14},{3,13},{4,8},{5,11},{6,10},{7,9},{8,4},{9,7},... | collective-permute-start | bytes 172040 | tf_op jit(solution)/shard_map/ppermute | solution.py:321
  12.6 0.2 collective-permute-start.4
  12.8 1.5 %collective-permute-start.1 = (f32[56,128]{1,0:T(8,128)S(1)}, f32[56,128]{1,0:T(8,128)S(1)}, u32[]{:S(2)}, u32[]{:S(2)}) collective-permute-start(f32[56,128]{1,0:T(8,128)S(1)} %get-tuple-element.10), channel_id=1, source_target_pairs={{0,2},{2,0},{4,6},{6,4},{8,10},{10,8},{12,14},{14,12},{1,3},{3,1},... | collective-permute-start | bytes 86024 | tf_op jit(solution)/shard_map/ppermute | solution.py:327
  14.4 0.0 collective-permute-done.2.refs_0_
  14.4 3.4 %collective-permute-done.3.refs_1_ = f32[56,256]{1,0:T(8,128)S(1)} collective-permute-done((f32[56,256]{1,0:T(8,128)S(1)}, f32[56,256]{1,0:T(8,128)S(1)}, u32[]{:S(2)}, u32[]{:S(2)}) %collective-permute-start.3) | collective-permute-done | bytes 57376 | tf_op jit(solution)/shard_map/ppermute | solution.py:321
  17.8 0.6 %collective-permute-done.4.refs_2_ = f32[56,256]{1,0:T(8,128)S(1)} collective-permute-done((f32[56,256]{1,0:T(8,128)S(1)}, f32[56,256]{1,0:T(8,128)S(1)}, u32[]{:S(2)}, u32[]{:S(2)}) %collective-permute-start.4) | collective-permute-done | bytes 57376 | tf_op jit(solution)/shard_map/ppermute | solution.py:321
  18.4 0.7 %grads.2.refs_1_ = f32[80,512]{1,0:T(8,128)S(1)} custom-call(f32[56,256]{1,0:T(8,128)S(1)} %collective-permute-done.2.refs_0_, f32[56,256]{1,0:T(8,128)S(1)} %collective-permute-done.3.refs_1_, f32[56,256]{1,0:T(8,128)S(1)} %collective-permute-done.4.refs_2_, f32[56,128]{1,0:T(8,128)S(1)} %get-tuple-element.14.refs_3_), custom_call_target="tpu_custom_call" | custom-call | flops 117440512 | bytes 172032 | tf_op jit(solution)/shard_map/grads/pallas_call | solution.py:213
  19.1 0.0 collective-permute-done.1.refs_0_
  19.1 0.2 grads.3.part_ref
  19.3 0.1 collective-permute-start.5
  19.5 1.3 %collective-permute-done.5.recv_ref = f32[80,512]{1,0:T(8,128)S(1)} collective-permute-done((f32[80,512]{1,0:T(8,128)S(1)}, f32[80,512]{1,0:T(8,128)S(1)}, u32[]{:S(2)}, u32[]{:S(2)}) %collective-permute-start.5) | collective-permute-done | bytes 163872 | tf_op jit(solution)/shard_map/ppermute | solution.py:313
  20.8 0.3 %gram.1 = f32[40,128]{1,0:T(8,128)S(1)} custom-call(f32[80,512]{1,0:T(8,128)S(1)} %grads.3.part_ref, f32[80,512]{1,0:T(8,128)S(1)} %collective-permute-done.5.recv_ref), custom_call_target="tpu_custom_call" | custom-call | tf_op jit(solution)/shard_map/gram/pallas_call | solution.py:238
  21.2 1.4 %collective-permute-start.6 = (f32[40,128]{1,0:T(8,128)S(1)}, f32[40,128]{1,0:T(8,128)S(1)}, u32[]{:S(2)}, u32[]{:S(2)}) collective-permute-start(f32[40,128]{1,0:T(8,128)S(1)} %gram.1), channel_id=1, source_target_pairs={{0,2},{2,0},{4,6},{6,4},{8,10},{10,8},{12,14},{14,12},{1,3},{3,1},... | collective-permute-start | bytes 61448 | tf_op jit(solution)/shard_map/ppermute | solution.py:327
  22.5 1.9 %collective-permute-start.7 = (f32[40,128]{1,0:T(8,128)S(1)}, f32[40,128]{1,0:T(8,128)S(1)}, u32[]{:S(2)}, u32[]{:S(2)}) collective-permute-start(f32[40,128]{1,0:T(8,128)S(1)} %gram.1), channel_id=1, source_target_pairs={{0,8},{1,11},{2,10},{3,9},{4,12},{5,15},{6,14},{7,13},{8,0},{9,3},... | collective-permute-start | bytes 61448 | tf_op jit(solution)/shard_map/ppermute | solution.py:321
  24.4 1.0 %collective-permute-start.8 = (f32[40,128]{1,0:T(8,128)S(1)}, f32[40,128]{1,0:T(8,128)S(1)}, u32[]{:S(2)}, u32[]{:S(2)}) collective-permute-start(f32[40,128]{1,0:T(8,128)S(1)} %gram.1), channel_id=1, source_target_pairs={{0,12},{1,15},{2,14},{3,13},{4,8},{5,11},{6,10},{7,9},{8,4},{9,7},... | collective-permute-start | bytes 61448 | tf_op jit(solution)/shard_map/ppermute | solution.py:321
  25.4 0.6 %collective-permute-start.9 = (f32[40,128]{1,0:T(8,128)S(1)}, f32[40,128]{1,0:T(8,128)S(1)}, u32[]{:S(2)}, u32[]{:S(2)}) collective-permute-start(f32[40,128]{1,0:T(8,128)S(1)} %gram.1), channel_id=1, source_target_pairs={{0,4},{1,7},{2,6},{3,5},{4,0},{5,3},{6,2},{7,1},{8,12},{9,15},{10,... | collective-permute-start | bytes 61448 | tf_op jit(solution)/shard_map/ppermute | solution.py:321
  26.0 0.0 collective-permute-done.6
  26.0 1.3 %collective-permute-done.7 = f32[40,128]{1,0:T(8,128)S(1)} collective-permute-done((f32[40,128]{1,0:T(8,128)S(1)}, f32[40,128]{1,0:T(8,128)S(1)}, u32[]{:S(2)}, u32[]{:S(2)}) %collective-permute-start.7) | collective-permute-done | bytes 20512 | tf_op jit(solution)/shard_map/ppermute | solution.py:321
  27.3 2.7 %collective-permute-done.8 = f32[40,128]{1,0:T(8,128)S(1)} collective-permute-done((f32[40,128]{1,0:T(8,128)S(1)}, f32[40,128]{1,0:T(8,128)S(1)}, u32[]{:S(2)}, u32[]{:S(2)}) %collective-permute-start.8) | collective-permute-done | bytes 20512 | tf_op jit(solution)/shard_map/ppermute | solution.py:321
  30.0 0.0 collective-permute-done.9
  30.0 0.1 collective-permute-start.10
  30.1 1.2 %collective-permute-done.10.recv_ref = f32[40,128]{1,0:T(8,128)S(1)} collective-permute-done((f32[40,128]{1,0:T(8,128)S(1)}, f32[40,128]{1,0:T(8,128)S(1)}, u32[]{:S(2)}, u32[]{:S(2)}) %collective-permute-start.10) | collective-permute-done | bytes 20512 | tf_op jit(solution)/shard_map/ppermute | solution.py:313
  31.3 2.9 %solve.1 = f32[8,16]{1,0:T(8,128)} custom-call(f32[40,128]{1,0:T(8,128)S(1)} %add_add_fusion.x_ref, f32[40,128]{1,0:T(8,128)S(1)} %collective-permute-done.10.recv_ref), custom_call_target="tpu_custom_call" | custom-call | tf_op jit(solution)/shard_map/solve/pallas_call | solution.py:292
  (5 shorter events, 0.1 us)
Async XLA Ops:
  0.0 6.2 %copy-start = (f32[2,4096]{1,0:T(2,128)S(1)}, f32[2,4096]{1,0:T(2,128)}, u32[]{:S(2)}) copy-start(f32[2,4096]{1,0:T(2,128)} %param.11) | copy-start | bytes 98308
  0.0 6.5 %copy-start.1 = (s32[256]{0:T(256)S(1)}, s32[256]{0:T(256)}, u32[]{:S(2)}) copy-start(s32[256]{0:T(256)} %param.10) | copy-start | bytes 3076
  5.7 1.5 %collective-permute-start = (f32[128,256]{1,0:T(8,128)S(1)}, f32[128,256]{1,0:T(8,128)S(1)}, u32[]{:S(2)}, u32[]{:S(2)}) collective-permute-start(f32[128,256]{1,0:T(8,128)S(1)} %project.1.part_ref), channel_id=1, source_target_pairs={{0,1},{1,0},{2,3},{3,2},{4,5},{5,4},{6,7},{7,6},{8,9},{9,8},{10,11... | collective-permute-start | bytes 393224 | tf_op jit(solution)/shard_map/ppermute | solution.py:313
  7.2 7.1 %collective-permute-start.2 = (f32[56,256]{1,0:T(8,128)S(1)}, f32[56,256]{1,0:T(8,128)S(1)}, u32[]{:S(2)}, u32[]{:S(2)}) collective-permute-start(f32[56,256]{1,0:T(8,128)S(1)} %get-tuple-element.11), channel_id=1, source_target_pairs={{0,8},{1,11},{2,10},{3,9},{4,12},{5,15},{6,14},{7,13},{8,0},{9,3},... | collective-permute-start | bytes 172040 | tf_op jit(solution)/shard_map/ppermute | solution.py:321
  11.3 6.5 %collective-permute-start.3 = (f32[56,256]{1,0:T(8,128)S(1)}, f32[56,256]{1,0:T(8,128)S(1)}, u32[]{:S(2)}, u32[]{:S(2)}) collective-permute-start(f32[56,256]{1,0:T(8,128)S(1)} %get-tuple-element.12), channel_id=1, source_target_pairs={{0,12},{1,15},{2,14},{3,13},{4,8},{5,11},{6,10},{7,9},{8,4},{9,7},... | collective-permute-start | bytes 172040 | tf_op jit(solution)/shard_map/ppermute | solution.py:321
  12.6 5.7 %collective-permute-start.4 = (f32[56,256]{1,0:T(8,128)S(1)}, f32[56,256]{1,0:T(8,128)S(1)}, u32[]{:S(2)}, u32[]{:S(2)}) collective-permute-start(f32[56,256]{1,0:T(8,128)S(1)} %get-tuple-element.13), channel_id=1, source_target_pairs={{0,4},{1,7},{2,6},{3,5},{4,0},{5,3},{6,2},{7,1},{8,12},{9,15},{10,... | collective-permute-start | bytes 172040 | tf_op jit(solution)/shard_map/ppermute | solution.py:321
  12.8 6.3 %collective-permute-start.1 = (f32[56,128]{1,0:T(8,128)S(1)}, f32[56,128]{1,0:T(8,128)S(1)}, u32[]{:S(2)}, u32[]{:S(2)}) collective-permute-start(f32[56,128]{1,0:T(8,128)S(1)} %get-tuple-element.10), channel_id=1, source_target_pairs={{0,2},{2,0},{4,6},{6,4},{8,10},{10,8},{12,14},{14,12},{1,3},{3,1},... | collective-permute-start | bytes 86024 | tf_op jit(solution)/shard_map/ppermute | solution.py:327
  19.3 1.5 %collective-permute-start.5 = (f32[80,512]{1,0:T(8,128)S(1)}, f32[80,512]{1,0:T(8,128)S(1)}, u32[]{:S(2)}, u32[]{:S(2)}) collective-permute-start(f32[80,512]{1,0:T(8,128)S(1)} %grads.3.part_ref), channel_id=1, source_target_pairs={{0,1},{1,0},{2,3},{3,2},{4,5},{5,4},{6,7},{7,6},{8,9},{9,8},{10,11... | collective-permute-start | bytes 491528 | tf_op jit(solution)/shard_map/ppermute | solution.py:313
  21.2 4.8 %collective-permute-start.6 = (f32[40,128]{1,0:T(8,128)S(1)}, f32[40,128]{1,0:T(8,128)S(1)}, u32[]{:S(2)}, u32[]{:S(2)}) collective-permute-start(f32[40,128]{1,0:T(8,128)S(1)} %gram.1), channel_id=1, source_target_pairs={{0,2},{2,0},{4,6},{6,4},{8,10},{10,8},{12,14},{14,12},{1,3},{3,1},... | collective-permute-start | bytes 61448 | tf_op jit(solution)/shard_map/ppermute | solution.py:327
  22.5 4.8 %collective-permute-start.7 = (f32[40,128]{1,0:T(8,128)S(1)}, f32[40,128]{1,0:T(8,128)S(1)}, u32[]{:S(2)}, u32[]{:S(2)}) collective-permute-start(f32[40,128]{1,0:T(8,128)S(1)} %gram.1), channel_id=1, source_target_pairs={{0,8},{1,11},{2,10},{3,9},{4,12},{5,15},{6,14},{7,13},{8,0},{9,3},... | collective-permute-start | bytes 61448 | tf_op jit(solution)/shard_map/ppermute | solution.py:321
  24.4 5.6 %collective-permute-start.8 = (f32[40,128]{1,0:T(8,128)S(1)}, f32[40,128]{1,0:T(8,128)S(1)}, u32[]{:S(2)}, u32[]{:S(2)}) collective-permute-start(f32[40,128]{1,0:T(8,128)S(1)} %gram.1), channel_id=1, source_target_pairs={{0,12},{1,15},{2,14},{3,13},{4,8},{5,11},{6,10},{7,9},{8,4},{9,7},... | collective-permute-start | bytes 61448 | tf_op jit(solution)/shard_map/ppermute | solution.py:321
  25.4 4.6 %collective-permute-start.9 = (f32[40,128]{1,0:T(8,128)S(1)}, f32[40,128]{1,0:T(8,128)S(1)}, u32[]{:S(2)}, u32[]{:S(2)}) collective-permute-start(f32[40,128]{1,0:T(8,128)S(1)} %gram.1), channel_id=1, source_target_pairs={{0,4},{1,7},{2,6},{3,5},{4,0},{5,3},{6,2},{7,1},{8,12},{9,15},{10,... | collective-permute-start | bytes 61448 | tf_op jit(solution)/shard_map/ppermute | solution.py:321
  30.0 1.3 %collective-permute-start.10 = (f32[40,128]{1,0:T(8,128)S(1)}, f32[40,128]{1,0:T(8,128)S(1)}, u32[]{:S(2)}, u32[]{:S(2)}) collective-permute-start(f32[40,128]{1,0:T(8,128)S(1)} %add_add_fusion.x_ref), channel_id=1, source_target_pairs={{0,1},{1,0},{2,3},{3,2},{4,5},{5,4},{6,7},{7,6},{8,9},{9,8},{10,11... | collective-permute-start | bytes 61448 | tf_op jit(solution)/shard_map/ppermute | solution.py:313

commit v12 on v10

--- a/solution.py
+++ b/solution.py
@@ -11,6 +11,7 @@
 DOC_DEV = 8
 LANES = 128
 FLIGHT = 7
+SHARED = 1
 NT = (((1,), (1,)), ((), ()))
 HIGHEST = lax.Precision.HIGHEST
 VMEM = pl.BlockSpec(memory_space=pltpu.VMEM)
@@ -33,7 +34,7 @@
     return [(sum(sizes[:i]), size) for i, size in enumerate(sizes)]
 
 
-def project_kernel(g_chunks, h_chunks, h_ref, g_ref, pin_ref, pout_ref, out_ref, h_buf, g_buf, pin_buf, pout_buf, sems):
+def project_kernel(g_chunks, h_chunks, h_ref, g_ref, pin_ref, pout_ref, out_ref, h_buf, g_buf, pin_buf, pout_buf, fold_ref, sems):
     plan = [(pout_ref, pout_buf, g_ref, g_buf, at) for at in g_chunks] + [(pin_ref, pin_buf, h_ref, h_buf, at) for at in h_chunks]
     copies = []
     for i, (proj, proj_buf, data, data_buf, (start, size)) in enumerate(plan):
@@ -50,36 +51,41 @@
 
     for i in range(FLIGHT):
         start(i)
+    lane = lax.broadcasted_iota(jnp.int32, fold_ref.shape, 0)
+    token = lax.broadcasted_iota(jnp.int32, fold_ref.shape, 1)
+    fold_ref[...] = jnp.where(lane // 16 * 8 + lane % 8 == token, 1.0, 0.0).astype(jnp.bfloat16)
 
     def line_up(ref, first, size):
         blocks = [ref[:, j].reshape(ref.shape[0] * 16, LANES) for j in range(first, first + size)]
         return jnp.concatenate(blocks, axis=1)
 
-    totals = [None, None]
-    for i, (_, proj_buf, _, data_buf, (first, size)) in enumerate(plan):
-        for copy in copies[i]:
-            copy.wait()
-        start(i + FLIGHT)
-        which = 0 if i < len(g_chunks) else 1
-        for j in range(first, first + size, 2):
-            n = min(2, first + size - j)
+    even = lax.broadcasted_iota(jnp.int32, (8, fold_ref.shape[0]), 1) % 16 < 8
+
+    def run(chunks):
+        total = None
+        for i in chunks:
+            _, proj_buf, _, data_buf, (first, size) = plan[i]
+            for copy in copies[i]:
+                copy.wait()
+            start(i + FLIGHT)
             part = lax.dot_general(
-                line_up(proj_buf, j, n), line_up(data_buf, j, n), NT, preferred_element_type=jnp.float32
+                line_up(proj_buf, first, size), line_up(data_buf, first, size), NT, preferred_element_type=jnp.float32
             )
-            totals[which] = part if totals[which] is None else totals[which] + part
-
-    spread = totals[0].shape[1]
-    even = lax.broadcasted_iota(jnp.int32, (8, spread), 1) % 16 < 8
-    lines = []
-    for total in totals:
-        for g in range(total.shape[0] // 16):
-            lines.append(jnp.where(even, total[16 * g:16 * g + 8], total[16 * g + 8:16 * g + 16]))
-    lane = lax.broadcasted_iota(jnp.int32, (spread, spread // 2), 0)
-    token = lax.broadcasted_iota(jnp.int32, (spread, spread // 2), 1)
-    fold = jnp.where(lane // 16 * 8 + lane % 8 == token, 1.0, 0.0)
-    out_ref[...] = jnp.dot(
-        jnp.concatenate(lines, axis=0), fold, precision=HIGHEST, preferred_element_type=jnp.float32
-    )
+            lines = [jnp.where(even, part[j:j + 8], part[j + 8:j + 16]) for j in range(0, part.shape[0], 16)]
+            total = lines if total is None else [x + y for x, y in zip(total, lines)]
+        lines = jnp.concatenate(total, axis=0)
+        rows = lines.shape[0]
+        split = []
+        for _ in range(3):
+            split.append(lines.astype(jnp.bfloat16))
+            lines = lines - split[-1].astype(jnp.float32)
+        sums = jnp.dot(jnp.concatenate(split, axis=0), fold_ref[...], preferred_element_type=jnp.float32)
+        return sums[2 * rows:] + sums[rows:2 * rows] + sums[:rows]
+
+    grad = run(range(len(g_chunks)))
+    ranks = grad.shape[0]
+    out_ref[0:ranks, :] = grad
+    out_ref[ranks:, :] = run(range(len(g_chunks), len(plan)))
 
 
 def project(hidden, out_grad, pin_t, pout_t):
@@ -95,7 +101,7 @@
         in_specs=[HBM] * 4,
         out_specs=VMEM,
         scratch_shapes=[pltpu.VMEM(x.shape, x.dtype) for x in operands]
-        + [pltpu.SemaphoreType.DMA((2 * len(g_chunks + h_chunks),))],
+        + [pltpu.VMEM((2 * tokens, tokens), jnp.bfloat16), pltpu.SemaphoreType.DMA((2 * len(g_chunks + h_chunks),))],
         compiler_params=vmem_params(53.5),
         cost_estimate=pl.CostEstimate(
             flops=2 * tokens * 64 * (units + width),
@@ -107,7 +113,7 @@
 
 
 def partners(dp):
-    order = [m for far in (True, False) for m in range(1, dp - 1) if (2 * m >= dp) == far]
+    order = [m for far in (True, False) for m in range(1, dp) if m != SHARED and (2 * m >= dp) == far]
     return order[0::2], order[1::2]
 
 
@@ -135,7 +141,7 @@
 
     for t, out_ref in enumerate(outs[:-2]):
         rows(out_ref, me ^ partner(dp, t), lambda x: x)
-    rows(outs[-2], me ^ (dp - 1), half)
+    rows(outs[-2], me ^ SHARED, half)
     rows(outs[-1], me, half)
 
 
@@ -312,9 +318,9 @@
     return got
 
 
-def trade_last(x):
+def trade_shared(x):
     dp = lax.axis_size("dp")
-    return lax.ppermute(x, "dp", [(i, i ^ (dp - 1)) for i in range(dp)])
+    return lax.ppermute(x, "dp", [(i, i ^ SHARED) for i in range(dp)])
 
 
 def local(hidden, out_grad, proj_in, proj_out, doc_ids, queries):
@@ -336,17 +342,20 @@
     extra = jnp.concatenate([jnp.broadcast_to(ids, (dp, 1, lanes)), asked], axis=1)
     extra = jnp.pad(extra, ((0, 0), (0, -extra.shape[1] % 8), (0, 0)))
 
-    *blocks, last, own = pack(part, recv, extra, pa, pb)
+    *blocks, shared, own = pack(part, recv, extra, pa, pb)
     gaps = list(zip(*partners(dp)))
     sizes = (rows_a, rows_b, docs, num_queries, dp, lanes)
-    last = trade_last(last)
-    grads = grads_of(trade(blocks) + [own], gaps + [(0, 0)], (), *sizes)
-    grads = grads_of([last], [(dp - 1, dp - 1)], (grads,), *sizes)
+    blocks = trade(blocks) + [trade_shared(shared), own]
+    gaps += [(SHARED, SHARED), (0, 0)]
+    late = min(1, len(blocks) - 3)
+    rest = [t for t in range(len(blocks)) if t != late]
+    grads = grads_of([blocks[t] for t in rest], [gaps[t] for t in rest], (), *sizes)
+    grads = grads_of([blocks[late]], [gaps[late]], (grads,), *sizes)
     share = gram(grads, swap_cores(grads), docs)
     scale = float(ranks * ranks) ** -0.5
     if docs <= 64:
-        halves = jnp.where(lax.axis_index("tensor") == 0, share, trade_last(share))
-        share = sum(trade([share] * (dp // 2 - 1)), halves)
+        others = sum(trade([share] * (dp // 2 - 1)))
+        share = others + jnp.where(lax.axis_index("tensor") == 0, share, trade_shared(share))
         return solve(share, swap_cores(share), docs, num_queries, scale).T
     share = lax.psum(share, "dp")
     return solve_large(jnp.concatenate([share[:, :docs], share[:, docs:]], axis=0).T, docs, num_queries, scale).T

time: 35.4 us -> 34.9 us (0.986)
  starting transfers between devices: 17.9 us -> 13.1 us
  waiting for transfers between devices: 6.87 us -> 9.66 us
  Pallas kernels: 10.1 us -> 11.6 us
    ppermute x2, starting transfers between devices: 7.58 us -> 3.11 us  [trade_shared(): return lax.ppermute(x, 'dp', [(i, i ^ SHARED) for i in range(dp)])]
    ppermute x2, waiting for transfers between devices: 0.96 us -> 3 us  [trade_shared(): return lax.ppermute(x, 'dp', [(i, i ^ SHARED) for i in range(dp)])]
    pallas_call x1, Pallas kernels: 6.2 us -> 7.7 us  [project(): pl.pallas_call(functools.partial(project_kernel, g_chunks, h_chunks), out...]
    ppermute x6, waiting for transfers between devices: 3.08 us -> 3.72 us  [trade(): got.append(lax.ppermute(x, ('dp', 'tensor'), pairs))]
where the time goes in v12:
time: 34.9 us; the launch traced here: 34.8 us
  starting transfers between devices  13.1 us (38%)
  Pallas kernels  11.6 us (33%)
  waiting for transfers between devices  9.66 us (28%)
    ppermute x6, starting transfers between devices, trade(): got.append(lax.ppermute(x, ('dp', 'tensor'), pairs))  9.11 us
    pallas_call x1, Pallas kernels, project(): pl.pallas_call(functools.partial(project_kernel, g_chunks, h_chunks), out...  7.7 us
    ppermute x6, waiting for transfers between devices, trade(): got.append(lax.ppermute(x, ('dp', 'tensor'), pairs))  3.72 us
    ppermute x2, starting transfers between devices, trade_shared(): return lax.ppermute(x, 'dp', [(i, i ^ SHARED) for i in range(dp)])  3.11 us
    ppermute x2, waiting for transfers between devices, trade_shared(): return lax.ppermute(x, 'dp', [(i, i ^ SHARED) for i in range(dp)])  3 us
    ppermute x3, waiting for transfers between devices, swap_cores(): return lax.ppermute(x, 'tensor', [(i, cores - 1 - i) for i in range(cores)])  2.94 us
    pallas_call x1, Pallas kernels, solve(): pl.pallas_call(functools.partial(solve_kernel, docs, queries, scale), out...  2.56 us
    pallas_call x2, Pallas kernels, grads_of(): pl.pallas_call(functools.partial(grads_kernel, rows_a, rows_b, docs, dp,...  0.94 us
  transfers between devices with their start and end apart: 11, of which 8 were waited for; matrix products, arithmetic and copies ran while one was open for 1% of the time, Pallas kernels for 2%

profile of v12, /device:TPU:0, one launch (start us, length us, event | category | flops | bytes accessed | tf_op | source)
XLA Modules:
  0.0 34.8 jit_solution(10671464915799295798)
XLA Ops:
  0.0 0.0 copy-start
  0.0 0.0 copy-start.1
  0.0 7.7 %project.1.part_ref = f32[128,256]{1,0:T(8,128)S(1)} custom-call(bf16[32,56,16,128]{3,2,1,0:T(8,128)(2,1)} %bitcast.30, bf16[32,16,16,128]{3,2,1,0:T(8,128)(2,1)} %bitcast.31, bf16[8,56,16,128]{3,2,1,0:T(8,128)(2,1)} %bitcast.32, bf16[8,16,16,128]{3,2,1,0:T(8,128)(2,1)} %bitcast.33), custom_call_target="tpu_custom_call" | custom-call | flops 603979776 | bytes 11796480 | tf_op jit(solution)/shard_map/project/pallas_call | solution.py:98
  7.7 0.5 %collective-permute-start = (f32[128,256]{1,0:T(8,128)S(1)}, f32[128,256]{1,0:T(8,128)S(1)}, u32[]{:S(2)}, u32[]{:S(2)}) collective-permute-start(f32[128,256]{1,0:T(8,128)S(1)} %project.1.part_ref), channel_id=1, source_target_pairs={{0,1},{1,0},{2,3},{3,2},{4,5},{5,4},{6,7},{7,6},{8,9},{9,8},{10,11... | collective-permute-start | bytes 393224 | tf_op jit(solution)/shard_map/ppermute | solution.py:309
  8.2 0.0 copy-done
  8.2 0.2 reshape.38
  8.4 0.1 reshape.39
  8.5 0.0 copy-done.1
  8.6 0.6 %collective-permute-done.recv_ref = f32[128,256]{1,0:T(8,128)S(1)} collective-permute-done((f32[128,256]{1,0:T(8,128)S(1)}, f32[128,256]{1,0:T(8,128)S(1)}, u32[]{:S(2)}, u32[]{:S(2)}) %collective-permute-start) | collective-permute-done | bytes 131104 | tf_op jit(solution)/shard_map/ppermute | solution.py:309
  9.2 0.1 pack.1
  9.3 4.0 %collective-permute-start.2 = (f32[56,256]{1,0:T(8,128)S(1)}, f32[56,256]{1,0:T(8,128)S(1)}, u32[]{:S(2)}, u32[]{:S(2)}) collective-permute-start(f32[56,256]{1,0:T(8,128)S(1)} %get-tuple-element.11), channel_id=1, source_target_pairs={{0,8},{1,11},{2,10},{3,9},{4,12},{5,15},{6,14},{7,13},{8,0},{9,3},... | collective-permute-start | bytes 172040 | tf_op jit(solution)/shard_map/ppermute | solution.py:317
  13.3 1.6 %collective-permute-start.3 = (f32[56,256]{1,0:T(8,128)S(1)}, f32[56,256]{1,0:T(8,128)S(1)}, u32[]{:S(2)}, u32[]{:S(2)}) collective-permute-start(f32[56,256]{1,0:T(8,128)S(1)} %get-tuple-element.12), channel_id=1, source_target_pairs={{0,4},{1,7},{2,6},{3,5},{4,0},{5,3},{6,2},{7,1},{8,12},{9,15},{10,... | collective-permute-start | bytes 172040 | tf_op jit(solution)/shard_map/ppermute | solution.py:317
  14.9 0.0 collective-permute-start.1
  14.9 1.7 %collective-permute-start.4 = (f32[56,128]{1,0:T(8,128)S(1)}, f32[56,128]{1,0:T(8,128)S(1)}, u32[]{:S(2)}, u32[]{:S(2)}) collective-permute-start(f32[56,128]{1,0:T(8,128)S(1)} %get-tuple-element.13), channel_id=1, source_target_pairs={{0,2},{2,0},{4,6},{6,4},{8,10},{10,8},{12,14},{14,12},{1,3},{3,1},... | collective-permute-start | bytes 86024 | tf_op jit(solution)/shard_map/ppermute | solution.py:323
  16.6 2.4 %collective-permute-done.4.refs_2_ = f32[56,128]{1,0:T(8,128)S(1)} collective-permute-done((f32[56,128]{1,0:T(8,128)S(1)}, f32[56,128]{1,0:T(8,128)S(1)}, u32[]{:S(2)}, u32[]{:S(2)}) %collective-permute-start.4) | collective-permute-done | bytes 28704 | tf_op jit(solution)/shard_map/ppermute | solution.py:323
  19.0 0.0 collective-permute-done.2.refs_0_
  19.0 0.0 collective-permute-done.3.refs_1_
  19.0 0.6 %grads.2.refs_1_ = f32[80,512]{1,0:T(8,128)S(1)} custom-call(f32[56,256]{1,0:T(8,128)S(1)} %collective-permute-done.2.refs_0_, f32[56,256]{1,0:T(8,128)S(1)} %collective-permute-done.3.refs_1_, f32[56,128]{1,0:T(8,128)S(1)} %collective-permute-done.4.refs_2_, f32[56,128]{1,0:T(8,128)S(1)} %get-tuple-element.14.refs_3_), custom_call_target="tpu_custom_call" | custom-call | flops 100663296 | bytes 147456 | tf_op jit(solution)/shard_map/grads/pallas_call | solution.py:215
  19.7 1.4 %collective-permute-done.1.refs_0_ = f32[56,256]{1,0:T(8,128)S(1)} collective-permute-done((f32[56,256]{1,0:T(8,128)S(1)}, f32[56,256]{1,0:T(8,128)S(1)}, u32[]{:S(2)}, u32[]{:S(2)}) %collective-permute-start.1) | collective-permute-done | bytes 57376 | tf_op jit(solution)/shard_map/ppermute | solution.py:317
  21.1 0.3 grads.3.part_ref
  21.4 0.2 collective-permute-start.5
  21.6 1.2 %collective-permute-done.5.recv_ref = f32[80,512]{1,0:T(8,128)S(1)} collective-permute-done((f32[80,512]{1,0:T(8,128)S(1)}, f32[80,512]{1,0:T(8,128)S(1)}, u32[]{:S(2)}, u32[]{:S(2)}) %collective-permute-start.5) | collective-permute-done | bytes 163872 | tf_op jit(solution)/shard_map/ppermute | solution.py:309
  22.8 0.4 %gram.1 = f32[40,128]{1,0:T(8,128)S(1)} custom-call(f32[80,512]{1,0:T(8,128)S(1)} %grads.3.part_ref, f32[80,512]{1,0:T(8,128)S(1)} %collective-permute-done.5.recv_ref), custom_call_target="tpu_custom_call" | custom-call | tf_op jit(solution)/shard_map/gram/pallas_call | solution.py:240
  23.2 1.6 %collective-permute-start.6 = (f32[40,128]{1,0:T(8,128)S(1)}, f32[40,128]{1,0:T(8,128)S(1)}, u32[]{:S(2)}, u32[]{:S(2)}) collective-permute-start(f32[40,128]{1,0:T(8,128)S(1)} %gram.1), channel_id=1, source_target_pairs={{0,8},{1,11},{2,10},{3,9},{4,12},{5,15},{6,14},{7,13},{8,0},{9,3},... | collective-permute-start | bytes 61448 | tf_op jit(solution)/shard_map/ppermute | solution.py:317
  24.8 1.4 %collective-permute-start.7 = (f32[40,128]{1,0:T(8,128)S(1)}, f32[40,128]{1,0:T(8,128)S(1)}, u32[]{:S(2)}, u32[]{:S(2)}) collective-permute-start(f32[40,128]{1,0:T(8,128)S(1)} %gram.1), channel_id=1, source_target_pairs={{0,12},{1,15},{2,14},{3,13},{4,8},{5,11},{6,10},{7,9},{8,4},{9,7},... | collective-permute-start | bytes 61448 | tf_op jit(solution)/shard_map/ppermute | solution.py:317
  26.2 0.5 %collective-permute-start.8 = (f32[40,128]{1,0:T(8,128)S(1)}, f32[40,128]{1,0:T(8,128)S(1)}, u32[]{:S(2)}, u32[]{:S(2)}) collective-permute-start(f32[40,128]{1,0:T(8,128)S(1)} %gram.1), channel_id=1, source_target_pairs={{0,4},{1,7},{2,6},{3,5},{4,0},{5,3},{6,2},{7,1},{8,12},{9,15},{10,... | collective-permute-start | bytes 61448 | tf_op jit(solution)/shard_map/ppermute | solution.py:317
  26.7 1.4 %collective-permute-start.9 = (f32[40,128]{1,0:T(8,128)S(1)}, f32[40,128]{1,0:T(8,128)S(1)}, u32[]{:S(2)}, u32[]{:S(2)}) collective-permute-start(f32[40,128]{1,0:T(8,128)S(1)} %gram.1), channel_id=1, source_target_pairs={{0,2},{2,0},{4,6},{6,4},{8,10},{10,8},{12,14},{14,12},{1,3},{3,1},... | collective-permute-start | bytes 61448 | tf_op jit(solution)/shard_map/ppermute | solution.py:323
  28.1 0.1 collective-permute-done.6
  28.2 2.2 %collective-permute-done.7 = f32[40,128]{1,0:T(8,128)S(1)} collective-permute-done((f32[40,128]{1,0:T(8,128)S(1)}, f32[40,128]{1,0:T(8,128)S(1)}, u32[]{:S(2)}, u32[]{:S(2)}) %collective-permute-start.7) | collective-permute-done | bytes 20512 | tf_op jit(solution)/shard_map/ppermute | solution.py:317
  30.4 0.0 collective-permute-done.8
  30.4 0.6 %collective-permute-done.9 = f32[40,128]{1,0:T(8,128)S(1)} collective-permute-done((f32[40,128]{1,0:T(8,128)S(1)}, f32[40,128]{1,0:T(8,128)S(1)}, u32[]{:S(2)}, u32[]{:S(2)}) %collective-permute-start.9) | collective-permute-done | bytes 20512 | tf_op jit(solution)/shard_map/ppermute | solution.py:323
  31.0 0.2 collective-permute-start.10
  31.2 1.1 %collective-permute-done.10.recv_ref = f32[40,128]{1,0:T(8,128)S(1)} collective-permute-done((f32[40,128]{1,0:T(8,128)S(1)}, f32[40,128]{1,0:T(8,128)S(1)}, u32[]{:S(2)}, u32[]{:S(2)}) %collective-permute-start.10) | collective-permute-done | bytes 20512 | tf_op jit(solution)/shard_map/ppermute | solution.py:309
  32.2 2.6 %solve.1 = f32[8,16]{1,0:T(8,128)} custom-call(f32[40,128]{1,0:T(8,128)S(1)} %select_add_fusion.x_ref, f32[40,128]{1,0:T(8,128)S(1)} %collective-permute-done.10.recv_ref), custom_call_target="tpu_custom_call" | custom-call | tf_op jit(solution)/shard_map/solve/pallas_call | solution.py:288
  (5 shorter events, 0.0 us)
Async XLA Ops:
  0.0 8.2 %copy-start = (f32[2,4096]{1,0:T(2,128)S(1)}, f32[2,4096]{1,0:T(2,128)}, u32[]{:S(2)}) copy-start(f32[2,4096]{1,0:T(2,128)} %param.11) | copy-start | bytes 98308
  0.0 8.5 %copy-start.1 = (s32[256]{0:T(256)S(1)}, s32[256]{0:T(256)}, u32[]{:S(2)}) copy-start(s32[256]{0:T(256)} %param.10) | copy-start | bytes 3076
  7.7 1.5 %collective-permute-start = (f32[128,256]{1,0:T(8,128)S(1)}, f32[128,256]{1,0:T(8,128)S(1)}, u32[]{:S(2)}, u32[]{:S(2)}) collective-permute-start(f32[128,256]{1,0:T(8,128)S(1)} %project.1.part_ref), channel_id=1, source_target_pairs={{0,1},{1,0},{2,3},{3,2},{4,5},{5,4},{6,7},{7,6},{8,9},{9,8},{10,11... | collective-permute-start | bytes 393224 | tf_op jit(solution)/shard_map/ppermute | solution.py:309
  9.3 9.8 %collective-permute-start.2 = (f32[56,256]{1,0:T(8,128)S(1)}, f32[56,256]{1,0:T(8,128)S(1)}, u32[]{:S(2)}, u32[]{:S(2)}) collective-permute-start(f32[56,256]{1,0:T(8,128)S(1)} %get-tuple-element.11), channel_id=1, source_target_pairs={{0,8},{1,11},{2,10},{3,9},{4,12},{5,15},{6,14},{7,13},{8,0},{9,3},... | collective-permute-start | bytes 172040 | tf_op jit(solution)/shard_map/ppermute | solution.py:317
  13.3 5.7 %collective-permute-start.3 = (f32[56,256]{1,0:T(8,128)S(1)}, f32[56,256]{1,0:T(8,128)S(1)}, u32[]{:S(2)}, u32[]{:S(2)}) collective-permute-start(f32[56,256]{1,0:T(8,128)S(1)} %get-tuple-element.12), channel_id=1, source_target_pairs={{0,4},{1,7},{2,6},{3,5},{4,0},{5,3},{6,2},{7,1},{8,12},{9,15},{10,... | collective-permute-start | bytes 172040 | tf_op jit(solution)/shard_map/ppermute | solution.py:317
  14.9 6.2 %collective-permute-start.1 = (f32[56,256]{1,0:T(8,128)S(1)}, f32[56,256]{1,0:T(8,128)S(1)}, u32[]{:S(2)}, u32[]{:S(2)}) collective-permute-start(f32[56,256]{1,0:T(8,128)S(1)} %get-tuple-element.10), channel_id=1, source_target_pairs={{0,12},{1,15},{2,14},{3,13},{4,8},{5,11},{6,10},{7,9},{8,4},{9,7},... | collective-permute-start | bytes 172040 | tf_op jit(solution)/shard_map/ppermute | solution.py:317
  14.9 4.2 %collective-permute-start.4 = (f32[56,128]{1,0:T(8,128)S(1)}, f32[56,128]{1,0:T(8,128)S(1)}, u32[]{:S(2)}, u32[]{:S(2)}) collective-permute-start(f32[56,128]{1,0:T(8,128)S(1)} %get-tuple-element.13), channel_id=1, source_target_pairs={{0,2},{2,0},{4,6},{6,4},{8,10},{10,8},{12,14},{14,12},{1,3},{3,1},... | collective-permute-start | bytes 86024 | tf_op jit(solution)/shard_map/ppermute | solution.py:323
  21.4 1.5 %collective-permute-start.5 = (f32[80,512]{1,0:T(8,128)S(1)}, f32[80,512]{1,0:T(8,128)S(1)}, u32[]{:S(2)}, u32[]{:S(2)}) collective-permute-start(f32[80,512]{1,0:T(8,128)S(1)} %grads.3.part_ref), channel_id=1, source_target_pairs={{0,1},{1,0},{2,3},{3,2},{4,5},{5,4},{6,7},{7,6},{8,9},{9,8},{10,11... | collective-permute-start | bytes 491528 | tf_op jit(solution)/shard_map/ppermute | solution.py:309
  23.2 5.0 %collective-permute-start.6 = (f32[40,128]{1,0:T(8,128)S(1)}, f32[40,128]{1,0:T(8,128)S(1)}, u32[]{:S(2)}, u32[]{:S(2)}) collective-permute-start(f32[40,128]{1,0:T(8,128)S(1)} %gram.1), channel_id=1, source_target_pairs={{0,8},{1,11},{2,10},{3,9},{4,12},{5,15},{6,14},{7,13},{8,0},{9,3},... | collective-permute-start | bytes 61448 | tf_op jit(solution)/shard_map/ppermute | solution.py:317
  24.8 5.6 %collective-permute-start.7 = (f32[40,128]{1,0:T(8,128)S(1)}, f32[40,128]{1,0:T(8,128)S(1)}, u32[]{:S(2)}, u32[]{:S(2)}) collective-permute-start(f32[40,128]{1,0:T(8,128)S(1)} %gram.1), channel_id=1, source_target_pairs={{0,12},{1,15},{2,14},{3,13},{4,8},{5,11},{6,10},{7,9},{8,4},{9,7},... | collective-permute-start | bytes 61448 | tf_op jit(solution)/shard_map/ppermute | solution.py:317
  26.2 4.2 %collective-permute-start.8 = (f32[40,128]{1,0:T(8,128)S(1)}, f32[40,128]{1,0:T(8,128)S(1)}, u32[]{:S(2)}, u32[]{:S(2)}) collective-permute-start(f32[40,128]{1,0:T(8,128)S(1)} %gram.1), channel_id=1, source_target_pairs={{0,4},{1,7},{2,6},{3,5},{4,0},{5,3},{6,2},{7,1},{8,12},{9,15},{10,... | collective-permute-start | bytes 61448 | tf_op jit(solution)/shard_map/ppermute | solution.py:317
  26.7 4.3 %collective-permute-start.9 = (f32[40,128]{1,0:T(8,128)S(1)}, f32[40,128]{1,0:T(8,128)S(1)}, u32[]{:S(2)}, u32[]{:S(2)}) collective-permute-start(f32[40,128]{1,0:T(8,128)S(1)} %gram.1), channel_id=1, source_target_pairs={{0,2},{2,0},{4,6},{6,4},{8,10},{10,8},{12,14},{14,12},{1,3},{3,1},... | collective-permute-start | bytes 61448 | tf_op jit(solution)/shard_map/ppermute | solution.py:323
  31.0 1.3 %collective-permute-start.10 = (f32[40,128]{1,0:T(8,128)S(1)}, f32[40,128]{1,0:T(8,128)S(1)}, u32[]{:S(2)}, u32[]{:S(2)}) collective-permute-start(f32[40,128]{1,0:T(8,128)S(1)} %select_add_fusion.x_ref), channel_id=1, source_target_pairs={{0,1},{1,0},{2,3},{3,2},{4,5},{5,4},{6,7},{7,6},{8,9},{9,8},{10,11... | collective-permute-start | bytes 61448 | tf_op jit(solution)/shard_map/ppermute | solution.py:309

commit v13 on v12

--- a/solution.py
+++ b/solution.py
@@ -71,9 +71,9 @@
             part = lax.dot_general(
                 line_up(proj_buf, first, size), line_up(data_buf, first, size), NT, preferred_element_type=jnp.float32
             )
-            lines = [jnp.where(even, part[j:j + 8], part[j + 8:j + 16]) for j in range(0, part.shape[0], 16)]
-            total = lines if total is None else [x + y for x, y in zip(total, lines)]
-        lines = jnp.concatenate(total, axis=0)
+            total = part if total is None else total + part
+        lines = [jnp.where(even, total[j:j + 8], total[j + 8:j + 16]) for j in range(0, total.shape[0], 16)]
+        lines = jnp.concatenate(lines, axis=0)
         rows = lines.shape[0]
         split = []
         for _ in range(3):
@@ -112,6 +112,10 @@
     )(*operands)
 
 
+def owners_of(dp):
+    return max(dp // 2, 1)
+
+
 def partners(dp):
     order = [m for far in (True, False) for m in range(1, dp) if m != SHARED and (2 * m >= dp) == far]
     return order[0::2], order[1::2]
@@ -122,15 +126,15 @@
     return jnp.where(lax.axis_index("tensor") == 0, first[t], second[t])
 
 
-def pack_kernel(pb, rows_a, rows_b, part_ref, recv_ref, extra_ref, *refs):
+def pack_kernel(dp, pb, rows_a, rows_b, part_ref, recv_ref, extra_ref, *refs):
     outs, total_ref = refs[:-1], refs[-1]
     total_ref[...] = part_ref[...] + recv_ref[...]
     ranks, lanes = total_ref.shape[0] // 2, total_ref.shape[1]
-    dp = extra_ref.shape[0]
     me = lax.axis_index("dp")
     lead = lax.axis_index("tensor") == 0
 
-    def rows(out_ref, owner, pick):
+    def rows(out_ref, to, pick):
+        owner = to % extra_ref.shape[0]
         p, q = owner // pb, owner % pb
         out_ref[0:rows_a, :] = pick(total_ref[pl.ds(pl.multiple_of(p * rows_a, rows_a), rows_a), :])
         out_ref[rows_a:rows_a + rows_b, :] = pick(total_ref[pl.ds(pl.multiple_of(ranks + q * rows_b, rows_b), rows_b), :])
@@ -145,14 +149,14 @@
     rows(outs[-1], me, half)
 
 
-def pack(part, recv, extra, pa, pb):
+def pack(part, recv, extra, dp, pa, pb):
     ranks, lanes = part.shape[0] // 2, part.shape[1]
     rows_a, rows_b = ranks // pa, ranks // pb
     rows = rows_a + rows_b + extra.shape[1]
-    count = pa * pb // 2 - 1
+    count = dp // 2 - 1
     whole, half = (jax.ShapeDtypeStruct((rows, n), jnp.float32) for n in (lanes, lanes // 2))
     return pl.pallas_call(
-        functools.partial(pack_kernel, pb, rows_a, rows_b),
+        functools.partial(pack_kernel, dp, pb, rows_a, rows_b),
         out_shape=(whole,) * count + (half, half),
         in_specs=[VMEM] * 3,
         out_specs=(VMEM,) * (count + 2),
@@ -309,10 +313,10 @@
     return lax.ppermute(x, "tensor", [(i, cores - 1 - i) for i in range(cores)])
 
 
-def trade(xs):
+def trade(xs, group):
     dp = lax.axis_size("dp")
     got = []
-    for x, ms in zip(xs, zip(*partners(dp))):
+    for x, ms in zip(xs, zip(*partners(group))):
         pairs = [(i * 2 + k, (i ^ m) * 2 + k) for i in range(dp) for k, m in enumerate(ms)]
         got.append(lax.ppermute(x, ("dp", "tensor"), pairs))
     return got
@@ -327,10 +331,11 @@
     dp = lax.axis_size("dp")
     docs, num_queries = DOC_DEV * dp, queries.shape[0] * dp
     ranks = proj_in.shape[1]
+    owners = owners_of(dp)
     pa = 1
-    while pa * pa < dp:
+    while pa * pa < owners:
         pa *= 2
-    pb = dp // pa
+    pb = owners // pa
     rows_a, rows_b = ranks // pa, ranks // pb
 
     part = project(hidden, out_grad, proj_in.T, proj_out.T)
@@ -338,14 +343,14 @@
 
     lanes = part.shape[1]
     ids = doc_ids.astype(jnp.float32)
-    asked = queries.reshape(-1, pa, rows_a, pb, rows_b).transpose(1, 3, 0, 2, 4).reshape(dp, -1, lanes)
-    extra = jnp.concatenate([jnp.broadcast_to(ids, (dp, 1, lanes)), asked], axis=1)
+    asked = queries.reshape(-1, pa, rows_a, pb, rows_b).transpose(1, 3, 0, 2, 4).reshape(owners, -1, lanes)
+    extra = jnp.concatenate([jnp.broadcast_to(ids, (owners, 1, lanes)), asked], axis=1)
     extra = jnp.pad(extra, ((0, 0), (0, -extra.shape[1] % 8), (0, 0)))
 
-    *blocks, shared, own = pack(part, recv, extra, pa, pb)
+    *blocks, shared, own = pack(part, recv, extra, dp, pa, pb)
     gaps = list(zip(*partners(dp)))
     sizes = (rows_a, rows_b, docs, num_queries, dp, lanes)
-    blocks = trade(blocks) + [trade_shared(shared), own]
+    blocks = trade(blocks, dp) + [trade_shared(shared), own]
     gaps += [(SHARED, SHARED), (0, 0)]
     late = min(1, len(blocks) - 3)
     rest = [t for t in range(len(blocks)) if t != late]
@@ -354,10 +359,10 @@
     share = gram(grads, swap_cores(grads), docs)
     scale = float(ranks * ranks) ** -0.5
     if docs <= 64:
-        others = sum(trade([share] * (dp // 2 - 1)))
+        others = sum(trade([share] * (owners // 2 - 1), owners))
         share = others + jnp.where(lax.axis_index("tensor") == 0, share, trade_shared(share))
         return solve(share, swap_cores(share), docs, num_queries, scale).T
-    share = lax.psum(share, "dp")
+    share = lax.psum(share, "dp") * (owners / dp)
     return solve_large(jnp.concatenate([share[:, :docs], share[:, docs:]], axis=0).T, docs, num_queries, scale).T
 
 

time: 34.9 us -> 31.5 us (0.903)
  starting transfers between devices: 13.1 us -> 10.4 us
  Pallas kernels: 11.6 us -> 10.6 us
    ppermute x6 -> x4, starting transfers between devices: 9.11 us -> 6.99 us  [trade(): got.append(lax.ppermute(x, ('dp', 'tensor'), pairs))]
    pallas_call x1, Pallas kernels: 7.7 us -> 5.89 us  [project(): pl.pallas_call(functools.partial(project_kernel, g_chunks, h_chunks), out...]
    ppermute x6 -> x4, waiting for transfers between devices: 3.72 us -> 2.51 us  [trade(): got.append(lax.ppermute(x, ('dp', 'tensor'), pairs))]
    ppermute x2, waiting for transfers between devices: 3 us -> 4.11 us  [trade_shared(): return lax.ppermute(x, 'dp', [(i, i ^ SHARED) for i in range(dp)])]
    pallas_call x2, Pallas kernels: 0.94 us -> 1.61 us  [grads_of(): pl.pallas_call(functools.partial(grads_kernel, rows_a, rows_b, docs, dp,...]
    ppermute x2, starting transfers between devices: 3.11 us -> 2.72 us  [trade_shared(): return lax.ppermute(x, 'dp', [(i, i ^ SHARED) for i in range(dp)])]
    ppermute x3, waiting for transfers between devices: 2.94 us -> 3.3 us  [swap_cores(): return lax.ppermute(x, 'tensor', [(i, cores - 1 - i) for i in range(cores)])]
  transfers between devices with their start and end apart: 11 -> 9, of which waited for: 8 -> 7; matrix products, arithmetic and copies ran while one was open for 1% -> 1% of each run, Pallas kernels for 2% -> 4%
where the time goes in v13:
time: 31.5 us; the launch traced here: 31.3 us
  Pallas kernels  10.6 us (34%)
  starting transfers between devices  10.4 us (33%)
  waiting for transfers between devices  9.92 us (31%)
    ppermute x4, starting transfers between devices, trade(): got.append(lax.ppermute(x, ('dp', 'tensor'), pairs))  6.99 us
    pallas_call x1, Pallas kernels, project(): pl.pallas_call(functools.partial(project_kernel, g_chunks, h_chunks), out...  5.89 us
    ppermute x2, waiting for transfers between devices, trade_shared(): return lax.ppermute(x, 'dp', [(i, i ^ SHARED) for i in range(dp)])  4.11 us
    ppermute x3, waiting for transfers between devices, swap_cores(): return lax.ppermute(x, 'tensor', [(i, cores - 1 - i) for i in range(cores)])  3.3 us
    ppermute x2, starting transfers between devices, trade_shared(): return lax.ppermute(x, 'dp', [(i, i ^ SHARED) for i in range(dp)])  2.72 us
    pallas_call x1, Pallas kernels, solve(): pl.pallas_call(functools.partial(solve_kernel, docs, queries, scale), out...  2.56 us
    ppermute x4, waiting for transfers between devices, trade(): got.append(lax.ppermute(x, ('dp', 'tensor'), pairs))  2.51 us
    pallas_call x2, Pallas kernels, grads_of(): pl.pallas_call(functools.partial(grads_kernel, rows_a, rows_b, docs, dp,...  1.61 us
  transfers between devices with their start and end apart: 9, of which 7 were waited for; matrix products, arithmetic and copies ran while one was open for 1% of the time, Pallas kernels for 4%

profile of v13, /device:TPU:0, one launch (start us, length us, event | category | flops | bytes accessed | tf_op | source)
XLA Modules:
  0.0 31.3 jit_solution(11738945381155850810)
XLA Ops:
  0.0 0.0 copy-start
  0.0 0.0 copy-start.1
  0.0 5.9 %project.1.part_ref = f32[128,256]{1,0:T(8,128)S(1)} custom-call(bf16[32,56,16,128]{3,2,1,0:T(8,128)(2,1)} %bitcast.30, bf16[32,16,16,128]{3,2,1,0:T(8,128)(2,1)} %bitcast.31, bf16[8,56,16,128]{3,2,1,0:T(8,128)(2,1)} %bitcast.32, bf16[8,16,16,128]{3,2,1,0:T(8,128)(2,1)} %bitcast.33), custom_call_target="tpu_custom_call" | custom-call | flops 603979776 | bytes 11796480 | tf_op jit(solution)/shard_map/project/pallas_call | solution.py:98
  5.9 0.5 %collective-permute-start = (f32[128,256]{1,0:T(8,128)S(1)}, f32[128,256]{1,0:T(8,128)S(1)}, u32[]{:S(2)}, u32[]{:S(2)}) collective-permute-start(f32[128,256]{1,0:T(8,128)S(1)} %project.1.part_ref), channel_id=1, source_target_pairs={{0,1},{1,0},{2,3},{3,2},{4,5},{5,4},{6,7},{7,6},{8,9},{9,8},{10,11... | collective-permute-start | bytes 393224 | tf_op jit(solution)/shard_map/ppermute | solution.py:313
  6.4 0.0 copy-done
  6.4 0.2 reshape.38
  6.6 0.1 reshape.39
  6.7 0.0 copy-done.1
  6.8 0.6 %collective-permute-done.recv_ref = f32[128,256]{1,0:T(8,128)S(1)} collective-permute-done((f32[128,256]{1,0:T(8,128)S(1)}, f32[128,256]{1,0:T(8,128)S(1)}, u32[]{:S(2)}, u32[]{:S(2)}) %collective-permute-start) | collective-permute-done | bytes 131104 | tf_op jit(solution)/shard_map/ppermute | solution.py:313
  7.4 0.1 pack.1
  7.5 4.0 %collective-permute-start.2 = (f32[80,256]{1,0:T(8,128)S(1)}, f32[80,256]{1,0:T(8,128)S(1)}, u32[]{:S(2)}, u32[]{:S(2)}) collective-permute-start(f32[80,256]{1,0:T(8,128)S(1)} %get-tuple-element.11), channel_id=1, source_target_pairs={{0,8},{1,11},{2,10},{3,9},{4,12},{5,15},{6,14},{7,13},{8,0},{9,3},... | collective-permute-start | bytes 245768 | tf_op jit(solution)/shard_map/ppermute | solution.py:321
  11.5 1.6 %collective-permute-start.3 = (f32[80,256]{1,0:T(8,128)S(1)}, f32[80,256]{1,0:T(8,128)S(1)}, u32[]{:S(2)}, u32[]{:S(2)}) collective-permute-start(f32[80,256]{1,0:T(8,128)S(1)} %get-tuple-element.12), channel_id=1, source_target_pairs={{0,4},{1,7},{2,6},{3,5},{4,0},{5,3},{6,2},{7,1},{8,12},{9,15},{10,... | collective-permute-start | bytes 245768 | tf_op jit(solution)/shard_map/ppermute | solution.py:321
  13.1 0.0 collective-permute-start.1
  13.1 1.7 %collective-permute-start.4 = (f32[80,128]{1,0:T(8,128)S(1)}, f32[80,128]{1,0:T(8,128)S(1)}, u32[]{:S(2)}, u32[]{:S(2)}) collective-permute-start(f32[80,128]{1,0:T(8,128)S(1)} %get-tuple-element.13), channel_id=1, source_target_pairs={{0,2},{2,0},{4,6},{6,4},{8,10},{10,8},{12,14},{14,12},{1,3},{3,1},... | collective-permute-start | bytes 122888 | tf_op jit(solution)/shard_map/ppermute | solution.py:327
  14.8 2.8 %collective-permute-done.4.refs_2_ = f32[80,128]{1,0:T(8,128)S(1)} collective-permute-done((f32[80,128]{1,0:T(8,128)S(1)}, f32[80,128]{1,0:T(8,128)S(1)}, u32[]{:S(2)}, u32[]{:S(2)}) %collective-permute-start.4) | collective-permute-done | bytes 40992 | tf_op jit(solution)/shard_map/ppermute | solution.py:327
  17.6 0.0 collective-permute-done.2.refs_0_
  17.6 0.0 collective-permute-done.3.refs_1_
  17.6 1.2 %grads.2.refs_1_ = f32[80,1024]{1,0:T(8,128)S(1)} custom-call(f32[80,256]{1,0:T(8,128)S(1)} %collective-permute-done.2.refs_0_, f32[80,256]{1,0:T(8,128)S(1)} %collective-permute-done.3.refs_1_, f32[80,128]{1,0:T(8,128)S(1)} %collective-permute-done.4.refs_2_, f32[80,128]{1,0:T(8,128)S(1)} %get-tuple-element.14.refs_3_), custom_call_target="tpu_custom_call" | custom-call | flops 201326592 | bytes 196608 | tf_op jit(solution)/shard_map/grads/pallas_call | solution.py:219
  18.8 1.0 %collective-permute-done.1.refs_0_ = f32[80,256]{1,0:T(8,128)S(1)} collective-permute-done((f32[80,256]{1,0:T(8,128)S(1)}, f32[80,256]{1,0:T(8,128)S(1)}, u32[]{:S(2)}, u32[]{:S(2)}) %collective-permute-start.1) | collective-permute-done | bytes 81952 | tf_op jit(solution)/shard_map/ppermute | solution.py:321
  19.8 0.4 %grads.3.part_ref = f32[80,1024]{1,0:T(8,128)S(1)} custom-call(f32[80,256]{1,0:T(8,128)S(1)} %collective-permute-done.1.refs_0_, f32[80,1024]{1,0:T(8,128)S(1)} %grads.2.refs_1_), custom_call_target="tpu_custom_call" | custom-call | flops 67108864 | bytes 65536 | tf_op jit(solution)/shard_map/grads/pallas_call | solution.py:219
  20.2 0.2 collective-permute-start.5
  20.5 1.5 %collective-permute-done.5.recv_ref = f32[80,1024]{1,0:T(8,128)S(1)} collective-permute-done((f32[80,1024]{1,0:T(8,128)S(1)}, f32[80,1024]{1,0:T(8,128)S(1)}, u32[]{:S(2)}, u32[]{:S(2)}) %collective-permute-start.5) | collective-permute-done | bytes 327712 | tf_op jit(solution)/shard_map/ppermute | solution.py:313
  21.9 0.5 %gram.1 = f32[40,128]{1,0:T(8,128)S(1)} custom-call(f32[80,1024]{1,0:T(8,128)S(1)} %grads.3.part_ref, f32[80,1024]{1,0:T(8,128)S(1)} %collective-permute-done.5.recv_ref), custom_call_target="tpu_custom_call" | custom-call | tf_op jit(solution)/shard_map/gram/pallas_call | solution.py:244
  22.4 1.4 %collective-permute-start.6 = (f32[40,128]{1,0:T(8,128)S(1)}, f32[40,128]{1,0:T(8,128)S(1)}, u32[]{:S(2)}, u32[]{:S(2)}) collective-permute-start(f32[40,128]{1,0:T(8,128)S(1)} %gram.1), channel_id=1, source_target_pairs={{0,4},{1,7},{2,6},{3,5},{4,0},{5,3},{6,2},{7,1},{8,12},{9,15},{10,... | collective-permute-start | bytes 61448 | tf_op jit(solution)/shard_map/ppermute | solution.py:321
  23.8 1.0 %collective-permute-start.7 = (f32[40,128]{1,0:T(8,128)S(1)}, f32[40,128]{1,0:T(8,128)S(1)}, u32[]{:S(2)}, u32[]{:S(2)}) collective-permute-start(f32[40,128]{1,0:T(8,128)S(1)} %gram.1), channel_id=1, source_target_pairs={{0,2},{2,0},{4,6},{6,4},{8,10},{10,8},{12,14},{14,12},{1,3},{3,1},... | collective-permute-start | bytes 61448 | tf_op jit(solution)/shard_map/ppermute | solution.py:327
  24.8 1.5 %collective-permute-done.6 = f32[40,128]{1,0:T(8,128)S(1)} collective-permute-done((f32[40,128]{1,0:T(8,128)S(1)}, f32[40,128]{1,0:T(8,128)S(1)}, u32[]{:S(2)}, u32[]{:S(2)}) %collective-permute-start.6) | collective-permute-done | bytes 20512 | tf_op jit(solution)/shard_map/ppermute | solution.py:321
  26.3 1.3 %collective-permute-done.7 = f32[40,128]{1,0:T(8,128)S(1)} collective-permute-done((f32[40,128]{1,0:T(8,128)S(1)}, f32[40,128]{1,0:T(8,128)S(1)}, u32[]{:S(2)}, u32[]{:S(2)}) %collective-permute-start.7) | collective-permute-done | bytes 20512 | tf_op jit(solution)/shard_map/ppermute | solution.py:327
  27.6 0.0 collective-permute-start.8
  27.6 1.2 %collective-permute-done.8.recv_ref = f32[40,128]{1,0:T(8,128)S(1)} collective-permute-done((f32[40,128]{1,0:T(8,128)S(1)}, f32[40,128]{1,0:T(8,128)S(1)}, u32[]{:S(2)}, u32[]{:S(2)}) %collective-permute-start.8) | collective-permute-done | bytes 20512 | tf_op jit(solution)/shard_map/ppermute | solution.py:313
  28.8 2.6 %solve.1 = f32[8,16]{1,0:T(8,128)} custom-call(f32[40,128]{1,0:T(8,128)S(1)} %select_add_fusion.x_ref, f32[40,128]{1,0:T(8,128)S(1)} %collective-permute-done.8.recv_ref), custom_call_target="tpu_custom_call" | custom-call | tf_op jit(solution)/shard_map/solve/pallas_call | solution.py:292
  (5 shorter events, 0.0 us)
Async XLA Ops:
  0.0 6.4 %copy-start = (f32[2,4096]{1,0:T(2,128)S(1)}, f32[2,4096]{1,0:T(2,128)}, u32[]{:S(2)}) copy-start(f32[2,4096]{1,0:T(2,128)} %param.11) | copy-start | bytes 98308
  0.0 6.7 %copy-start.1 = (s32[256]{0:T(256)S(1)}, s32[256]{0:T(256)}, u32[]{:S(2)}) copy-start(s32[256]{0:T(256)} %param.10) | copy-start | bytes 3076
  5.9 1.5 %collective-permute-start = (f32[128,256]{1,0:T(8,128)S(1)}, f32[128,256]{1,0:T(8,128)S(1)}, u32[]{:S(2)}, u32[]{:S(2)}) collective-permute-start(f32[128,256]{1,0:T(8,128)S(1)} %project.1.part_ref), channel_id=1, source_target_pairs={{0,1},{1,0},{2,3},{3,2},{4,5},{5,4},{6,7},{7,6},{8,9},{9,8},{10,11... | collective-permute-start | bytes 393224 | tf_op jit(solution)/shard_map/ppermute | solution.py:313
  7.5 10.2 %collective-permute-start.2 = (f32[80,256]{1,0:T(8,128)S(1)}, f32[80,256]{1,0:T(8,128)S(1)}, u32[]{:S(2)}, u32[]{:S(2)}) collective-permute-start(f32[80,256]{1,0:T(8,128)S(1)} %get-tuple-element.11), channel_id=1, source_target_pairs={{0,8},{1,11},{2,10},{3,9},{4,12},{5,15},{6,14},{7,13},{8,0},{9,3},... | collective-permute-start | bytes 245768 | tf_op jit(solution)/shard_map/ppermute | solution.py:321
  11.5 6.1 %collective-permute-start.3 = (f32[80,256]{1,0:T(8,128)S(1)}, f32[80,256]{1,0:T(8,128)S(1)}, u32[]{:S(2)}, u32[]{:S(2)}) collective-permute-start(f32[80,256]{1,0:T(8,128)S(1)} %get-tuple-element.12), channel_id=1, source_target_pairs={{0,4},{1,7},{2,6},{3,5},{4,0},{5,3},{6,2},{7,1},{8,12},{9,15},{10,... | collective-permute-start | bytes 245768 | tf_op jit(solution)/shard_map/ppermute | solution.py:321
  13.1 6.7 %collective-permute-start.1 = (f32[80,256]{1,0:T(8,128)S(1)}, f32[80,256]{1,0:T(8,128)S(1)}, u32[]{:S(2)}, u32[]{:S(2)}) collective-permute-start(f32[80,256]{1,0:T(8,128)S(1)} %get-tuple-element.10), channel_id=1, source_target_pairs={{0,12},{1,15},{2,14},{3,13},{4,8},{5,11},{6,10},{7,9},{8,4},{9,7},... | collective-permute-start | bytes 245768 | tf_op jit(solution)/shard_map/ppermute | solution.py:321
  13.1 4.6 %collective-permute-start.4 = (f32[80,128]{1,0:T(8,128)S(1)}, f32[80,128]{1,0:T(8,128)S(1)}, u32[]{:S(2)}, u32[]{:S(2)}) collective-permute-start(f32[80,128]{1,0:T(8,128)S(1)} %get-tuple-element.13), channel_id=1, source_target_pairs={{0,2},{2,0},{4,6},{6,4},{8,10},{10,8},{12,14},{14,12},{1,3},{3,1},... | collective-permute-start | bytes 122888 | tf_op jit(solution)/shard_map/ppermute | solution.py:327
  20.2 1.7 %collective-permute-start.5 = (f32[80,1024]{1,0:T(8,128)S(1)}, f32[80,1024]{1,0:T(8,128)S(1)}, u32[]{:S(2)}, u32[]{:S(2)}) collective-permute-start(f32[80,1024]{1,0:T(8,128)S(1)} %grads.3.part_ref), channel_id=1, source_target_pairs={{0,1},{1,0},{2,3},{3,2},{4,5},{5,4},{6,7},{7,6},{8,9},{9,8},{10,11... | collective-permute-start | bytes 983048 | tf_op jit(solution)/shard_map/ppermute | solution.py:313
  22.4 3.9 %collective-permute-start.6 = (f32[40,128]{1,0:T(8,128)S(1)}, f32[40,128]{1,0:T(8,128)S(1)}, u32[]{:S(2)}, u32[]{:S(2)}) collective-permute-start(f32[40,128]{1,0:T(8,128)S(1)} %gram.1), channel_id=1, source_target_pairs={{0,4},{1,7},{2,6},{3,5},{4,0},{5,3},{6,2},{7,1},{8,12},{9,15},{10,... | collective-permute-start | bytes 61448 | tf_op jit(solution)/shard_map/ppermute | solution.py:321
  23.8 3.8 %collective-permute-start.7 = (f32[40,128]{1,0:T(8,128)S(1)}, f32[40,128]{1,0:T(8,128)S(1)}, u32[]{:S(2)}, u32[]{:S(2)}) collective-permute-start(f32[40,128]{1,0:T(8,128)S(1)} %gram.1), channel_id=1, source_target_pairs={{0,2},{2,0},{4,6},{6,4},{8,10},{10,8},{12,14},{14,12},{1,3},{3,1},... | collective-permute-start | bytes 61448 | tf_op jit(solution)/shard_map/ppermute | solution.py:327
  27.6 1.2 %collective-permute-start.8 = (f32[40,128]{1,0:T(8,128)S(1)}, f32[40,128]{1,0:T(8,128)S(1)}, u32[]{:S(2)}, u32[]{:S(2)}) collective-permute-start(f32[40,128]{1,0:T(8,128)S(1)} %select_add_fusion.x_ref), channel_id=1, source_target_pairs={{0,1},{1,0},{2,3},{3,2},{4,5},{5,4},{6,7},{7,6},{8,9},{9,8},{10,11... | collective-permute-start | bytes 61448 | tf_op jit(solution)/shard_map/ppermute | solution.py:313

commit v14 on v13

--- a/solution.py
+++ b/solution.py
@@ -59,33 +59,31 @@
         blocks = [ref[:, j].reshape(ref.shape[0] * 16, LANES) for j in range(first, first + size)]
         return jnp.concatenate(blocks, axis=1)
 
-    even = lax.broadcasted_iota(jnp.int32, (8, fold_ref.shape[0]), 1) % 16 < 8
-
-    def run(chunks):
-        total = None
-        for i in chunks:
-            _, proj_buf, _, data_buf, (first, size) = plan[i]
-            for copy in copies[i]:
-                copy.wait()
-            start(i + FLIGHT)
-            part = lax.dot_general(
-                line_up(proj_buf, first, size), line_up(data_buf, first, size), NT, preferred_element_type=jnp.float32
-            )
-            total = part if total is None else total + part
-        lines = [jnp.where(even, total[j:j + 8], total[j + 8:j + 16]) for j in range(0, total.shape[0], 16)]
-        lines = jnp.concatenate(lines, axis=0)
-        rows = lines.shape[0]
-        split = []
-        for _ in range(3):
-            split.append(lines.astype(jnp.bfloat16))
-            lines = lines - split[-1].astype(jnp.float32)
-        sums = jnp.dot(jnp.concatenate(split, axis=0), fold_ref[...], preferred_element_type=jnp.float32)
-        return sums[2 * rows:] + sums[rows:2 * rows] + sums[:rows]
-
-    grad = run(range(len(g_chunks)))
-    ranks = grad.shape[0]
-    out_ref[0:ranks, :] = grad
-    out_ref[ranks:, :] = run(range(len(g_chunks), len(plan)))
+    totals = [None, None]
+    for i, (_, proj_buf, _, data_buf, (first, size)) in enumerate(plan):
+        for copy in copies[i]:
+            copy.wait()
+        start(i + FLIGHT)
+        which = 0 if i < len(g_chunks) else 1
+        part = lax.dot_general(
+            line_up(proj_buf, first, size), line_up(data_buf, first, size), NT, preferred_element_type=jnp.float32
+        )
+        totals[which] = part if totals[which] is None else totals[which] + part
+
+    spread = totals[0].shape[1]
+    even = lax.broadcasted_iota(jnp.int32, (8, spread), 1) % 16 < 8
+    lines = []
+    for total in totals:
+        for g in range(total.shape[0] // 16):
+            lines.append(jnp.where(even, total[16 * g:16 * g + 8], total[16 * g + 8:16 * g + 16]))
+    lines = jnp.concatenate(lines, axis=0)
+    split = []
+    for _ in range(3):
+        split.append(lines.astype(jnp.bfloat16))
+        lines = lines - split[-1].astype(jnp.float32)
+    rows = out_ref.shape[0]
+    sums = jnp.dot(jnp.concatenate(split, axis=0), fold_ref[...], preferred_element_type=jnp.float32)
+    out_ref[...] = sums[2 * rows:] + sums[rows:2 * rows] + sums[:rows]
 
 
 def project(hidden, out_grad, pin_t, pout_t):
@@ -251,15 +249,23 @@
     )(part, recv)
 
 
+def reciprocal(x):
+    y = pl.reciprocal(x, approx=True)
+    for _ in range(2):
+        y = y * (2.0 - x * y)
+    return y
+
+
 def solve_kernel(docs, queries, scale, x_ref, recv_ref, out_ref, done_ref):
     total = x_ref[...] + recv_ref[...]
     stack = jnp.concatenate([total[:, :docs], total[:, docs:]], axis=0)
     cols = done_ref.shape[1]
+    diagonal = [lax.broadcasted_iota(jnp.int32, (docs, docs), i) for i in range(2)]
+    mean_diag = jnp.sum(jnp.where(diagonal[0] == diagonal[1], stack[:docs], 0.0)) * (1.0 / docs)
     stack = jnp.concatenate([stack, jnp.zeros((cols - stack.shape[0], docs), jnp.float32)], axis=0)
     total = stack.T
     row = lax.broadcasted_iota(jnp.int32, (docs, cols), 0)
     col = lax.broadcasted_iota(jnp.int32, (docs, cols), 1)
-    mean_diag = jnp.sum(jnp.where(row == col, total, 0.0)) * (1.0 / docs)
     work = total + jnp.where(row == col, 0.1 * mean_diag, 0.0)
     size = 8
     here = lax.broadcasted_iota(jnp.int32, (size, cols), 0)
@@ -269,7 +275,7 @@
         pivot, line = wide[r], rows[r]
         scale_rows = jnp.ones((size, cols), jnp.float32)
         for j in range(size):
-            inverse = 1.0 / pivot[j][j:j + 1]
+            inverse = reciprocal(pivot[j][j:j + 1])
             factor = jnp.where(here == j, 0.0, pivot[j]) * inverse
             pivot = [x if i <= j else x - factor * x[j:j + 1] for i, x in enumerate(pivot)]
             line = line - factor * line[j:j + 1]
@@ -352,10 +358,11 @@
     sizes = (rows_a, rows_b, docs, num_queries, dp, lanes)
     blocks = trade(blocks, dp) + [trade_shared(shared), own]
     gaps += [(SHARED, SHARED), (0, 0)]
-    late = min(1, len(blocks) - 3)
-    rest = [t for t in range(len(blocks)) if t != late]
-    grads = grads_of([blocks[t] for t in rest], [gaps[t] for t in rest], (), *sizes)
-    grads = grads_of([blocks[late]], [gaps[late]], (grads,), *sizes)
+    count = len(blocks) - 2
+    grads = ()
+    for part in ([count + 1, 0], [1], [count, *range(2, count)]):
+        grads = (grads_of([blocks[t] for t in part], [gaps[t] for t in part], grads, *sizes),)
+    grads = grads[0]
     share = gram(grads, swap_cores(grads), docs)
     scale = float(ranks * ranks) ** -0.5
     if docs <= 64:

time: 31.5 us -> 32.6 us (1.035)
  Pallas kernels: 10.6 us -> 11.3 us
  waiting for transfers between devices: 9.92 us -> 10.6 us
    ppermute x4, waiting for transfers between devices: 2.51 us -> 5.78 us  [trade(): got.append(lax.ppermute(x, ('dp', 'tensor'), pairs))]
    ppermute x2, waiting for transfers between devices: 4.11 us -> 1.48 us  [trade_shared(): return lax.ppermute(x, 'dp', [(i, i ^ SHARED) for i in range(dp)])]
    pallas_call x1, Pallas kernels: 2.56 us -> 3.21 us  [solve(): pl.pallas_call(functools.partial(solve_kernel, docs, queries, scale), out...]
    ppermute x2, starting transfers between devices: 2.72 us -> 2.17 us  [trade_shared(): return lax.ppermute(x, 'dp', [(i, i ^ SHARED) for i in range(dp)])]
    pallas_call x2 -> x3, Pallas kernels: 1.61 us -> 1.87 us  [grads_of(): pl.pallas_call(functools.partial(grads_kernel, rows_a, rows_b, docs, dp,...]
where the time goes in v14:
time: 32.6 us; the launch traced here: 32.4 us
  Pallas kernels  11.3 us (35%)
  waiting for transfers between devices  10.6 us (33%)
  starting transfers between devices  10.1 us (31%)
    ppermute x4, starting transfers between devices, trade(): got.append(lax.ppermute(x, ('dp', 'tensor'), pairs))  7.29 us
    ppermute x4, waiting for transfers between devices, trade(): got.append(lax.ppermute(x, ('dp', 'tensor'), pairs))  5.78 us
    pallas_call x1, Pallas kernels, project(): pl.pallas_call(functools.partial(project_kernel, g_chunks, h_chunks), out...  5.67 us
    ppermute x3, waiting for transfers between devices, swap_cores(): return lax.ppermute(x, 'tensor', [(i, cores - 1 - i) for i in range(cores)])  3.36 us
    pallas_call x1, Pallas kernels, solve(): pl.pallas_call(functools.partial(solve_kernel, docs, queries, scale), out...  3.21 us
    ppermute x2, starting transfers between devices, trade_shared(): return lax.ppermute(x, 'dp', [(i, i ^ SHARED) for i in range(dp)])  2.17 us
    pallas_call x3, Pallas kernels, grads_of(): pl.pallas_call(functools.partial(grads_kernel, rows_a, rows_b, docs, dp,...  1.87 us
    ppermute x2, waiting for transfers between devices, trade_shared(): return lax.ppermute(x, 'dp', [(i, i ^ SHARED) for i in range(dp)])  1.48 us
  transfers between devices with their start and end apart: 9, of which 7 were waited for; matrix products, arithmetic and copies ran while one was open for 1% of the time, Pallas kernels for 4%

profile of v14, /device:TPU:0, one launch (start us, length us, event | category | flops | bytes accessed | tf_op | source)
XLA Modules:
  0.0 32.4 jit_solution(7751539148666664085)
XLA Ops:
  0.0 0.0 copy-start
  0.0 0.0 copy-start.1
  0.0 5.7 %project.1.part_ref = f32[128,256]{1,0:T(8,128)S(1)} custom-call(bf16[32,56,16,128]{3,2,1,0:T(8,128)(2,1)} %bitcast.30, bf16[32,16,16,128]{3,2,1,0:T(8,128)(2,1)} %bitcast.31, bf16[8,56,16,128]{3,2,1,0:T(8,128)(2,1)} %bitcast.32, bf16[8,16,16,128]{3,2,1,0:T(8,128)(2,1)} %bitcast.33), custom_call_target="tpu_custom_call" | custom-call | flops 603979776 | bytes 11796480 | tf_op jit(solution)/shard_map/project/pallas_call | solution.py:96
  5.7 0.5 %collective-permute-start = (f32[128,256]{1,0:T(8,128)S(1)}, f32[128,256]{1,0:T(8,128)S(1)}, u32[]{:S(2)}, u32[]{:S(2)}) collective-permute-start(f32[128,256]{1,0:T(8,128)S(1)} %project.1.part_ref), channel_id=1, source_target_pairs={{0,1},{1,0},{2,3},{3,2},{4,5},{5,4},{6,7},{7,6},{8,9},{9,8},{10,11... | collective-permute-start | bytes 393224 | tf_op jit(solution)/shard_map/ppermute | solution.py:319
  6.2 0.0 copy-done
  6.2 0.2 reshape.38
  6.4 0.1 reshape.39
  6.5 0.0 copy-done.1
  6.5 0.6 %collective-permute-done.recv_ref = f32[128,256]{1,0:T(8,128)S(1)} collective-permute-done((f32[128,256]{1,0:T(8,128)S(1)}, f32[128,256]{1,0:T(8,128)S(1)}, u32[]{:S(2)}, u32[]{:S(2)}) %collective-permute-start) | collective-permute-done | bytes 131104 | tf_op jit(solution)/shard_map/ppermute | solution.py:319
  7.2 0.1 pack.1
  7.3 4.0 %collective-permute-start.4 = (f32[80,256]{1,0:T(8,128)S(1)}, f32[80,256]{1,0:T(8,128)S(1)}, u32[]{:S(2)}, u32[]{:S(2)}) collective-permute-start(f32[80,256]{1,0:T(8,128)S(1)} %get-tuple-element.14), channel_id=1, source_target_pairs={{0,8},{1,11},{2,10},{3,9},{4,12},{5,15},{6,14},{7,13},{8,0},{9,3},... | collective-permute-start | bytes 245768 | tf_op jit(solution)/shard_map/ppermute | solution.py:327
  11.3 1.4 %collective-permute-start.3 = (f32[80,256]{1,0:T(8,128)S(1)}, f32[80,256]{1,0:T(8,128)S(1)}, u32[]{:S(2)}, u32[]{:S(2)}) collective-permute-start(f32[80,256]{1,0:T(8,128)S(1)} %get-tuple-element.12), channel_id=1, source_target_pairs={{0,12},{1,15},{2,14},{3,13},{4,8},{5,11},{6,10},{7,9},{8,4},{9,7},... | collective-permute-start | bytes 245768 | tf_op jit(solution)/shard_map/ppermute | solution.py:327
  12.6 0.2 collective-permute-start.2
  12.9 1.5 %collective-permute-start.1 = (f32[80,128]{1,0:T(8,128)S(1)}, f32[80,128]{1,0:T(8,128)S(1)}, u32[]{:S(2)}, u32[]{:S(2)}) collective-permute-start(f32[80,128]{1,0:T(8,128)S(1)} %get-tuple-element.10), channel_id=1, source_target_pairs={{0,2},{2,0},{4,6},{6,4},{8,10},{10,8},{12,14},{14,12},{1,3},{3,1},... | collective-permute-start | bytes 122888 | tf_op jit(solution)/shard_map/ppermute | solution.py:333
  14.4 0.0 collective-permute-done.4.refs_1_
  14.4 0.7 %grads.3.refs_1_ = f32[80,1024]{1,0:T(8,128)S(1)} custom-call(f32[80,128]{1,0:T(8,128)S(1)} %get-tuple-element.13.refs_0_, f32[80,256]{1,0:T(8,128)S(1)} %collective-permute-done.4.refs_1_), custom_call_target="tpu_custom_call" | custom-call | flops 100663296 | bytes 98304 | tf_op jit(solution)/shard_map/grads/pallas_call | solution.py:217
  15.1 3.3 %collective-permute-done.3.refs_0_ = f32[80,256]{1,0:T(8,128)S(1)} collective-permute-done((f32[80,256]{1,0:T(8,128)S(1)}, f32[80,256]{1,0:T(8,128)S(1)}, u32[]{:S(2)}, u32[]{:S(2)}) %collective-permute-start.3) | collective-permute-done | bytes 81952 | tf_op jit(solution)/shard_map/ppermute | solution.py:327
  18.4 0.4 %grads.4.refs_2_ = f32[80,1024]{1,0:T(8,128)S(1)} custom-call(f32[80,256]{1,0:T(8,128)S(1)} %collective-permute-done.3.refs_0_, f32[80,1024]{1,0:T(8,128)S(1)} %grads.3.refs_1_), custom_call_target="tpu_custom_call" | custom-call | flops 67108864 | bytes 65536 | tf_op jit(solution)/shard_map/grads/pallas_call | solution.py:217
  18.8 0.0 collective-permute-done.1.refs_0_
  18.8 0.8 %collective-permute-done.2.refs_1_ = f32[80,256]{1,0:T(8,128)S(1)} collective-permute-done((f32[80,256]{1,0:T(8,128)S(1)}, f32[80,256]{1,0:T(8,128)S(1)}, u32[]{:S(2)}, u32[]{:S(2)}) %collective-permute-start.2) | collective-permute-done | bytes 81952 | tf_op jit(solution)/shard_map/ppermute | solution.py:327
  19.7 0.7 %grads.5.part_ref = f32[80,1024]{1,0:T(8,128)S(1)} custom-call(f32[80,128]{1,0:T(8,128)S(1)} %collective-permute-done.1.refs_0_, f32[80,256]{1,0:T(8,128)S(1)} %collective-permute-done.2.refs_1_, f32[80,1024]{1,0:T(8,128)S(1)} %grads.4.refs_2_), custom_call_target="tpu_custom_call" | custom-call | flops 100663296 | bytes 98304 | tf_op jit(solution)/shard_map/grads/pallas_call | solution.py:217
  20.4 0.2 collective-permute-start.5
  20.5 1.5 %collective-permute-done.5.recv_ref = f32[80,1024]{1,0:T(8,128)S(1)} collective-permute-done((f32[80,1024]{1,0:T(8,128)S(1)}, f32[80,1024]{1,0:T(8,128)S(1)}, u32[]{:S(2)}, u32[]{:S(2)}) %collective-permute-start.5) | collective-permute-done | bytes 327712 | tf_op jit(solution)/shard_map/ppermute | solution.py:319
  22.1 0.5 %gram.1 = f32[40,128]{1,0:T(8,128)S(1)} custom-call(f32[80,1024]{1,0:T(8,128)S(1)} %grads.5.part_ref, f32[80,1024]{1,0:T(8,128)S(1)} %collective-permute-done.5.recv_ref), custom_call_target="tpu_custom_call" | custom-call | tf_op jit(solution)/shard_map/gram/pallas_call | solution.py:242
  22.5 1.7 %collective-permute-start.6 = (f32[40,128]{1,0:T(8,128)S(1)}, f32[40,128]{1,0:T(8,128)S(1)}, u32[]{:S(2)}, u32[]{:S(2)}) collective-permute-start(f32[40,128]{1,0:T(8,128)S(1)} %gram.1), channel_id=1, source_target_pairs={{0,4},{1,7},{2,6},{3,5},{4,0},{5,3},{6,2},{7,1},{8,12},{9,15},{10,... | collective-permute-start | bytes 61448 | tf_op jit(solution)/shard_map/ppermute | solution.py:327
  24.2 0.7 %collective-permute-start.7 = (f32[40,128]{1,0:T(8,128)S(1)}, f32[40,128]{1,0:T(8,128)S(1)}, u32[]{:S(2)}, u32[]{:S(2)}) collective-permute-start(f32[40,128]{1,0:T(8,128)S(1)} %gram.1), channel_id=1, source_target_pairs={{0,2},{2,0},{4,6},{6,4},{8,10},{10,8},{12,14},{14,12},{1,3},{3,1},... | collective-permute-start | bytes 61448 | tf_op jit(solution)/shard_map/ppermute | solution.py:333
  24.9 1.7 %collective-permute-done.6 = f32[40,128]{1,0:T(8,128)S(1)} collective-permute-done((f32[40,128]{1,0:T(8,128)S(1)}, f32[40,128]{1,0:T(8,128)S(1)}, u32[]{:S(2)}, u32[]{:S(2)}) %collective-permute-start.6) | collective-permute-done | bytes 20512 | tf_op jit(solution)/shard_map/ppermute | solution.py:327
  26.5 1.5 %collective-permute-done.7 = f32[40,128]{1,0:T(8,128)S(1)} collective-permute-done((f32[40,128]{1,0:T(8,128)S(1)}, f32[40,128]{1,0:T(8,128)S(1)}, u32[]{:S(2)}, u32[]{:S(2)}) %collective-permute-start.7) | collective-permute-done | bytes 20512 | tf_op jit(solution)/shard_map/ppermute | solution.py:333
  28.0 0.0 collective-permute-start.8
  28.0 1.2 %collective-permute-done.8.recv_ref = f32[40,128]{1,0:T(8,128)S(1)} collective-permute-done((f32[40,128]{1,0:T(8,128)S(1)}, f32[40,128]{1,0:T(8,128)S(1)}, u32[]{:S(2)}, u32[]{:S(2)}) %collective-permute-start.8) | collective-permute-done | bytes 20512 | tf_op jit(solution)/shard_map/ppermute | solution.py:319
  29.2 3.2 %solve.1 = f32[8,16]{1,0:T(8,128)} custom-call(f32[40,128]{1,0:T(8,128)S(1)} %select_add_fusion.x_ref, f32[40,128]{1,0:T(8,128)S(1)} %collective-permute-done.8.recv_ref), custom_call_target="tpu_custom_call" | custom-call | tf_op jit(solution)/shard_map/solve/pallas_call | solution.py:298
  (5 shorter events, 0.0 us)
Async XLA Ops:
  0.0 6.2 %copy-start = (f32[2,4096]{1,0:T(2,128)S(1)}, f32[2,4096]{1,0:T(2,128)}, u32[]{:S(2)}) copy-start(f32[2,4096]{1,0:T(2,128)} %param.11) | copy-start | bytes 98308
  0.0 6.5 %copy-start.1 = (s32[256]{0:T(256)S(1)}, s32[256]{0:T(256)}, u32[]{:S(2)}) copy-start(s32[256]{0:T(256)} %param.10) | copy-start | bytes 3076
  5.7 1.5 %collective-permute-start = (f32[128,256]{1,0:T(8,128)S(1)}, f32[128,256]{1,0:T(8,128)S(1)}, u32[]{:S(2)}, u32[]{:S(2)}) collective-permute-start(f32[128,256]{1,0:T(8,128)S(1)} %project.1.part_ref), channel_id=1, source_target_pairs={{0,1},{1,0},{2,3},{3,2},{4,5},{5,4},{6,7},{7,6},{8,9},{9,8},{10,11... | collective-permute-start | bytes 393224 | tf_op jit(solution)/shard_map/ppermute | solution.py:319
  7.3 7.1 %collective-permute-start.4 = (f32[80,256]{1,0:T(8,128)S(1)}, f32[80,256]{1,0:T(8,128)S(1)}, u32[]{:S(2)}, u32[]{:S(2)}) collective-permute-start(f32[80,256]{1,0:T(8,128)S(1)} %get-tuple-element.14), channel_id=1, source_target_pairs={{0,8},{1,11},{2,10},{3,9},{4,12},{5,15},{6,14},{7,13},{8,0},{9,3},... | collective-permute-start | bytes 245768 | tf_op jit(solution)/shard_map/ppermute | solution.py:327
  11.3 7.1 %collective-permute-start.3 = (f32[80,256]{1,0:T(8,128)S(1)}, f32[80,256]{1,0:T(8,128)S(1)}, u32[]{:S(2)}, u32[]{:S(2)}) collective-permute-start(f32[80,256]{1,0:T(8,128)S(1)} %get-tuple-element.12), channel_id=1, source_target_pairs={{0,12},{1,15},{2,14},{3,13},{4,8},{5,11},{6,10},{7,9},{8,4},{9,7},... | collective-permute-start | bytes 245768 | tf_op jit(solution)/shard_map/ppermute | solution.py:327
  12.6 7.0 %collective-permute-start.2 = (f32[80,256]{1,0:T(8,128)S(1)}, f32[80,256]{1,0:T(8,128)S(1)}, u32[]{:S(2)}, u32[]{:S(2)}) collective-permute-start(f32[80,256]{1,0:T(8,128)S(1)} %get-tuple-element.11), channel_id=1, source_target_pairs={{0,4},{1,7},{2,6},{3,5},{4,0},{5,3},{6,2},{7,1},{8,12},{9,15},{10,... | collective-permute-start | bytes 245768 | tf_op jit(solution)/shard_map/ppermute | solution.py:327
  12.9 6.0 %collective-permute-start.1 = (f32[80,128]{1,0:T(8,128)S(1)}, f32[80,128]{1,0:T(8,128)S(1)}, u32[]{:S(2)}, u32[]{:S(2)}) collective-permute-start(f32[80,128]{1,0:T(8,128)S(1)} %get-tuple-element.10), channel_id=1, source_target_pairs={{0,2},{2,0},{4,6},{6,4},{8,10},{10,8},{12,14},{14,12},{1,3},{3,1},... | collective-permute-start | bytes 122888 | tf_op jit(solution)/shard_map/ppermute | solution.py:333
  20.4 1.7 %collective-permute-start.5 = (f32[80,1024]{1,0:T(8,128)S(1)}, f32[80,1024]{1,0:T(8,128)S(1)}, u32[]{:S(2)}, u32[]{:S(2)}) collective-permute-start(f32[80,1024]{1,0:T(8,128)S(1)} %grads.5.part_ref), channel_id=1, source_target_pairs={{0,1},{1,0},{2,3},{3,2},{4,5},{5,4},{6,7},{7,6},{8,9},{9,8},{10,11... | collective-permute-start | bytes 983048 | tf_op jit(solution)/shard_map/ppermute | solution.py:319
  22.5 4.0 %collective-permute-start.6 = (f32[40,128]{1,0:T(8,128)S(1)}, f32[40,128]{1,0:T(8,128)S(1)}, u32[]{:S(2)}, u32[]{:S(2)}) collective-permute-start(f32[40,128]{1,0:T(8,128)S(1)} %gram.1), channel_id=1, source_target_pairs={{0,4},{1,7},{2,6},{3,5},{4,0},{5,3},{6,2},{7,1},{8,12},{9,15},{10,... | collective-permute-start | bytes 61448 | tf_op jit(solution)/shard_map/ppermute | solution.py:327
  24.2 3.8 %collective-permute-start.7 = (f32[40,128]{1,0:T(8,128)S(1)}, f32[40,128]{1,0:T(8,128)S(1)}, u32[]{:S(2)}, u32[]{:S(2)}) collective-permute-start(f32[40,128]{1,0:T(8,128)S(1)} %gram.1), channel_id=1, source_target_pairs={{0,2},{2,0},{4,6},{6,4},{8,10},{10,8},{12,14},{14,12},{1,3},{3,1},... | collective-permute-start | bytes 61448 | tf_op jit(solution)/shard_map/ppermute | solution.py:333
  28.0 1.2 %collective-permute-start.8 = (f32[40,128]{1,0:T(8,128)S(1)}, f32[40,128]{1,0:T(8,128)S(1)}, u32[]{:S(2)}, u32[]{:S(2)}) collective-permute-start(f32[40,128]{1,0:T(8,128)S(1)} %select_add_fusion.x_ref), channel_id=1, source_target_pairs={{0,1},{1,0},{2,3},{3,2},{4,5},{5,4},{6,7},{7,6},{8,9},{9,8},{10,11... | collective-permute-start | bytes 61448 | tf_op jit(solution)/shard_map/ppermute | solution.py:319

commit v15 on v14

--- a/solution.py
+++ b/solution.py
@@ -30,7 +30,7 @@
 
 def chunks_of(length, ramp, tail):
     left = length - sum(ramp) - sum(tail)
-    sizes = [*ramp, *([4] * (left // 4)), *([left % 4] if left % 4 else []), *tail]
+    sizes = [*ramp, *([6] * (left // 6)), *([left % 6] if left % 6 else []), *tail]
     return [(sum(sizes[:i]), size) for i, size in enumerate(sizes)]
 
 
@@ -91,8 +91,8 @@
     width = out_grad.shape[1]
     ranks = pin_t.shape[0] + pout_t.shape[0]
     operands = [pieces(x) for x in (hidden, out_grad, pin_t, pout_t)]
-    g_chunks = chunks_of(operands[1].shape[1], (2,), ())
-    h_chunks = chunks_of(operands[0].shape[1], (), (2, 2))
+    g_chunks = chunks_of(operands[1].shape[1], (1, 2, 3, 4), ())
+    h_chunks = chunks_of(operands[0].shape[1], (), (4, 2, 2))
     return pl.pallas_call(
         functools.partial(project_kernel, g_chunks, h_chunks),
         out_shape=jax.ShapeDtypeStruct((ranks, tokens), jnp.float32),
@@ -124,37 +124,47 @@
     return jnp.where(lax.axis_index("tensor") == 0, first[t], second[t])
 
 
-def pack_kernel(dp, pb, rows_a, rows_b, part_ref, recv_ref, extra_ref, *refs):
+def pack_kernel(dp, pb, rows_a, rows_b, span, part_ref, recv_ref, extra_ref, *refs):
     outs, total_ref = refs[:-1], refs[-1]
     total_ref[...] = part_ref[...] + recv_ref[...]
-    ranks, lanes = total_ref.shape[0] // 2, total_ref.shape[1]
+    ranks = total_ref.shape[0] // 2
+    rows = rows_a + rows_b
+    owners, ids = extra_ref.shape[0], 2 * span
     me = lax.axis_index("dp")
     lead = lax.axis_index("tensor") == 0
 
-    def rows(out_ref, to, pick):
-        owner = to % extra_ref.shape[0]
+    def slices(owner):
         p, q = owner // pb, owner % pb
-        out_ref[0:rows_a, :] = pick(total_ref[pl.ds(pl.multiple_of(p * rows_a, rows_a), rows_a), :])
-        out_ref[rows_a:rows_a + rows_b, :] = pick(total_ref[pl.ds(pl.multiple_of(ranks + q * rows_b, rows_b), rows_b), :])
-        out_ref[rows_a + rows_b:, :] = pick(extra_ref[owner])
-
-    def half(x):
-        return jnp.where(lead, x[:, :lanes // 2], x[:, lanes // 2:])
+        g = total_ref[pl.ds(pl.multiple_of(p * rows_a, rows_a), rows_a), :]
+        b = total_ref[pl.ds(pl.multiple_of(ranks + q * rows_b, rows_b), rows_b), :]
+        return [(g[:, i:i + LANES], b[:, i:i + LANES]) for i in (0, LANES)]
 
     for t, out_ref in enumerate(outs[:-2]):
-        rows(out_ref, me ^ partner(dp, t), lambda x: x)
-    rows(outs[-2], me ^ SHARED, half)
-    rows(outs[-1], me, half)
+        owner = (me ^ partner(dp, t)) % owners
+        for i, (g, b) in enumerate(slices(owner)):
+            out_ref[i * rows:i * rows + rows_a, :] = g
+            out_ref[i * rows + rows_a:(i + 1) * rows, :] = b
+        out_ref[2 * rows:, :] = extra_ref[owner]
+    for out_ref, to in zip(outs[-2:], (me ^ SHARED, me)):
+        owner = to % owners
+        (g, b), (later_g, later_b) = slices(owner)
+        extra = extra_ref[owner]
+        out_ref[0:rows_a, :] = jnp.where(lead, g, later_g)
+        out_ref[rows_a:rows, :] = jnp.where(lead, b, later_b)
+        out_ref[rows:rows + span, :] = jnp.where(lead, extra[0:span], extra[span:ids])
+        rest = out_ref.shape[0] - rows - span
+        out_ref[rows + span:, :] = jnp.broadcast_to(jnp.where(lead, extra[ids:ids + 1], extra[ids + 1:ids + 2]), (rest, LANES))
 
 
 def pack(part, recv, extra, dp, pa, pb):
-    ranks, lanes = part.shape[0] // 2, part.shape[1]
+    ranks = part.shape[0] // 2
     rows_a, rows_b = ranks // pa, ranks // pb
-    rows = rows_a + rows_b + extra.shape[1]
+    rows, span = rows_a + rows_b, rows_a * rows_b // LANES
+    whole = jax.ShapeDtypeStruct((2 * rows + extra.shape[1], LANES), jnp.float32)
+    half = jax.ShapeDtypeStruct((rows + 8 * (span // 8 + 1), LANES), jnp.float32)
     count = dp // 2 - 1
-    whole, half = (jax.ShapeDtypeStruct((rows, n), jnp.float32) for n in (lanes, lanes // 2))
-    return pl.pallas_call(
-        functools.partial(pack_kernel, dp, pb, rows_a, rows_b),
+    return pl.pallas_call(
+        functools.partial(pack_kernel, dp, pb, rows_a, rows_b, span),
         out_shape=(whole,) * count + (half, half),
         in_specs=[VMEM] * 3,
         out_specs=(VMEM,) * (count + 2),
@@ -164,58 +174,51 @@
     )(part, recv, extra)
 
 
-def grads_kernel(rows_a, rows_b, docs, dp, whole, gaps, *refs):
+def grads_kernel(rows_a, rows_b, docs, dp, gaps, wholes, *refs):
     xs, before, (out_ref, outer_ref, member_ref) = refs[:len(gaps)], refs[len(gaps):-3], refs[-3:]
-    wide = rows_a * rows_b
-    first = rows_a + rows_b
+    rows, wide = rows_a + rows_b, rows_a * rows_b
+    span = wide // LANES
     queries = out_ref.shape[0] - docs
-    per = queries // dp
-    place = lax.broadcasted_iota(jnp.int32, (queries, whole), 0)
-    lane = lax.broadcasted_iota(jnp.int32, (queries, whole), 1)
+    doc = lax.broadcasted_iota(jnp.int32, (docs, LANES), 0)
+    place = lax.broadcasted_iota(jnp.int32, (queries, LANES), 0)
     me = lax.axis_index("dp")
     core = lax.axis_index("tensor")
-    mine = lane // (whole // 2) == core
-    flat = [jnp.zeros((queries, whole), jnp.float32)] * (per * wide // whole)
+    asked = [jnp.zeros((queries, LANES), jnp.float32)] * span
     start = 0
-    for x_ref, gap in zip(xs, gaps):
-        lanes = x_ref.shape[1]
-        at = slice(start, start + lanes)
-        start += lanes
-        g, b = x_ref[0:rows_a, :], x_ref[rows_a:first, :]
-        ids = x_ref[first:first + 1, :].astype(jnp.int32)
-        doc = lax.broadcasted_iota(jnp.int32, (docs, lanes), 0)
-        member_ref[:, at] = jnp.where(doc == ids, 1.0, 0.0).astype(jnp.bfloat16)
-        outer = (g[:, None, :] * b[None, :, :]).reshape(wide, lanes)
-        high = outer.astype(jnp.bfloat16)
-        outer_ref[0:wide, at] = high
-        outer_ref[wide:, at] = (outer - high.astype(jnp.float32)).astype(jnp.bfloat16)
-        held = place // per == me ^ jnp.where(core == 0, gap[0], gap[1])
-        if lanes < whole:
-            held = jnp.logical_and(held, mine)
-        for j in range(len(flat)):
-            line = x_ref[first + 1 + j:first + 2 + j, :]
-            if lanes < whole:
-                line = jnp.concatenate([line, line], axis=1)
-            flat[j] = jnp.where(held, line, flat[j])
+    for x_ref, gap, whole in zip(xs, gaps, wholes):
+        parts = 2 if whole else 1
+        base = parts * rows
+        for i in range(parts):
+            at = slice(start, start + LANES)
+            start += LANES
+            g, b = x_ref[i * rows:i * rows + rows_a, :], x_ref[i * rows + rows_a:(i + 1) * rows, :]
+            ids = base + parts * span + i
+            member_ref[:, at] = jnp.where(doc == x_ref[ids:ids + 1, :].astype(jnp.int32), 1.0, 0.0).astype(jnp.bfloat16)
+            outer = (g[:, None, :] * b[None, :, :]).reshape(wide, LANES)
+            high = outer.astype(jnp.bfloat16)
+            outer_ref[0:wide, at] = high
+            outer_ref[wide:, at] = (outer - high.astype(jnp.float32)).astype(jnp.bfloat16)
+        source = 2 * (me ^ jnp.where(core == 0, gap[0], gap[1]))
+        for i in range(parts):
+            held = place == source + (i if whole else core)
+            for j in range(span):
+                row = base + i * span + j
+                asked[j] = jnp.where(held, x_ref[row:row + 1, :], asked[j])
     sums = lax.dot_general(member_ref[...], outer_ref[...], NT, preferred_element_type=jnp.float32)
     sums = (sums[:, wide:] + sums[:, :wide]) * (TOK_DEV ** -0.5)
-    flat = jnp.concatenate(flat, axis=1)
-    asked = jnp.zeros((queries, wide), jnp.float32)
-    which = lax.broadcasted_iota(jnp.int32, (queries, wide), 0) % per
-    for q in range(per):
-        asked = jnp.where(which == q, flat[:, q * wide:(q + 1) * wide], asked)
+    asked = jnp.concatenate(asked, axis=1)
     if before:
         sums, asked = sums + before[0][0:docs, :], asked + before[0][docs:, :]
     out_ref[0:docs, :] = sums
     out_ref[docs:, :] = asked
 
 
-def grads_of(xs, gaps, before, rows_a, rows_b, docs, queries, dp, whole):
-    tokens = sum(x.shape[1] for x in xs)
+def grads_of(xs, gaps, wholes, before, rows_a, rows_b, docs, queries, dp):
+    tokens = LANES * (len(xs) + sum(wholes))
     wide = rows_a * rows_b
     operands = (*xs, *before)
     return pl.pallas_call(
-        functools.partial(grads_kernel, rows_a, rows_b, docs, dp, whole, gaps),
+        functools.partial(grads_kernel, rows_a, rows_b, docs, dp, gaps, wholes),
         out_shape=jax.ShapeDtypeStruct((docs + queries, wide), jnp.float32),
         in_specs=[VMEM] * len(operands),
         out_specs=VMEM,
@@ -247,13 +250,6 @@
         compiler_params=vmem_params(16),
         name="gram",
     )(part, recv)
-
-
-def reciprocal(x):
-    y = pl.reciprocal(x, approx=True)
-    for _ in range(2):
-        y = y * (2.0 - x * y)
-    return y
 
 
 def solve_kernel(docs, queries, scale, x_ref, recv_ref, out_ref, done_ref):
@@ -275,7 +271,7 @@
         pivot, line = wide[r], rows[r]
         scale_rows = jnp.ones((size, cols), jnp.float32)
         for j in range(size):
-            inverse = reciprocal(pivot[j][j:j + 1])
+            inverse = 1.0 / pivot[j][j:j + 1]
             factor = jnp.where(here == j, 0.0, pivot[j]) * inverse
             pivot = [x if i <= j else x - factor * x[j:j + 1] for i, x in enumerate(pivot)]
             line = line - factor * line[j:j + 1]
@@ -347,21 +343,21 @@
     part = project(hidden, out_grad, proj_in.T, proj_out.T)
     recv = swap_cores(part)
 
-    lanes = part.shape[1]
-    ids = doc_ids.astype(jnp.float32)
-    asked = queries.reshape(-1, pa, rows_a, pb, rows_b).transpose(1, 3, 0, 2, 4).reshape(owners, -1, lanes)
-    extra = jnp.concatenate([jnp.broadcast_to(ids, (owners, 1, lanes)), asked], axis=1)
+    ids = jnp.broadcast_to(doc_ids.astype(jnp.float32).reshape(2, LANES), (owners, 2, LANES))
+    asked = queries.reshape(-1, pa, rows_a, pb, rows_b).transpose(1, 3, 0, 2, 4).reshape(owners, -1, LANES)
+    extra = jnp.concatenate([asked, ids], axis=1)
     extra = jnp.pad(extra, ((0, 0), (0, -extra.shape[1] % 8), (0, 0)))
 
     *blocks, shared, own = pack(part, recv, extra, dp, pa, pb)
-    gaps = list(zip(*partners(dp)))
-    sizes = (rows_a, rows_b, docs, num_queries, dp, lanes)
     blocks = trade(blocks, dp) + [trade_shared(shared), own]
-    gaps += [(SHARED, SHARED), (0, 0)]
-    count = len(blocks) - 2
+    gaps = [*zip(*partners(dp)), (SHARED, SHARED), (0, 0)]
+    wholes = [True] * (len(blocks) - 2) + [False, False]
+    sizes = (rows_a, rows_b, docs, num_queries, dp)
+    late = min(1, len(blocks) - 3)
+    rest = [t for t in range(len(blocks)) if t != late]
     grads = ()
-    for part in ([count + 1, 0], [1], [count, *range(2, count)]):
-        grads = (grads_of([blocks[t] for t in part], [gaps[t] for t in part], grads, *sizes),)
+    for part in (rest, [late]):
+        grads = (grads_of(*([x[t] for t in part] for x in (blocks, gaps, wholes)), grads, *sizes),)
     grads = grads[0]
     share = gram(grads, swap_cores(grads), docs)
     scale = float(ranks * ranks) ** -0.5

time: 32.6 us -> 31.2 us (0.957)
  Pallas kernels: 11.3 us -> 10.4 us
  waiting for transfers between devices: 10.6 us -> 9.88 us
    ppermute x4, waiting for transfers between devices: 5.78 us -> 2.28 us  [trade(): got.append(lax.ppermute(x, ('dp', 'tensor'), pairs))]
    ppermute x2, waiting for transfers between devices: 1.48 us -> 4.27 us  [trade_shared(): return lax.ppermute(x, 'dp', [(i, i ^ SHARED) for i in range(dp)])]
    pallas_call x1, Pallas kernels: 3.21 us -> 2.46 us  [solve(): pl.pallas_call(functools.partial(solve_kernel, docs, queries, scale), out...]
    ppermute x2, starting transfers between devices: 2.17 us -> 2.64 us  [trade_shared(): return lax.ppermute(x, 'dp', [(i, i ^ SHARED) for i in range(dp)])]
    pallas_call x3 -> x2, Pallas kernels: 1.87 us -> 1.73 us  [grads_of(): pl.pallas_call(functools.partial(grads_kernel, rows_a, rows_b, docs, dp,...]
where the time goes in v15:
time: 31.2 us; the launch traced here: 31.1 us
  Pallas kernels  10.4 us (33%)
  starting transfers between devices  10.4 us (33%)
  waiting for transfers between devices  9.88 us (32%)
    ppermute x4, starting transfers between devices, trade(): got.append(lax.ppermute(x, ('dp', 'tensor'), pairs))  7.07 us
    pallas_call x1, Pallas kernels, project(): pl.pallas_call(functools.partial(project_kernel, g_chunks, h_chunks), out...  5.65 us
    ppermute x2, waiting for transfers between devices, trade_shared(): return lax.ppermute(x, 'dp', [(i, i ^ SHARED) for i in range(dp)])  4.27 us
    ppermute x3, waiting for transfers between devices, swap_cores(): return lax.ppermute(x, 'tensor', [(i, cores - 1 - i) for i in range(cores)])  3.33 us
    ppermute x2, starting transfers between devices, trade_shared(): return lax.ppermute(x, 'dp', [(i, i ^ SHARED) for i in range(dp)])  2.64 us
    pallas_call x1, Pallas kernels, solve(): pl.pallas_call(functools.partial(solve_kernel, docs, queries, scale), out...  2.46 us
    ppermute x4, waiting for transfers between devices, trade(): got.append(lax.ppermute(x, ('dp', 'tensor'), pairs))  2.28 us
    pallas_call x2, Pallas kernels, grads_of(): pl.pallas_call(functools.partial(grads_kernel, rows_a, rows_b, docs, dp,...  1.73 us
  transfers between devices with their start and end apart: 9, of which 7 were waited for; matrix products, arithmetic and copies ran while one was open for 1% of the time, Pallas kernels for 4%

profile of v15, /device:TPU:0, one launch (start us, length us, event | category | flops | bytes accessed | tf_op | source)
XLA Modules:
  0.0 31.1 jit_solution(3807975371884866252)
XLA Ops:
  0.0 0.0 copy-start.1
  0.0 0.0 copy-start
  0.0 5.7 %project.1.part_ref = f32[128,256]{1,0:T(8,128)S(1)} custom-call(bf16[32,56,16,128]{3,2,1,0:T(8,128)(2,1)} %bitcast.32, bf16[32,16,16,128]{3,2,1,0:T(8,128)(2,1)} %bitcast.33, bf16[8,56,16,128]{3,2,1,0:T(8,128)(2,1)} %bitcast.34, bf16[8,16,16,128]{3,2,1,0:T(8,128)(2,1)} %bitcast.35), custom_call_target="tpu_custom_call" | custom-call | flops 603979776 | bytes 11796480 | tf_op jit(solution)/shard_map/project/pallas_call | solution.py:96
  5.7 0.5 %collective-permute-start = (f32[128,256]{1,0:T(8,128)S(1)}, f32[128,256]{1,0:T(8,128)S(1)}, u32[]{:S(2)}, u32[]{:S(2)}) collective-permute-start(f32[128,256]{1,0:T(8,128)S(1)} %project.1.part_ref), channel_id=1, source_target_pairs={{0,1},{1,0},{2,3},{3,2},{4,5},{5,4},{6,7},{7,6},{8,9},{9,8},{10,11... | collective-permute-start | bytes 393224 | tf_op jit(solution)/shard_map/ppermute | solution.py:315
  6.2 0.0 copy-done.1
  6.2 0.0 copy-done
  6.2 0.2 reshape.41
  6.4 0.1 reshape.42
  6.5 0.7 %collective-permute-done.recv_ref = f32[128,256]{1,0:T(8,128)S(1)} collective-permute-done((f32[128,256]{1,0:T(8,128)S(1)}, f32[128,256]{1,0:T(8,128)S(1)}, u32[]{:S(2)}, u32[]{:S(2)}) %collective-permute-start) | collective-permute-done | bytes 131104 | tf_op jit(solution)/shard_map/ppermute | solution.py:315
  7.2 0.1 pack.1
  7.2 4.0 %collective-permute-start.2 = (f32[152,128]{1,0:T(8,128)S(1)}, f32[152,128]{1,0:T(8,128)S(1)}, u32[]{:S(2)}, u32[]{:S(2)}) collective-permute-start(f32[152,128]{1,0:T(8,128)S(1)} %get-tuple-element.11), channel_id=1, source_target_pairs={{0,8},{1,11},{2,10},{3,9},{4,12},{5,15},{6,14},{7,13},{8,0},{9,3},... | collective-permute-start | bytes 233480 | tf_op jit(solution)/shard_map/ppermute | solution.py:323
  11.2 1.6 %collective-permute-start.3 = (f32[152,128]{1,0:T(8,128)S(1)}, f32[152,128]{1,0:T(8,128)S(1)}, u32[]{:S(2)}, u32[]{:S(2)}) collective-permute-start(f32[152,128]{1,0:T(8,128)S(1)} %get-tuple-element.12), channel_id=1, source_target_pairs={{0,4},{1,7},{2,6},{3,5},{4,0},{5,3},{6,2},{7,1},{8,12},{9,15},{10,... | collective-permute-start | bytes 233480 | tf_op jit(solution)/shard_map/ppermute | solution.py:323
  12.8 0.0 collective-permute-start.1
  12.8 1.7 %collective-permute-start.4 = (f32[80,128]{1,0:T(8,128)S(1)}, f32[80,128]{1,0:T(8,128)S(1)}, u32[]{:S(2)}, u32[]{:S(2)}) collective-permute-start(f32[80,128]{1,0:T(8,128)S(1)} %get-tuple-element.13), channel_id=1, source_target_pairs={{0,2},{2,0},{4,6},{6,4},{8,10},{10,8},{12,14},{14,12},{1,3},{3,1},... | collective-permute-start | bytes 122888 | tf_op jit(solution)/shard_map/ppermute | solution.py:329
  14.6 2.9 %collective-permute-done.4.refs_2_ = f32[80,128]{1,0:T(8,128)S(1)} collective-permute-done((f32[80,128]{1,0:T(8,128)S(1)}, f32[80,128]{1,0:T(8,128)S(1)}, u32[]{:S(2)}, u32[]{:S(2)}) %collective-permute-start.4) | collective-permute-done | bytes 40992 | tf_op jit(solution)/shard_map/ppermute | solution.py:329
  17.5 0.0 collective-permute-done.2.refs_0_
  17.5 0.0 collective-permute-done.3.refs_1_
  17.5 1.2 %grads.2.refs_1_ = f32[80,1024]{1,0:T(8,128)S(1)} custom-call(f32[152,128]{1,0:T(8,128)S(1)} %collective-permute-done.2.refs_0_, f32[152,128]{1,0:T(8,128)S(1)} %collective-permute-done.3.refs_1_, f32[80,128]{1,0:T(8,128)S(1)} %collective-permute-done.4.refs_2_, f32[80,128]{1,0:T(8,128)S(1)} %get-tuple-element.14.refs_3_), custom_call_target="tpu_custom_call" | custom-call | flops 201326592 | bytes 196608 | tf_op jit(solution)/shard_map/grads/pallas_call | solution.py:220
  18.7 0.8 %collective-permute-done.1.refs_0_ = f32[152,128]{1,0:T(8,128)S(1)} collective-permute-done((f32[152,128]{1,0:T(8,128)S(1)}, f32[152,128]{1,0:T(8,128)S(1)}, u32[]{:S(2)}, u32[]{:S(2)}) %collective-permute-start.1) | collective-permute-done | bytes 77856 | tf_op jit(solution)/shard_map/ppermute | solution.py:323
  19.5 0.5 %grads.3.part_ref = f32[80,1024]{1,0:T(8,128)S(1)} custom-call(f32[152,128]{1,0:T(8,128)S(1)} %collective-permute-done.1.refs_0_, f32[80,1024]{1,0:T(8,128)S(1)} %grads.2.refs_1_), custom_call_target="tpu_custom_call" | custom-call | flops 67108864 | bytes 65536 | tf_op jit(solution)/shard_map/grads/pallas_call | solution.py:220
  20.0 0.2 collective-permute-start.5
  20.2 1.5 %collective-permute-done.5.recv_ref = f32[80,1024]{1,0:T(8,128)S(1)} collective-permute-done((f32[80,1024]{1,0:T(8,128)S(1)}, f32[80,1024]{1,0:T(8,128)S(1)}, u32[]{:S(2)}, u32[]{:S(2)}) %collective-permute-start.5) | collective-permute-done | bytes 327712 | tf_op jit(solution)/shard_map/ppermute | solution.py:315
  21.7 0.5 %gram.1 = f32[40,128]{1,0:T(8,128)S(1)} custom-call(f32[80,1024]{1,0:T(8,128)S(1)} %grads.3.part_ref, f32[80,1024]{1,0:T(8,128)S(1)} %collective-permute-done.5.recv_ref), custom_call_target="tpu_custom_call" | custom-call | tf_op jit(solution)/shard_map/gram/pallas_call | solution.py:245
  22.1 1.5 %collective-permute-start.6 = (f32[40,128]{1,0:T(8,128)S(1)}, f32[40,128]{1,0:T(8,128)S(1)}, u32[]{:S(2)}, u32[]{:S(2)}) collective-permute-start(f32[40,128]{1,0:T(8,128)S(1)} %gram.1), channel_id=1, source_target_pairs={{0,4},{1,7},{2,6},{3,5},{4,0},{5,3},{6,2},{7,1},{8,12},{9,15},{10,... | collective-permute-start | bytes 61448 | tf_op jit(solution)/shard_map/ppermute | solution.py:323
  23.6 0.9 %collective-permute-start.7 = (f32[40,128]{1,0:T(8,128)S(1)}, f32[40,128]{1,0:T(8,128)S(1)}, u32[]{:S(2)}, u32[]{:S(2)}) collective-permute-start(f32[40,128]{1,0:T(8,128)S(1)} %gram.1), channel_id=1, source_target_pairs={{0,2},{2,0},{4,6},{6,4},{8,10},{10,8},{12,14},{14,12},{1,3},{3,1},... | collective-permute-start | bytes 61448 | tf_op jit(solution)/shard_map/ppermute | solution.py:329
  24.5 1.5 %collective-permute-done.6 = f32[40,128]{1,0:T(8,128)S(1)} collective-permute-done((f32[40,128]{1,0:T(8,128)S(1)}, f32[40,128]{1,0:T(8,128)S(1)}, u32[]{:S(2)}, u32[]{:S(2)}) %collective-permute-start.6) | collective-permute-done | bytes 20512 | tf_op jit(solution)/shard_map/ppermute | solution.py:323
  26.0 1.4 %collective-permute-done.7 = f32[40,128]{1,0:T(8,128)S(1)} collective-permute-done((f32[40,128]{1,0:T(8,128)S(1)}, f32[40,128]{1,0:T(8,128)S(1)}, u32[]{:S(2)}, u32[]{:S(2)}) %collective-permute-start.7) | collective-permute-done | bytes 20512 | tf_op jit(solution)/shard_map/ppermute | solution.py:329
  27.4 0.0 collective-permute-start.8
  27.4 1.2 %collective-permute-done.8.recv_ref = f32[40,128]{1,0:T(8,128)S(1)} collective-permute-done((f32[40,128]{1,0:T(8,128)S(1)}, f32[40,128]{1,0:T(8,128)S(1)}, u32[]{:S(2)}, u32[]{:S(2)}) %collective-permute-start.8) | collective-permute-done | bytes 20512 | tf_op jit(solution)/shard_map/ppermute | solution.py:315
  28.6 2.5 %solve.1 = f32[8,16]{1,0:T(8,128)} custom-call(f32[40,128]{1,0:T(8,128)S(1)} %select_add_fusion.x_ref, f32[40,128]{1,0:T(8,128)S(1)} %collective-permute-done.8.recv_ref), custom_call_target="tpu_custom_call" | custom-call | tf_op jit(solution)/shard_map/solve/pallas_call | solution.py:294
  (5 shorter events, 0.0 us)
Async XLA Ops:
  0.0 6.2 %copy-start.1 = (s32[256]{0:T(256)S(1)}, s32[256]{0:T(256)}, u32[]{:S(2)}) copy-start(s32[256]{0:T(256)} %param.10) | copy-start | bytes 3076
  0.0 6.2 %copy-start = (f32[2,4096]{1,0:T(2,128)S(1)}, f32[2,4096]{1,0:T(2,128)}, u32[]{:S(2)}) copy-start(f32[2,4096]{1,0:T(2,128)} %param.11) | copy-start | bytes 98308
  5.7 1.5 %collective-permute-start = (f32[128,256]{1,0:T(8,128)S(1)}, f32[128,256]{1,0:T(8,128)S(1)}, u32[]{:S(2)}, u32[]{:S(2)}) collective-permute-start(f32[128,256]{1,0:T(8,128)S(1)} %project.1.part_ref), channel_id=1, source_target_pairs={{0,1},{1,0},{2,3},{3,2},{4,5},{5,4},{6,7},{7,6},{8,9},{9,8},{10,11... | collective-permute-start | bytes 393224 | tf_op jit(solution)/shard_map/ppermute | solution.py:315
  7.2 10.2 %collective-permute-start.2 = (f32[152,128]{1,0:T(8,128)S(1)}, f32[152,128]{1,0:T(8,128)S(1)}, u32[]{:S(2)}, u32[]{:S(2)}) collective-permute-start(f32[152,128]{1,0:T(8,128)S(1)} %get-tuple-element.11), channel_id=1, source_target_pairs={{0,8},{1,11},{2,10},{3,9},{4,12},{5,15},{6,14},{7,13},{8,0},{9,3},... | collective-permute-start | bytes 233480 | tf_op jit(solution)/shard_map/ppermute | solution.py:323
  11.2 6.2 %collective-permute-start.3 = (f32[152,128]{1,0:T(8,128)S(1)}, f32[152,128]{1,0:T(8,128)S(1)}, u32[]{:S(2)}, u32[]{:S(2)}) collective-permute-start(f32[152,128]{1,0:T(8,128)S(1)} %get-tuple-element.12), channel_id=1, source_target_pairs={{0,4},{1,7},{2,6},{3,5},{4,0},{5,3},{6,2},{7,1},{8,12},{9,15},{10,... | collective-permute-start | bytes 233480 | tf_op jit(solution)/shard_map/ppermute | solution.py:323
  12.8 6.6 %collective-permute-start.1 = (f32[152,128]{1,0:T(8,128)S(1)}, f32[152,128]{1,0:T(8,128)S(1)}, u32[]{:S(2)}, u32[]{:S(2)}) collective-permute-start(f32[152,128]{1,0:T(8,128)S(1)} %get-tuple-element.10), channel_id=1, source_target_pairs={{0,12},{1,15},{2,14},{3,13},{4,8},{5,11},{6,10},{7,9},{8,4},{9,7},... | collective-permute-start | bytes 233480 | tf_op jit(solution)/shard_map/ppermute | solution.py:323
  12.8 4.6 %collective-permute-start.4 = (f32[80,128]{1,0:T(8,128)S(1)}, f32[80,128]{1,0:T(8,128)S(1)}, u32[]{:S(2)}, u32[]{:S(2)}) collective-permute-start(f32[80,128]{1,0:T(8,128)S(1)} %get-tuple-element.13), channel_id=1, source_target_pairs={{0,2},{2,0},{4,6},{6,4},{8,10},{10,8},{12,14},{14,12},{1,3},{3,1},... | collective-permute-start | bytes 122888 | tf_op jit(solution)/shard_map/ppermute | solution.py:329
  20.0 1.7 %collective-permute-start.5 = (f32[80,1024]{1,0:T(8,128)S(1)}, f32[80,1024]{1,0:T(8,128)S(1)}, u32[]{:S(2)}, u32[]{:S(2)}) collective-permute-start(f32[80,1024]{1,0:T(8,128)S(1)} %grads.3.part_ref), channel_id=1, source_target_pairs={{0,1},{1,0},{2,3},{3,2},{4,5},{5,4},{6,7},{7,6},{8,9},{9,8},{10,11... | collective-permute-start | bytes 983048 | tf_op jit(solution)/shard_map/ppermute | solution.py:315
  22.1 3.9 %collective-permute-start.6 = (f32[40,128]{1,0:T(8,128)S(1)}, f32[40,128]{1,0:T(8,128)S(1)}, u32[]{:S(2)}, u32[]{:S(2)}) collective-permute-start(f32[40,128]{1,0:T(8,128)S(1)} %gram.1), channel_id=1, source_target_pairs={{0,4},{1,7},{2,6},{3,5},{4,0},{5,3},{6,2},{7,1},{8,12},{9,15},{10,... | collective-permute-start | bytes 61448 | tf_op jit(solution)/shard_map/ppermute | solution.py:323
  23.6 3.8 %collective-permute-start.7 = (f32[40,128]{1,0:T(8,128)S(1)}, f32[40,128]{1,0:T(8,128)S(1)}, u32[]{:S(2)}, u32[]{:S(2)}) collective-permute-start(f32[40,128]{1,0:T(8,128)S(1)} %gram.1), channel_id=1, source_target_pairs={{0,2},{2,0},{4,6},{6,4},{8,10},{10,8},{12,14},{14,12},{1,3},{3,1},... | collective-permute-start | bytes 61448 | tf_op jit(solution)/shard_map/ppermute | solution.py:329
  27.4 1.2 %collective-permute-start.8 = (f32[40,128]{1,0:T(8,128)S(1)}, f32[40,128]{1,0:T(8,128)S(1)}, u32[]{:S(2)}, u32[]{:S(2)}) collective-permute-start(f32[40,128]{1,0:T(8,128)S(1)} %select_add_fusion.x_ref), channel_id=1, source_target_pairs={{0,1},{1,0},{2,3},{3,2},{4,5},{5,4},{6,7},{7,6},{8,9},{9,8},{10,11... | collective-permute-start | bytes 61448 | tf_op jit(solution)/shard_map/ppermute | solution.py:315

commit v16 on v15

--- a/solution.py
+++ b/solution.py
@@ -34,7 +34,7 @@
     return [(sum(sizes[:i]), size) for i, size in enumerate(sizes)]
 
 
-def project_kernel(g_chunks, h_chunks, h_ref, g_ref, pin_ref, pout_ref, out_ref, h_buf, g_buf, pin_buf, pout_buf, fold_ref, sems):
+def project_kernel(g_chunks, h_chunks, h_ref, g_ref, pin_ref, pout_ref, out_ref, h_buf, g_buf, pin_buf, pout_buf, sems):
     plan = [(pout_ref, pout_buf, g_ref, g_buf, at) for at in g_chunks] + [(pin_ref, pin_buf, h_ref, h_buf, at) for at in h_chunks]
     copies = []
     for i, (proj, proj_buf, data, data_buf, (start, size)) in enumerate(plan):
@@ -51,9 +51,6 @@
 
     for i in range(FLIGHT):
         start(i)
-    lane = lax.broadcasted_iota(jnp.int32, fold_ref.shape, 0)
-    token = lax.broadcasted_iota(jnp.int32, fold_ref.shape, 1)
-    fold_ref[...] = jnp.where(lane // 16 * 8 + lane % 8 == token, 1.0, 0.0).astype(jnp.bfloat16)
 
     def line_up(ref, first, size):
         blocks = [ref[:, j].reshape(ref.shape[0] * 16, LANES) for j in range(first, first + size)]
@@ -66,24 +63,18 @@
         start(i + FLIGHT)
         which = 0 if i < len(g_chunks) else 1
         part = lax.dot_general(
-            line_up(proj_buf, first, size), line_up(data_buf, first, size), NT, preferred_element_type=jnp.float32
+            line_up(data_buf, first, size), line_up(proj_buf, first, size), NT, preferred_element_type=jnp.float32
         )
         totals[which] = part if totals[which] is None else totals[which] + part
 
-    spread = totals[0].shape[1]
-    even = lax.broadcasted_iota(jnp.int32, (8, spread), 1) % 16 < 8
-    lines = []
+    even = lax.broadcasted_iota(jnp.int32, (8, totals[0].shape[1]), 1) % 16 < 8
+    done = 0
     for total in totals:
-        for g in range(total.shape[0] // 16):
-            lines.append(jnp.where(even, total[16 * g:16 * g + 8], total[16 * g + 8:16 * g + 16]))
-    lines = jnp.concatenate(lines, axis=0)
-    split = []
-    for _ in range(3):
-        split.append(lines.astype(jnp.bfloat16))
-        lines = lines - split[-1].astype(jnp.float32)
-    rows = out_ref.shape[0]
-    sums = jnp.dot(jnp.concatenate(split, axis=0), fold_ref[...], preferred_element_type=jnp.float32)
-    out_ref[...] = sums[2 * rows:] + sums[rows:2 * rows] + sums[:rows]
+        lines = [jnp.where(even, total[j:j + 8], total[j + 8:j + 16]) for j in range(0, total.shape[0], 16)]
+        lines = jnp.concatenate(lines, axis=0).T
+        for j in range(0, lines.shape[0], 16):
+            out_ref[done:done + 8, :] = lines[j:j + 8] + lines[j + 8:j + 16]
+            done += 8
 
 
 def project(hidden, out_grad, pin_t, pout_t):
@@ -99,7 +90,7 @@
         in_specs=[HBM] * 4,
         out_specs=VMEM,
         scratch_shapes=[pltpu.VMEM(x.shape, x.dtype) for x in operands]
-        + [pltpu.VMEM((2 * tokens, tokens), jnp.bfloat16), pltpu.SemaphoreType.DMA((2 * len(g_chunks + h_chunks),))],
+        + [pltpu.SemaphoreType.DMA((2 * len(g_chunks + h_chunks),))],
         compiler_params=vmem_params(53.5),
         cost_estimate=pl.CostEstimate(
             flops=2 * tokens * 64 * (units + width),
@@ -252,8 +243,11 @@
     )(part, recv)
 
 
-def solve_kernel(docs, queries, scale, x_ref, recv_ref, out_ref, done_ref):
-    total = x_ref[...] + recv_ref[...]
+def solve_kernel(docs, queries, scale, *refs):
+    xs, out_ref, done_ref = [x_ref[...] for x_ref in refs[:-2]], refs[-2], refs[-1]
+    while len(xs) > 1:
+        xs = [x + y for x, y in zip(xs[0::2], xs[1::2])]
+    total = xs[0]
     stack = jnp.concatenate([total[:, :docs], total[:, docs:]], axis=0)
     cols = done_ref.shape[1]
     diagonal = [lax.broadcasted_iota(jnp.int32, (docs, docs), i) for i in range(2)]
@@ -290,16 +284,16 @@
     out_ref[...] = done_ref[mine, :][:, docs:docs + queries]
 
 
-def solve(x, recv, docs, queries, scale):
+def solve(xs, docs, queries, scale):
     return pl.pallas_call(
         functools.partial(solve_kernel, docs, queries, scale),
         out_shape=jax.ShapeDtypeStruct((DOC_DEV, queries), jnp.float32),
-        in_specs=[VMEM] * 2,
+        in_specs=[VMEM] * len(xs),
         out_specs=VMEM,
         scratch_shapes=[pltpu.VMEM((docs, -(-(docs + queries) // LANES) * LANES), jnp.float32)],
         compiler_params=vmem_params(16),
         name="solve",
-    )(x, recv)
+    )(*xs)
 
 
 def solve_large(total, docs, queries, scale):
@@ -315,10 +309,10 @@
     return lax.ppermute(x, "tensor", [(i, cores - 1 - i) for i in range(cores)])
 
 
-def trade(xs, group):
+def trade(xs):
     dp = lax.axis_size("dp")
     got = []
-    for x, ms in zip(xs, zip(*partners(group))):
+    for x, ms in zip(xs, zip(*partners(dp))):
         pairs = [(i * 2 + k, (i ^ m) * 2 + k) for i in range(dp) for k, m in enumerate(ms)]
         got.append(lax.ppermute(x, ("dp", "tensor"), pairs))
     return got
@@ -349,7 +343,7 @@
     extra = jnp.pad(extra, ((0, 0), (0, -extra.shape[1] % 8), (0, 0)))
 
     *blocks, shared, own = pack(part, recv, extra, dp, pa, pb)
-    blocks = trade(blocks, dp) + [trade_shared(shared), own]
+    blocks = trade(blocks) + [trade_shared(shared), own]
     gaps = [*zip(*partners(dp)), (SHARED, SHARED), (0, 0)]
     wholes = [True] * (len(blocks) - 2) + [False, False]
     sizes = (rows_a, rows_b, docs, num_queries, dp)
@@ -362,9 +356,8 @@
     share = gram(grads, swap_cores(grads), docs)
     scale = float(ranks * ranks) ** -0.5
     if docs <= 64:
-        others = sum(trade([share] * (owners // 2 - 1), owners))
-        share = others + jnp.where(lax.axis_index("tensor") == 0, share, trade_shared(share))
-        return solve(share, swap_cores(share), docs, num_queries, scale).T
+        others = [lax.ppermute(share, "dp", [(i, i ^ m) for i in range(dp)]) for m in range(owners - 1, 0, -1)]
+        return solve([share] + others, docs, num_queries, scale).T
     share = lax.psum(share, "dp") * (owners / dp)
     return solve_large(jnp.concatenate([share[:, :docs], share[:, docs:]], axis=0).T, docs, num_queries, scale).T
 

time: 31.2 us -> 33.5 us (1.074)
  Pallas kernels: 10.4 us -> 12.1 us
  starting transfers between devices: 10.4 us -> 11.6 us
  waiting for transfers between devices: 9.88 us -> 9.35 us
    ppermute x0 -> x3, waiting for transfers between devices: none -> 3.56 us  [local(): lax.ppermute(share, 'dp', [(i, i ^ m) for i in range(dp)])]
    ppermute x0 -> x3, starting transfers between devices: none -> 3.51 us  [local(): lax.ppermute(share, 'dp', [(i, i ^ m) for i in range(dp)])]
    pallas_call x1, Pallas kernels: 5.65 us -> 7.33 us  [project(): pl.pallas_call(functools.partial(project_kernel, g_chunks, h_chunks), out...]
    ppermute x4 -> x3, waiting for transfers between devices: 2.28 us -> 0.74 us  [trade(): got.append(lax.ppermute(x, ('dp', 'tensor'), pairs))]
    ppermute x4 -> x3, starting transfers between devices: 7.07 us -> 5.59 us  [trade(): got.append(lax.ppermute(x, ('dp', 'tensor'), pairs))]
    ppermute x2 -> x1, waiting for transfers between devices: 4.27 us -> 2.91 us  [trade_shared(): return lax.ppermute(x, 'dp', [(i, i ^ SHARED) for i in range(dp)])]
    ppermute x3 -> x2, waiting for transfers between devices: 3.33 us -> 2.14 us  [swap_cores(): return lax.ppermute(x, 'tensor', [(i, cores - 1 - i) for i in range(cores)])]
    ppermute x2 -> x1, starting transfers between devices: 2.64 us -> 1.74 us  [trade_shared(): return lax.ppermute(x, 'dp', [(i, i ^ SHARED) for i in range(dp)])]
where the time goes in v16:
time: 33.5 us; the launch traced here: 33.4 us
  Pallas kernels  12.1 us (36%)
  starting transfers between devices  11.6 us (35%)
  waiting for transfers between devices  9.35 us (28%)
    pallas_call x1, Pallas kernels, project(): pl.pallas_call(functools.partial(project_kernel, g_chunks, h_chunks), out...  7.33 us
    ppermute x3, starting transfers between devices, trade(): got.append(lax.ppermute(x, ('dp', 'tensor'), pairs))  5.59 us
    ppermute x3, waiting for transfers between devices, local(): lax.ppermute(share, 'dp', [(i, i ^ m) for i in range(dp)])  3.56 us
    ppermute x3, starting transfers between devices, local(): lax.ppermute(share, 'dp', [(i, i ^ m) for i in range(dp)])  3.51 us
    ppermute x1, waiting for transfers between devices, trade_shared(): return lax.ppermute(x, 'dp', [(i, i ^ SHARED) for i in range(dp)])  2.91 us
    pallas_call x1, Pallas kernels, solve(): pl.pallas_call(functools.partial(solve_kernel, docs, queries, scale), out...  2.46 us
    ppermute x2, waiting for transfers between devices, swap_cores(): return lax.ppermute(x, 'tensor', [(i, cores - 1 - i) for i in range(cores)])  2.14 us
    ppermute x1, starting transfers between devices, trade_shared(): return lax.ppermute(x, 'dp', [(i, i ^ SHARED) for i in range(dp)])  1.74 us
  transfers between devices with their start and end apart: 9, of which 7 were waited for; matrix products, arithmetic and copies ran while one was open for 1% of the time, Pallas kernels for 4%

profile of v16, /device:TPU:0, one launch (start us, length us, event | category | flops | bytes accessed | tf_op | source)
XLA Modules:
  0.0 33.4 jit_solution(9885651881353420522)
XLA Ops:
  0.0 0.0 copy-start.1
  0.0 0.0 copy-start
  0.0 7.3 %project.1.part_ref = f32[128,256]{1,0:T(8,128)S(1)} custom-call(bf16[32,56,16,128]{3,2,1,0:T(8,128)(2,1)} %bitcast.32, bf16[32,16,16,128]{3,2,1,0:T(8,128)(2,1)} %bitcast.33, bf16[8,56,16,128]{3,2,1,0:T(8,128)(2,1)} %bitcast.34, bf16[8,16,16,128]{3,2,1,0:T(8,128)(2,1)} %bitcast.35), custom_call_target="tpu_custom_call" | custom-call | flops 603979776 | bytes 11796480 | tf_op jit(solution)/shard_map/project/pallas_call | solution.py:87
  7.3 0.5 %collective-permute-start = (f32[128,256]{1,0:T(8,128)S(1)}, f32[128,256]{1,0:T(8,128)S(1)}, u32[]{:S(2)}, u32[]{:S(2)}) collective-permute-start(f32[128,256]{1,0:T(8,128)S(1)} %project.1.part_ref), channel_id=1, source_target_pairs={{0,1},{1,0},{2,3},{3,2},{4,5},{5,4},{6,7},{7,6},{8,9},{9,8},{10,11... | collective-permute-start | bytes 393224 | tf_op jit(solution)/shard_map/ppermute | solution.py:309
  7.9 0.0 copy-done.1
  7.9 0.0 copy-done
  7.9 0.2 reshape.41
  8.1 0.1 reshape.42
  8.2 0.7 %collective-permute-done.recv_ref = f32[128,256]{1,0:T(8,128)S(1)} collective-permute-done((f32[128,256]{1,0:T(8,128)S(1)}, f32[128,256]{1,0:T(8,128)S(1)}, u32[]{:S(2)}, u32[]{:S(2)}) %collective-permute-start) | collective-permute-done | bytes 131104 | tf_op jit(solution)/shard_map/ppermute | solution.py:309
  8.8 0.1 pack.1
  8.9 4.0 %collective-permute-start.2 = (f32[152,128]{1,0:T(8,128)S(1)}, f32[152,128]{1,0:T(8,128)S(1)}, u32[]{:S(2)}, u32[]{:S(2)}) collective-permute-start(f32[152,128]{1,0:T(8,128)S(1)} %get-tuple-element.11), channel_id=1, source_target_pairs={{0,8},{1,11},{2,10},{3,9},{4,12},{5,15},{6,14},{7,13},{8,0},{9,3},... | collective-permute-start | bytes 233480 | tf_op jit(solution)/shard_map/ppermute | solution.py:317
  12.9 1.6 %collective-permute-start.3 = (f32[152,128]{1,0:T(8,128)S(1)}, f32[152,128]{1,0:T(8,128)S(1)}, u32[]{:S(2)}, u32[]{:S(2)}) collective-permute-start(f32[152,128]{1,0:T(8,128)S(1)} %get-tuple-element.12), channel_id=1, source_target_pairs={{0,4},{1,7},{2,6},{3,5},{4,0},{5,3},{6,2},{7,1},{8,12},{9,15},{10,... | collective-permute-start | bytes 233480 | tf_op jit(solution)/shard_map/ppermute | solution.py:317
  14.5 0.0 collective-permute-start.1
  14.5 1.7 %collective-permute-start.4 = (f32[80,128]{1,0:T(8,128)S(1)}, f32[80,128]{1,0:T(8,128)S(1)}, u32[]{:S(2)}, u32[]{:S(2)}) collective-permute-start(f32[80,128]{1,0:T(8,128)S(1)} %get-tuple-element.13), channel_id=1, source_target_pairs={{0,2},{2,0},{4,6},{6,4},{8,10},{10,8},{12,14},{14,12},{1,3},{3,1},... | collective-permute-start | bytes 122888 | tf_op jit(solution)/shard_map/ppermute | solution.py:323
  16.3 2.9 %collective-permute-done.4.refs_2_ = f32[80,128]{1,0:T(8,128)S(1)} collective-permute-done((f32[80,128]{1,0:T(8,128)S(1)}, f32[80,128]{1,0:T(8,128)S(1)}, u32[]{:S(2)}, u32[]{:S(2)}) %collective-permute-start.4) | collective-permute-done | bytes 40992 | tf_op jit(solution)/shard_map/ppermute | solution.py:323
  19.2 0.0 collective-permute-done.2.refs_0_
  19.2 0.0 collective-permute-done.3.refs_1_
  19.2 1.2 %grads.2.refs_1_ = f32[80,1024]{1,0:T(8,128)S(1)} custom-call(f32[152,128]{1,0:T(8,128)S(1)} %collective-permute-done.2.refs_0_, f32[152,128]{1,0:T(8,128)S(1)} %collective-permute-done.3.refs_1_, f32[80,128]{1,0:T(8,128)S(1)} %collective-permute-done.4.refs_2_, f32[80,128]{1,0:T(8,128)S(1)} %get-tuple-element.14.refs_3_), custom_call_target="tpu_custom_call" | custom-call | flops 201326592 | bytes 196608 | tf_op jit(solution)/shard_map/grads/pallas_call | solution.py:211
  20.4 0.7 %collective-permute-done.1.refs_0_ = f32[152,128]{1,0:T(8,128)S(1)} collective-permute-done((f32[152,128]{1,0:T(8,128)S(1)}, f32[152,128]{1,0:T(8,128)S(1)}, u32[]{:S(2)}, u32[]{:S(2)}) %collective-permute-start.1) | collective-permute-done | bytes 77856 | tf_op jit(solution)/shard_map/ppermute | solution.py:317
  21.1 0.5 %grads.3.part_ref = f32[80,1024]{1,0:T(8,128)S(1)} custom-call(f32[152,128]{1,0:T(8,128)S(1)} %collective-permute-done.1.refs_0_, f32[80,1024]{1,0:T(8,128)S(1)} %grads.2.refs_1_), custom_call_target="tpu_custom_call" | custom-call | flops 67108864 | bytes 65536 | tf_op jit(solution)/shard_map/grads/pallas_call | solution.py:211
  21.6 0.2 collective-permute-start.5
  21.9 1.5 %collective-permute-done.5.recv_ref = f32[80,1024]{1,0:T(8,128)S(1)} collective-permute-done((f32[80,1024]{1,0:T(8,128)S(1)}, f32[80,1024]{1,0:T(8,128)S(1)}, u32[]{:S(2)}, u32[]{:S(2)}) %collective-permute-start.5) | collective-permute-done | bytes 327712 | tf_op jit(solution)/shard_map/ppermute | solution.py:309
  23.3 0.5 %gram.1.refs_0_ = f32[40,128]{1,0:T(8,128)S(1)} custom-call(f32[80,1024]{1,0:T(8,128)S(1)} %grads.3.part_ref, f32[80,1024]{1,0:T(8,128)S(1)} %collective-permute-done.5.recv_ref), custom_call_target="tpu_custom_call" | custom-call | tf_op jit(solution)/shard_map/gram/pallas_call | solution.py:236
  23.8 1.4 %collective-permute-start.8 = (f32[40,128]{1,0:T(8,128)S(1)}, f32[40,128]{1,0:T(8,128)S(1)}, u32[]{:S(2)}, u32[]{:S(2)}) collective-permute-start(f32[40,128]{1,0:T(8,128)S(1)} %gram.1.refs_0_), channel_id=1, source_target_pairs={{0,2},{2,0},{4,6},{6,4},{8,10},{10,8},{12,14},{14,12},{1,3},{3,1},... | collective-permute-start | bytes 61448 | tf_op jit(solution)/shard_map/ppermute | solution.py:359
  25.2 1.0 %collective-permute-start.7 = (f32[40,128]{1,0:T(8,128)S(1)}, f32[40,128]{1,0:T(8,128)S(1)}, u32[]{:S(2)}, u32[]{:S(2)}) collective-permute-start(f32[40,128]{1,0:T(8,128)S(1)} %gram.1.refs_0_), channel_id=1, source_target_pairs={{0,4},{2,6},{4,0},{6,2},{8,12},{10,14},{12,8},{14,10},{1,5},{3,7},... | collective-permute-start | bytes 61448 | tf_op jit(solution)/shard_map/ppermute | solution.py:359
  26.2 1.1 %collective-permute-start.6 = (f32[40,128]{1,0:T(8,128)S(1)}, f32[40,128]{1,0:T(8,128)S(1)}, u32[]{:S(2)}, u32[]{:S(2)}) collective-permute-start(f32[40,128]{1,0:T(8,128)S(1)} %gram.1.refs_0_), channel_id=1, source_target_pairs={{0,6},{2,4},{4,2},{6,0},{8,14},{10,12},{12,10},{14,8},{1,7},{3,5},... | collective-permute-start | bytes 61448 | tf_op jit(solution)/shard_map/ppermute | solution.py:359
  27.3 0.3 collective-permute-done.8.refs_3_
  27.6 1.5 %collective-permute-done.7.refs_2_ = f32[40,128]{1,0:T(8,128)S(1)} collective-permute-done((f32[40,128]{1,0:T(8,128)S(1)}, f32[40,128]{1,0:T(8,128)S(1)}, u32[]{:S(2)}, u32[]{:S(2)}) %collective-permute-start.7) | collective-permute-done | bytes 20512 | tf_op jit(solution)/shard_map/ppermute | solution.py:359
  29.1 1.8 %collective-permute-done.6.refs_1_ = f32[40,128]{1,0:T(8,128)S(1)} collective-permute-done((f32[40,128]{1,0:T(8,128)S(1)}, f32[40,128]{1,0:T(8,128)S(1)}, u32[]{:S(2)}, u32[]{:S(2)}) %collective-permute-start.6) | collective-permute-done | bytes 20512 | tf_op jit(solution)/shard_map/ppermute | solution.py:359
  30.9 2.5 %solve.1 = f32[8,16]{1,0:T(8,128)} custom-call(f32[40,128]{1,0:T(8,128)S(1)} %gram.1.refs_0_, f32[40,128]{1,0:T(8,128)S(1)} %collective-permute-done.6.refs_1_, f32[40,128]{1,0:T(8,128)S(1)} %collective-permute-done.7.refs_2_, f32[40,128]{1,0:T(8,128)S(1)} %collective-permute-done.8.refs_3_), custom_call_target="tpu_custom_call" | custom-call | tf_op jit(solution)/shard_map/solve/pallas_call | solution.py:288
  (4 shorter events, 0.0 us)
Async XLA Ops:
  0.0 7.9 %copy-start.1 = (s32[256]{0:T(256)S(1)}, s32[256]{0:T(256)}, u32[]{:S(2)}) copy-start(s32[256]{0:T(256)} %param.10) | copy-start | bytes 3076
  0.0 7.9 %copy-start = (f32[2,4096]{1,0:T(2,128)S(1)}, f32[2,4096]{1,0:T(2,128)}, u32[]{:S(2)}) copy-start(f32[2,4096]{1,0:T(2,128)} %param.11) | copy-start | bytes 98308
  7.3 1.5 %collective-permute-start = (f32[128,256]{1,0:T(8,128)S(1)}, f32[128,256]{1,0:T(8,128)S(1)}, u32[]{:S(2)}, u32[]{:S(2)}) collective-permute-start(f32[128,256]{1,0:T(8,128)S(1)} %project.1.part_ref), channel_id=1, source_target_pairs={{0,1},{1,0},{2,3},{3,2},{4,5},{5,4},{6,7},{7,6},{8,9},{9,8},{10,11... | collective-permute-start | bytes 393224 | tf_op jit(solution)/shard_map/ppermute | solution.py:309
  8.9 10.2 %collective-permute-start.2 = (f32[152,128]{1,0:T(8,128)S(1)}, f32[152,128]{1,0:T(8,128)S(1)}, u32[]{:S(2)}, u32[]{:S(2)}) collective-permute-start(f32[152,128]{1,0:T(8,128)S(1)} %get-tuple-element.11), channel_id=1, source_target_pairs={{0,8},{1,11},{2,10},{3,9},{4,12},{5,15},{6,14},{7,13},{8,0},{9,3},... | collective-permute-start | bytes 233480 | tf_op jit(solution)/shard_map/ppermute | solution.py:317
  12.9 6.2 %collective-permute-start.3 = (f32[152,128]{1,0:T(8,128)S(1)}, f32[152,128]{1,0:T(8,128)S(1)}, u32[]{:S(2)}, u32[]{:S(2)}) collective-permute-start(f32[152,128]{1,0:T(8,128)S(1)} %get-tuple-element.12), channel_id=1, source_target_pairs={{0,4},{1,7},{2,6},{3,5},{4,0},{5,3},{6,2},{7,1},{8,12},{9,15},{10,... | collective-permute-start | bytes 233480 | tf_op jit(solution)/shard_map/ppermute | solution.py:317
  14.5 6.6 %collective-permute-start.1 = (f32[152,128]{1,0:T(8,128)S(1)}, f32[152,128]{1,0:T(8,128)S(1)}, u32[]{:S(2)}, u32[]{:S(2)}) collective-permute-start(f32[152,128]{1,0:T(8,128)S(1)} %get-tuple-element.10), channel_id=1, source_target_pairs={{0,12},{1,15},{2,14},{3,13},{4,8},{5,11},{6,10},{7,9},{8,4},{9,7},... | collective-permute-start | bytes 233480 | tf_op jit(solution)/shard_map/ppermute | solution.py:317
  14.5 4.7 %collective-permute-start.4 = (f32[80,128]{1,0:T(8,128)S(1)}, f32[80,128]{1,0:T(8,128)S(1)}, u32[]{:S(2)}, u32[]{:S(2)}) collective-permute-start(f32[80,128]{1,0:T(8,128)S(1)} %get-tuple-element.13), channel_id=1, source_target_pairs={{0,2},{2,0},{4,6},{6,4},{8,10},{10,8},{12,14},{14,12},{1,3},{3,1},... | collective-permute-start | bytes 122888 | tf_op jit(solution)/shard_map/ppermute | solution.py:323
  21.6 1.7 %collective-permute-start.5 = (f32[80,1024]{1,0:T(8,128)S(1)}, f32[80,1024]{1,0:T(8,128)S(1)}, u32[]{:S(2)}, u32[]{:S(2)}) collective-permute-start(f32[80,1024]{1,0:T(8,128)S(1)} %grads.3.part_ref), channel_id=1, source_target_pairs={{0,1},{1,0},{2,3},{3,2},{4,5},{5,4},{6,7},{7,6},{8,9},{9,8},{10,11... | collective-permute-start | bytes 983048 | tf_op jit(solution)/shard_map/ppermute | solution.py:309
  23.8 3.8 %collective-permute-start.8 = (f32[40,128]{1,0:T(8,128)S(1)}, f32[40,128]{1,0:T(8,128)S(1)}, u32[]{:S(2)}, u32[]{:S(2)}) collective-permute-start(f32[40,128]{1,0:T(8,128)S(1)} %gram.1.refs_0_), channel_id=1, source_target_pairs={{0,2},{2,0},{4,6},{6,4},{8,10},{10,8},{12,14},{14,12},{1,3},{3,1},... | collective-permute-start | bytes 61448 | tf_op jit(solution)/shard_map/ppermute | solution.py:359
  25.2 3.8 %collective-permute-start.7 = (f32[40,128]{1,0:T(8,128)S(1)}, f32[40,128]{1,0:T(8,128)S(1)}, u32[]{:S(2)}, u32[]{:S(2)}) collective-permute-start(f32[40,128]{1,0:T(8,128)S(1)} %gram.1.refs_0_), channel_id=1, source_target_pairs={{0,4},{2,6},{4,0},{6,2},{8,12},{10,14},{12,8},{14,10},{1,5},{3,7},... | collective-permute-start | bytes 61448 | tf_op jit(solution)/shard_map/ppermute | solution.py:359
  26.2 4.7 %collective-permute-start.6 = (f32[40,128]{1,0:T(8,128)S(1)}, f32[40,128]{1,0:T(8,128)S(1)}, u32[]{:S(2)}, u32[]{:S(2)}) collective-permute-start(f32[40,128]{1,0:T(8,128)S(1)} %gram.1.refs_0_), channel_id=1, source_target_pairs={{0,6},{2,4},{4,2},{6,0},{8,14},{10,12},{12,10},{14,8},{1,7},{3,5},... | collective-permute-start | bytes 61448 | tf_op jit(solution)/shard_map/ppermute | solution.py:359

commit v17 on v15

--- a/solution.py
+++ b/solution.py
@@ -22,27 +22,27 @@
     return pltpu.CompilerParams(vmem_limit_bytes=int(mib * (1 << 20)))
 
 
-def pieces(x):
+def tiles(x):
     rows, units = x.shape
-    split = x.reshape(rows // 8, 8, units // (2 * LANES), 2, LANES).transpose(0, 2, 3, 1, 4)
-    return split.reshape(rows // 8, units // (2 * LANES), 16, LANES)
+    return x.reshape(rows // 16, 2, 8, units // LANES, LANES).transpose(0, 1, 3, 2, 4)
 
 
 def chunks_of(length, ramp, tail):
     left = length - sum(ramp) - sum(tail)
     sizes = [*ramp, *([6] * (left // 6)), *([left % 6] if left % 6 else []), *tail]
-    return [(sum(sizes[:i]), size) for i, size in enumerate(sizes)]
-
-
-def project_kernel(g_chunks, h_chunks, h_ref, g_ref, pin_ref, pout_ref, out_ref, h_buf, g_buf, pin_buf, pout_buf, fold_ref, sems):
+    return [(2 * sum(sizes[:i]), 2 * size) for i, size in enumerate(sizes)]
+
+
+def project_kernel(g_chunks, h_chunks, h_ref, g_ref, pin_ref, pout_ref, out_ref, h_buf, g_buf, pin_buf, pout_buf, sems):
     plan = [(pout_ref, pout_buf, g_ref, g_buf, at) for at in g_chunks] + [(pin_ref, pin_buf, h_ref, h_buf, at) for at in h_chunks]
     copies = []
     for i, (proj, proj_buf, data, data_buf, (start, size)) in enumerate(plan):
         at = pl.ds(start, size)
-        copies.append((
-            pltpu.make_async_copy(proj.at[:, at], proj_buf.at[:, at], sems.at[2 * i]),
-            pltpu.make_async_copy(data.at[:, at], data_buf.at[:, at], sems.at[2 * i + 1]),
-        ))
+        copies.append([
+            pltpu.make_async_copy(src.at[:, h, at], dst.at[:, at, pl.ds(8 * h, 8)], sems.at[4 * i + 2 * j + h])
+            for j, (src, dst) in enumerate(((proj, proj_buf), (data, data_buf)))
+            for h in range(2)
+        ])
 
     def start(i):
         if i < len(copies):
@@ -51,9 +51,6 @@
 
     for i in range(FLIGHT):
         start(i)
-    lane = lax.broadcasted_iota(jnp.int32, fold_ref.shape, 0)
-    token = lax.broadcasted_iota(jnp.int32, fold_ref.shape, 1)
-    fold_ref[...] = jnp.where(lane // 16 * 8 + lane % 8 == token, 1.0, 0.0).astype(jnp.bfloat16)
 
     def line_up(ref, first, size):
         blocks = [ref[:, j].reshape(ref.shape[0] * 16, LANES) for j in range(first, first + size)]
@@ -69,37 +66,23 @@
             line_up(proj_buf, first, size), line_up(data_buf, first, size), NT, preferred_element_type=jnp.float32
         )
         totals[which] = part if totals[which] is None else totals[which] + part
-
-    spread = totals[0].shape[1]
-    even = lax.broadcasted_iota(jnp.int32, (8, spread), 1) % 16 < 8
-    lines = []
-    for total in totals:
-        for g in range(total.shape[0] // 16):
-            lines.append(jnp.where(even, total[16 * g:16 * g + 8], total[16 * g + 8:16 * g + 16]))
-    lines = jnp.concatenate(lines, axis=0)
-    split = []
-    for _ in range(3):
-        split.append(lines.astype(jnp.bfloat16))
-        lines = lines - split[-1].astype(jnp.float32)
-    rows = out_ref.shape[0]
-    sums = jnp.dot(jnp.concatenate(split, axis=0), fold_ref[...], preferred_element_type=jnp.float32)
-    out_ref[...] = sums[2 * rows:] + sums[rows:2 * rows] + sums[:rows]
+    out_ref[...] = jnp.concatenate(totals, axis=0)
 
 
 def project(hidden, out_grad, pin_t, pout_t):
     tokens, units = hidden.shape
     width = out_grad.shape[1]
     ranks = pin_t.shape[0] + pout_t.shape[0]
-    operands = [pieces(x) for x in (hidden, out_grad, pin_t, pout_t)]
-    g_chunks = chunks_of(operands[1].shape[1], (1, 2, 3, 4), ())
-    h_chunks = chunks_of(operands[0].shape[1], (), (4, 2, 2))
+    operands = [tiles(x) for x in (hidden, out_grad, pin_t, pout_t)]
+    g_chunks = chunks_of(operands[1].shape[2] // 2, (1, 2, 3, 4), ())
+    h_chunks = chunks_of(operands[0].shape[2] // 2, (), (4, 2, 2))
     return pl.pallas_call(
         functools.partial(project_kernel, g_chunks, h_chunks),
         out_shape=jax.ShapeDtypeStruct((ranks, tokens), jnp.float32),
         in_specs=[HBM] * 4,
         out_specs=VMEM,
-        scratch_shapes=[pltpu.VMEM(x.shape, x.dtype) for x in operands]
-        + [pltpu.VMEM((2 * tokens, tokens), jnp.bfloat16), pltpu.SemaphoreType.DMA((2 * len(g_chunks + h_chunks),))],
+        scratch_shapes=[pltpu.VMEM((x.shape[0], x.shape[2], 16, LANES), x.dtype) for x in operands]
+        + [pltpu.SemaphoreType.DMA((4 * len(g_chunks + h_chunks),))],
         compiler_params=vmem_params(53.5),
         cost_estimate=pl.CostEstimate(
             flops=2 * tokens * 64 * (units + width),
@@ -236,7 +219,21 @@
 
 def gram_kernel(docs, part_ref, recv_ref, out_ref):
     both = part_ref[...] + recv_ref[...]
-    share = lax.dot_general(both, both[:docs], NT, precision=HIGHEST, preferred_element_type=jnp.float32)
+    rows = both.shape[0]
+    split = []
+    for _ in range(3):
+        split.append(both.astype(jnp.bfloat16))
+        both = both - split[-1].astype(jnp.float32)
+    every = lax.dot_general(
+        jnp.concatenate(split, axis=0),
+        jnp.concatenate([x[:docs] for x in split], axis=0),
+        NT,
+        preferred_element_type=jnp.float32,
+    )
+    share = None
+    for i, j in ((2, 0), (1, 1), (0, 2), (1, 0), (0, 1), (0, 0)):
+        term = every[i * rows:(i + 1) * rows, j * docs:(j + 1) * docs]
+        share = term if share is None else share + term
     half = share.shape[0] // 2
     out_ref[...] = jnp.concatenate([share[:half], share[half:]], axis=1)
 
@@ -271,7 +268,7 @@
         pivot, line = wide[r], rows[r]
         scale_rows = jnp.ones((size, cols), jnp.float32)
         for j in range(size):
-            inverse = 1.0 / pivot[j][j:j + 1]
+            inverse = pltpu.reciprocal(pivot[j][j:j + 1], full_range=False)
             factor = jnp.where(here == j, 0.0, pivot[j]) * inverse
             pivot = [x if i <= j else x - factor * x[j:j + 1] for i, x in enumerate(pivot)]
             line = line - factor * line[j:j + 1]

time: 31.2 us -> 32.6 us (1.045)
  Pallas kernels: 10.4 us -> 11.8 us
    pallas_call x1, Pallas kernels: 5.65 us -> 7.11 us  [project(): pl.pallas_call(functools.partial(project_kernel, g_chunks, h_chunks), out...]
where the time goes in v17:
time: 32.6 us; the launch traced here: 32.5 us
  Pallas kernels  11.8 us (36%)
  starting transfers between devices  10.4 us (32%)
  waiting for transfers between devices  9.89 us (30%)
    pallas_call x1, Pallas kernels, project(): pl.pallas_call(functools.partial(project_kernel, g_chunks, h_chunks), out...  7.11 us
    ppermute x4, starting transfers between devices, trade(): got.append(lax.ppermute(x, ('dp', 'tensor'), pairs))  7.06 us
    ppermute x2, waiting for transfers between devices, trade_shared(): return lax.ppermute(x, 'dp', [(i, i ^ SHARED) for i in range(dp)])  4.32 us
    ppermute x3, waiting for transfers between devices, swap_cores(): return lax.ppermute(x, 'tensor', [(i, cores - 1 - i) for i in range(cores)])  3.33 us
    ppermute x2, starting transfers between devices, trade_shared(): return lax.ppermute(x, 'dp', [(i, i ^ SHARED) for i in range(dp)])  2.63 us
    pallas_call x1, Pallas kernels, solve(): pl.pallas_call(functools.partial(solve_kernel, docs, queries, scale), out...  2.46 us
    ppermute x4, waiting for transfers between devices, trade(): got.append(lax.ppermute(x, ('dp', 'tensor'), pairs))  2.24 us
    pallas_call x2, Pallas kernels, grads_of(): pl.pallas_call(functools.partial(grads_kernel, rows_a, rows_b, docs, dp,...  1.73 us
  transfers between devices with their start and end apart: 9, of which 7 were waited for; matrix products, arithmetic and copies ran while one was open for 1% of the time, Pallas kernels for 4%

profile of v17, /device:TPU:0, one launch (start us, length us, event | category | flops | bytes accessed | tf_op | source)
XLA Modules:
  0.0 32.5 jit_solution(8965186539263103746)
XLA Ops:
  0.0 0.0 copy-start.1
  0.0 0.0 copy-start
  0.0 7.1 %project.1.part_ref = f32[128,256]{1,0:T(8,128)S(1)} custom-call(bf16[16,2,112,8,128]{4,3,2,1,0:T(8,128)(2,1)} %bitcast.24, bf16[16,2,32,8,128]{4,3,2,1,0:T(8,128)(2,1)} %bitcast.25, bf16[4,2,112,8,128]{4,3,2,1,0:T(8,128)(2,1)} %bitcast.26, bf16[4,2,32,8,128]{4,3,2,1,0:T(8,128)(2,1)} %bitcast.27), custom_call_target="tpu_custom_call" | custom-call | flops 603979776 | bytes 11796480 | tf_op jit(solution)/shard_map/project/pallas_call | solution.py:79
  7.1 0.5 %collective-permute-start = (f32[128,256]{1,0:T(8,128)S(1)}, f32[128,256]{1,0:T(8,128)S(1)}, u32[]{:S(2)}, u32[]{:S(2)}) collective-permute-start(f32[128,256]{1,0:T(8,128)S(1)} %project.1.part_ref), channel_id=1, source_target_pairs={{0,1},{1,0},{2,3},{3,2},{4,5},{5,4},{6,7},{7,6},{8,9},{9,8},{10,11... | collective-permute-start | bytes 393224 | tf_op jit(solution)/shard_map/ppermute | solution.py:312
  7.6 0.0 copy-done.1
  7.6 0.0 copy-done
  7.7 0.2 reshape.25
  7.8 0.1 reshape.26
  8.0 0.7 %collective-permute-done.recv_ref = f32[128,256]{1,0:T(8,128)S(1)} collective-permute-done((f32[128,256]{1,0:T(8,128)S(1)}, f32[128,256]{1,0:T(8,128)S(1)}, u32[]{:S(2)}, u32[]{:S(2)}) %collective-permute-start) | collective-permute-done | bytes 131104 | tf_op jit(solution)/shard_map/ppermute | solution.py:312
  8.6 0.1 pack.1
  8.7 4.0 %collective-permute-start.2 = (f32[152,128]{1,0:T(8,128)S(1)}, f32[152,128]{1,0:T(8,128)S(1)}, u32[]{:S(2)}, u32[]{:S(2)}) collective-permute-start(f32[152,128]{1,0:T(8,128)S(1)} %get-tuple-element.11), channel_id=1, source_target_pairs={{0,8},{1,11},{2,10},{3,9},{4,12},{5,15},{6,14},{7,13},{8,0},{9,3},... | collective-permute-start | bytes 233480 | tf_op jit(solution)/shard_map/ppermute | solution.py:320
  12.7 1.6 %collective-permute-start.3 = (f32[152,128]{1,0:T(8,128)S(1)}, f32[152,128]{1,0:T(8,128)S(1)}, u32[]{:S(2)}, u32[]{:S(2)}) collective-permute-start(f32[152,128]{1,0:T(8,128)S(1)} %get-tuple-element.12), channel_id=1, source_target_pairs={{0,4},{1,7},{2,6},{3,5},{4,0},{5,3},{6,2},{7,1},{8,12},{9,15},{10,... | collective-permute-start | bytes 233480 | tf_op jit(solution)/shard_map/ppermute | solution.py:320
  14.3 0.0 collective-permute-start.1
  14.3 1.7 %collective-permute-start.4 = (f32[80,128]{1,0:T(8,128)S(1)}, f32[80,128]{1,0:T(8,128)S(1)}, u32[]{:S(2)}, u32[]{:S(2)}) collective-permute-start(f32[80,128]{1,0:T(8,128)S(1)} %get-tuple-element.13), channel_id=1, source_target_pairs={{0,2},{2,0},{4,6},{6,4},{8,10},{10,8},{12,14},{14,12},{1,3},{3,1},... | collective-permute-start | bytes 122888 | tf_op jit(solution)/shard_map/ppermute | solution.py:326
  16.0 2.9 %collective-permute-done.4.refs_2_ = f32[80,128]{1,0:T(8,128)S(1)} collective-permute-done((f32[80,128]{1,0:T(8,128)S(1)}, f32[80,128]{1,0:T(8,128)S(1)}, u32[]{:S(2)}, u32[]{:S(2)}) %collective-permute-start.4) | collective-permute-done | bytes 40992 | tf_op jit(solution)/shard_map/ppermute | solution.py:326
  19.0 0.0 collective-permute-done.2.refs_0_
  19.0 0.0 collective-permute-done.3.refs_1_
  19.0 1.2 %grads.2.refs_1_ = f32[80,1024]{1,0:T(8,128)S(1)} custom-call(f32[152,128]{1,0:T(8,128)S(1)} %collective-permute-done.2.refs_0_, f32[152,128]{1,0:T(8,128)S(1)} %collective-permute-done.3.refs_1_, f32[80,128]{1,0:T(8,128)S(1)} %collective-permute-done.4.refs_2_, f32[80,128]{1,0:T(8,128)S(1)} %get-tuple-element.14.refs_3_), custom_call_target="tpu_custom_call" | custom-call | flops 201326592 | bytes 196608 | tf_op jit(solution)/shard_map/grads/pallas_call | solution.py:203
  20.2 0.7 %collective-permute-done.1.refs_0_ = f32[152,128]{1,0:T(8,128)S(1)} collective-permute-done((f32[152,128]{1,0:T(8,128)S(1)}, f32[152,128]{1,0:T(8,128)S(1)}, u32[]{:S(2)}, u32[]{:S(2)}) %collective-permute-start.1) | collective-permute-done | bytes 77856 | tf_op jit(solution)/shard_map/ppermute | solution.py:320
  20.9 0.5 %grads.3.part_ref = f32[80,1024]{1,0:T(8,128)S(1)} custom-call(f32[152,128]{1,0:T(8,128)S(1)} %collective-permute-done.1.refs_0_, f32[80,1024]{1,0:T(8,128)S(1)} %grads.2.refs_1_), custom_call_target="tpu_custom_call" | custom-call | flops 67108864 | bytes 65536 | tf_op jit(solution)/shard_map/grads/pallas_call | solution.py:203
  21.4 0.2 collective-permute-start.5
  21.7 1.5 %collective-permute-done.5.recv_ref = f32[80,1024]{1,0:T(8,128)S(1)} collective-permute-done((f32[80,1024]{1,0:T(8,128)S(1)}, f32[80,1024]{1,0:T(8,128)S(1)}, u32[]{:S(2)}, u32[]{:S(2)}) %collective-permute-start.5) | collective-permute-done | bytes 327712 | tf_op jit(solution)/shard_map/ppermute | solution.py:312
  23.1 0.4 %gram.1 = f32[40,128]{1,0:T(8,128)S(1)} custom-call(f32[80,1024]{1,0:T(8,128)S(1)} %grads.3.part_ref, f32[80,1024]{1,0:T(8,128)S(1)} %collective-permute-done.5.recv_ref), custom_call_target="tpu_custom_call" | custom-call | tf_op jit(solution)/shard_map/gram/pallas_call | solution.py:242
  23.6 1.5 %collective-permute-start.6 = (f32[40,128]{1,0:T(8,128)S(1)}, f32[40,128]{1,0:T(8,128)S(1)}, u32[]{:S(2)}, u32[]{:S(2)}) collective-permute-start(f32[40,128]{1,0:T(8,128)S(1)} %gram.1), channel_id=1, source_target_pairs={{0,4},{1,7},{2,6},{3,5},{4,0},{5,3},{6,2},{7,1},{8,12},{9,15},{10,... | collective-permute-start | bytes 61448 | tf_op jit(solution)/shard_map/ppermute | solution.py:320
  25.0 0.9 %collective-permute-start.7 = (f32[40,128]{1,0:T(8,128)S(1)}, f32[40,128]{1,0:T(8,128)S(1)}, u32[]{:S(2)}, u32[]{:S(2)}) collective-permute-start(f32[40,128]{1,0:T(8,128)S(1)} %gram.1), channel_id=1, source_target_pairs={{0,2},{2,0},{4,6},{6,4},{8,10},{10,8},{12,14},{14,12},{1,3},{3,1},... | collective-permute-start | bytes 61448 | tf_op jit(solution)/shard_map/ppermute | solution.py:326
  25.9 1.5 %collective-permute-done.6 = f32[40,128]{1,0:T(8,128)S(1)} collective-permute-done((f32[40,128]{1,0:T(8,128)S(1)}, f32[40,128]{1,0:T(8,128)S(1)}, u32[]{:S(2)}, u32[]{:S(2)}) %collective-permute-start.6) | collective-permute-done | bytes 20512 | tf_op jit(solution)/shard_map/ppermute | solution.py:320
  27.4 1.4 %collective-permute-done.7 = f32[40,128]{1,0:T(8,128)S(1)} collective-permute-done((f32[40,128]{1,0:T(8,128)S(1)}, f32[40,128]{1,0:T(8,128)S(1)}, u32[]{:S(2)}, u32[]{:S(2)}) %collective-permute-start.7) | collective-permute-done | bytes 20512 | tf_op jit(solution)/shard_map/ppermute | solution.py:326
  28.8 0.0 collective-permute-start.8
  28.8 1.2 %collective-permute-done.8.recv_ref = f32[40,128]{1,0:T(8,128)S(1)} collective-permute-done((f32[40,128]{1,0:T(8,128)S(1)}, f32[40,128]{1,0:T(8,128)S(1)}, u32[]{:S(2)}, u32[]{:S(2)}) %collective-permute-start.8) | collective-permute-done | bytes 20512 | tf_op jit(solution)/shard_map/ppermute | solution.py:312
  30.0 2.5 %solve.1 = f32[8,16]{1,0:T(8,128)} custom-call(f32[40,128]{1,0:T(8,128)S(1)} %select_add_fusion.x_ref, f32[40,128]{1,0:T(8,128)S(1)} %collective-permute-done.8.recv_ref), custom_call_target="tpu_custom_call" | custom-call | tf_op jit(solution)/shard_map/solve/pallas_call | solution.py:291
  (5 shorter events, 0.0 us)
Async XLA Ops:
  0.0 7.6 %copy-start.1 = (s32[256]{0:T(256)S(1)}, s32[256]{0:T(256)}, u32[]{:S(2)}) copy-start(s32[256]{0:T(256)} %param.10) | copy-start | bytes 3076
  0.0 7.6 %copy-start = (f32[2,4096]{1,0:T(2,128)S(1)}, f32[2,4096]{1,0:T(2,128)}, u32[]{:S(2)}) copy-start(f32[2,4096]{1,0:T(2,128)} %param.11) | copy-start | bytes 98308
  7.1 1.5 %collective-permute-start = (f32[128,256]{1,0:T(8,128)S(1)}, f32[128,256]{1,0:T(8,128)S(1)}, u32[]{:S(2)}, u32[]{:S(2)}) collective-permute-start(f32[128,256]{1,0:T(8,128)S(1)} %project.1.part_ref), channel_id=1, source_target_pairs={{0,1},{1,0},{2,3},{3,2},{4,5},{5,4},{6,7},{7,6},{8,9},{9,8},{10,11... | collective-permute-start | bytes 393224 | tf_op jit(solution)/shard_map/ppermute | solution.py:312
  8.7 10.3 %collective-permute-start.2 = (f32[152,128]{1,0:T(8,128)S(1)}, f32[152,128]{1,0:T(8,128)S(1)}, u32[]{:S(2)}, u32[]{:S(2)}) collective-permute-start(f32[152,128]{1,0:T(8,128)S(1)} %get-tuple-element.11), channel_id=1, source_target_pairs={{0,8},{1,11},{2,10},{3,9},{4,12},{5,15},{6,14},{7,13},{8,0},{9,3},... | collective-permute-start | bytes 233480 | tf_op jit(solution)/shard_map/ppermute | solution.py:320
  12.7 6.3 %collective-permute-start.3 = (f32[152,128]{1,0:T(8,128)S(1)}, f32[152,128]{1,0:T(8,128)S(1)}, u32[]{:S(2)}, u32[]{:S(2)}) collective-permute-start(f32[152,128]{1,0:T(8,128)S(1)} %get-tuple-element.12), channel_id=1, source_target_pairs={{0,4},{1,7},{2,6},{3,5},{4,0},{5,3},{6,2},{7,1},{8,12},{9,15},{10,... | collective-permute-start | bytes 233480 | tf_op jit(solution)/shard_map/ppermute | solution.py:320
  14.3 6.6 %collective-permute-start.1 = (f32[152,128]{1,0:T(8,128)S(1)}, f32[152,128]{1,0:T(8,128)S(1)}, u32[]{:S(2)}, u32[]{:S(2)}) collective-permute-start(f32[152,128]{1,0:T(8,128)S(1)} %get-tuple-element.10), channel_id=1, source_target_pairs={{0,12},{1,15},{2,14},{3,13},{4,8},{5,11},{6,10},{7,9},{8,4},{9,7},... | collective-permute-start | bytes 233480 | tf_op jit(solution)/shard_map/ppermute | solution.py:320
  14.3 4.7 %collective-permute-start.4 = (f32[80,128]{1,0:T(8,128)S(1)}, f32[80,128]{1,0:T(8,128)S(1)}, u32[]{:S(2)}, u32[]{:S(2)}) collective-permute-start(f32[80,128]{1,0:T(8,128)S(1)} %get-tuple-element.13), channel_id=1, source_target_pairs={{0,2},{2,0},{4,6},{6,4},{8,10},{10,8},{12,14},{14,12},{1,3},{3,1},... | collective-permute-start | bytes 122888 | tf_op jit(solution)/shard_map/ppermute | solution.py:326
  21.4 1.7 %collective-permute-start.5 = (f32[80,1024]{1,0:T(8,128)S(1)}, f32[80,1024]{1,0:T(8,128)S(1)}, u32[]{:S(2)}, u32[]{:S(2)}) collective-permute-start(f32[80,1024]{1,0:T(8,128)S(1)} %grads.3.part_ref), channel_id=1, source_target_pairs={{0,1},{1,0},{2,3},{3,2},{4,5},{5,4},{6,7},{7,6},{8,9},{9,8},{10,11... | collective-permute-start | bytes 983048 | tf_op jit(solution)/shard_map/ppermute | solution.py:312
  23.6 3.9 %collective-permute-start.6 = (f32[40,128]{1,0:T(8,128)S(1)}, f32[40,128]{1,0:T(8,128)S(1)}, u32[]{:S(2)}, u32[]{:S(2)}) collective-permute-start(f32[40,128]{1,0:T(8,128)S(1)} %gram.1), channel_id=1, source_target_pairs={{0,4},{1,7},{2,6},{3,5},{4,0},{5,3},{6,2},{7,1},{8,12},{9,15},{10,... | collective-permute-start | bytes 61448 | tf_op jit(solution)/shard_map/ppermute | solution.py:320
  25.0 3.8 %collective-permute-start.7 = (f32[40,128]{1,0:T(8,128)S(1)}, f32[40,128]{1,0:T(8,128)S(1)}, u32[]{:S(2)}, u32[]{:S(2)}) collective-permute-start(f32[40,128]{1,0:T(8,128)S(1)} %gram.1), channel_id=1, source_target_pairs={{0,2},{2,0},{4,6},{6,4},{8,10},{10,8},{12,14},{14,12},{1,3},{3,1},... | collective-permute-start | bytes 61448 | tf_op jit(solution)/shard_map/ppermute | solution.py:326
  28.8 1.2 %collective-permute-start.8 = (f32[40,128]{1,0:T(8,128)S(1)}, f32[40,128]{1,0:T(8,128)S(1)}, u32[]{:S(2)}, u32[]{:S(2)}) collective-permute-start(f32[40,128]{1,0:T(8,128)S(1)} %select_add_fusion.x_ref), channel_id=1, source_target_pairs={{0,1},{1,0},{2,3},{3,2},{4,5},{5,4},{6,7},{7,6},{8,9},{9,8},{10,11... | collective-permute-start | bytes 61448 | tf_op jit(solution)/shard_map/ppermute | solution.py:312

commit v18 on v17

--- a/solution.py
+++ b/solution.py
@@ -13,7 +13,6 @@
 FLIGHT = 7
 SHARED = 1
 NT = (((1,), (1,)), ((), ()))
-HIGHEST = lax.Precision.HIGHEST
 VMEM = pl.BlockSpec(memory_space=pltpu.VMEM)
 HBM = pl.BlockSpec(memory_space=pltpu.HBM)
 
@@ -22,15 +21,16 @@
     return pltpu.CompilerParams(vmem_limit_bytes=int(mib * (1 << 20)))
 
 
-def tiles(x):
+def pieces(x):
     rows, units = x.shape
-    return x.reshape(rows // 16, 2, 8, units // LANES, LANES).transpose(0, 1, 3, 2, 4)
+    split = x.reshape(rows // 8, 8, units // (2 * LANES), 2, LANES).transpose(0, 2, 3, 1, 4)
+    return split.reshape(rows // 8, units // (2 * LANES), 16, LANES)
 
 
 def chunks_of(length, ramp, tail):
     left = length - sum(ramp) - sum(tail)
     sizes = [*ramp, *([6] * (left // 6)), *([left % 6] if left % 6 else []), *tail]
-    return [(2 * sum(sizes[:i]), 2 * size) for i, size in enumerate(sizes)]
+    return [(sum(sizes[:i]), size) for i, size in enumerate(sizes)]
 
 
 def project_kernel(g_chunks, h_chunks, h_ref, g_ref, pin_ref, pout_ref, out_ref, h_buf, g_buf, pin_buf, pout_buf, sems):
@@ -38,11 +38,10 @@
     copies = []
     for i, (proj, proj_buf, data, data_buf, (start, size)) in enumerate(plan):
         at = pl.ds(start, size)
-        copies.append([
-            pltpu.make_async_copy(src.at[:, h, at], dst.at[:, at, pl.ds(8 * h, 8)], sems.at[4 * i + 2 * j + h])
-            for j, (src, dst) in enumerate(((proj, proj_buf), (data, data_buf)))
-            for h in range(2)
-        ])
+        copies.append((
+            pltpu.make_async_copy(proj.at[:, at], proj_buf.at[:, at], sems.at[2 * i]),
+            pltpu.make_async_copy(data.at[:, at], data_buf.at[:, at], sems.at[2 * i + 1]),
+        ))
 
     def start(i):
         if i < len(copies):
@@ -66,23 +65,41 @@
             line_up(proj_buf, first, size), line_up(data_buf, first, size), NT, preferred_element_type=jnp.float32
         )
         totals[which] = part if totals[which] is None else totals[which] + part
-    out_ref[...] = jnp.concatenate(totals, axis=0)
+
+    lane = lax.broadcasted_iota(jnp.int32, (8, LANES), 1)
+    even = lane % 16 < 8
+    later = lane // (LANES // 2)
+    order = lane % (LANES // 2) // 8 * 16 + lane % 8 + 8 * later
+    done = 0
+    for total in totals:
+        for g in range(0, total.shape[0], 16):
+            lines = []
+            for i in range(0, total.shape[1], LANES):
+                upper, lower = total[g:g + 8, i:i + LANES], total[g + 8:g + 16, i:i + LANES]
+                lines.append(jnp.where(even, upper, lower))
+            for i in range(0, len(lines), 2):
+                first = lines[i] + pltpu.roll(lines[i], LANES - 8, 1)
+                second = lines[i + 1] + pltpu.roll(lines[i + 1], 8, 1)
+                both = jnp.where(even, first, second)
+                at = i // 2 * LANES
+                out_ref[done:done + 8, at:at + LANES] = jnp.take_along_axis(both, order, axis=1)
+            done += 8
 
 
 def project(hidden, out_grad, pin_t, pout_t):
     tokens, units = hidden.shape
     width = out_grad.shape[1]
     ranks = pin_t.shape[0] + pout_t.shape[0]
-    operands = [tiles(x) for x in (hidden, out_grad, pin_t, pout_t)]
-    g_chunks = chunks_of(operands[1].shape[2] // 2, (1, 2, 3, 4), ())
-    h_chunks = chunks_of(operands[0].shape[2] // 2, (), (4, 2, 2))
+    operands = [pieces(x) for x in (hidden, out_grad, pin_t, pout_t)]
+    g_chunks = chunks_of(operands[1].shape[1], (1, 2, 3, 4), ())
+    h_chunks = chunks_of(operands[0].shape[1], (), (4, 2, 2))
     return pl.pallas_call(
         functools.partial(project_kernel, g_chunks, h_chunks),
         out_shape=jax.ShapeDtypeStruct((ranks, tokens), jnp.float32),
         in_specs=[HBM] * 4,
         out_specs=VMEM,
-        scratch_shapes=[pltpu.VMEM((x.shape[0], x.shape[2], 16, LANES), x.dtype) for x in operands]
-        + [pltpu.SemaphoreType.DMA((4 * len(g_chunks + h_chunks),))],
+        scratch_shapes=[pltpu.VMEM(x.shape, x.dtype) for x in operands]
+        + [pltpu.SemaphoreType.DMA((2 * len(g_chunks + h_chunks),))],
         compiler_params=vmem_params(53.5),
         cost_estimate=pl.CostEstimate(
             flops=2 * tokens * 64 * (units + width),
@@ -268,7 +285,7 @@
         pivot, line = wide[r], rows[r]
         scale_rows = jnp.ones((size, cols), jnp.float32)
         for j in range(size):
-            inverse = pltpu.reciprocal(pivot[j][j:j + 1], full_range=False)
+            inverse = 1.0 / pivot[j][j:j + 1]
             factor = jnp.where(here == j, 0.0, pivot[j]) * inverse
             pivot = [x if i <= j else x - factor * x[j:j + 1] for i, x in enumerate(pivot)]
             line = line - factor * line[j:j + 1]

time: 32.6 us -> 31.1 us (0.954)
  Pallas kernels: 11.8 us -> 10.3 us
    pallas_call x1, Pallas kernels: 7.11 us -> 5.59 us  [project(): pl.pallas_call(functools.partial(project_kernel, g_chunks, h_chunks), out...]
where the time goes in v18:
time: 31.1 us; the launch traced here: 31 us
  starting transfers between devices  10.4 us (33%)
  Pallas kernels  10.3 us (33%)
  waiting for transfers between devices  9.88 us (32%)
    ppermute x4, starting transfers between devices, trade(): got.append(lax.ppermute(x, ('dp', 'tensor'), pairs))  7.04 us
    pallas_call x1, Pallas kernels, project(): pl.pallas_call(functools.partial(project_kernel, g_chunks, h_chunks), out...  5.59 us
    ppermute x2, waiting for transfers between devices, trade_shared(): return lax.ppermute(x, 'dp', [(i, i ^ SHARED) for i in range(dp)])  4.26 us
    ppermute x3, waiting for transfers between devices, swap_cores(): return lax.ppermute(x, 'tensor', [(i, cores - 1 - i) for i in range(cores)])  3.33 us
    ppermute x2, starting transfers between devices, trade_shared(): return lax.ppermute(x, 'dp', [(i, i ^ SHARED) for i in range(dp)])  2.64 us
    pallas_call x1, Pallas kernels, solve(): pl.pallas_call(functools.partial(solve_kernel, docs, queries, scale), out...  2.46 us
    ppermute x4, waiting for transfers between devices, trade(): got.append(lax.ppermute(x, ('dp', 'tensor'), pairs))  2.29 us
    pallas_call x2, Pallas kernels, grads_of(): pl.pallas_call(functools.partial(grads_kernel, rows_a, rows_b, docs, dp,...  1.73 us
  transfers between devices with their start and end apart: 9, of which 7 were waited for; matrix products, arithmetic and copies ran while one was open for 1% of the time, Pallas kernels for 4%

profile of v18, /device:TPU:0, one launch (start us, length us, event | category | flops | bytes accessed | tf_op | source)
XLA Modules:
  0.0 31.0 jit_solution(17177495778747909284)
XLA Ops:
  0.0 0.0 copy-start.1
  0.0 0.0 copy-start
  0.0 5.6 %project.1.part_ref = f32[128,256]{1,0:T(8,128)S(1)} custom-call(bf16[32,56,16,128]{3,2,1,0:T(8,128)(2,1)} %bitcast.32, bf16[32,16,16,128]{3,2,1,0:T(8,128)(2,1)} %bitcast.33, bf16[8,56,16,128]{3,2,1,0:T(8,128)(2,1)} %bitcast.34, bf16[8,16,16,128]{3,2,1,0:T(8,128)(2,1)} %bitcast.35), custom_call_target="tpu_custom_call" | custom-call | flops 603979776 | bytes 11796480 | tf_op jit(solution)/shard_map/project/pallas_call | solution.py:96
  5.6 0.5 %collective-permute-start = (f32[128,256]{1,0:T(8,128)S(1)}, f32[128,256]{1,0:T(8,128)S(1)}, u32[]{:S(2)}, u32[]{:S(2)}) collective-permute-start(f32[128,256]{1,0:T(8,128)S(1)} %project.1.part_ref), channel_id=1, source_target_pairs={{0,1},{1,0},{2,3},{3,2},{4,5},{5,4},{6,7},{7,6},{8,9},{9,8},{10,11... | collective-permute-start | bytes 393224 | tf_op jit(solution)/shard_map/ppermute | solution.py:329
  6.1 0.0 copy-done.1
  6.1 0.0 copy-done
  6.1 0.2 reshape.41
  6.3 0.1 reshape.42
  6.4 0.7 %collective-permute-done.recv_ref = f32[128,256]{1,0:T(8,128)S(1)} collective-permute-done((f32[128,256]{1,0:T(8,128)S(1)}, f32[128,256]{1,0:T(8,128)S(1)}, u32[]{:S(2)}, u32[]{:S(2)}) %collective-permute-start) | collective-permute-done | bytes 131104 | tf_op jit(solution)/shard_map/ppermute | solution.py:329
  7.1 0.1 pack.1
  7.2 4.0 %collective-permute-start.2 = (f32[152,128]{1,0:T(8,128)S(1)}, f32[152,128]{1,0:T(8,128)S(1)}, u32[]{:S(2)}, u32[]{:S(2)}) collective-permute-start(f32[152,128]{1,0:T(8,128)S(1)} %get-tuple-element.11), channel_id=1, source_target_pairs={{0,8},{1,11},{2,10},{3,9},{4,12},{5,15},{6,14},{7,13},{8,0},{9,3},... | collective-permute-start | bytes 233480 | tf_op jit(solution)/shard_map/ppermute | solution.py:337
  11.2 1.6 %collective-permute-start.3 = (f32[152,128]{1,0:T(8,128)S(1)}, f32[152,128]{1,0:T(8,128)S(1)}, u32[]{:S(2)}, u32[]{:S(2)}) collective-permute-start(f32[152,128]{1,0:T(8,128)S(1)} %get-tuple-element.12), channel_id=1, source_target_pairs={{0,4},{1,7},{2,6},{3,5},{4,0},{5,3},{6,2},{7,1},{8,12},{9,15},{10,... | collective-permute-start | bytes 233480 | tf_op jit(solution)/shard_map/ppermute | solution.py:337
  12.8 0.0 collective-permute-start.1
  12.8 1.7 %collective-permute-start.4 = (f32[80,128]{1,0:T(8,128)S(1)}, f32[80,128]{1,0:T(8,128)S(1)}, u32[]{:S(2)}, u32[]{:S(2)}) collective-permute-start(f32[80,128]{1,0:T(8,128)S(1)} %get-tuple-element.13), channel_id=1, source_target_pairs={{0,2},{2,0},{4,6},{6,4},{8,10},{10,8},{12,14},{14,12},{1,3},{3,1},... | collective-permute-start | bytes 122888 | tf_op jit(solution)/shard_map/ppermute | solution.py:343
  14.5 2.9 %collective-permute-done.4.refs_2_ = f32[80,128]{1,0:T(8,128)S(1)} collective-permute-done((f32[80,128]{1,0:T(8,128)S(1)}, f32[80,128]{1,0:T(8,128)S(1)}, u32[]{:S(2)}, u32[]{:S(2)}) %collective-permute-start.4) | collective-permute-done | bytes 40992 | tf_op jit(solution)/shard_map/ppermute | solution.py:343
  17.4 0.0 collective-permute-done.2.refs_0_
  17.4 0.0 collective-permute-done.3.refs_1_
  17.4 1.2 %grads.2.refs_1_ = f32[80,1024]{1,0:T(8,128)S(1)} custom-call(f32[152,128]{1,0:T(8,128)S(1)} %collective-permute-done.2.refs_0_, f32[152,128]{1,0:T(8,128)S(1)} %collective-permute-done.3.refs_1_, f32[80,128]{1,0:T(8,128)S(1)} %collective-permute-done.4.refs_2_, f32[80,128]{1,0:T(8,128)S(1)} %get-tuple-element.14.refs_3_), custom_call_target="tpu_custom_call" | custom-call | flops 201326592 | bytes 196608 | tf_op jit(solution)/shard_map/grads/pallas_call | solution.py:220
  18.6 0.8 %collective-permute-done.1.refs_0_ = f32[152,128]{1,0:T(8,128)S(1)} collective-permute-done((f32[152,128]{1,0:T(8,128)S(1)}, f32[152,128]{1,0:T(8,128)S(1)}, u32[]{:S(2)}, u32[]{:S(2)}) %collective-permute-start.1) | collective-permute-done | bytes 77856 | tf_op jit(solution)/shard_map/ppermute | solution.py:337
  19.4 0.5 %grads.3.part_ref = f32[80,1024]{1,0:T(8,128)S(1)} custom-call(f32[152,128]{1,0:T(8,128)S(1)} %collective-permute-done.1.refs_0_, f32[80,1024]{1,0:T(8,128)S(1)} %grads.2.refs_1_), custom_call_target="tpu_custom_call" | custom-call | flops 67108864 | bytes 65536 | tf_op jit(solution)/shard_map/grads/pallas_call | solution.py:220
  19.9 0.2 collective-permute-start.5
  20.1 1.5 %collective-permute-done.5.recv_ref = f32[80,1024]{1,0:T(8,128)S(1)} collective-permute-done((f32[80,1024]{1,0:T(8,128)S(1)}, f32[80,1024]{1,0:T(8,128)S(1)}, u32[]{:S(2)}, u32[]{:S(2)}) %collective-permute-start.5) | collective-permute-done | bytes 327712 | tf_op jit(solution)/shard_map/ppermute | solution.py:329
  21.6 0.4 %gram.1 = f32[40,128]{1,0:T(8,128)S(1)} custom-call(f32[80,1024]{1,0:T(8,128)S(1)} %grads.3.part_ref, f32[80,1024]{1,0:T(8,128)S(1)} %collective-permute-done.5.recv_ref), custom_call_target="tpu_custom_call" | custom-call | tf_op jit(solution)/shard_map/gram/pallas_call | solution.py:259
  22.1 1.5 %collective-permute-start.6 = (f32[40,128]{1,0:T(8,128)S(1)}, f32[40,128]{1,0:T(8,128)S(1)}, u32[]{:S(2)}, u32[]{:S(2)}) collective-permute-start(f32[40,128]{1,0:T(8,128)S(1)} %gram.1), channel_id=1, source_target_pairs={{0,4},{1,7},{2,6},{3,5},{4,0},{5,3},{6,2},{7,1},{8,12},{9,15},{10,... | collective-permute-start | bytes 61448 | tf_op jit(solution)/shard_map/ppermute | solution.py:337
  23.5 0.9 %collective-permute-start.7 = (f32[40,128]{1,0:T(8,128)S(1)}, f32[40,128]{1,0:T(8,128)S(1)}, u32[]{:S(2)}, u32[]{:S(2)}) collective-permute-start(f32[40,128]{1,0:T(8,128)S(1)} %gram.1), channel_id=1, source_target_pairs={{0,2},{2,0},{4,6},{6,4},{8,10},{10,8},{12,14},{14,12},{1,3},{3,1},... | collective-permute-start | bytes 61448 | tf_op jit(solution)/shard_map/ppermute | solution.py:343
  24.4 1.5 %collective-permute-done.6 = f32[40,128]{1,0:T(8,128)S(1)} collective-permute-done((f32[40,128]{1,0:T(8,128)S(1)}, f32[40,128]{1,0:T(8,128)S(1)}, u32[]{:S(2)}, u32[]{:S(2)}) %collective-permute-start.6) | collective-permute-done | bytes 20512 | tf_op jit(solution)/shard_map/ppermute | solution.py:337
  25.9 1.4 %collective-permute-done.7 = f32[40,128]{1,0:T(8,128)S(1)} collective-permute-done((f32[40,128]{1,0:T(8,128)S(1)}, f32[40,128]{1,0:T(8,128)S(1)}, u32[]{:S(2)}, u32[]{:S(2)}) %collective-permute-start.7) | collective-permute-done | bytes 20512 | tf_op jit(solution)/shard_map/ppermute | solution.py:343
  27.3 0.0 collective-permute-start.8
  27.3 1.2 %collective-permute-done.8.recv_ref = f32[40,128]{1,0:T(8,128)S(1)} collective-permute-done((f32[40,128]{1,0:T(8,128)S(1)}, f32[40,128]{1,0:T(8,128)S(1)}, u32[]{:S(2)}, u32[]{:S(2)}) %collective-permute-start.8) | collective-permute-done | bytes 20512 | tf_op jit(solution)/shard_map/ppermute | solution.py:329
  28.5 2.5 %solve.1 = f32[8,16]{1,0:T(8,128)} custom-call(f32[40,128]{1,0:T(8,128)S(1)} %select_add_fusion.x_ref, f32[40,128]{1,0:T(8,128)S(1)} %collective-permute-done.8.recv_ref), custom_call_target="tpu_custom_call" | custom-call | tf_op jit(solution)/shard_map/solve/pallas_call | solution.py:308
  (5 shorter events, 0.0 us)
Async XLA Ops:
  0.0 6.1 %copy-start.1 = (s32[256]{0:T(256)S(1)}, s32[256]{0:T(256)}, u32[]{:S(2)}) copy-start(s32[256]{0:T(256)} %param.10) | copy-start | bytes 3076
  0.0 6.1 %copy-start = (f32[2,4096]{1,0:T(2,128)S(1)}, f32[2,4096]{1,0:T(2,128)}, u32[]{:S(2)}) copy-start(f32[2,4096]{1,0:T(2,128)} %param.11) | copy-start | bytes 98308
  5.6 1.5 %collective-permute-start = (f32[128,256]{1,0:T(8,128)S(1)}, f32[128,256]{1,0:T(8,128)S(1)}, u32[]{:S(2)}, u32[]{:S(2)}) collective-permute-start(f32[128,256]{1,0:T(8,128)S(1)} %project.1.part_ref), channel_id=1, source_target_pairs={{0,1},{1,0},{2,3},{3,2},{4,5},{5,4},{6,7},{7,6},{8,9},{9,8},{10,11... | collective-permute-start | bytes 393224 | tf_op jit(solution)/shard_map/ppermute | solution.py:329
  7.2 10.2 %collective-permute-start.2 = (f32[152,128]{1,0:T(8,128)S(1)}, f32[152,128]{1,0:T(8,128)S(1)}, u32[]{:S(2)}, u32[]{:S(2)}) collective-permute-start(f32[152,128]{1,0:T(8,128)S(1)} %get-tuple-element.11), channel_id=1, source_target_pairs={{0,8},{1,11},{2,10},{3,9},{4,12},{5,15},{6,14},{7,13},{8,0},{9,3},... | collective-permute-start | bytes 233480 | tf_op jit(solution)/shard_map/ppermute | solution.py:337
  11.2 6.2 %collective-permute-start.3 = (f32[152,128]{1,0:T(8,128)S(1)}, f32[152,128]{1,0:T(8,128)S(1)}, u32[]{:S(2)}, u32[]{:S(2)}) collective-permute-start(f32[152,128]{1,0:T(8,128)S(1)} %get-tuple-element.12), channel_id=1, source_target_pairs={{0,4},{1,7},{2,6},{3,5},{4,0},{5,3},{6,2},{7,1},{8,12},{9,15},{10,... | collective-permute-start | bytes 233480 | tf_op jit(solution)/shard_map/ppermute | solution.py:337
  12.8 6.6 %collective-permute-start.1 = (f32[152,128]{1,0:T(8,128)S(1)}, f32[152,128]{1,0:T(8,128)S(1)}, u32[]{:S(2)}, u32[]{:S(2)}) collective-permute-start(f32[152,128]{1,0:T(8,128)S(1)} %get-tuple-element.10), channel_id=1, source_target_pairs={{0,12},{1,15},{2,14},{3,13},{4,8},{5,11},{6,10},{7,9},{8,4},{9,7},... | collective-permute-start | bytes 233480 | tf_op jit(solution)/shard_map/ppermute | solution.py:337
  12.8 4.6 %collective-permute-start.4 = (f32[80,128]{1,0:T(8,128)S(1)}, f32[80,128]{1,0:T(8,128)S(1)}, u32[]{:S(2)}, u32[]{:S(2)}) collective-permute-start(f32[80,128]{1,0:T(8,128)S(1)} %get-tuple-element.13), channel_id=1, source_target_pairs={{0,2},{2,0},{4,6},{6,4},{8,10},{10,8},{12,14},{14,12},{1,3},{3,1},... | collective-permute-start | bytes 122888 | tf_op jit(solution)/shard_map/ppermute | solution.py:343
  19.9 1.7 %collective-permute-start.5 = (f32[80,1024]{1,0:T(8,128)S(1)}, f32[80,1024]{1,0:T(8,128)S(1)}, u32[]{:S(2)}, u32[]{:S(2)}) collective-permute-start(f32[80,1024]{1,0:T(8,128)S(1)} %grads.3.part_ref), channel_id=1, source_target_pairs={{0,1},{1,0},{2,3},{3,2},{4,5},{5,4},{6,7},{7,6},{8,9},{9,8},{10,11... | collective-permute-start | bytes 983048 | tf_op jit(solution)/shard_map/ppermute | solution.py:329
  22.1 3.9 %collective-permute-start.6 = (f32[40,128]{1,0:T(8,128)S(1)}, f32[40,128]{1,0:T(8,128)S(1)}, u32[]{:S(2)}, u32[]{:S(2)}) collective-permute-start(f32[40,128]{1,0:T(8,128)S(1)} %gram.1), channel_id=1, source_target_pairs={{0,4},{1,7},{2,6},{3,5},{4,0},{5,3},{6,2},{7,1},{8,12},{9,15},{10,... | collective-permute-start | bytes 61448 | tf_op jit(solution)/shard_map/ppermute | solution.py:337
  23.5 3.8 %collective-permute-start.7 = (f32[40,128]{1,0:T(8,128)S(1)}, f32[40,128]{1,0:T(8,128)S(1)}, u32[]{:S(2)}, u32[]{:S(2)}) collective-permute-start(f32[40,128]{1,0:T(8,128)S(1)} %gram.1), channel_id=1, source_target_pairs={{0,2},{2,0},{4,6},{6,4},{8,10},{10,8},{12,14},{14,12},{1,3},{3,1},... | collective-permute-start | bytes 61448 | tf_op jit(solution)/shard_map/ppermute | solution.py:343
  27.3 1.2 %collective-permute-start.8 = (f32[40,128]{1,0:T(8,128)S(1)}, f32[40,128]{1,0:T(8,128)S(1)}, u32[]{:S(2)}, u32[]{:S(2)}) collective-permute-start(f32[40,128]{1,0:T(8,128)S(1)} %select_add_fusion.x_ref), channel_id=1, source_target_pairs={{0,1},{1,0},{2,3},{3,2},{4,5},{5,4},{6,7},{7,6},{8,9},{9,8},{10,11... | collective-permute-start | bytes 61448 | tf_op jit(solution)/shard_map/ppermute | solution.py:329

commit v19 on v17

--- a/solution.py
+++ b/solution.py
@@ -13,7 +13,6 @@
 FLIGHT = 7
 SHARED = 1
 NT = (((1,), (1,)), ((), ()))
-HIGHEST = lax.Precision.HIGHEST
 VMEM = pl.BlockSpec(memory_space=pltpu.VMEM)
 HBM = pl.BlockSpec(memory_space=pltpu.HBM)
 
@@ -33,16 +32,17 @@
     return [(2 * sum(sizes[:i]), 2 * size) for i, size in enumerate(sizes)]
 
 
-def project_kernel(g_chunks, h_chunks, h_ref, g_ref, pin_ref, pout_ref, out_ref, h_buf, g_buf, pin_buf, pout_buf, sems):
-    plan = [(pout_ref, pout_buf, g_ref, g_buf, at) for at in g_chunks] + [(pin_ref, pin_buf, h_ref, h_buf, at) for at in h_chunks]
+def project_kernel(g_chunks, h_chunks, h_ref, g_ref, pin_ref, pout_ref, out_ref, *refs):
+    bufs, sems = refs[:-1], refs[-1]
+    plan = [(pout_ref, g_ref, at) for at in g_chunks] + [(pin_ref, h_ref, at) for at in h_chunks]
     copies = []
-    for i, (proj, proj_buf, data, data_buf, (start, size)) in enumerate(plan):
+    for i, (proj, data, (start, size)) in enumerate(plan):
         at = pl.ds(start, size)
-        copies.append([
-            pltpu.make_async_copy(src.at[:, h, at], dst.at[:, at, pl.ds(8 * h, 8)], sems.at[4 * i + 2 * j + h])
-            for j, (src, dst) in enumerate(((proj, proj_buf), (data, data_buf)))
-            for h in range(2)
-        ])
+        copies.append([])
+        for j, src in enumerate((proj, data)):
+            for h in range(2):
+                dst = bufs[4 * i + 2 * j + h].at[:, pl.ds(h, size)]
+                copies[-1].append(pltpu.make_async_copy(src.at[:, h, at], dst, sems.at[4 * i + 2 * j + h]))
 
     def start(i):
         if i < len(copies):
@@ -52,21 +52,38 @@
     for i in range(FLIGHT):
         start(i)
 
-    def line_up(ref, first, size):
-        blocks = [ref[:, j].reshape(ref.shape[0] * 16, LANES) for j in range(first, first + size)]
-        return jnp.concatenate(blocks, axis=1)
-
-    totals = [None, None]
-    for i, (_, proj_buf, _, data_buf, (first, size)) in enumerate(plan):
+    def line_up(one_ref, two_ref):
+        groups, count = one_ref.shape[0], one_ref.shape[1] // 2
+        one_ref = one_ref.reshape(groups, count, 16, LANES)
+        two_ref = two_ref.reshape(groups, count + 1, 16, LANES)
+        top = lax.broadcasted_iota(jnp.int32, (groups, 16, LANES), 1) < 8
+        one = [one_ref[:, k] for k in range(count)]
+        two = [two_ref[:, k] for k in range(count + 1)]
+        even = [jnp.where(top, one[k], two[k]).reshape(groups * 16, LANES) for k in range(count)]
+        odd = [jnp.where(top, two[k + 1], one[k]).reshape(groups * 16, LANES) for k in range(count)]
+        return jnp.concatenate(even, axis=1), jnp.concatenate(odd, axis=1)
+
+    totals = [[None, None], [None, None]]
+    for i in range(len(plan)):
         for copy in copies[i]:
             copy.wait()
         start(i + FLIGHT)
-        which = 0 if i < len(g_chunks) else 1
-        part = lax.dot_general(
-            line_up(proj_buf, first, size), line_up(data_buf, first, size), NT, preferred_element_type=jnp.float32
-        )
-        totals[which] = part if totals[which] is None else totals[which] + part
-    out_ref[...] = jnp.concatenate(totals, axis=0)
+        total = totals[0 if i < len(g_chunks) else 1]
+        sides = zip(line_up(*bufs[4 * i:4 * i + 2]), line_up(*bufs[4 * i + 2:4 * i + 4]))
+        for j, (proj, data) in enumerate(sides):
+            part = lax.dot_general(proj, data, NT, preferred_element_type=jnp.float32)
+            total[j] = part if total[j] is None else total[j] + part
+
+    lane = lax.broadcasted_iota(jnp.int32, (8, LANES), 1)
+    first = lane % 16 < 8
+    done = 0
+    for even, odd in totals:
+        for g in range(0, even.shape[0], 8):
+            for i in range(0, even.shape[1], LANES):
+                line = odd[g ^ 8:(g ^ 8) + 8, i:i + LANES]
+                line = jnp.where(first, pltpu.roll(line, LANES - 8, 1), pltpu.roll(line, 8, 1))
+                out_ref[done:done + 8, i:i + LANES] = even[g:g + 8, i:i + LANES] + line
+            done += 8
 
 
 def project(hidden, out_grad, pin_t, pout_t):
@@ -76,13 +93,19 @@
     operands = [tiles(x) for x in (hidden, out_grad, pin_t, pout_t)]
     g_chunks = chunks_of(operands[1].shape[2] // 2, (1, 2, 3, 4), ())
     h_chunks = chunks_of(operands[0].shape[2] // 2, (), (4, 2, 2))
+    bufs = [
+        pltpu.VMEM((x.shape[0], size + 2 * h, 8, LANES), x.dtype)
+        for chunks, pair in ((g_chunks, (operands[3], operands[1])), (h_chunks, (operands[2], operands[0])))
+        for _, size in chunks
+        for x in pair
+        for h in range(2)
+    ]
     return pl.pallas_call(
         functools.partial(project_kernel, g_chunks, h_chunks),
         out_shape=jax.ShapeDtypeStruct((ranks, tokens), jnp.float32),
         in_specs=[HBM] * 4,
         out_specs=VMEM,
-        scratch_shapes=[pltpu.VMEM((x.shape[0], x.shape[2], 16, LANES), x.dtype) for x in operands]
-        + [pltpu.SemaphoreType.DMA((4 * len(g_chunks + h_chunks),))],
+        scratch_shapes=bufs + [pltpu.SemaphoreType.DMA((len(bufs),))],
         compiler_params=vmem_params(53.5),
         cost_estimate=pl.CostEstimate(
             flops=2 * tokens * 64 * (units + width),
@@ -268,7 +291,7 @@
         pivot, line = wide[r], rows[r]
         scale_rows = jnp.ones((size, cols), jnp.float32)
         for j in range(size):
-            inverse = pltpu.reciprocal(pivot[j][j:j + 1], full_range=False)
+            inverse = 1.0 / pivot[j][j:j + 1]
             factor = jnp.where(here == j, 0.0, pivot[j]) * inverse
             pivot = [x if i <= j else x - factor * x[j:j + 1] for i, x in enumerate(pivot)]
             line = line - factor * line[j:j + 1]

time: 32.6 us -> 31.2 us (0.957)
  Pallas kernels: 11.8 us -> 10.4 us
    pallas_call x1, Pallas kernels: 7.11 us -> 5.72 us  [project(): pl.pallas_call(functools.partial(project_kernel, g_chunks, h_chunks), out...]
where the time goes in v19:
time: 31.2 us; the launch traced here: 31.1 us
  Pallas kernels  10.4 us (33%)
  starting transfers between devices  10.4 us (33%)
  waiting for transfers between devices  9.86 us (32%)
    ppermute x4, starting transfers between devices, trade(): got.append(lax.ppermute(x, ('dp', 'tensor'), pairs))  7.06 us
    pallas_call x1, Pallas kernels, project(): pl.pallas_call(functools.partial(project_kernel, g_chunks, h_chunks), out...  5.72 us
    ppermute x2, waiting for transfers between devices, trade_shared(): return lax.ppermute(x, 'dp', [(i, i ^ SHARED) for i in range(dp)])  4.29 us
    ppermute x3, waiting for transfers between devices, swap_cores(): return lax.ppermute(x, 'tensor', [(i, cores - 1 - i) for i in range(cores)])  3.32 us
    ppermute x2, starting transfers between devices, trade_shared(): return lax.ppermute(x, 'dp', [(i, i ^ SHARED) for i in range(dp)])  2.65 us
    pallas_call x1, Pallas kernels, solve(): pl.pallas_call(functools.partial(solve_kernel, docs, queries, scale), out...  2.46 us
    ppermute x4, waiting for transfers between devices, trade(): got.append(lax.ppermute(x, ('dp', 'tensor'), pairs))  2.25 us
    pallas_call x2, Pallas kernels, grads_of(): pl.pallas_call(functools.partial(grads_kernel, rows_a, rows_b, docs, dp,...  1.73 us
  transfers between devices with their start and end apart: 9, of which 7 were waited for; matrix products, arithmetic and copies ran while one was open for 1% of the time, Pallas kernels for 4%

profile of v19, /device:TPU:0, one launch (start us, length us, event | category | flops | bytes accessed | tf_op | source)
XLA Modules:
  0.0 31.1 jit_solution(14895412597745759526)
XLA Ops:
  0.0 0.0 copy-start.1
  0.0 0.0 copy-start
  0.0 5.7 %project.1.part_ref = f32[128,256]{1,0:T(8,128)S(1)} custom-call(bf16[16,2,112,8,128]{4,3,2,1,0:T(8,128)(2,1)} %bitcast.24, bf16[16,2,32,8,128]{4,3,2,1,0:T(8,128)(2,1)} %bitcast.25, bf16[4,2,112,8,128]{4,3,2,1,0:T(8,128)(2,1)} %bitcast.26, bf16[4,2,32,8,128]{4,3,2,1,0:T(8,128)(2,1)} %bitcast.27), custom_call_target="tpu_custom_call" | custom-call | flops 603979776 | bytes 11796480 | tf_op jit(solution)/shard_map/project/pallas_call | solution.py:103
  5.7 0.5 %collective-permute-start = (f32[128,256]{1,0:T(8,128)S(1)}, f32[128,256]{1,0:T(8,128)S(1)}, u32[]{:S(2)}, u32[]{:S(2)}) collective-permute-start(f32[128,256]{1,0:T(8,128)S(1)} %project.1.part_ref), channel_id=1, source_target_pairs={{0,1},{1,0},{2,3},{3,2},{4,5},{5,4},{6,7},{7,6},{8,9},{9,8},{10,11... | collective-permute-start | bytes 393224 | tf_op jit(solution)/shard_map/ppermute | solution.py:335
  6.2 0.0 copy-done.1
  6.3 0.0 copy-done
  6.3 0.2 reshape.25
  6.4 0.1 reshape.26
  6.6 0.7 %collective-permute-done.recv_ref = f32[128,256]{1,0:T(8,128)S(1)} collective-permute-done((f32[128,256]{1,0:T(8,128)S(1)}, f32[128,256]{1,0:T(8,128)S(1)}, u32[]{:S(2)}, u32[]{:S(2)}) %collective-permute-start) | collective-permute-done | bytes 131104 | tf_op jit(solution)/shard_map/ppermute | solution.py:335
  7.2 0.1 pack.1
  7.3 4.0 %collective-permute-start.2 = (f32[152,128]{1,0:T(8,128)S(1)}, f32[152,128]{1,0:T(8,128)S(1)}, u32[]{:S(2)}, u32[]{:S(2)}) collective-permute-start(f32[152,128]{1,0:T(8,128)S(1)} %get-tuple-element.11), channel_id=1, source_target_pairs={{0,8},{1,11},{2,10},{3,9},{4,12},{5,15},{6,14},{7,13},{8,0},{9,3},... | collective-permute-start | bytes 233480 | tf_op jit(solution)/shard_map/ppermute | solution.py:343
  11.3 1.6 %collective-permute-start.3 = (f32[152,128]{1,0:T(8,128)S(1)}, f32[152,128]{1,0:T(8,128)S(1)}, u32[]{:S(2)}, u32[]{:S(2)}) collective-permute-start(f32[152,128]{1,0:T(8,128)S(1)} %get-tuple-element.12), channel_id=1, source_target_pairs={{0,4},{1,7},{2,6},{3,5},{4,0},{5,3},{6,2},{7,1},{8,12},{9,15},{10,... | collective-permute-start | bytes 233480 | tf_op jit(solution)/shard_map/ppermute | solution.py:343
  12.9 0.0 collective-permute-start.1
  12.9 1.7 %collective-permute-start.4 = (f32[80,128]{1,0:T(8,128)S(1)}, f32[80,128]{1,0:T(8,128)S(1)}, u32[]{:S(2)}, u32[]{:S(2)}) collective-permute-start(f32[80,128]{1,0:T(8,128)S(1)} %get-tuple-element.13), channel_id=1, source_target_pairs={{0,2},{2,0},{4,6},{6,4},{8,10},{10,8},{12,14},{14,12},{1,3},{3,1},... | collective-permute-start | bytes 122888 | tf_op jit(solution)/shard_map/ppermute | solution.py:349
  14.6 2.9 %collective-permute-done.4.refs_2_ = f32[80,128]{1,0:T(8,128)S(1)} collective-permute-done((f32[80,128]{1,0:T(8,128)S(1)}, f32[80,128]{1,0:T(8,128)S(1)}, u32[]{:S(2)}, u32[]{:S(2)}) %collective-permute-start.4) | collective-permute-done | bytes 40992 | tf_op jit(solution)/shard_map/ppermute | solution.py:349
  17.6 0.0 collective-permute-done.2.refs_0_
  17.6 0.0 collective-permute-done.3.refs_1_
  17.6 1.2 %grads.2.refs_1_ = f32[80,1024]{1,0:T(8,128)S(1)} custom-call(f32[152,128]{1,0:T(8,128)S(1)} %collective-permute-done.2.refs_0_, f32[152,128]{1,0:T(8,128)S(1)} %collective-permute-done.3.refs_1_, f32[80,128]{1,0:T(8,128)S(1)} %collective-permute-done.4.refs_2_, f32[80,128]{1,0:T(8,128)S(1)} %get-tuple-element.14.refs_3_), custom_call_target="tpu_custom_call" | custom-call | flops 201326592 | bytes 196608 | tf_op jit(solution)/shard_map/grads/pallas_call | solution.py:226
  18.8 0.7 %collective-permute-done.1.refs_0_ = f32[152,128]{1,0:T(8,128)S(1)} collective-permute-done((f32[152,128]{1,0:T(8,128)S(1)}, f32[152,128]{1,0:T(8,128)S(1)}, u32[]{:S(2)}, u32[]{:S(2)}) %collective-permute-start.1) | collective-permute-done | bytes 77856 | tf_op jit(solution)/shard_map/ppermute | solution.py:343
  19.5 0.5 %grads.3.part_ref = f32[80,1024]{1,0:T(8,128)S(1)} custom-call(f32[152,128]{1,0:T(8,128)S(1)} %collective-permute-done.1.refs_0_, f32[80,1024]{1,0:T(8,128)S(1)} %grads.2.refs_1_), custom_call_target="tpu_custom_call" | custom-call | flops 67108864 | bytes 65536 | tf_op jit(solution)/shard_map/grads/pallas_call | solution.py:226
  20.0 0.2 collective-permute-start.5
  20.3 1.5 %collective-permute-done.5.recv_ref = f32[80,1024]{1,0:T(8,128)S(1)} collective-permute-done((f32[80,1024]{1,0:T(8,128)S(1)}, f32[80,1024]{1,0:T(8,128)S(1)}, u32[]{:S(2)}, u32[]{:S(2)}) %collective-permute-start.5) | collective-permute-done | bytes 327712 | tf_op jit(solution)/shard_map/ppermute | solution.py:335
  21.7 0.4 %gram.1 = f32[40,128]{1,0:T(8,128)S(1)} custom-call(f32[80,1024]{1,0:T(8,128)S(1)} %grads.3.part_ref, f32[80,1024]{1,0:T(8,128)S(1)} %collective-permute-done.5.recv_ref), custom_call_target="tpu_custom_call" | custom-call | tf_op jit(solution)/shard_map/gram/pallas_call | solution.py:265
  22.2 1.5 %collective-permute-start.6 = (f32[40,128]{1,0:T(8,128)S(1)}, f32[40,128]{1,0:T(8,128)S(1)}, u32[]{:S(2)}, u32[]{:S(2)}) collective-permute-start(f32[40,128]{1,0:T(8,128)S(1)} %gram.1), channel_id=1, source_target_pairs={{0,4},{1,7},{2,6},{3,5},{4,0},{5,3},{6,2},{7,1},{8,12},{9,15},{10,... | collective-permute-start | bytes 61448 | tf_op jit(solution)/shard_map/ppermute | solution.py:343
  23.6 0.9 %collective-permute-start.7 = (f32[40,128]{1,0:T(8,128)S(1)}, f32[40,128]{1,0:T(8,128)S(1)}, u32[]{:S(2)}, u32[]{:S(2)}) collective-permute-start(f32[40,128]{1,0:T(8,128)S(1)} %gram.1), channel_id=1, source_target_pairs={{0,2},{2,0},{4,6},{6,4},{8,10},{10,8},{12,14},{14,12},{1,3},{3,1},... | collective-permute-start | bytes 61448 | tf_op jit(solution)/shard_map/ppermute | solution.py:349
  24.5 1.5 %collective-permute-done.6 = f32[40,128]{1,0:T(8,128)S(1)} collective-permute-done((f32[40,128]{1,0:T(8,128)S(1)}, f32[40,128]{1,0:T(8,128)S(1)}, u32[]{:S(2)}, u32[]{:S(2)}) %collective-permute-start.6) | collective-permute-done | bytes 20512 | tf_op jit(solution)/shard_map/ppermute | solution.py:343
  26.0 1.4 %collective-permute-done.7 = f32[40,128]{1,0:T(8,128)S(1)} collective-permute-done((f32[40,128]{1,0:T(8,128)S(1)}, f32[40,128]{1,0:T(8,128)S(1)}, u32[]{:S(2)}, u32[]{:S(2)}) %collective-permute-start.7) | collective-permute-done | bytes 20512 | tf_op jit(solution)/shard_map/ppermute | solution.py:349
  27.4 0.0 collective-permute-start.8
  27.4 1.2 %collective-permute-done.8.recv_ref = f32[40,128]{1,0:T(8,128)S(1)} collective-permute-done((f32[40,128]{1,0:T(8,128)S(1)}, f32[40,128]{1,0:T(8,128)S(1)}, u32[]{:S(2)}, u32[]{:S(2)}) %collective-permute-start.8) | collective-permute-done | bytes 20512 | tf_op jit(solution)/shard_map/ppermute | solution.py:335
  28.6 2.5 %solve.1 = f32[8,16]{1,0:T(8,128)} custom-call(f32[40,128]{1,0:T(8,128)S(1)} %select_add_fusion.x_ref, f32[40,128]{1,0:T(8,128)S(1)} %collective-permute-done.8.recv_ref), custom_call_target="tpu_custom_call" | custom-call | tf_op jit(solution)/shard_map/solve/pallas_call | solution.py:314
  (5 shorter events, 0.0 us)
Async XLA Ops:
  0.0 6.2 %copy-start.1 = (s32[256]{0:T(256)S(1)}, s32[256]{0:T(256)}, u32[]{:S(2)}) copy-start(s32[256]{0:T(256)} %param.10) | copy-start | bytes 3076
  0.0 6.3 %copy-start = (f32[2,4096]{1,0:T(2,128)S(1)}, f32[2,4096]{1,0:T(2,128)}, u32[]{:S(2)}) copy-start(f32[2,4096]{1,0:T(2,128)} %param.11) | copy-start | bytes 98308
  5.7 1.5 %collective-permute-start = (f32[128,256]{1,0:T(8,128)S(1)}, f32[128,256]{1,0:T(8,128)S(1)}, u32[]{:S(2)}, u32[]{:S(2)}) collective-permute-start(f32[128,256]{1,0:T(8,128)S(1)} %project.1.part_ref), channel_id=1, source_target_pairs={{0,1},{1,0},{2,3},{3,2},{4,5},{5,4},{6,7},{7,6},{8,9},{9,8},{10,11... | collective-permute-start | bytes 393224 | tf_op jit(solution)/shard_map/ppermute | solution.py:335
  7.3 10.2 %collective-permute-start.2 = (f32[152,128]{1,0:T(8,128)S(1)}, f32[152,128]{1,0:T(8,128)S(1)}, u32[]{:S(2)}, u32[]{:S(2)}) collective-permute-start(f32[152,128]{1,0:T(8,128)S(1)} %get-tuple-element.11), channel_id=1, source_target_pairs={{0,8},{1,11},{2,10},{3,9},{4,12},{5,15},{6,14},{7,13},{8,0},{9,3},... | collective-permute-start | bytes 233480 | tf_op jit(solution)/shard_map/ppermute | solution.py:343
  11.3 6.2 %collective-permute-start.3 = (f32[152,128]{1,0:T(8,128)S(1)}, f32[152,128]{1,0:T(8,128)S(1)}, u32[]{:S(2)}, u32[]{:S(2)}) collective-permute-start(f32[152,128]{1,0:T(8,128)S(1)} %get-tuple-element.12), channel_id=1, source_target_pairs={{0,4},{1,7},{2,6},{3,5},{4,0},{5,3},{6,2},{7,1},{8,12},{9,15},{10,... | collective-permute-start | bytes 233480 | tf_op jit(solution)/shard_map/ppermute | solution.py:343
  12.9 6.6 %collective-permute-start.1 = (f32[152,128]{1,0:T(8,128)S(1)}, f32[152,128]{1,0:T(8,128)S(1)}, u32[]{:S(2)}, u32[]{:S(2)}) collective-permute-start(f32[152,128]{1,0:T(8,128)S(1)} %get-tuple-element.10), channel_id=1, source_target_pairs={{0,12},{1,15},{2,14},{3,13},{4,8},{5,11},{6,10},{7,9},{8,4},{9,7},... | collective-permute-start | bytes 233480 | tf_op jit(solution)/shard_map/ppermute | solution.py:343
  12.9 4.7 %collective-permute-start.4 = (f32[80,128]{1,0:T(8,128)S(1)}, f32[80,128]{1,0:T(8,128)S(1)}, u32[]{:S(2)}, u32[]{:S(2)}) collective-permute-start(f32[80,128]{1,0:T(8,128)S(1)} %get-tuple-element.13), channel_id=1, source_target_pairs={{0,2},{2,0},{4,6},{6,4},{8,10},{10,8},{12,14},{14,12},{1,3},{3,1},... | collective-permute-start | bytes 122888 | tf_op jit(solution)/shard_map/ppermute | solution.py:349
  20.0 1.7 %collective-permute-start.5 = (f32[80,1024]{1,0:T(8,128)S(1)}, f32[80,1024]{1,0:T(8,128)S(1)}, u32[]{:S(2)}, u32[]{:S(2)}) collective-permute-start(f32[80,1024]{1,0:T(8,128)S(1)} %grads.3.part_ref), channel_id=1, source_target_pairs={{0,1},{1,0},{2,3},{3,2},{4,5},{5,4},{6,7},{7,6},{8,9},{9,8},{10,11... | collective-permute-start | bytes 983048 | tf_op jit(solution)/shard_map/ppermute | solution.py:335
  22.2 3.9 %collective-permute-start.6 = (f32[40,128]{1,0:T(8,128)S(1)}, f32[40,128]{1,0:T(8,128)S(1)}, u32[]{:S(2)}, u32[]{:S(2)}) collective-permute-start(f32[40,128]{1,0:T(8,128)S(1)} %gram.1), channel_id=1, source_target_pairs={{0,4},{1,7},{2,6},{3,5},{4,0},{5,3},{6,2},{7,1},{8,12},{9,15},{10,... | collective-permute-start | bytes 61448 | tf_op jit(solution)/shard_map/ppermute | solution.py:343
  23.6 3.8 %collective-permute-start.7 = (f32[40,128]{1,0:T(8,128)S(1)}, f32[40,128]{1,0:T(8,128)S(1)}, u32[]{:S(2)}, u32[]{:S(2)}) collective-permute-start(f32[40,128]{1,0:T(8,128)S(1)} %gram.1), channel_id=1, source_target_pairs={{0,2},{2,0},{4,6},{6,4},{8,10},{10,8},{12,14},{14,12},{1,3},{3,1},... | collective-permute-start | bytes 61448 | tf_op jit(solution)/shard_map/ppermute | solution.py:349
  27.4 1.2 %collective-permute-start.8 = (f32[40,128]{1,0:T(8,128)S(1)}, f32[40,128]{1,0:T(8,128)S(1)}, u32[]{:S(2)}, u32[]{:S(2)}) collective-permute-start(f32[40,128]{1,0:T(8,128)S(1)} %select_add_fusion.x_ref), channel_id=1, source_target_pairs={{0,1},{1,0},{2,3},{3,2},{4,5},{5,4},{6,7},{7,6},{8,9},{9,8},{10,11... | collective-permute-start | bytes 61448 | tf_op jit(solution)/shard_map/ppermute | solution.py:335

commit v20 on v18

--- a/solution.py
+++ b/solution.py
@@ -10,7 +10,7 @@
 TOK_DEV = 256
 DOC_DEV = 8
 LANES = 128
-FLIGHT = 7
+FLIGHT = 10
 SHARED = 1
 NT = (((1,), (1,)), ((), ()))
 VMEM = pl.BlockSpec(memory_space=pltpu.VMEM)
@@ -282,20 +282,26 @@
     rows = [work[i:i + size] for i in range(0, docs, size)]
     for r in range(len(rows)):
         wide = [[jnp.broadcast_to(x[:, c:c + 1], (size, cols)) for c in range(r * size, (r + 1) * size)] for x in rows]
-        pivot, line = wide[r], rows[r]
-        scale_rows = jnp.ones((size, cols), jnp.float32)
+        pivot = [[jnp.broadcast_to(x[i:i + 1], (size, cols)) for x in wide[r]] for i in range(size)]
+        line = [jnp.broadcast_to(rows[r][i:i + 1], (size, cols)) for i in range(size)]
+        inverses = []
         for j in range(size):
-            inverse = 1.0 / pivot[j][j:j + 1]
-            factor = jnp.where(here == j, 0.0, pivot[j]) * inverse
-            pivot = [x if i <= j else x - factor * x[j:j + 1] for i, x in enumerate(pivot)]
-            line = line - factor * line[j:j + 1]
-            scale_rows = jnp.where(here == j, inverse, scale_rows)
-        line = line * scale_rows
+            inverse = 1.0 / pivot[j][j]
+            inverses.append(inverse)
+            for i in range(size):
+                if i != j:
+                    factor = pivot[i][j] * inverse
+                    for k in range(j + 1, size):
+                        pivot[i][k] = pivot[i][k] - factor * pivot[j][k]
+                    line[i] = line[i] - factor * line[j]
+        line = [x * inverse for x, inverse in zip(line, inverses)]
         for s in range(len(rows)):
             if s == r:
-                rows[s] = line
+                rows[s] = line[0]
+                for j in range(1, size):
+                    rows[s] = jnp.where(here == j, line[j], rows[s])
             else:
-                terms = [wide[s][j] * line[j:j + 1] for j in range(size)]
+                terms = [wide[s][j] * line[j] for j in range(size)]
                 rows[s] = rows[s] - (((terms[0] + terms[1]) + (terms[2] + terms[3]))
                                      + ((terms[4] + terms[5]) + (terms[6] + terms[7])))
     for r, x in enumerate(rows):

time: 31.1 us -> 32 us (1.029)
  Pallas kernels: 10.3 us -> 11.2 us
    pallas_call x1, Pallas kernels: 2.46 us -> 3.42 us  [solve(): pl.pallas_call(functools.partial(solve_kernel, docs, queries, scale), out...]
where the time goes in v20:
time: 32 us; the launch traced here: 31.9 us
  Pallas kernels  11.2 us (35%)
  starting transfers between devices  10.5 us (33%)
  waiting for transfers between devices  9.85 us (31%)
    ppermute x4, starting transfers between devices, trade(): got.append(lax.ppermute(x, ('dp', 'tensor'), pairs))  7.06 us
    pallas_call x1, Pallas kernels, project(): pl.pallas_call(functools.partial(project_kernel, g_chunks, h_chunks), out...  5.58 us
    ppermute x2, waiting for transfers between devices, trade_shared(): return lax.ppermute(x, 'dp', [(i, i ^ SHARED) for i in range(dp)])  4.32 us
    pallas_call x1, Pallas kernels, solve(): pl.pallas_call(functools.partial(solve_kernel, docs, queries, scale), out...  3.42 us
    ppermute x3, waiting for transfers between devices, swap_cores(): return lax.ppermute(x, 'tensor', [(i, cores - 1 - i) for i in range(cores)])  3.32 us
    ppermute x2, starting transfers between devices, trade_shared(): return lax.ppermute(x, 'dp', [(i, i ^ SHARED) for i in range(dp)])  2.65 us
    ppermute x4, waiting for transfers between devices, trade(): got.append(lax.ppermute(x, ('dp', 'tensor'), pairs))  2.22 us
    pallas_call x2, Pallas kernels, grads_of(): pl.pallas_call(functools.partial(grads_kernel, rows_a, rows_b, docs, dp,...  1.73 us
  transfers between devices with their start and end apart: 9, of which 7 were waited for; matrix products, arithmetic and copies ran while one was open for 1% of the time, Pallas kernels for 4%

profile of v20, /device:TPU:0, one launch (start us, length us, event | category | flops | bytes accessed | tf_op | source)
XLA Modules:
  0.0 31.9 jit_solution(11923508799984719071)
XLA Ops:
  0.0 0.0 copy-start.1
  0.0 0.0 copy-start
  0.0 5.6 %project.1.part_ref = f32[128,256]{1,0:T(8,128)S(1)} custom-call(bf16[32,56,16,128]{3,2,1,0:T(8,128)(2,1)} %bitcast.32, bf16[32,16,16,128]{3,2,1,0:T(8,128)(2,1)} %bitcast.33, bf16[8,56,16,128]{3,2,1,0:T(8,128)(2,1)} %bitcast.34, bf16[8,16,16,128]{3,2,1,0:T(8,128)(2,1)} %bitcast.35), custom_call_target="tpu_custom_call" | custom-call | flops 603979776 | bytes 11796480 | tf_op jit(solution)/shard_map/project/pallas_call | solution.py:96
  5.6 0.5 %collective-permute-start = (f32[128,256]{1,0:T(8,128)S(1)}, f32[128,256]{1,0:T(8,128)S(1)}, u32[]{:S(2)}, u32[]{:S(2)}) collective-permute-start(f32[128,256]{1,0:T(8,128)S(1)} %project.1.part_ref), channel_id=1, source_target_pairs={{0,1},{1,0},{2,3},{3,2},{4,5},{5,4},{6,7},{7,6},{8,9},{9,8},{10,11... | collective-permute-start | bytes 393224 | tf_op jit(solution)/shard_map/ppermute | solution.py:335
  6.1 0.0 copy-done.1
  6.1 0.0 copy-done
  6.1 0.2 reshape.41
  6.3 0.1 reshape.42
  6.4 0.7 %collective-permute-done.recv_ref = f32[128,256]{1,0:T(8,128)S(1)} collective-permute-done((f32[128,256]{1,0:T(8,128)S(1)}, f32[128,256]{1,0:T(8,128)S(1)}, u32[]{:S(2)}, u32[]{:S(2)}) %collective-permute-start) | collective-permute-done | bytes 131104 | tf_op jit(solution)/shard_map/ppermute | solution.py:335
  7.1 0.1 pack.1
  7.2 4.0 %collective-permute-start.2 = (f32[152,128]{1,0:T(8,128)S(1)}, f32[152,128]{1,0:T(8,128)S(1)}, u32[]{:S(2)}, u32[]{:S(2)}) collective-permute-start(f32[152,128]{1,0:T(8,128)S(1)} %get-tuple-element.11), channel_id=1, source_target_pairs={{0,8},{1,11},{2,10},{3,9},{4,12},{5,15},{6,14},{7,13},{8,0},{9,3},... | collective-permute-start | bytes 233480 | tf_op jit(solution)/shard_map/ppermute | solution.py:343
  11.2 1.6 %collective-permute-start.3 = (f32[152,128]{1,0:T(8,128)S(1)}, f32[152,128]{1,0:T(8,128)S(1)}, u32[]{:S(2)}, u32[]{:S(2)}) collective-permute-start(f32[152,128]{1,0:T(8,128)S(1)} %get-tuple-element.12), channel_id=1, source_target_pairs={{0,4},{1,7},{2,6},{3,5},{4,0},{5,3},{6,2},{7,1},{8,12},{9,15},{10,... | collective-permute-start | bytes 233480 | tf_op jit(solution)/shard_map/ppermute | solution.py:343
  12.8 0.0 collective-permute-start.1
  12.8 1.7 %collective-permute-start.4 = (f32[80,128]{1,0:T(8,128)S(1)}, f32[80,128]{1,0:T(8,128)S(1)}, u32[]{:S(2)}, u32[]{:S(2)}) collective-permute-start(f32[80,128]{1,0:T(8,128)S(1)} %get-tuple-element.13), channel_id=1, source_target_pairs={{0,2},{2,0},{4,6},{6,4},{8,10},{10,8},{12,14},{14,12},{1,3},{3,1},... | collective-permute-start | bytes 122888 | tf_op jit(solution)/shard_map/ppermute | solution.py:349
  14.5 2.9 %collective-permute-done.4.refs_2_ = f32[80,128]{1,0:T(8,128)S(1)} collective-permute-done((f32[80,128]{1,0:T(8,128)S(1)}, f32[80,128]{1,0:T(8,128)S(1)}, u32[]{:S(2)}, u32[]{:S(2)}) %collective-permute-start.4) | collective-permute-done | bytes 40992 | tf_op jit(solution)/shard_map/ppermute | solution.py:349
  17.4 0.0 collective-permute-done.2.refs_0_
  17.4 0.0 collective-permute-done.3.refs_1_
  17.4 1.2 %grads.2.refs_1_ = f32[80,1024]{1,0:T(8,128)S(1)} custom-call(f32[152,128]{1,0:T(8,128)S(1)} %collective-permute-done.2.refs_0_, f32[152,128]{1,0:T(8,128)S(1)} %collective-permute-done.3.refs_1_, f32[80,128]{1,0:T(8,128)S(1)} %collective-permute-done.4.refs_2_, f32[80,128]{1,0:T(8,128)S(1)} %get-tuple-element.14.refs_3_), custom_call_target="tpu_custom_call" | custom-call | flops 201326592 | bytes 196608 | tf_op jit(solution)/shard_map/grads/pallas_call | solution.py:220
  18.6 0.7 %collective-permute-done.1.refs_0_ = f32[152,128]{1,0:T(8,128)S(1)} collective-permute-done((f32[152,128]{1,0:T(8,128)S(1)}, f32[152,128]{1,0:T(8,128)S(1)}, u32[]{:S(2)}, u32[]{:S(2)}) %collective-permute-start.1) | collective-permute-done | bytes 77856 | tf_op jit(solution)/shard_map/ppermute | solution.py:343
  19.4 0.5 %grads.3.part_ref = f32[80,1024]{1,0:T(8,128)S(1)} custom-call(f32[152,128]{1,0:T(8,128)S(1)} %collective-permute-done.1.refs_0_, f32[80,1024]{1,0:T(8,128)S(1)} %grads.2.refs_1_), custom_call_target="tpu_custom_call" | custom-call | flops 67108864 | bytes 65536 | tf_op jit(solution)/shard_map/grads/pallas_call | solution.py:220
  19.9 0.2 collective-permute-start.5
  20.1 1.5 %collective-permute-done.5.recv_ref = f32[80,1024]{1,0:T(8,128)S(1)} collective-permute-done((f32[80,1024]{1,0:T(8,128)S(1)}, f32[80,1024]{1,0:T(8,128)S(1)}, u32[]{:S(2)}, u32[]{:S(2)}) %collective-permute-start.5) | collective-permute-done | bytes 327712 | tf_op jit(solution)/shard_map/ppermute | solution.py:335
  21.6 0.4 %gram.1 = f32[40,128]{1,0:T(8,128)S(1)} custom-call(f32[80,1024]{1,0:T(8,128)S(1)} %grads.3.part_ref, f32[80,1024]{1,0:T(8,128)S(1)} %collective-permute-done.5.recv_ref), custom_call_target="tpu_custom_call" | custom-call | tf_op jit(solution)/shard_map/gram/pallas_call | solution.py:259
  22.0 1.5 %collective-permute-start.6 = (f32[40,128]{1,0:T(8,128)S(1)}, f32[40,128]{1,0:T(8,128)S(1)}, u32[]{:S(2)}, u32[]{:S(2)}) collective-permute-start(f32[40,128]{1,0:T(8,128)S(1)} %gram.1), channel_id=1, source_target_pairs={{0,4},{1,7},{2,6},{3,5},{4,0},{5,3},{6,2},{7,1},{8,12},{9,15},{10,... | collective-permute-start | bytes 61448 | tf_op jit(solution)/shard_map/ppermute | solution.py:343
  23.5 0.9 %collective-permute-start.7 = (f32[40,128]{1,0:T(8,128)S(1)}, f32[40,128]{1,0:T(8,128)S(1)}, u32[]{:S(2)}, u32[]{:S(2)}) collective-permute-start(f32[40,128]{1,0:T(8,128)S(1)} %gram.1), channel_id=1, source_target_pairs={{0,2},{2,0},{4,6},{6,4},{8,10},{10,8},{12,14},{14,12},{1,3},{3,1},... | collective-permute-start | bytes 61448 | tf_op jit(solution)/shard_map/ppermute | solution.py:349
  24.4 1.5 %collective-permute-done.6 = f32[40,128]{1,0:T(8,128)S(1)} collective-permute-done((f32[40,128]{1,0:T(8,128)S(1)}, f32[40,128]{1,0:T(8,128)S(1)}, u32[]{:S(2)}, u32[]{:S(2)}) %collective-permute-start.6) | collective-permute-done | bytes 20512 | tf_op jit(solution)/shard_map/ppermute | solution.py:343
  25.9 1.4 %collective-permute-done.7 = f32[40,128]{1,0:T(8,128)S(1)} collective-permute-done((f32[40,128]{1,0:T(8,128)S(1)}, f32[40,128]{1,0:T(8,128)S(1)}, u32[]{:S(2)}, u32[]{:S(2)}) %collective-permute-start.7) | collective-permute-done | bytes 20512 | tf_op jit(solution)/shard_map/ppermute | solution.py:349
  27.3 0.0 collective-permute-start.8
  27.3 1.2 %collective-permute-done.8.recv_ref = f32[40,128]{1,0:T(8,128)S(1)} collective-permute-done((f32[40,128]{1,0:T(8,128)S(1)}, f32[40,128]{1,0:T(8,128)S(1)}, u32[]{:S(2)}, u32[]{:S(2)}) %collective-permute-start.8) | collective-permute-done | bytes 20512 | tf_op jit(solution)/shard_map/ppermute | solution.py:335
  28.5 3.4 %solve.1 = f32[8,16]{1,0:T(8,128)} custom-call(f32[40,128]{1,0:T(8,128)S(1)} %select_add_fusion.x_ref, f32[40,128]{1,0:T(8,128)S(1)} %collective-permute-done.8.recv_ref), custom_call_target="tpu_custom_call" | custom-call | tf_op jit(solution)/shard_map/solve/pallas_call | solution.py:314
  (5 shorter events, 0.0 us)
Async XLA Ops:
  0.0 6.1 %copy-start.1 = (s32[256]{0:T(256)S(1)}, s32[256]{0:T(256)}, u32[]{:S(2)}) copy-start(s32[256]{0:T(256)} %param.10) | copy-start | bytes 3076
  0.0 6.1 %copy-start = (f32[2,4096]{1,0:T(2,128)S(1)}, f32[2,4096]{1,0:T(2,128)}, u32[]{:S(2)}) copy-start(f32[2,4096]{1,0:T(2,128)} %param.11) | copy-start | bytes 98308
  5.6 1.5 %collective-permute-start = (f32[128,256]{1,0:T(8,128)S(1)}, f32[128,256]{1,0:T(8,128)S(1)}, u32[]{:S(2)}, u32[]{:S(2)}) collective-permute-start(f32[128,256]{1,0:T(8,128)S(1)} %project.1.part_ref), channel_id=1, source_target_pairs={{0,1},{1,0},{2,3},{3,2},{4,5},{5,4},{6,7},{7,6},{8,9},{9,8},{10,11... | collective-permute-start | bytes 393224 | tf_op jit(solution)/shard_map/ppermute | solution.py:335
  7.2 10.2 %collective-permute-start.2 = (f32[152,128]{1,0:T(8,128)S(1)}, f32[152,128]{1,0:T(8,128)S(1)}, u32[]{:S(2)}, u32[]{:S(2)}) collective-permute-start(f32[152,128]{1,0:T(8,128)S(1)} %get-tuple-element.11), channel_id=1, source_target_pairs={{0,8},{1,11},{2,10},{3,9},{4,12},{5,15},{6,14},{7,13},{8,0},{9,3},... | collective-permute-start | bytes 233480 | tf_op jit(solution)/shard_map/ppermute | solution.py:343
  11.2 6.2 %collective-permute-start.3 = (f32[152,128]{1,0:T(8,128)S(1)}, f32[152,128]{1,0:T(8,128)S(1)}, u32[]{:S(2)}, u32[]{:S(2)}) collective-permute-start(f32[152,128]{1,0:T(8,128)S(1)} %get-tuple-element.12), channel_id=1, source_target_pairs={{0,4},{1,7},{2,6},{3,5},{4,0},{5,3},{6,2},{7,1},{8,12},{9,15},{10,... | collective-permute-start | bytes 233480 | tf_op jit(solution)/shard_map/ppermute | solution.py:343
  12.8 6.6 %collective-permute-start.1 = (f32[152,128]{1,0:T(8,128)S(1)}, f32[152,128]{1,0:T(8,128)S(1)}, u32[]{:S(2)}, u32[]{:S(2)}) collective-permute-start(f32[152,128]{1,0:T(8,128)S(1)} %get-tuple-element.10), channel_id=1, source_target_pairs={{0,12},{1,15},{2,14},{3,13},{4,8},{5,11},{6,10},{7,9},{8,4},{9,7},... | collective-permute-start | bytes 233480 | tf_op jit(solution)/shard_map/ppermute | solution.py:343
  12.8 4.7 %collective-permute-start.4 = (f32[80,128]{1,0:T(8,128)S(1)}, f32[80,128]{1,0:T(8,128)S(1)}, u32[]{:S(2)}, u32[]{:S(2)}) collective-permute-start(f32[80,128]{1,0:T(8,128)S(1)} %get-tuple-element.13), channel_id=1, source_target_pairs={{0,2},{2,0},{4,6},{6,4},{8,10},{10,8},{12,14},{14,12},{1,3},{3,1},... | collective-permute-start | bytes 122888 | tf_op jit(solution)/shard_map/ppermute | solution.py:349
  19.9 1.7 %collective-permute-start.5 = (f32[80,1024]{1,0:T(8,128)S(1)}, f32[80,1024]{1,0:T(8,128)S(1)}, u32[]{:S(2)}, u32[]{:S(2)}) collective-permute-start(f32[80,1024]{1,0:T(8,128)S(1)} %grads.3.part_ref), channel_id=1, source_target_pairs={{0,1},{1,0},{2,3},{3,2},{4,5},{5,4},{6,7},{7,6},{8,9},{9,8},{10,11... | collective-permute-start | bytes 983048 | tf_op jit(solution)/shard_map/ppermute | solution.py:335
  22.0 3.9 %collective-permute-start.6 = (f32[40,128]{1,0:T(8,128)S(1)}, f32[40,128]{1,0:T(8,128)S(1)}, u32[]{:S(2)}, u32[]{:S(2)}) collective-permute-start(f32[40,128]{1,0:T(8,128)S(1)} %gram.1), channel_id=1, source_target_pairs={{0,4},{1,7},{2,6},{3,5},{4,0},{5,3},{6,2},{7,1},{8,12},{9,15},{10,... | collective-permute-start | bytes 61448 | tf_op jit(solution)/shard_map/ppermute | solution.py:343
  23.5 3.8 %collective-permute-start.7 = (f32[40,128]{1,0:T(8,128)S(1)}, f32[40,128]{1,0:T(8,128)S(1)}, u32[]{:S(2)}, u32[]{:S(2)}) collective-permute-start(f32[40,128]{1,0:T(8,128)S(1)} %gram.1), channel_id=1, source_target_pairs={{0,2},{2,0},{4,6},{6,4},{8,10},{10,8},{12,14},{14,12},{1,3},{3,1},... | collective-permute-start | bytes 61448 | tf_op jit(solution)/shard_map/ppermute | solution.py:349
  27.3 1.2 %collective-permute-start.8 = (f32[40,128]{1,0:T(8,128)S(1)}, f32[40,128]{1,0:T(8,128)S(1)}, u32[]{:S(2)}, u32[]{:S(2)}) collective-permute-start(f32[40,128]{1,0:T(8,128)S(1)} %select_add_fusion.x_ref), channel_id=1, source_target_pairs={{0,1},{1,0},{2,3},{3,2},{4,5},{5,4},{6,7},{7,6},{8,9},{9,8},{10,11... | collective-permute-start | bytes 61448 | tf_op jit(solution)/shard_map/ppermute | solution.py:335

commit v21 on v18

--- a/solution.py
+++ b/solution.py
@@ -367,10 +367,9 @@
     gaps = [*zip(*partners(dp)), (SHARED, SHARED), (0, 0)]
     wholes = [True] * (len(blocks) - 2) + [False, False]
     sizes = (rows_a, rows_b, docs, num_queries, dp)
-    late = min(1, len(blocks) - 3)
-    rest = [t for t in range(len(blocks)) if t != late]
+    count = len(blocks) - 2
     grads = ()
-    for part in (rest, [late]):
+    for part in ([count + 1, *range(2, count)], [0, count], [1]):
         grads = (grads_of(*([x[t] for t in part] for x in (blocks, gaps, wholes)), grads, *sizes),)
     grads = grads[0]
     share = gram(grads, swap_cores(grads), docs)

time: 31.1 us -> 32.2 us (1.035)
  starting transfers between devices: 10.4 us -> 11.7 us
  waiting for transfers between devices: 9.88 us -> 9.45 us
    ppermute x4, starting transfers between devices: 7.04 us -> 8.01 us  [trade(): got.append(lax.ppermute(x, ('dp', 'tensor'), pairs))]
    ppermute x2, waiting for transfers between devices: 4.26 us -> 3.84 us  [trade_shared(): return lax.ppermute(x, 'dp', [(i, i ^ SHARED) for i in range(dp)])]
    ppermute x2, starting transfers between devices: 2.64 us -> 2.97 us  [trade_shared(): return lax.ppermute(x, 'dp', [(i, i ^ SHARED) for i in range(dp)])]
    pallas_call x2 -> x3, Pallas kernels: 1.73 us -> 1.92 us  [grads_of(): pl.pallas_call(functools.partial(grads_kernel, rows_a, rows_b, docs, dp,...]
  transfers between devices with their start and end apart: 9 -> 9, of which waited for: 7 -> 8; matrix products, arithmetic and copies ran while one was open for 1% -> 1% of each run, Pallas kernels for 4% -> 4%
where the time goes in v21:
time: 32.2 us; the launch traced here: 32 us
  starting transfers between devices  11.7 us (36%)
  Pallas kernels  10.5 us (33%)
  waiting for transfers between devices  9.45 us (29%)
    ppermute x4, starting transfers between devices, trade(): got.append(lax.ppermute(x, ('dp', 'tensor'), pairs))  8.01 us
    pallas_call x1, Pallas kernels, project(): pl.pallas_call(functools.partial(project_kernel, g_chunks, h_chunks), out...  5.59 us
    ppermute x2, waiting for transfers between devices, trade_shared(): return lax.ppermute(x, 'dp', [(i, i ^ SHARED) for i in range(dp)])  3.84 us
    ppermute x3, waiting for transfers between devices, swap_cores(): return lax.ppermute(x, 'tensor', [(i, cores - 1 - i) for i in range(cores)])  3.32 us
    ppermute x2, starting transfers between devices, trade_shared(): return lax.ppermute(x, 'dp', [(i, i ^ SHARED) for i in range(dp)])  2.97 us
    pallas_call x1, Pallas kernels, solve(): pl.pallas_call(functools.partial(solve_kernel, docs, queries, scale), out...  2.46 us
    ppermute x4, waiting for transfers between devices, trade(): got.append(lax.ppermute(x, ('dp', 'tensor'), pairs))  2.28 us
    pallas_call x3, Pallas kernels, grads_of(): pl.pallas_call(functools.partial(grads_kernel, rows_a, rows_b, docs, dp,...  1.92 us
  transfers between devices with their start and end apart: 9, of which 8 were waited for; matrix products, arithmetic and copies ran while one was open for 1% of the time, Pallas kernels for 4%

profile of v21, /device:TPU:0, one launch (start us, length us, event | category | flops | bytes accessed | tf_op | source)
XLA Modules:
  0.0 32.0 jit_solution(632579115139360744)
XLA Ops:
  0.0 0.0 copy-start.1
  0.0 0.0 copy-start
  0.0 5.6 %project.1.part_ref = f32[128,256]{1,0:T(8,128)S(1)} custom-call(bf16[32,56,16,128]{3,2,1,0:T(8,128)(2,1)} %bitcast.32, bf16[32,16,16,128]{3,2,1,0:T(8,128)(2,1)} %bitcast.33, bf16[8,56,16,128]{3,2,1,0:T(8,128)(2,1)} %bitcast.34, bf16[8,16,16,128]{3,2,1,0:T(8,128)(2,1)} %bitcast.35), custom_call_target="tpu_custom_call" | custom-call | flops 603979776 | bytes 11796480 | tf_op jit(solution)/shard_map/project/pallas_call | solution.py:96
  5.6 0.5 %collective-permute-start = (f32[128,256]{1,0:T(8,128)S(1)}, f32[128,256]{1,0:T(8,128)S(1)}, u32[]{:S(2)}, u32[]{:S(2)}) collective-permute-start(f32[128,256]{1,0:T(8,128)S(1)} %project.1.part_ref), channel_id=1, source_target_pairs={{0,1},{1,0},{2,3},{3,2},{4,5},{5,4},{6,7},{7,6},{8,9},{9,8},{10,11... | collective-permute-start | bytes 393224 | tf_op jit(solution)/shard_map/ppermute | solution.py:329
  6.1 0.0 copy-done.1
  6.1 0.0 copy-done
  6.1 0.2 reshape.41
  6.3 0.1 reshape.42
  6.4 0.7 %collective-permute-done.recv_ref = f32[128,256]{1,0:T(8,128)S(1)} collective-permute-done((f32[128,256]{1,0:T(8,128)S(1)}, f32[128,256]{1,0:T(8,128)S(1)}, u32[]{:S(2)}, u32[]{:S(2)}) %collective-permute-start) | collective-permute-done | bytes 131104 | tf_op jit(solution)/shard_map/ppermute | solution.py:329
  7.1 0.1 pack.1
  7.2 3.0 %collective-permute-start.4 = (f32[152,128]{1,0:T(8,128)S(1)}, f32[152,128]{1,0:T(8,128)S(1)}, u32[]{:S(2)}, u32[]{:S(2)}) collective-permute-start(f32[152,128]{1,0:T(8,128)S(1)} %get-tuple-element.14), channel_id=1, source_target_pairs={{0,4},{1,7},{2,6},{3,5},{4,0},{5,3},{6,2},{7,1},{8,12},{9,15},{10,... | collective-permute-start | bytes 233480 | tf_op jit(solution)/shard_map/ppermute | solution.py:337
  10.2 2.6 %collective-permute-start.2 = (f32[152,128]{1,0:T(8,128)S(1)}, f32[152,128]{1,0:T(8,128)S(1)}, u32[]{:S(2)}, u32[]{:S(2)}) collective-permute-start(f32[152,128]{1,0:T(8,128)S(1)} %get-tuple-element.11), channel_id=1, source_target_pairs={{0,8},{1,11},{2,10},{3,9},{4,12},{5,15},{6,14},{7,13},{8,0},{9,3},... | collective-permute-start | bytes 233480 | tf_op jit(solution)/shard_map/ppermute | solution.py:337
  12.8 0.0 collective-permute-start.1
  12.8 1.7 %collective-permute-start.3 = (f32[80,128]{1,0:T(8,128)S(1)}, f32[80,128]{1,0:T(8,128)S(1)}, u32[]{:S(2)}, u32[]{:S(2)}) collective-permute-start(f32[80,128]{1,0:T(8,128)S(1)} %get-tuple-element.12), channel_id=1, source_target_pairs={{0,2},{2,0},{4,6},{6,4},{8,10},{10,8},{12,14},{14,12},{1,3},{3,1},... | collective-permute-start | bytes 122888 | tf_op jit(solution)/shard_map/ppermute | solution.py:343
  14.5 0.0 collective-permute-done.4.refs_1_
  14.5 0.7 %grads.3.refs_2_ = f32[80,1024]{1,0:T(8,128)S(1)} custom-call(f32[80,128]{1,0:T(8,128)S(1)} %get-tuple-element.13.refs_0_, f32[152,128]{1,0:T(8,128)S(1)} %collective-permute-done.4.refs_1_), custom_call_target="tpu_custom_call" | custom-call | flops 100663296 | bytes 98304 | tf_op jit(solution)/shard_map/grads/pallas_call | solution.py:220
  15.2 1.8 %collective-permute-done.3.refs_1_ = f32[80,128]{1,0:T(8,128)S(1)} collective-permute-done((f32[80,128]{1,0:T(8,128)S(1)}, f32[80,128]{1,0:T(8,128)S(1)}, u32[]{:S(2)}, u32[]{:S(2)}) %collective-permute-start.3) | collective-permute-done | bytes 40992 | tf_op jit(solution)/shard_map/ppermute | solution.py:343
  17.0 0.8 %collective-permute-done.2.refs_0_ = f32[152,128]{1,0:T(8,128)S(1)} collective-permute-done((f32[152,128]{1,0:T(8,128)S(1)}, f32[152,128]{1,0:T(8,128)S(1)}, u32[]{:S(2)}, u32[]{:S(2)}) %collective-permute-start.2) | collective-permute-done | bytes 77856 | tf_op jit(solution)/shard_map/ppermute | solution.py:337
  17.9 0.7 %grads.4.refs_1_ = f32[80,1024]{1,0:T(8,128)S(1)} custom-call(f32[152,128]{1,0:T(8,128)S(1)} %collective-permute-done.2.refs_0_, f32[80,128]{1,0:T(8,128)S(1)} %collective-permute-done.3.refs_1_, f32[80,1024]{1,0:T(8,128)S(1)} %grads.3.refs_2_), custom_call_target="tpu_custom_call" | custom-call | flops 100663296 | bytes 98304 | tf_op jit(solution)/shard_map/grads/pallas_call | solution.py:220
  18.6 0.9 %collective-permute-done.1.refs_0_ = f32[152,128]{1,0:T(8,128)S(1)} collective-permute-done((f32[152,128]{1,0:T(8,128)S(1)}, f32[152,128]{1,0:T(8,128)S(1)}, u32[]{:S(2)}, u32[]{:S(2)}) %collective-permute-start.1) | collective-permute-done | bytes 77856 | tf_op jit(solution)/shard_map/ppermute | solution.py:337
  19.5 0.5 %grads.5.part_ref = f32[80,1024]{1,0:T(8,128)S(1)} custom-call(f32[152,128]{1,0:T(8,128)S(1)} %collective-permute-done.1.refs_0_, f32[80,1024]{1,0:T(8,128)S(1)} %grads.4.refs_1_), custom_call_target="tpu_custom_call" | custom-call | flops 67108864 | bytes 65536 | tf_op jit(solution)/shard_map/grads/pallas_call | solution.py:220
  20.0 0.2 collective-permute-start.5
  20.2 1.5 %collective-permute-done.5.recv_ref = f32[80,1024]{1,0:T(8,128)S(1)} collective-permute-done((f32[80,1024]{1,0:T(8,128)S(1)}, f32[80,1024]{1,0:T(8,128)S(1)}, u32[]{:S(2)}, u32[]{:S(2)}) %collective-permute-start.5) | collective-permute-done | bytes 327712 | tf_op jit(solution)/shard_map/ppermute | solution.py:329
  21.7 0.4 %gram.1 = f32[40,128]{1,0:T(8,128)S(1)} custom-call(f32[80,1024]{1,0:T(8,128)S(1)} %grads.5.part_ref, f32[80,1024]{1,0:T(8,128)S(1)} %collective-permute-done.5.recv_ref), custom_call_target="tpu_custom_call" | custom-call | tf_op jit(solution)/shard_map/gram/pallas_call | solution.py:259
  22.1 2.4 %collective-permute-start.6 = (f32[40,128]{1,0:T(8,128)S(1)}, f32[40,128]{1,0:T(8,128)S(1)}, u32[]{:S(2)}, u32[]{:S(2)}) collective-permute-start(f32[40,128]{1,0:T(8,128)S(1)} %gram.1), channel_id=1, source_target_pairs={{0,4},{1,7},{2,6},{3,5},{4,0},{5,3},{6,2},{7,1},{8,12},{9,15},{10,... | collective-permute-start | bytes 61448 | tf_op jit(solution)/shard_map/ppermute | solution.py:337
  24.6 1.2 %collective-permute-start.7 = (f32[40,128]{1,0:T(8,128)S(1)}, f32[40,128]{1,0:T(8,128)S(1)}, u32[]{:S(2)}, u32[]{:S(2)}) collective-permute-start(f32[40,128]{1,0:T(8,128)S(1)} %gram.1), channel_id=1, source_target_pairs={{0,2},{2,0},{4,6},{6,4},{8,10},{10,8},{12,14},{14,12},{1,3},{3,1},... | collective-permute-start | bytes 61448 | tf_op jit(solution)/shard_map/ppermute | solution.py:343
  25.8 0.5 %collective-permute-done.6 = f32[40,128]{1,0:T(8,128)S(1)} collective-permute-done((f32[40,128]{1,0:T(8,128)S(1)}, f32[40,128]{1,0:T(8,128)S(1)}, u32[]{:S(2)}, u32[]{:S(2)}) %collective-permute-start.6) | collective-permute-done | bytes 20512 | tf_op jit(solution)/shard_map/ppermute | solution.py:337
  26.3 2.0 %collective-permute-done.7 = f32[40,128]{1,0:T(8,128)S(1)} collective-permute-done((f32[40,128]{1,0:T(8,128)S(1)}, f32[40,128]{1,0:T(8,128)S(1)}, u32[]{:S(2)}, u32[]{:S(2)}) %collective-permute-start.7) | collective-permute-done | bytes 20512 | tf_op jit(solution)/shard_map/ppermute | solution.py:343
  28.4 0.0 collective-permute-start.8
  28.4 1.2 %collective-permute-done.8.recv_ref = f32[40,128]{1,0:T(8,128)S(1)} collective-permute-done((f32[40,128]{1,0:T(8,128)S(1)}, f32[40,128]{1,0:T(8,128)S(1)}, u32[]{:S(2)}, u32[]{:S(2)}) %collective-permute-start.8) | collective-permute-done | bytes 20512 | tf_op jit(solution)/shard_map/ppermute | solution.py:329
  29.6 2.5 %solve.1 = f32[8,16]{1,0:T(8,128)} custom-call(f32[40,128]{1,0:T(8,128)S(1)} %select_add_fusion.x_ref, f32[40,128]{1,0:T(8,128)S(1)} %collective-permute-done.8.recv_ref), custom_call_target="tpu_custom_call" | custom-call | tf_op jit(solution)/shard_map/solve/pallas_call | solution.py:308
  (5 shorter events, 0.0 us)
Async XLA Ops:
  0.0 6.1 %copy-start.1 = (s32[256]{0:T(256)S(1)}, s32[256]{0:T(256)}, u32[]{:S(2)}) copy-start(s32[256]{0:T(256)} %param.10) | copy-start | bytes 3076
  0.0 6.1 %copy-start = (f32[2,4096]{1,0:T(2,128)S(1)}, f32[2,4096]{1,0:T(2,128)}, u32[]{:S(2)}) copy-start(f32[2,4096]{1,0:T(2,128)} %param.11) | copy-start | bytes 98308
  5.6 1.5 %collective-permute-start = (f32[128,256]{1,0:T(8,128)S(1)}, f32[128,256]{1,0:T(8,128)S(1)}, u32[]{:S(2)}, u32[]{:S(2)}) collective-permute-start(f32[128,256]{1,0:T(8,128)S(1)} %project.1.part_ref), channel_id=1, source_target_pairs={{0,1},{1,0},{2,3},{3,2},{4,5},{5,4},{6,7},{7,6},{8,9},{9,8},{10,11... | collective-permute-start | bytes 393224 | tf_op jit(solution)/shard_map/ppermute | solution.py:329
  7.2 7.3 %collective-permute-start.4 = (f32[152,128]{1,0:T(8,128)S(1)}, f32[152,128]{1,0:T(8,128)S(1)}, u32[]{:S(2)}, u32[]{:S(2)}) collective-permute-start(f32[152,128]{1,0:T(8,128)S(1)} %get-tuple-element.14), channel_id=1, source_target_pairs={{0,4},{1,7},{2,6},{3,5},{4,0},{5,3},{6,2},{7,1},{8,12},{9,15},{10,... | collective-permute-start | bytes 233480 | tf_op jit(solution)/shard_map/ppermute | solution.py:337
  10.2 7.7 %collective-permute-start.2 = (f32[152,128]{1,0:T(8,128)S(1)}, f32[152,128]{1,0:T(8,128)S(1)}, u32[]{:S(2)}, u32[]{:S(2)}) collective-permute-start(f32[152,128]{1,0:T(8,128)S(1)} %get-tuple-element.11), channel_id=1, source_target_pairs={{0,8},{1,11},{2,10},{3,9},{4,12},{5,15},{6,14},{7,13},{8,0},{9,3},... | collective-permute-start | bytes 233480 | tf_op jit(solution)/shard_map/ppermute | solution.py:337
  12.8 6.7 %collective-permute-start.1 = (f32[152,128]{1,0:T(8,128)S(1)}, f32[152,128]{1,0:T(8,128)S(1)}, u32[]{:S(2)}, u32[]{:S(2)}) collective-permute-start(f32[152,128]{1,0:T(8,128)S(1)} %get-tuple-element.10), channel_id=1, source_target_pairs={{0,12},{1,15},{2,14},{3,13},{4,8},{5,11},{6,10},{7,9},{8,4},{9,7},... | collective-permute-start | bytes 233480 | tf_op jit(solution)/shard_map/ppermute | solution.py:337
  12.8 4.3 %collective-permute-start.3 = (f32[80,128]{1,0:T(8,128)S(1)}, f32[80,128]{1,0:T(8,128)S(1)}, u32[]{:S(2)}, u32[]{:S(2)}) collective-permute-start(f32[80,128]{1,0:T(8,128)S(1)} %get-tuple-element.12), channel_id=1, source_target_pairs={{0,2},{2,0},{4,6},{6,4},{8,10},{10,8},{12,14},{14,12},{1,3},{3,1},... | collective-permute-start | bytes 122888 | tf_op jit(solution)/shard_map/ppermute | solution.py:343
  20.0 1.7 %collective-permute-start.5 = (f32[80,1024]{1,0:T(8,128)S(1)}, f32[80,1024]{1,0:T(8,128)S(1)}, u32[]{:S(2)}, u32[]{:S(2)}) collective-permute-start(f32[80,1024]{1,0:T(8,128)S(1)} %grads.5.part_ref), channel_id=1, source_target_pairs={{0,1},{1,0},{2,3},{3,2},{4,5},{5,4},{6,7},{7,6},{8,9},{9,8},{10,11... | collective-permute-start | bytes 983048 | tf_op jit(solution)/shard_map/ppermute | solution.py:329
  22.1 4.2 %collective-permute-start.6 = (f32[40,128]{1,0:T(8,128)S(1)}, f32[40,128]{1,0:T(8,128)S(1)}, u32[]{:S(2)}, u32[]{:S(2)}) collective-permute-start(f32[40,128]{1,0:T(8,128)S(1)} %gram.1), channel_id=1, source_target_pairs={{0,4},{1,7},{2,6},{3,5},{4,0},{5,3},{6,2},{7,1},{8,12},{9,15},{10,... | collective-permute-start | bytes 61448 | tf_op jit(solution)/shard_map/ppermute | solution.py:337
  24.6 3.8 %collective-permute-start.7 = (f32[40,128]{1,0:T(8,128)S(1)}, f32[40,128]{1,0:T(8,128)S(1)}, u32[]{:S(2)}, u32[]{:S(2)}) collective-permute-start(f32[40,128]{1,0:T(8,128)S(1)} %gram.1), channel_id=1, source_target_pairs={{0,2},{2,0},{4,6},{6,4},{8,10},{10,8},{12,14},{14,12},{1,3},{3,1},... | collective-permute-start | bytes 61448 | tf_op jit(solution)/shard_map/ppermute | solution.py:343
  28.4 1.2 %collective-permute-start.8 = (f32[40,128]{1,0:T(8,128)S(1)}, f32[40,128]{1,0:T(8,128)S(1)}, u32[]{:S(2)}, u32[]{:S(2)}) collective-permute-start(f32[40,128]{1,0:T(8,128)S(1)} %select_add_fusion.x_ref), channel_id=1, source_target_pairs={{0,1},{1,0},{2,3},{3,2},{4,5},{5,4},{6,7},{7,6},{8,9},{9,8},{10,11... | collective-permute-start | bytes 61448 | tf_op jit(solution)/shard_map/ppermute | solution.py:329

commit v22 on v18

--- a/solution.py
+++ b/solution.py
@@ -266,14 +266,20 @@
     )(part, recv)
 
 
-def solve_kernel(docs, queries, scale, x_ref, recv_ref, out_ref, done_ref):
+def solve_kernel(docs, queries, scale, x_ref, recv_ref, out_ref, kernel_ref, work_ref):
     total = x_ref[...] + recv_ref[...]
     stack = jnp.concatenate([total[:, :docs], total[:, docs:]], axis=0)
-    cols = done_ref.shape[1]
+    cols = work_ref.shape[1]
+    turned = pl.ds(pl.multiple_of((lax.axis_index("dp") + 1) * DOC_DEV, DOC_DEV), docs)
     diagonal = [lax.broadcasted_iota(jnp.int32, (docs, docs), i) for i in range(2)]
     mean_diag = jnp.sum(jnp.where(diagonal[0] == diagonal[1], stack[:docs], 0.0)) * (1.0 / docs)
-    stack = jnp.concatenate([stack, jnp.zeros((cols - stack.shape[0], docs), jnp.float32)], axis=0)
-    total = stack.T
+    for i in range(2):
+        kernel_ref[i * docs:(i + 1) * docs, :] = stack[:docs]
+    rest = jnp.zeros((cols - stack.shape[0], docs), jnp.float32)
+    total = jnp.concatenate([kernel_ref[turned, :], stack[docs:], rest], axis=0).T
+    for i in range(2):
+        work_ref[i * docs:(i + 1) * docs, :] = total
+    total = work_ref[turned, :]
     row = lax.broadcasted_iota(jnp.int32, (docs, cols), 0)
     col = lax.broadcasted_iota(jnp.int32, (docs, cols), 1)
     work = total + jnp.where(row == col, 0.1 * mean_diag, 0.0)
@@ -281,8 +287,8 @@
     here = lax.broadcasted_iota(jnp.int32, (size, cols), 0)
     rows = [work[i:i + size] for i in range(0, docs, size)]
     for r in range(len(rows)):
-        wide = [[jnp.broadcast_to(x[:, c:c + 1], (size, cols)) for c in range(r * size, (r + 1) * size)] for x in rows]
-        pivot, line = wide[r], rows[r]
+        wide = [[jnp.broadcast_to(x[:, c:c + 1], (size, cols)) for c in range(r * size, (r + 1) * size)] for x in rows[r:]]
+        pivot, line = wide[0], rows[r]
         scale_rows = jnp.ones((size, cols), jnp.float32)
         for j in range(size):
             inverse = 1.0 / pivot[j][j:j + 1]
@@ -291,17 +297,12 @@
             line = line - factor * line[j:j + 1]
             scale_rows = jnp.where(here == j, inverse, scale_rows)
         line = line * scale_rows
-        for s in range(len(rows)):
-            if s == r:
-                rows[s] = line
-            else:
-                terms = [wide[s][j] * line[j:j + 1] for j in range(size)]
-                rows[s] = rows[s] - (((terms[0] + terms[1]) + (terms[2] + terms[3]))
-                                     + ((terms[4] + terms[5]) + (terms[6] + terms[7])))
-    for r, x in enumerate(rows):
-        done_ref[r * size:(r + 1) * size, :] = x * (mean_diag * scale)
-    mine = pl.ds(pl.multiple_of(lax.axis_index("dp") * DOC_DEV, DOC_DEV), DOC_DEV)
-    out_ref[...] = done_ref[mine, :][:, docs:docs + queries]
+        rows[r] = line
+        for s in range(r + 1, len(rows)):
+            terms = [wide[s - r][j] * line[j:j + 1] for j in range(size)]
+            rows[s] = rows[s] - (((terms[0] + terms[1]) + (terms[2] + terms[3]))
+                                 + ((terms[4] + terms[5]) + (terms[6] + terms[7])))
+    out_ref[...] = rows[-1][:, docs:docs + queries] * (mean_diag * scale)
 
 
 def solve(x, recv, docs, queries, scale):
@@ -310,7 +311,10 @@
         out_shape=jax.ShapeDtypeStruct((DOC_DEV, queries), jnp.float32),
         in_specs=[VMEM] * 2,
         out_specs=VMEM,
-        scratch_shapes=[pltpu.VMEM((docs, -(-(docs + queries) // LANES) * LANES), jnp.float32)],
+        scratch_shapes=[
+            pltpu.VMEM((2 * docs, docs), jnp.float32),
+            pltpu.VMEM((2 * docs, -(-(docs + queries) // LANES) * LANES), jnp.float32),
+        ],
         compiler_params=vmem_params(16),
         name="solve",
     )(x, recv)

time: 31.1 us -> 31.5 us (1.013)
  Pallas kernels: 10.3 us -> 10.7 us
    pallas_call x1, Pallas kernels: 2.46 us -> 2.86 us  [solve(): pl.pallas_call(functools.partial(solve_kernel, docs, queries, scale), out...]
where the time goes in v22:
time: 31.5 us; the launch traced here: 31.4 us
  Pallas kernels  10.7 us (34%)
  starting transfers between devices  10.4 us (33%)
  waiting for transfers between devices  9.88 us (31%)
    ppermute x4, starting transfers between devices, trade(): got.append(lax.ppermute(x, ('dp', 'tensor'), pairs))  7.04 us
    pallas_call x1, Pallas kernels, project(): pl.pallas_call(functools.partial(project_kernel, g_chunks, h_chunks), out...  5.59 us
    ppermute x2, waiting for transfers between devices, trade_shared(): return lax.ppermute(x, 'dp', [(i, i ^ SHARED) for i in range(dp)])  4.26 us
    ppermute x3, waiting for transfers between devices, swap_cores(): return lax.ppermute(x, 'tensor', [(i, cores - 1 - i) for i in range(cores)])  3.33 us
    pallas_call x1, Pallas kernels, solve(): pl.pallas_call(functools.partial(solve_kernel, docs, queries, scale), out...  2.86 us
    ppermute x2, starting transfers between devices, trade_shared(): return lax.ppermute(x, 'dp', [(i, i ^ SHARED) for i in range(dp)])  2.64 us
    ppermute x4, waiting for transfers between devices, trade(): got.append(lax.ppermute(x, ('dp', 'tensor'), pairs))  2.29 us
    pallas_call x2, Pallas kernels, grads_of(): pl.pallas_call(functools.partial(grads_kernel, rows_a, rows_b, docs, dp,...  1.73 us
  transfers between devices with their start and end apart: 9, of which 7 were waited for; matrix products, arithmetic and copies ran while one was open for 1% of the time, Pallas kernels for 4%

profile of v22, /device:TPU:0, one launch (start us, length us, event | category | flops | bytes accessed | tf_op | source)
XLA Modules:
  0.0 31.4 jit_solution(2159798252489727304)
XLA Ops:
  0.0 0.0 copy-start.1
  0.0 0.0 copy-start
  0.0 5.6 %project.1.part_ref = f32[128,256]{1,0:T(8,128)S(1)} custom-call(bf16[32,56,16,128]{3,2,1,0:T(8,128)(2,1)} %bitcast.32, bf16[32,16,16,128]{3,2,1,0:T(8,128)(2,1)} %bitcast.33, bf16[8,56,16,128]{3,2,1,0:T(8,128)(2,1)} %bitcast.34, bf16[8,16,16,128]{3,2,1,0:T(8,128)(2,1)} %bitcast.35), custom_call_target="tpu_custom_call" | custom-call | flops 603979776 | bytes 11796480 | tf_op jit(solution)/shard_map/project/pallas_call | solution.py:96
  5.6 0.5 %collective-permute-start = (f32[128,256]{1,0:T(8,128)S(1)}, f32[128,256]{1,0:T(8,128)S(1)}, u32[]{:S(2)}, u32[]{:S(2)}) collective-permute-start(f32[128,256]{1,0:T(8,128)S(1)} %project.1.part_ref), channel_id=1, source_target_pairs={{0,1},{1,0},{2,3},{3,2},{4,5},{5,4},{6,7},{7,6},{8,9},{9,8},{10,11... | collective-permute-start | bytes 393224 | tf_op jit(solution)/shard_map/ppermute | solution.py:333
  6.1 0.0 copy-done.1
  6.1 0.0 copy-done
  6.1 0.2 reshape.41
  6.3 0.1 reshape.42
  6.4 0.7 %collective-permute-done.recv_ref = f32[128,256]{1,0:T(8,128)S(1)} collective-permute-done((f32[128,256]{1,0:T(8,128)S(1)}, f32[128,256]{1,0:T(8,128)S(1)}, u32[]{:S(2)}, u32[]{:S(2)}) %collective-permute-start) | collective-permute-done | bytes 131104 | tf_op jit(solution)/shard_map/ppermute | solution.py:333
  7.1 0.1 pack.1
  7.2 4.0 %collective-permute-start.2 = (f32[152,128]{1,0:T(8,128)S(1)}, f32[152,128]{1,0:T(8,128)S(1)}, u32[]{:S(2)}, u32[]{:S(2)}) collective-permute-start(f32[152,128]{1,0:T(8,128)S(1)} %get-tuple-element.11), channel_id=1, source_target_pairs={{0,8},{1,11},{2,10},{3,9},{4,12},{5,15},{6,14},{7,13},{8,0},{9,3},... | collective-permute-start | bytes 233480 | tf_op jit(solution)/shard_map/ppermute | solution.py:341
  11.2 1.6 %collective-permute-start.3 = (f32[152,128]{1,0:T(8,128)S(1)}, f32[152,128]{1,0:T(8,128)S(1)}, u32[]{:S(2)}, u32[]{:S(2)}) collective-permute-start(f32[152,128]{1,0:T(8,128)S(1)} %get-tuple-element.12), channel_id=1, source_target_pairs={{0,4},{1,7},{2,6},{3,5},{4,0},{5,3},{6,2},{7,1},{8,12},{9,15},{10,... | collective-permute-start | bytes 233480 | tf_op jit(solution)/shard_map/ppermute | solution.py:341
  12.8 0.0 collective-permute-start.1
  12.8 1.7 %collective-permute-start.4 = (f32[80,128]{1,0:T(8,128)S(1)}, f32[80,128]{1,0:T(8,128)S(1)}, u32[]{:S(2)}, u32[]{:S(2)}) collective-permute-start(f32[80,128]{1,0:T(8,128)S(1)} %get-tuple-element.13), channel_id=1, source_target_pairs={{0,2},{2,0},{4,6},{6,4},{8,10},{10,8},{12,14},{14,12},{1,3},{3,1},... | collective-permute-start | bytes 122888 | tf_op jit(solution)/shard_map/ppermute | solution.py:347
  14.5 2.9 %collective-permute-done.4.refs_2_ = f32[80,128]{1,0:T(8,128)S(1)} collective-permute-done((f32[80,128]{1,0:T(8,128)S(1)}, f32[80,128]{1,0:T(8,128)S(1)}, u32[]{:S(2)}, u32[]{:S(2)}) %collective-permute-start.4) | collective-permute-done | bytes 40992 | tf_op jit(solution)/shard_map/ppermute | solution.py:347
  17.4 0.0 collective-permute-done.2.refs_0_
  17.4 0.0 collective-permute-done.3.refs_1_
  17.4 1.2 %grads.2.refs_1_ = f32[80,1024]{1,0:T(8,128)S(1)} custom-call(f32[152,128]{1,0:T(8,128)S(1)} %collective-permute-done.2.refs_0_, f32[152,128]{1,0:T(8,128)S(1)} %collective-permute-done.3.refs_1_, f32[80,128]{1,0:T(8,128)S(1)} %collective-permute-done.4.refs_2_, f32[80,128]{1,0:T(8,128)S(1)} %get-tuple-element.14.refs_3_), custom_call_target="tpu_custom_call" | custom-call | flops 201326592 | bytes 196608 | tf_op jit(solution)/shard_map/grads/pallas_call | solution.py:220
  18.6 0.8 %collective-permute-done.1.refs_0_ = f32[152,128]{1,0:T(8,128)S(1)} collective-permute-done((f32[152,128]{1,0:T(8,128)S(1)}, f32[152,128]{1,0:T(8,128)S(1)}, u32[]{:S(2)}, u32[]{:S(2)}) %collective-permute-start.1) | collective-permute-done | bytes 77856 | tf_op jit(solution)/shard_map/ppermute | solution.py:341
  19.4 0.5 %grads.3.part_ref = f32[80,1024]{1,0:T(8,128)S(1)} custom-call(f32[152,128]{1,0:T(8,128)S(1)} %collective-permute-done.1.refs_0_, f32[80,1024]{1,0:T(8,128)S(1)} %grads.2.refs_1_), custom_call_target="tpu_custom_call" | custom-call | flops 67108864 | bytes 65536 | tf_op jit(solution)/shard_map/grads/pallas_call | solution.py:220
  19.9 0.2 collective-permute-start.5
  20.1 1.5 %collective-permute-done.5.recv_ref = f32[80,1024]{1,0:T(8,128)S(1)} collective-permute-done((f32[80,1024]{1,0:T(8,128)S(1)}, f32[80,1024]{1,0:T(8,128)S(1)}, u32[]{:S(2)}, u32[]{:S(2)}) %collective-permute-start.5) | collective-permute-done | bytes 327712 | tf_op jit(solution)/shard_map/ppermute | solution.py:333
  21.6 0.4 %gram.1 = f32[40,128]{1,0:T(8,128)S(1)} custom-call(f32[80,1024]{1,0:T(8,128)S(1)} %grads.3.part_ref, f32[80,1024]{1,0:T(8,128)S(1)} %collective-permute-done.5.recv_ref), custom_call_target="tpu_custom_call" | custom-call | tf_op jit(solution)/shard_map/gram/pallas_call | solution.py:259
  22.1 1.5 %collective-permute-start.6 = (f32[40,128]{1,0:T(8,128)S(1)}, f32[40,128]{1,0:T(8,128)S(1)}, u32[]{:S(2)}, u32[]{:S(2)}) collective-permute-start(f32[40,128]{1,0:T(8,128)S(1)} %gram.1), channel_id=1, source_target_pairs={{0,4},{1,7},{2,6},{3,5},{4,0},{5,3},{6,2},{7,1},{8,12},{9,15},{10,... | collective-permute-start | bytes 61448 | tf_op jit(solution)/shard_map/ppermute | solution.py:341
  23.5 0.9 %collective-permute-start.7 = (f32[40,128]{1,0:T(8,128)S(1)}, f32[40,128]{1,0:T(8,128)S(1)}, u32[]{:S(2)}, u32[]{:S(2)}) collective-permute-start(f32[40,128]{1,0:T(8,128)S(1)} %gram.1), channel_id=1, source_target_pairs={{0,2},{2,0},{4,6},{6,4},{8,10},{10,8},{12,14},{14,12},{1,3},{3,1},... | collective-permute-start | bytes 61448 | tf_op jit(solution)/shard_map/ppermute | solution.py:347
  24.4 1.5 %collective-permute-done.6 = f32[40,128]{1,0:T(8,128)S(1)} collective-permute-done((f32[40,128]{1,0:T(8,128)S(1)}, f32[40,128]{1,0:T(8,128)S(1)}, u32[]{:S(2)}, u32[]{:S(2)}) %collective-permute-start.6) | collective-permute-done | bytes 20512 | tf_op jit(solution)/shard_map/ppermute | solution.py:341
  25.9 1.4 %collective-permute-done.7 = f32[40,128]{1,0:T(8,128)S(1)} collective-permute-done((f32[40,128]{1,0:T(8,128)S(1)}, f32[40,128]{1,0:T(8,128)S(1)}, u32[]{:S(2)}, u32[]{:S(2)}) %collective-permute-start.7) | collective-permute-done | bytes 20512 | tf_op jit(solution)/shard_map/ppermute | solution.py:347
  27.3 0.0 collective-permute-start.8
  27.3 1.2 %collective-permute-done.8.recv_ref = f32[40,128]{1,0:T(8,128)S(1)} collective-permute-done((f32[40,128]{1,0:T(8,128)S(1)}, f32[40,128]{1,0:T(8,128)S(1)}, u32[]{:S(2)}, u32[]{:S(2)}) %collective-permute-start.8) | collective-permute-done | bytes 20512 | tf_op jit(solution)/shard_map/ppermute | solution.py:333
  28.5 2.9 %solve.1 = f32[8,16]{1,0:T(8,128)} custom-call(f32[40,128]{1,0:T(8,128)S(1)} %select_add_fusion.x_ref, f32[40,128]{1,0:T(8,128)S(1)} %collective-permute-done.8.recv_ref), custom_call_target="tpu_custom_call" | custom-call | tf_op jit(solution)/shard_map/solve/pallas_call | solution.py:309
  (5 shorter events, 0.0 us)
Async XLA Ops:
  0.0 6.1 %copy-start.1 = (s32[256]{0:T(256)S(1)}, s32[256]{0:T(256)}, u32[]{:S(2)}) copy-start(s32[256]{0:T(256)} %param.10) | copy-start | bytes 3076
  0.0 6.1 %copy-start = (f32[2,4096]{1,0:T(2,128)S(1)}, f32[2,4096]{1,0:T(2,128)}, u32[]{:S(2)}) copy-start(f32[2,4096]{1,0:T(2,128)} %param.11) | copy-start | bytes 98308
  5.6 1.5 %collective-permute-start = (f32[128,256]{1,0:T(8,128)S(1)}, f32[128,256]{1,0:T(8,128)S(1)}, u32[]{:S(2)}, u32[]{:S(2)}) collective-permute-start(f32[128,256]{1,0:T(8,128)S(1)} %project.1.part_ref), channel_id=1, source_target_pairs={{0,1},{1,0},{2,3},{3,2},{4,5},{5,4},{6,7},{7,6},{8,9},{9,8},{10,11... | collective-permute-start | bytes 393224 | tf_op jit(solution)/shard_map/ppermute | solution.py:333
  7.2 10.2 %collective-permute-start.2 = (f32[152,128]{1,0:T(8,128)S(1)}, f32[152,128]{1,0:T(8,128)S(1)}, u32[]{:S(2)}, u32[]{:S(2)}) collective-permute-start(f32[152,128]{1,0:T(8,128)S(1)} %get-tuple-element.11), channel_id=1, source_target_pairs={{0,8},{1,11},{2,10},{3,9},{4,12},{5,15},{6,14},{7,13},{8,0},{9,3},... | collective-permute-start | bytes 233480 | tf_op jit(solution)/shard_map/ppermute | solution.py:341
  11.2 6.2 %collective-permute-start.3 = (f32[152,128]{1,0:T(8,128)S(1)}, f32[152,128]{1,0:T(8,128)S(1)}, u32[]{:S(2)}, u32[]{:S(2)}) collective-permute-start(f32[152,128]{1,0:T(8,128)S(1)} %get-tuple-element.12), channel_id=1, source_target_pairs={{0,4},{1,7},{2,6},{3,5},{4,0},{5,3},{6,2},{7,1},{8,12},{9,15},{10,... | collective-permute-start | bytes 233480 | tf_op jit(solution)/shard_map/ppermute | solution.py:341
  12.8 6.6 %collective-permute-start.1 = (f32[152,128]{1,0:T(8,128)S(1)}, f32[152,128]{1,0:T(8,128)S(1)}, u32[]{:S(2)}, u32[]{:S(2)}) collective-permute-start(f32[152,128]{1,0:T(8,128)S(1)} %get-tuple-element.10), channel_id=1, source_target_pairs={{0,12},{1,15},{2,14},{3,13},{4,8},{5,11},{6,10},{7,9},{8,4},{9,7},... | collective-permute-start | bytes 233480 | tf_op jit(solution)/shard_map/ppermute | solution.py:341
  12.8 4.6 %collective-permute-start.4 = (f32[80,128]{1,0:T(8,128)S(1)}, f32[80,128]{1,0:T(8,128)S(1)}, u32[]{:S(2)}, u32[]{:S(2)}) collective-permute-start(f32[80,128]{1,0:T(8,128)S(1)} %get-tuple-element.13), channel_id=1, source_target_pairs={{0,2},{2,0},{4,6},{6,4},{8,10},{10,8},{12,14},{14,12},{1,3},{3,1},... | collective-permute-start | bytes 122888 | tf_op jit(solution)/shard_map/ppermute | solution.py:347
  19.9 1.7 %collective-permute-start.5 = (f32[80,1024]{1,0:T(8,128)S(1)}, f32[80,1024]{1,0:T(8,128)S(1)}, u32[]{:S(2)}, u32[]{:S(2)}) collective-permute-start(f32[80,1024]{1,0:T(8,128)S(1)} %grads.3.part_ref), channel_id=1, source_target_pairs={{0,1},{1,0},{2,3},{3,2},{4,5},{5,4},{6,7},{7,6},{8,9},{9,8},{10,11... | collective-permute-start | bytes 983048 | tf_op jit(solution)/shard_map/ppermute | solution.py:333
  22.1 3.9 %collective-permute-start.6 = (f32[40,128]{1,0:T(8,128)S(1)}, f32[40,128]{1,0:T(8,128)S(1)}, u32[]{:S(2)}, u32[]{:S(2)}) collective-permute-start(f32[40,128]{1,0:T(8,128)S(1)} %gram.1), channel_id=1, source_target_pairs={{0,4},{1,7},{2,6},{3,5},{4,0},{5,3},{6,2},{7,1},{8,12},{9,15},{10,... | collective-permute-start | bytes 61448 | tf_op jit(solution)/shard_map/ppermute | solution.py:341
  23.5 3.8 %collective-permute-start.7 = (f32[40,128]{1,0:T(8,128)S(1)}, f32[40,128]{1,0:T(8,128)S(1)}, u32[]{:S(2)}, u32[]{:S(2)}) collective-permute-start(f32[40,128]{1,0:T(8,128)S(1)} %gram.1), channel_id=1, source_target_pairs={{0,2},{2,0},{4,6},{6,4},{8,10},{10,8},{12,14},{14,12},{1,3},{3,1},... | collective-permute-start | bytes 61448 | tf_op jit(solution)/shard_map/ppermute | solution.py:347
  27.3 1.2 %collective-permute-start.8 = (f32[40,128]{1,0:T(8,128)S(1)}, f32[40,128]{1,0:T(8,128)S(1)}, u32[]{:S(2)}, u32[]{:S(2)}) collective-permute-start(f32[40,128]{1,0:T(8,128)S(1)} %select_add_fusion.x_ref), channel_id=1, source_target_pairs={{0,1},{1,0},{2,3},{3,2},{4,5},{5,4},{6,7},{7,6},{8,9},{9,8},{10,11... | collective-permute-start | bytes 61448 | tf_op jit(solution)/shard_map/ppermute | solution.py:333

commit v23 on v18

--- a/solution.py
+++ b/solution.py
@@ -282,12 +282,16 @@
     rows = [work[i:i + size] for i in range(0, docs, size)]
     for r in range(len(rows)):
         wide = [[jnp.broadcast_to(x[:, c:c + 1], (size, cols)) for c in range(r * size, (r + 1) * size)] for x in rows]
-        pivot, line = wide[r], rows[r]
+        pivot, line = list(wide[r]), rows[r]
         scale_rows = jnp.ones((size, cols), jnp.float32)
+        diagonals = [jnp.broadcast_to(x[i:i + 1], (size, cols)) for i, x in enumerate(pivot)]
         for j in range(size):
-            inverse = 1.0 / pivot[j][j:j + 1]
+            inverse = 1.0 / diagonals[j]
             factor = jnp.where(here == j, 0.0, pivot[j]) * inverse
-            pivot = [x if i <= j else x - factor * x[j:j + 1] for i, x in enumerate(pivot)]
+            for k in range(j + 1, size):
+                across = jnp.broadcast_to(pivot[k][j:j + 1], (size, cols))
+                diagonals[k] = diagonals[k] - (across * across) * inverse
+                pivot[k] = pivot[k] - factor * across
             line = line - factor * line[j:j + 1]
             scale_rows = jnp.where(here == j, inverse, scale_rows)
         line = line * scale_rows

time: 31.1 us -> 31.4 us (level)
    pallas_call x1, Pallas kernels: 2.46 us -> 2.78 us  [solve(): pl.pallas_call(functools.partial(solve_kernel, docs, queries, scale), out...]
where the time goes in v23:
time: 31.4 us; the launch traced here: 31.3 us
  Pallas kernels  10.6 us (34%)
  starting transfers between devices  10.4 us (33%)
  waiting for transfers between devices  9.88 us (31%)
    ppermute x4, starting transfers between devices, trade(): got.append(lax.ppermute(x, ('dp', 'tensor'), pairs))  7.04 us
    pallas_call x1, Pallas kernels, project(): pl.pallas_call(functools.partial(project_kernel, g_chunks, h_chunks), out...  5.59 us
    ppermute x2, waiting for transfers between devices, trade_shared(): return lax.ppermute(x, 'dp', [(i, i ^ SHARED) for i in range(dp)])  4.26 us
    ppermute x3, waiting for transfers between devices, swap_cores(): return lax.ppermute(x, 'tensor', [(i, cores - 1 - i) for i in range(cores)])  3.33 us
    pallas_call x1, Pallas kernels, solve(): pl.pallas_call(functools.partial(solve_kernel, docs, queries, scale), out...  2.78 us
    ppermute x2, starting transfers between devices, trade_shared(): return lax.ppermute(x, 'dp', [(i, i ^ SHARED) for i in range(dp)])  2.64 us
    ppermute x4, waiting for transfers between devices, trade(): got.append(lax.ppermute(x, ('dp', 'tensor'), pairs))  2.29 us
    pallas_call x2, Pallas kernels, grads_of(): pl.pallas_call(functools.partial(grads_kernel, rows_a, rows_b, docs, dp,...  1.73 us
  transfers between devices with their start and end apart: 9, of which 7 were waited for; matrix products, arithmetic and copies ran while one was open for 1% of the time, Pallas kernels for 4%

profile of v23, /device:TPU:0, one launch (start us, length us, event | category | flops | bytes accessed | tf_op | source)
XLA Modules:
  0.0 31.3 jit_solution(14929428474995984612)
XLA Ops:
  0.0 0.0 copy-start.1
  0.0 0.0 copy-start
  0.0 5.6 %project.1.part_ref = f32[128,256]{1,0:T(8,128)S(1)} custom-call(bf16[32,56,16,128]{3,2,1,0:T(8,128)(2,1)} %bitcast.32, bf16[32,16,16,128]{3,2,1,0:T(8,128)(2,1)} %bitcast.33, bf16[8,56,16,128]{3,2,1,0:T(8,128)(2,1)} %bitcast.34, bf16[8,16,16,128]{3,2,1,0:T(8,128)(2,1)} %bitcast.35), custom_call_target="tpu_custom_call" | custom-call | flops 603979776 | bytes 11796480 | tf_op jit(solution)/shard_map/project/pallas_call | solution.py:96
  5.6 0.5 %collective-permute-start = (f32[128,256]{1,0:T(8,128)S(1)}, f32[128,256]{1,0:T(8,128)S(1)}, u32[]{:S(2)}, u32[]{:S(2)}) collective-permute-start(f32[128,256]{1,0:T(8,128)S(1)} %project.1.part_ref), channel_id=1, source_target_pairs={{0,1},{1,0},{2,3},{3,2},{4,5},{5,4},{6,7},{7,6},{8,9},{9,8},{10,11... | collective-permute-start | bytes 393224 | tf_op jit(solution)/shard_map/ppermute | solution.py:333
  6.1 0.0 copy-done.1
  6.1 0.0 copy-done
  6.1 0.2 reshape.41
  6.3 0.1 reshape.42
  6.4 0.7 %collective-permute-done.recv_ref = f32[128,256]{1,0:T(8,128)S(1)} collective-permute-done((f32[128,256]{1,0:T(8,128)S(1)}, f32[128,256]{1,0:T(8,128)S(1)}, u32[]{:S(2)}, u32[]{:S(2)}) %collective-permute-start) | collective-permute-done | bytes 131104 | tf_op jit(solution)/shard_map/ppermute | solution.py:333
  7.1 0.1 pack.1
  7.2 4.0 %collective-permute-start.2 = (f32[152,128]{1,0:T(8,128)S(1)}, f32[152,128]{1,0:T(8,128)S(1)}, u32[]{:S(2)}, u32[]{:S(2)}) collective-permute-start(f32[152,128]{1,0:T(8,128)S(1)} %get-tuple-element.11), channel_id=1, source_target_pairs={{0,8},{1,11},{2,10},{3,9},{4,12},{5,15},{6,14},{7,13},{8,0},{9,3},... | collective-permute-start | bytes 233480 | tf_op jit(solution)/shard_map/ppermute | solution.py:341
  11.2 1.6 %collective-permute-start.3 = (f32[152,128]{1,0:T(8,128)S(1)}, f32[152,128]{1,0:T(8,128)S(1)}, u32[]{:S(2)}, u32[]{:S(2)}) collective-permute-start(f32[152,128]{1,0:T(8,128)S(1)} %get-tuple-element.12), channel_id=1, source_target_pairs={{0,4},{1,7},{2,6},{3,5},{4,0},{5,3},{6,2},{7,1},{8,12},{9,15},{10,... | collective-permute-start | bytes 233480 | tf_op jit(solution)/shard_map/ppermute | solution.py:341
  12.8 0.0 collective-permute-start.1
  12.8 1.7 %collective-permute-start.4 = (f32[80,128]{1,0:T(8,128)S(1)}, f32[80,128]{1,0:T(8,128)S(1)}, u32[]{:S(2)}, u32[]{:S(2)}) collective-permute-start(f32[80,128]{1,0:T(8,128)S(1)} %get-tuple-element.13), channel_id=1, source_target_pairs={{0,2},{2,0},{4,6},{6,4},{8,10},{10,8},{12,14},{14,12},{1,3},{3,1},... | collective-permute-start | bytes 122888 | tf_op jit(solution)/shard_map/ppermute | solution.py:347
  14.5 2.9 %collective-permute-done.4.refs_2_ = f32[80,128]{1,0:T(8,128)S(1)} collective-permute-done((f32[80,128]{1,0:T(8,128)S(1)}, f32[80,128]{1,0:T(8,128)S(1)}, u32[]{:S(2)}, u32[]{:S(2)}) %collective-permute-start.4) | collective-permute-done | bytes 40992 | tf_op jit(solution)/shard_map/ppermute | solution.py:347
  17.4 0.0 collective-permute-done.2.refs_0_
  17.4 0.0 collective-permute-done.3.refs_1_
  17.4 1.2 %grads.2.refs_1_ = f32[80,1024]{1,0:T(8,128)S(1)} custom-call(f32[152,128]{1,0:T(8,128)S(1)} %collective-permute-done.2.refs_0_, f32[152,128]{1,0:T(8,128)S(1)} %collective-permute-done.3.refs_1_, f32[80,128]{1,0:T(8,128)S(1)} %collective-permute-done.4.refs_2_, f32[80,128]{1,0:T(8,128)S(1)} %get-tuple-element.14.refs_3_), custom_call_target="tpu_custom_call" | custom-call | flops 201326592 | bytes 196608 | tf_op jit(solution)/shard_map/grads/pallas_call | solution.py:220
  18.6 0.8 %collective-permute-done.1.refs_0_ = f32[152,128]{1,0:T(8,128)S(1)} collective-permute-done((f32[152,128]{1,0:T(8,128)S(1)}, f32[152,128]{1,0:T(8,128)S(1)}, u32[]{:S(2)}, u32[]{:S(2)}) %collective-permute-start.1) | collective-permute-done | bytes 77856 | tf_op jit(solution)/shard_map/ppermute | solution.py:341
  19.4 0.5 %grads.3.part_ref = f32[80,1024]{1,0:T(8,128)S(1)} custom-call(f32[152,128]{1,0:T(8,128)S(1)} %collective-permute-done.1.refs_0_, f32[80,1024]{1,0:T(8,128)S(1)} %grads.2.refs_1_), custom_call_target="tpu_custom_call" | custom-call | flops 67108864 | bytes 65536 | tf_op jit(solution)/shard_map/grads/pallas_call | solution.py:220
  19.9 0.2 collective-permute-start.5
  20.1 1.5 %collective-permute-done.5.recv_ref = f32[80,1024]{1,0:T(8,128)S(1)} collective-permute-done((f32[80,1024]{1,0:T(8,128)S(1)}, f32[80,1024]{1,0:T(8,128)S(1)}, u32[]{:S(2)}, u32[]{:S(2)}) %collective-permute-start.5) | collective-permute-done | bytes 327712 | tf_op jit(solution)/shard_map/ppermute | solution.py:333
  21.6 0.4 %gram.1 = f32[40,128]{1,0:T(8,128)S(1)} custom-call(f32[80,1024]{1,0:T(8,128)S(1)} %grads.3.part_ref, f32[80,1024]{1,0:T(8,128)S(1)} %collective-permute-done.5.recv_ref), custom_call_target="tpu_custom_call" | custom-call | tf_op jit(solution)/shard_map/gram/pallas_call | solution.py:259
  22.1 1.5 %collective-permute-start.6 = (f32[40,128]{1,0:T(8,128)S(1)}, f32[40,128]{1,0:T(8,128)S(1)}, u32[]{:S(2)}, u32[]{:S(2)}) collective-permute-start(f32[40,128]{1,0:T(8,128)S(1)} %gram.1), channel_id=1, source_target_pairs={{0,4},{1,7},{2,6},{3,5},{4,0},{5,3},{6,2},{7,1},{8,12},{9,15},{10,... | collective-permute-start | bytes 61448 | tf_op jit(solution)/shard_map/ppermute | solution.py:341
  23.5 0.9 %collective-permute-start.7 = (f32[40,128]{1,0:T(8,128)S(1)}, f32[40,128]{1,0:T(8,128)S(1)}, u32[]{:S(2)}, u32[]{:S(2)}) collective-permute-start(f32[40,128]{1,0:T(8,128)S(1)} %gram.1), channel_id=1, source_target_pairs={{0,2},{2,0},{4,6},{6,4},{8,10},{10,8},{12,14},{14,12},{1,3},{3,1},... | collective-permute-start | bytes 61448 | tf_op jit(solution)/shard_map/ppermute | solution.py:347
  24.4 1.5 %collective-permute-done.6 = f32[40,128]{1,0:T(8,128)S(1)} collective-permute-done((f32[40,128]{1,0:T(8,128)S(1)}, f32[40,128]{1,0:T(8,128)S(1)}, u32[]{:S(2)}, u32[]{:S(2)}) %collective-permute-start.6) | collective-permute-done | bytes 20512 | tf_op jit(solution)/shard_map/ppermute | solution.py:341
  25.9 1.4 %collective-permute-done.7 = f32[40,128]{1,0:T(8,128)S(1)} collective-permute-done((f32[40,128]{1,0:T(8,128)S(1)}, f32[40,128]{1,0:T(8,128)S(1)}, u32[]{:S(2)}, u32[]{:S(2)}) %collective-permute-start.7) | collective-permute-done | bytes 20512 | tf_op jit(solution)/shard_map/ppermute | solution.py:347
  27.3 0.0 collective-permute-start.8
  27.3 1.2 %collective-permute-done.8.recv_ref = f32[40,128]{1,0:T(8,128)S(1)} collective-permute-done((f32[40,128]{1,0:T(8,128)S(1)}, f32[40,128]{1,0:T(8,128)S(1)}, u32[]{:S(2)}, u32[]{:S(2)}) %collective-permute-start.8) | collective-permute-done | bytes 20512 | tf_op jit(solution)/shard_map/ppermute | solution.py:333
  28.5 2.8 %solve.1 = f32[8,16]{1,0:T(8,128)} custom-call(f32[40,128]{1,0:T(8,128)S(1)} %select_add_fusion.x_ref, f32[40,128]{1,0:T(8,128)S(1)} %collective-permute-done.8.recv_ref), custom_call_target="tpu_custom_call" | custom-call | tf_op jit(solution)/shard_map/solve/pallas_call | solution.py:312
  (5 shorter events, 0.0 us)
Async XLA Ops:
  0.0 6.1 %copy-start.1 = (s32[256]{0:T(256)S(1)}, s32[256]{0:T(256)}, u32[]{:S(2)}) copy-start(s32[256]{0:T(256)} %param.10) | copy-start | bytes 3076
  0.0 6.1 %copy-start = (f32[2,4096]{1,0:T(2,128)S(1)}, f32[2,4096]{1,0:T(2,128)}, u32[]{:S(2)}) copy-start(f32[2,4096]{1,0:T(2,128)} %param.11) | copy-start | bytes 98308
  5.6 1.5 %collective-permute-start = (f32[128,256]{1,0:T(8,128)S(1)}, f32[128,256]{1,0:T(8,128)S(1)}, u32[]{:S(2)}, u32[]{:S(2)}) collective-permute-start(f32[128,256]{1,0:T(8,128)S(1)} %project.1.part_ref), channel_id=1, source_target_pairs={{0,1},{1,0},{2,3},{3,2},{4,5},{5,4},{6,7},{7,6},{8,9},{9,8},{10,11... | collective-permute-start | bytes 393224 | tf_op jit(solution)/shard_map/ppermute | solution.py:333
  7.2 10.2 %collective-permute-start.2 = (f32[152,128]{1,0:T(8,128)S(1)}, f32[152,128]{1,0:T(8,128)S(1)}, u32[]{:S(2)}, u32[]{:S(2)}) collective-permute-start(f32[152,128]{1,0:T(8,128)S(1)} %get-tuple-element.11), channel_id=1, source_target_pairs={{0,8},{1,11},{2,10},{3,9},{4,12},{5,15},{6,14},{7,13},{8,0},{9,3},... | collective-permute-start | bytes 233480 | tf_op jit(solution)/shard_map/ppermute | solution.py:341
  11.2 6.2 %collective-permute-start.3 = (f32[152,128]{1,0:T(8,128)S(1)}, f32[152,128]{1,0:T(8,128)S(1)}, u32[]{:S(2)}, u32[]{:S(2)}) collective-permute-start(f32[152,128]{1,0:T(8,128)S(1)} %get-tuple-element.12), channel_id=1, source_target_pairs={{0,4},{1,7},{2,6},{3,5},{4,0},{5,3},{6,2},{7,1},{8,12},{9,15},{10,... | collective-permute-start | bytes 233480 | tf_op jit(solution)/shard_map/ppermute | solution.py:341
  12.8 6.6 %collective-permute-start.1 = (f32[152,128]{1,0:T(8,128)S(1)}, f32[152,128]{1,0:T(8,128)S(1)}, u32[]{:S(2)}, u32[]{:S(2)}) collective-permute-start(f32[152,128]{1,0:T(8,128)S(1)} %get-tuple-element.10), channel_id=1, source_target_pairs={{0,12},{1,15},{2,14},{3,13},{4,8},{5,11},{6,10},{7,9},{8,4},{9,7},... | collective-permute-start | bytes 233480 | tf_op jit(solution)/shard_map/ppermute | solution.py:341
  12.8 4.6 %collective-permute-start.4 = (f32[80,128]{1,0:T(8,128)S(1)}, f32[80,128]{1,0:T(8,128)S(1)}, u32[]{:S(2)}, u32[]{:S(2)}) collective-permute-start(f32[80,128]{1,0:T(8,128)S(1)} %get-tuple-element.13), channel_id=1, source_target_pairs={{0,2},{2,0},{4,6},{6,4},{8,10},{10,8},{12,14},{14,12},{1,3},{3,1},... | collective-permute-start | bytes 122888 | tf_op jit(solution)/shard_map/ppermute | solution.py:347
  19.9 1.7 %collective-permute-start.5 = (f32[80,1024]{1,0:T(8,128)S(1)}, f32[80,1024]{1,0:T(8,128)S(1)}, u32[]{:S(2)}, u32[]{:S(2)}) collective-permute-start(f32[80,1024]{1,0:T(8,128)S(1)} %grads.3.part_ref), channel_id=1, source_target_pairs={{0,1},{1,0},{2,3},{3,2},{4,5},{5,4},{6,7},{7,6},{8,9},{9,8},{10,11... | collective-permute-start | bytes 983048 | tf_op jit(solution)/shard_map/ppermute | solution.py:333
  22.1 3.9 %collective-permute-start.6 = (f32[40,128]{1,0:T(8,128)S(1)}, f32[40,128]{1,0:T(8,128)S(1)}, u32[]{:S(2)}, u32[]{:S(2)}) collective-permute-start(f32[40,128]{1,0:T(8,128)S(1)} %gram.1), channel_id=1, source_target_pairs={{0,4},{1,7},{2,6},{3,5},{4,0},{5,3},{6,2},{7,1},{8,12},{9,15},{10,... | collective-permute-start | bytes 61448 | tf_op jit(solution)/shard_map/ppermute | solution.py:341
  23.5 3.8 %collective-permute-start.7 = (f32[40,128]{1,0:T(8,128)S(1)}, f32[40,128]{1,0:T(8,128)S(1)}, u32[]{:S(2)}, u32[]{:S(2)}) collective-permute-start(f32[40,128]{1,0:T(8,128)S(1)} %gram.1), channel_id=1, source_target_pairs={{0,2},{2,0},{4,6},{6,4},{8,10},{10,8},{12,14},{14,12},{1,3},{3,1},... | collective-permute-start | bytes 61448 | tf_op jit(solution)/shard_map/ppermute | solution.py:347
  27.3 1.2 %collective-permute-start.8 = (f32[40,128]{1,0:T(8,128)S(1)}, f32[40,128]{1,0:T(8,128)S(1)}, u32[]{:S(2)}, u32[]{:S(2)}) collective-permute-start(f32[40,128]{1,0:T(8,128)S(1)} %select_add_fusion.x_ref), channel_id=1, source_target_pairs={{0,1},{1,0},{2,3},{3,2},{4,5},{5,4},{6,7},{7,6},{8,9},{9,8},{10,11... | collective-permute-start | bytes 61448 | tf_op jit(solution)/shard_map/ppermute | solution.py:333

commit v24 on v18

--- a/solution.py
+++ b/solution.py
@@ -115,7 +115,7 @@
 
 
 def partners(dp):
-    order = [m for far in (True, False) for m in range(1, dp) if m != SHARED and (2 * m >= dp) == far]
+    order = [m for m in range(dp - 1, 0, -1) if m != SHARED]
     return order[0::2], order[1::2]
 
 
@@ -376,8 +376,8 @@
     share = gram(grads, swap_cores(grads), docs)
     scale = float(ranks * ranks) ** -0.5
     if docs <= 64:
-        others = sum(trade([share] * (owners // 2 - 1), owners))
-        share = others + jnp.where(lax.axis_index("tensor") == 0, share, trade_shared(share))
+        both = jnp.where(lax.axis_index("tensor") == 0, share, trade_shared(share))
+        share = both + sum(trade([share] * (owners // 2 - 1), owners))
         return solve(share, swap_cores(share), docs, num_queries, scale).T
     share = lax.psum(share, "dp") * (owners / dp)
     return solve_large(jnp.concatenate([share[:, :docs], share[:, docs:]], axis=0).T, docs, num_queries, scale).T

time: 31.1 us -> 33 us (1.061)
  waiting for transfers between devices: 9.88 us -> 11.7 us
    ppermute x2, waiting for transfers between devices: 4.26 us -> 6.48 us  [trade_shared(): return lax.ppermute(x, 'dp', [(i, i ^ SHARED) for i in range(dp)])]
    ppermute x4, starting transfers between devices: 7.04 us -> 8.58 us  [trade(): got.append(lax.ppermute(x, ('dp', 'tensor'), pairs))]
    ppermute x2, starting transfers between devices: 2.64 us -> 1.3 us  [trade_shared(): return lax.ppermute(x, 'dp', [(i, i ^ SHARED) for i in range(dp)])]
    ppermute x4, waiting for transfers between devices: 2.29 us -> 1.78 us  [trade(): got.append(lax.ppermute(x, ('dp', 'tensor'), pairs))]
  transfers between devices with their start and end apart: 9 -> 9, of which waited for: 7 -> 6; matrix products, arithmetic and copies ran while one was open for 1% -> 1% of each run, Pallas kernels for 4% -> 4%
where the time goes in v24:
time: 33 us; the launch traced here: 32.9 us
  waiting for transfers between devices  11.7 us (35%)
  starting transfers between devices  10.5 us (32%)
  Pallas kernels  10.3 us (31%)
    ppermute x4, starting transfers between devices, trade(): got.append(lax.ppermute(x, ('dp', 'tensor'), pairs))  8.58 us
    ppermute x2, waiting for transfers between devices, trade_shared(): return lax.ppermute(x, 'dp', [(i, i ^ SHARED) for i in range(dp)])  6.48 us
    pallas_call x1, Pallas kernels, project(): pl.pallas_call(functools.partial(project_kernel, g_chunks, h_chunks), out...  5.59 us
    ppermute x3, waiting for transfers between devices, swap_cores(): return lax.ppermute(x, 'tensor', [(i, cores - 1 - i) for i in range(cores)])  3.47 us
    pallas_call x1, Pallas kernels, solve(): pl.pallas_call(functools.partial(solve_kernel, docs, queries, scale), out...  2.46 us
    ppermute x4, waiting for transfers between devices, trade(): got.append(lax.ppermute(x, ('dp', 'tensor'), pairs))  1.78 us
    pallas_call x2, Pallas kernels, grads_of(): pl.pallas_call(functools.partial(grads_kernel, rows_a, rows_b, docs, dp,...  1.74 us
    ppermute x2, starting transfers between devices, trade_shared(): return lax.ppermute(x, 'dp', [(i, i ^ SHARED) for i in range(dp)])  1.3 us
  transfers between devices with their start and end apart: 9, of which 6 were waited for; matrix products, arithmetic and copies ran while one was open for 1% of the time, Pallas kernels for 4%

profile of v24, /device:TPU:0, one launch (start us, length us, event | category | flops | bytes accessed | tf_op | source)
XLA Modules:
  0.0 32.9 jit_solution(2635172887213361199)
XLA Ops:
  0.0 0.0 copy-start.1
  0.0 0.0 copy-start
  0.0 5.6 %project.1.part_ref = f32[128,256]{1,0:T(8,128)S(1)} custom-call(bf16[32,56,16,128]{3,2,1,0:T(8,128)(2,1)} %bitcast.32, bf16[32,16,16,128]{3,2,1,0:T(8,128)(2,1)} %bitcast.33, bf16[8,56,16,128]{3,2,1,0:T(8,128)(2,1)} %bitcast.34, bf16[8,16,16,128]{3,2,1,0:T(8,128)(2,1)} %bitcast.35), custom_call_target="tpu_custom_call" | custom-call | flops 603979776 | bytes 11796480 | tf_op jit(solution)/shard_map/project/pallas_call | solution.py:96
  5.6 0.5 %collective-permute-start = (f32[128,256]{1,0:T(8,128)S(1)}, f32[128,256]{1,0:T(8,128)S(1)}, u32[]{:S(2)}, u32[]{:S(2)}) collective-permute-start(f32[128,256]{1,0:T(8,128)S(1)} %project.1.part_ref), channel_id=1, source_target_pairs={{0,1},{1,0},{2,3},{3,2},{4,5},{5,4},{6,7},{7,6},{8,9},{9,8},{10,11... | collective-permute-start | bytes 393224 | tf_op jit(solution)/shard_map/ppermute | solution.py:329
  6.1 0.0 copy-done.1
  6.1 0.0 copy-done
  6.1 0.2 reshape.41
  6.3 0.1 reshape.42
  6.4 0.7 %collective-permute-done.recv_ref = f32[128,256]{1,0:T(8,128)S(1)} collective-permute-done((f32[128,256]{1,0:T(8,128)S(1)}, f32[128,256]{1,0:T(8,128)S(1)}, u32[]{:S(2)}, u32[]{:S(2)}) %collective-permute-start) | collective-permute-done | bytes 131104 | tf_op jit(solution)/shard_map/ppermute | solution.py:329
  7.1 0.1 pack.1
  7.2 6.0 %collective-permute-start.2 = (f32[152,128]{1,0:T(8,128)S(1)}, f32[152,128]{1,0:T(8,128)S(1)}, u32[]{:S(2)}, u32[]{:S(2)}) collective-permute-start(f32[152,128]{1,0:T(8,128)S(1)} %get-tuple-element.11), channel_id=1, source_target_pairs={{0,14},{1,13},{2,12},{3,15},{4,10},{5,9},{6,8},{7,11},{8,6},{9,5},... | collective-permute-start | bytes 233480 | tf_op jit(solution)/shard_map/ppermute | solution.py:337
  13.2 0.0 collective-permute-start.3
  13.2 1.7 %collective-permute-start.1 = (f32[152,128]{1,0:T(8,128)S(1)}, f32[152,128]{1,0:T(8,128)S(1)}, u32[]{:S(2)}, u32[]{:S(2)}) collective-permute-start(f32[152,128]{1,0:T(8,128)S(1)} %get-tuple-element.10), channel_id=1, source_target_pairs={{0,10},{1,9},{2,8},{3,11},{4,14},{5,13},{6,12},{7,15},{8,2},{9,1},... | collective-permute-start | bytes 233480 | tf_op jit(solution)/shard_map/ppermute | solution.py:337
  14.8 0.4 %collective-permute-start.4 = (f32[80,128]{1,0:T(8,128)S(1)}, f32[80,128]{1,0:T(8,128)S(1)}, u32[]{:S(2)}, u32[]{:S(2)}) collective-permute-start(f32[80,128]{1,0:T(8,128)S(1)} %get-tuple-element.13), channel_id=1, source_target_pairs={{0,2},{2,0},{4,6},{6,4},{8,10},{10,8},{12,14},{14,12},{1,3},{3,1},... | collective-permute-start | bytes 122888 | tf_op jit(solution)/shard_map/ppermute | solution.py:343
  15.3 4.5 %collective-permute-done.4.refs_2_ = f32[80,128]{1,0:T(8,128)S(1)} collective-permute-done((f32[80,128]{1,0:T(8,128)S(1)}, f32[80,128]{1,0:T(8,128)S(1)}, u32[]{:S(2)}, u32[]{:S(2)}) %collective-permute-start.4) | collective-permute-done | bytes 40992 | tf_op jit(solution)/shard_map/ppermute | solution.py:343
  19.8 0.0 collective-permute-done.2.refs_0_
  19.8 0.0 collective-permute-done.3.refs_1_
  19.8 1.2 %grads.2.refs_1_ = f32[80,1024]{1,0:T(8,128)S(1)} custom-call(f32[152,128]{1,0:T(8,128)S(1)} %collective-permute-done.2.refs_0_, f32[152,128]{1,0:T(8,128)S(1)} %collective-permute-done.3.refs_1_, f32[80,128]{1,0:T(8,128)S(1)} %collective-permute-done.4.refs_2_, f32[80,128]{1,0:T(8,128)S(1)} %get-tuple-element.14.refs_3_), custom_call_target="tpu_custom_call" | custom-call | flops 201326592 | bytes 196608 | tf_op jit(solution)/shard_map/grads/pallas_call | solution.py:220
  21.0 0.0 collective-permute-done.1.refs_0_
  21.0 0.5 %grads.3.part_ref = f32[80,1024]{1,0:T(8,128)S(1)} custom-call(f32[152,128]{1,0:T(8,128)S(1)} %collective-permute-done.1.refs_0_, f32[80,1024]{1,0:T(8,128)S(1)} %grads.2.refs_1_), custom_call_target="tpu_custom_call" | custom-call | flops 67108864 | bytes 65536 | tf_op jit(solution)/shard_map/grads/pallas_call | solution.py:220
  21.5 0.1 collective-permute-start.5
  21.6 1.6 %collective-permute-done.5.recv_ref = f32[80,1024]{1,0:T(8,128)S(1)} collective-permute-done((f32[80,1024]{1,0:T(8,128)S(1)}, f32[80,1024]{1,0:T(8,128)S(1)}, u32[]{:S(2)}, u32[]{:S(2)}) %collective-permute-start.5) | collective-permute-done | bytes 327712 | tf_op jit(solution)/shard_map/ppermute | solution.py:329
  23.2 0.4 %gram.1 = f32[40,128]{1,0:T(8,128)S(1)} custom-call(f32[80,1024]{1,0:T(8,128)S(1)} %grads.3.part_ref, f32[80,1024]{1,0:T(8,128)S(1)} %collective-permute-done.5.recv_ref), custom_call_target="tpu_custom_call" | custom-call | tf_op jit(solution)/shard_map/gram/pallas_call | solution.py:259
  23.6 0.9 %collective-permute-start.6 = (f32[40,128]{1,0:T(8,128)S(1)}, f32[40,128]{1,0:T(8,128)S(1)}, u32[]{:S(2)}, u32[]{:S(2)}) collective-permute-start(f32[40,128]{1,0:T(8,128)S(1)} %gram.1), channel_id=1, source_target_pairs={{0,2},{2,0},{4,6},{6,4},{8,10},{10,8},{12,14},{14,12},{1,3},{3,1},... | collective-permute-start | bytes 61448 | tf_op jit(solution)/shard_map/ppermute | solution.py:343
  24.5 0.9 %collective-permute-start.7 = (f32[40,128]{1,0:T(8,128)S(1)}, f32[40,128]{1,0:T(8,128)S(1)}, u32[]{:S(2)}, u32[]{:S(2)}) collective-permute-start(f32[40,128]{1,0:T(8,128)S(1)} %gram.1), channel_id=1, source_target_pairs={{0,6},{1,5},{2,4},{3,7},{4,2},{5,1},{6,0},{7,3},{8,14},{9,13},{10,... | collective-permute-start | bytes 61448 | tf_op jit(solution)/shard_map/ppermute | solution.py:337
  25.5 2.0 %collective-permute-done.6 = f32[40,128]{1,0:T(8,128)S(1)} collective-permute-done((f32[40,128]{1,0:T(8,128)S(1)}, f32[40,128]{1,0:T(8,128)S(1)}, u32[]{:S(2)}, u32[]{:S(2)}) %collective-permute-start.6) | collective-permute-done | bytes 20512 | tf_op jit(solution)/shard_map/ppermute | solution.py:343
  27.4 1.8 %collective-permute-done.7 = f32[40,128]{1,0:T(8,128)S(1)} collective-permute-done((f32[40,128]{1,0:T(8,128)S(1)}, f32[40,128]{1,0:T(8,128)S(1)}, u32[]{:S(2)}, u32[]{:S(2)}) %collective-permute-start.7) | collective-permute-done | bytes 20512 | tf_op jit(solution)/shard_map/ppermute | solution.py:337
  29.2 0.0 collective-permute-start.8
  29.2 1.2 %collective-permute-done.8.recv_ref = f32[40,128]{1,0:T(8,128)S(1)} collective-permute-done((f32[40,128]{1,0:T(8,128)S(1)}, f32[40,128]{1,0:T(8,128)S(1)}, u32[]{:S(2)}, u32[]{:S(2)}) %collective-permute-start.8) | collective-permute-done | bytes 20512 | tf_op jit(solution)/shard_map/ppermute | solution.py:329
  30.4 2.5 %solve.1 = f32[8,16]{1,0:T(8,128)} custom-call(f32[40,128]{1,0:T(8,128)S(1)} %select_add_fusion.x_ref, f32[40,128]{1,0:T(8,128)S(1)} %collective-permute-done.8.recv_ref), custom_call_target="tpu_custom_call" | custom-call | tf_op jit(solution)/shard_map/solve/pallas_call | solution.py:308
  (5 shorter events, 0.0 us)
Async XLA Ops:
  0.0 6.1 %copy-start.1 = (s32[256]{0:T(256)S(1)}, s32[256]{0:T(256)}, u32[]{:S(2)}) copy-start(s32[256]{0:T(256)} %param.10) | copy-start | bytes 3076
  0.0 6.1 %copy-start = (f32[2,4096]{1,0:T(2,128)S(1)}, f32[2,4096]{1,0:T(2,128)}, u32[]{:S(2)}) copy-start(f32[2,4096]{1,0:T(2,128)} %param.11) | copy-start | bytes 98308
  5.6 1.5 %collective-permute-start = (f32[128,256]{1,0:T(8,128)S(1)}, f32[128,256]{1,0:T(8,128)S(1)}, u32[]{:S(2)}, u32[]{:S(2)}) collective-permute-start(f32[128,256]{1,0:T(8,128)S(1)} %project.1.part_ref), channel_id=1, source_target_pairs={{0,1},{1,0},{2,3},{3,2},{4,5},{5,4},{6,7},{7,6},{8,9},{9,8},{10,11... | collective-permute-start | bytes 393224 | tf_op jit(solution)/shard_map/ppermute | solution.py:329
  7.2 12.6 %collective-permute-start.2 = (f32[152,128]{1,0:T(8,128)S(1)}, f32[152,128]{1,0:T(8,128)S(1)}, u32[]{:S(2)}, u32[]{:S(2)}) collective-permute-start(f32[152,128]{1,0:T(8,128)S(1)} %get-tuple-element.11), channel_id=1, source_target_pairs={{0,14},{1,13},{2,12},{3,15},{4,10},{5,9},{6,8},{7,11},{8,6},{9,5},... | collective-permute-start | bytes 233480 | tf_op jit(solution)/shard_map/ppermute | solution.py:337
  13.2 6.6 %collective-permute-start.3 = (f32[152,128]{1,0:T(8,128)S(1)}, f32[152,128]{1,0:T(8,128)S(1)}, u32[]{:S(2)}, u32[]{:S(2)}) collective-permute-start(f32[152,128]{1,0:T(8,128)S(1)} %get-tuple-element.12), channel_id=1, source_target_pairs={{0,6},{1,5},{2,4},{3,7},{4,2},{5,1},{6,0},{7,3},{8,14},{9,13},{10,... | collective-permute-start | bytes 233480 | tf_op jit(solution)/shard_map/ppermute | solution.py:337
  13.2 7.8 %collective-permute-start.1 = (f32[152,128]{1,0:T(8,128)S(1)}, f32[152,128]{1,0:T(8,128)S(1)}, u32[]{:S(2)}, u32[]{:S(2)}) collective-permute-start(f32[152,128]{1,0:T(8,128)S(1)} %get-tuple-element.10), channel_id=1, source_target_pairs={{0,10},{1,9},{2,8},{3,11},{4,14},{5,13},{6,12},{7,15},{8,2},{9,1},... | collective-permute-start | bytes 233480 | tf_op jit(solution)/shard_map/ppermute | solution.py:337
  14.8 4.9 %collective-permute-start.4 = (f32[80,128]{1,0:T(8,128)S(1)}, f32[80,128]{1,0:T(8,128)S(1)}, u32[]{:S(2)}, u32[]{:S(2)}) collective-permute-start(f32[80,128]{1,0:T(8,128)S(1)} %get-tuple-element.13), channel_id=1, source_target_pairs={{0,2},{2,0},{4,6},{6,4},{8,10},{10,8},{12,14},{14,12},{1,3},{3,1},... | collective-permute-start | bytes 122888 | tf_op jit(solution)/shard_map/ppermute | solution.py:343
  21.5 1.7 %collective-permute-start.5 = (f32[80,1024]{1,0:T(8,128)S(1)}, f32[80,1024]{1,0:T(8,128)S(1)}, u32[]{:S(2)}, u32[]{:S(2)}) collective-permute-start(f32[80,1024]{1,0:T(8,128)S(1)} %grads.3.part_ref), channel_id=1, source_target_pairs={{0,1},{1,0},{2,3},{3,2},{4,5},{5,4},{6,7},{7,6},{8,9},{9,8},{10,11... | collective-permute-start | bytes 983048 | tf_op jit(solution)/shard_map/ppermute | solution.py:329
  23.6 3.8 %collective-permute-start.6 = (f32[40,128]{1,0:T(8,128)S(1)}, f32[40,128]{1,0:T(8,128)S(1)}, u32[]{:S(2)}, u32[]{:S(2)}) collective-permute-start(f32[40,128]{1,0:T(8,128)S(1)} %gram.1), channel_id=1, source_target_pairs={{0,2},{2,0},{4,6},{6,4},{8,10},{10,8},{12,14},{14,12},{1,3},{3,1},... | collective-permute-start | bytes 61448 | tf_op jit(solution)/shard_map/ppermute | solution.py:343
  24.5 4.7 %collective-permute-start.7 = (f32[40,128]{1,0:T(8,128)S(1)}, f32[40,128]{1,0:T(8,128)S(1)}, u32[]{:S(2)}, u32[]{:S(2)}) collective-permute-start(f32[40,128]{1,0:T(8,128)S(1)} %gram.1), channel_id=1, source_target_pairs={{0,6},{1,5},{2,4},{3,7},{4,2},{5,1},{6,0},{7,3},{8,14},{9,13},{10,... | collective-permute-start | bytes 61448 | tf_op jit(solution)/shard_map/ppermute | solution.py:337
  29.2 1.2 %collective-permute-start.8 = (f32[40,128]{1,0:T(8,128)S(1)}, f32[40,128]{1,0:T(8,128)S(1)}, u32[]{:S(2)}, u32[]{:S(2)}) collective-permute-start(f32[40,128]{1,0:T(8,128)S(1)} %select_add_fusion.x_ref), channel_id=1, source_target_pairs={{0,1},{1,0},{2,3},{3,2},{4,5},{5,4},{6,7},{7,6},{8,9},{9,8},{10,11... | collective-permute-start | bytes 61448 | tf_op jit(solution)/shard_map/ppermute | solution.py:329

commit v25 on v18

--- a/solution.py
+++ b/solution.py
@@ -116,7 +116,8 @@
 
 def partners(dp):
     order = [m for far in (True, False) for m in range(1, dp) if m != SHARED and (2 * m >= dp) == far]
-    return order[0::2], order[1::2]
+    pairs = [order[i:i + 2] if i % 4 == 0 else order[i:i + 2][::-1] for i in range(0, len(order), 2)]
+    return [x for x, _ in pairs], [y for _, y in pairs]
 
 
 def partner(dp, t):

time: 31.1 us -> 30.9 us (level)
  starting transfers between devices: 10.4 us -> 8.91 us
  waiting for transfers between devices: 9.88 us -> 11.2 us
    ppermute x2, starting transfers between devices: 2.64 us -> 1.19 us  [trade_shared(): return lax.ppermute(x, 'dp', [(i, i ^ SHARED) for i in range(dp)])]
    ppermute x4, waiting for transfers between devices: 2.29 us -> 3.62 us  [trade(): got.append(lax.ppermute(x, ('dp', 'tensor'), pairs))]
where the time goes in v25:
time: 30.9 us; the launch traced here: 30.7 us
  waiting for transfers between devices  11.2 us (36%)
  Pallas kernels  10.3 us (33%)
  starting transfers between devices  8.91 us (29%)
    ppermute x4, starting transfers between devices, trade(): got.append(lax.ppermute(x, ('dp', 'tensor'), pairs))  7.13 us
    pallas_call x1, Pallas kernels, project(): pl.pallas_call(functools.partial(project_kernel, g_chunks, h_chunks), out...  5.59 us
    ppermute x2, waiting for transfers between devices, trade_shared(): return lax.ppermute(x, 'dp', [(i, i ^ SHARED) for i in range(dp)])  4.07 us
    ppermute x4, waiting for transfers between devices, trade(): got.append(lax.ppermute(x, ('dp', 'tensor'), pairs))  3.62 us
    ppermute x3, waiting for transfers between devices, swap_cores(): return lax.ppermute(x, 'tensor', [(i, cores - 1 - i) for i in range(cores)])  3.47 us
    pallas_call x1, Pallas kernels, solve(): pl.pallas_call(functools.partial(solve_kernel, docs, queries, scale), out...  2.46 us
    pallas_call x2, Pallas kernels, grads_of(): pl.pallas_call(functools.partial(grads_kernel, rows_a, rows_b, docs, dp,...  1.74 us
    ppermute x2, starting transfers between devices, trade_shared(): return lax.ppermute(x, 'dp', [(i, i ^ SHARED) for i in range(dp)])  1.19 us
  transfers between devices with their start and end apart: 9, of which 7 were waited for; matrix products, arithmetic and copies ran while one was open for 1% of the time, Pallas kernels for 4%

profile of v25, /device:TPU:0, one launch (start us, length us, event | category | flops | bytes accessed | tf_op | source)
XLA Modules:
  0.0 30.7 jit_solution(5814779194732946289)
XLA Ops:
  0.0 0.0 copy-start.1
  0.0 0.0 copy-start
  0.0 5.6 %project.1.part_ref = f32[128,256]{1,0:T(8,128)S(1)} custom-call(bf16[32,56,16,128]{3,2,1,0:T(8,128)(2,1)} %bitcast.32, bf16[32,16,16,128]{3,2,1,0:T(8,128)(2,1)} %bitcast.33, bf16[8,56,16,128]{3,2,1,0:T(8,128)(2,1)} %bitcast.34, bf16[8,16,16,128]{3,2,1,0:T(8,128)(2,1)} %bitcast.35), custom_call_target="tpu_custom_call" | custom-call | flops 603979776 | bytes 11796480 | tf_op jit(solution)/shard_map/project/pallas_call | solution.py:96
  5.6 0.5 %collective-permute-start = (f32[128,256]{1,0:T(8,128)S(1)}, f32[128,256]{1,0:T(8,128)S(1)}, u32[]{:S(2)}, u32[]{:S(2)}) collective-permute-start(f32[128,256]{1,0:T(8,128)S(1)} %project.1.part_ref), channel_id=1, source_target_pairs={{0,1},{1,0},{2,3},{3,2},{4,5},{5,4},{6,7},{7,6},{8,9},{9,8},{10,11... | collective-permute-start | bytes 393224 | tf_op jit(solution)/shard_map/ppermute | solution.py:330
  6.1 0.0 copy-done.1
  6.1 0.0 copy-done
  6.1 0.2 reshape.41
  6.3 0.1 reshape.42
  6.4 0.7 %collective-permute-done.recv_ref = f32[128,256]{1,0:T(8,128)S(1)} collective-permute-done((f32[128,256]{1,0:T(8,128)S(1)}, f32[128,256]{1,0:T(8,128)S(1)}, u32[]{:S(2)}, u32[]{:S(2)}) %collective-permute-start) | collective-permute-done | bytes 131104 | tf_op jit(solution)/shard_map/ppermute | solution.py:330
  7.1 0.1 pack.1
  7.2 4.0 %collective-permute-start.2 = (f32[152,128]{1,0:T(8,128)S(1)}, f32[152,128]{1,0:T(8,128)S(1)}, u32[]{:S(2)}, u32[]{:S(2)}) collective-permute-start(f32[152,128]{1,0:T(8,128)S(1)} %get-tuple-element.11), channel_id=1, source_target_pairs={{0,8},{1,11},{2,10},{3,9},{4,12},{5,15},{6,14},{7,13},{8,0},{9,3},... | collective-permute-start | bytes 233480 | tf_op jit(solution)/shard_map/ppermute | solution.py:338
  11.2 1.6 %collective-permute-start.3 = (f32[152,128]{1,0:T(8,128)S(1)}, f32[152,128]{1,0:T(8,128)S(1)}, u32[]{:S(2)}, u32[]{:S(2)}) collective-permute-start(f32[152,128]{1,0:T(8,128)S(1)} %get-tuple-element.12), channel_id=1, source_target_pairs={{0,4},{1,7},{2,6},{3,5},{4,0},{5,3},{6,2},{7,1},{8,12},{9,15},{10,... | collective-permute-start | bytes 233480 | tf_op jit(solution)/shard_map/ppermute | solution.py:338
  12.8 1.2 %collective-permute-start.1 = (f32[152,128]{1,0:T(8,128)S(1)}, f32[152,128]{1,0:T(8,128)S(1)}, u32[]{:S(2)}, u32[]{:S(2)}) collective-permute-start(f32[152,128]{1,0:T(8,128)S(1)} %get-tuple-element.10), channel_id=1, source_target_pairs={{0,14},{1,13},{2,12},{3,15},{4,10},{5,9},{6,8},{7,11},{8,6},{9,5},... | collective-permute-start | bytes 233480 | tf_op jit(solution)/shard_map/ppermute | solution.py:338
  13.9 0.3 %collective-permute-start.4 = (f32[80,128]{1,0:T(8,128)S(1)}, f32[80,128]{1,0:T(8,128)S(1)}, u32[]{:S(2)}, u32[]{:S(2)}) collective-permute-start(f32[80,128]{1,0:T(8,128)S(1)} %get-tuple-element.13), channel_id=1, source_target_pairs={{0,2},{2,0},{4,6},{6,4},{8,10},{10,8},{12,14},{14,12},{1,3},{3,1},... | collective-permute-start | bytes 122888 | tf_op jit(solution)/shard_map/ppermute | solution.py:344
  14.3 3.7 %collective-permute-done.4.refs_2_ = f32[80,128]{1,0:T(8,128)S(1)} collective-permute-done((f32[80,128]{1,0:T(8,128)S(1)}, f32[80,128]{1,0:T(8,128)S(1)}, u32[]{:S(2)}, u32[]{:S(2)}) %collective-permute-start.4) | collective-permute-done | bytes 40992 | tf_op jit(solution)/shard_map/ppermute | solution.py:344
  18.0 0.0 collective-permute-done.2.refs_0_
  18.0 0.0 collective-permute-done.3.refs_1_
  18.0 1.2 %grads.2.refs_1_ = f32[80,1024]{1,0:T(8,128)S(1)} custom-call(f32[152,128]{1,0:T(8,128)S(1)} %collective-permute-done.2.refs_0_, f32[152,128]{1,0:T(8,128)S(1)} %collective-permute-done.3.refs_1_, f32[80,128]{1,0:T(8,128)S(1)} %collective-permute-done.4.refs_2_, f32[80,128]{1,0:T(8,128)S(1)} %get-tuple-element.14.refs_3_), custom_call_target="tpu_custom_call" | custom-call | flops 201326592 | bytes 196608 | tf_op jit(solution)/shard_map/grads/pallas_call | solution.py:221
  19.2 1.0 %collective-permute-done.1.refs_0_ = f32[152,128]{1,0:T(8,128)S(1)} collective-permute-done((f32[152,128]{1,0:T(8,128)S(1)}, f32[152,128]{1,0:T(8,128)S(1)}, u32[]{:S(2)}, u32[]{:S(2)}) %collective-permute-start.1) | collective-permute-done | bytes 77856 | tf_op jit(solution)/shard_map/ppermute | solution.py:338
  20.3 0.5 %grads.3.part_ref = f32[80,1024]{1,0:T(8,128)S(1)} custom-call(f32[152,128]{1,0:T(8,128)S(1)} %collective-permute-done.1.refs_0_, f32[80,1024]{1,0:T(8,128)S(1)} %grads.2.refs_1_), custom_call_target="tpu_custom_call" | custom-call | flops 67108864 | bytes 65536 | tf_op jit(solution)/shard_map/grads/pallas_call | solution.py:221
  20.8 0.1 collective-permute-start.5
  20.9 1.6 %collective-permute-done.5.recv_ref = f32[80,1024]{1,0:T(8,128)S(1)} collective-permute-done((f32[80,1024]{1,0:T(8,128)S(1)}, f32[80,1024]{1,0:T(8,128)S(1)}, u32[]{:S(2)}, u32[]{:S(2)}) %collective-permute-start.5) | collective-permute-done | bytes 327712 | tf_op jit(solution)/shard_map/ppermute | solution.py:330
  22.5 0.4 %gram.1 = f32[40,128]{1,0:T(8,128)S(1)} custom-call(f32[80,1024]{1,0:T(8,128)S(1)} %grads.3.part_ref, f32[80,1024]{1,0:T(8,128)S(1)} %collective-permute-done.5.recv_ref), custom_call_target="tpu_custom_call" | custom-call | tf_op jit(solution)/shard_map/gram/pallas_call | solution.py:260
  22.9 0.4 %collective-permute-start.6 = (f32[40,128]{1,0:T(8,128)S(1)}, f32[40,128]{1,0:T(8,128)S(1)}, u32[]{:S(2)}, u32[]{:S(2)}) collective-permute-start(f32[40,128]{1,0:T(8,128)S(1)} %gram.1), channel_id=1, source_target_pairs={{0,4},{1,7},{2,6},{3,5},{4,0},{5,3},{6,2},{7,1},{8,12},{9,15},{10,... | collective-permute-start | bytes 61448 | tf_op jit(solution)/shard_map/ppermute | solution.py:338
  23.3 0.8 %collective-permute-start.7 = (f32[40,128]{1,0:T(8,128)S(1)}, f32[40,128]{1,0:T(8,128)S(1)}, u32[]{:S(2)}, u32[]{:S(2)}) collective-permute-start(f32[40,128]{1,0:T(8,128)S(1)} %gram.1), channel_id=1, source_target_pairs={{0,2},{2,0},{4,6},{6,4},{8,10},{10,8},{12,14},{14,12},{1,3},{3,1},... | collective-permute-start | bytes 61448 | tf_op jit(solution)/shard_map/ppermute | solution.py:344
  24.1 2.6 %collective-permute-done.6 = f32[40,128]{1,0:T(8,128)S(1)} collective-permute-done((f32[40,128]{1,0:T(8,128)S(1)}, f32[40,128]{1,0:T(8,128)S(1)}, u32[]{:S(2)}, u32[]{:S(2)}) %collective-permute-start.6) | collective-permute-done | bytes 20512 | tf_op jit(solution)/shard_map/ppermute | solution.py:338
  26.7 0.4 %collective-permute-done.7 = f32[40,128]{1,0:T(8,128)S(1)} collective-permute-done((f32[40,128]{1,0:T(8,128)S(1)}, f32[40,128]{1,0:T(8,128)S(1)}, u32[]{:S(2)}, u32[]{:S(2)}) %collective-permute-start.7) | collective-permute-done | bytes 20512 | tf_op jit(solution)/shard_map/ppermute | solution.py:344
  27.1 0.0 collective-permute-start.8
  27.1 1.2 %collective-permute-done.8.recv_ref = f32[40,128]{1,0:T(8,128)S(1)} collective-permute-done((f32[40,128]{1,0:T(8,128)S(1)}, f32[40,128]{1,0:T(8,128)S(1)}, u32[]{:S(2)}, u32[]{:S(2)}) %collective-permute-start.8) | collective-permute-done | bytes 20512 | tf_op jit(solution)/shard_map/ppermute | solution.py:330
  28.3 2.5 %solve.1 = f32[8,16]{1,0:T(8,128)} custom-call(f32[40,128]{1,0:T(8,128)S(1)} %select_add_fusion.x_ref, f32[40,128]{1,0:T(8,128)S(1)} %collective-permute-done.8.recv_ref), custom_call_target="tpu_custom_call" | custom-call | tf_op jit(solution)/shard_map/solve/pallas_call | solution.py:309
  (5 shorter events, 0.0 us)
Async XLA Ops:
  0.0 6.1 %copy-start.1 = (s32[256]{0:T(256)S(1)}, s32[256]{0:T(256)}, u32[]{:S(2)}) copy-start(s32[256]{0:T(256)} %param.10) | copy-start | bytes 3076
  0.0 6.1 %copy-start = (f32[2,4096]{1,0:T(2,128)S(1)}, f32[2,4096]{1,0:T(2,128)}, u32[]{:S(2)}) copy-start(f32[2,4096]{1,0:T(2,128)} %param.11) | copy-start | bytes 98308
  5.6 1.5 %collective-permute-start = (f32[128,256]{1,0:T(8,128)S(1)}, f32[128,256]{1,0:T(8,128)S(1)}, u32[]{:S(2)}, u32[]{:S(2)}) collective-permute-start(f32[128,256]{1,0:T(8,128)S(1)} %project.1.part_ref), channel_id=1, source_target_pairs={{0,1},{1,0},{2,3},{3,2},{4,5},{5,4},{6,7},{7,6},{8,9},{9,8},{10,11... | collective-permute-start | bytes 393224 | tf_op jit(solution)/shard_map/ppermute | solution.py:330
  7.2 10.8 %collective-permute-start.2 = (f32[152,128]{1,0:T(8,128)S(1)}, f32[152,128]{1,0:T(8,128)S(1)}, u32[]{:S(2)}, u32[]{:S(2)}) collective-permute-start(f32[152,128]{1,0:T(8,128)S(1)} %get-tuple-element.11), channel_id=1, source_target_pairs={{0,8},{1,11},{2,10},{3,9},{4,12},{5,15},{6,14},{7,13},{8,0},{9,3},... | collective-permute-start | bytes 233480 | tf_op jit(solution)/shard_map/ppermute | solution.py:338
  11.2 6.8 %collective-permute-start.3 = (f32[152,128]{1,0:T(8,128)S(1)}, f32[152,128]{1,0:T(8,128)S(1)}, u32[]{:S(2)}, u32[]{:S(2)}) collective-permute-start(f32[152,128]{1,0:T(8,128)S(1)} %get-tuple-element.12), channel_id=1, source_target_pairs={{0,4},{1,7},{2,6},{3,5},{4,0},{5,3},{6,2},{7,1},{8,12},{9,15},{10,... | collective-permute-start | bytes 233480 | tf_op jit(solution)/shard_map/ppermute | solution.py:338
  12.8 7.5 %collective-permute-start.1 = (f32[152,128]{1,0:T(8,128)S(1)}, f32[152,128]{1,0:T(8,128)S(1)}, u32[]{:S(2)}, u32[]{:S(2)}) collective-permute-start(f32[152,128]{1,0:T(8,128)S(1)} %get-tuple-element.10), channel_id=1, source_target_pairs={{0,14},{1,13},{2,12},{3,15},{4,10},{5,9},{6,8},{7,11},{8,6},{9,5},... | collective-permute-start | bytes 233480 | tf_op jit(solution)/shard_map/ppermute | solution.py:338
  13.9 4.1 %collective-permute-start.4 = (f32[80,128]{1,0:T(8,128)S(1)}, f32[80,128]{1,0:T(8,128)S(1)}, u32[]{:S(2)}, u32[]{:S(2)}) collective-permute-start(f32[80,128]{1,0:T(8,128)S(1)} %get-tuple-element.13), channel_id=1, source_target_pairs={{0,2},{2,0},{4,6},{6,4},{8,10},{10,8},{12,14},{14,12},{1,3},{3,1},... | collective-permute-start | bytes 122888 | tf_op jit(solution)/shard_map/ppermute | solution.py:344
  20.8 1.7 %collective-permute-start.5 = (f32[80,1024]{1,0:T(8,128)S(1)}, f32[80,1024]{1,0:T(8,128)S(1)}, u32[]{:S(2)}, u32[]{:S(2)}) collective-permute-start(f32[80,1024]{1,0:T(8,128)S(1)} %grads.3.part_ref), channel_id=1, source_target_pairs={{0,1},{1,0},{2,3},{3,2},{4,5},{5,4},{6,7},{7,6},{8,9},{9,8},{10,11... | collective-permute-start | bytes 983048 | tf_op jit(solution)/shard_map/ppermute | solution.py:330
  22.9 3.8 %collective-permute-start.6 = (f32[40,128]{1,0:T(8,128)S(1)}, f32[40,128]{1,0:T(8,128)S(1)}, u32[]{:S(2)}, u32[]{:S(2)}) collective-permute-start(f32[40,128]{1,0:T(8,128)S(1)} %gram.1), channel_id=1, source_target_pairs={{0,4},{1,7},{2,6},{3,5},{4,0},{5,3},{6,2},{7,1},{8,12},{9,15},{10,... | collective-permute-start | bytes 61448 | tf_op jit(solution)/shard_map/ppermute | solution.py:338
  23.3 3.8 %collective-permute-start.7 = (f32[40,128]{1,0:T(8,128)S(1)}, f32[40,128]{1,0:T(8,128)S(1)}, u32[]{:S(2)}, u32[]{:S(2)}) collective-permute-start(f32[40,128]{1,0:T(8,128)S(1)} %gram.1), channel_id=1, source_target_pairs={{0,2},{2,0},{4,6},{6,4},{8,10},{10,8},{12,14},{14,12},{1,3},{3,1},... | collective-permute-start | bytes 61448 | tf_op jit(solution)/shard_map/ppermute | solution.py:344
  27.1 1.2 %collective-permute-start.8 = (f32[40,128]{1,0:T(8,128)S(1)}, f32[40,128]{1,0:T(8,128)S(1)}, u32[]{:S(2)}, u32[]{:S(2)}) collective-permute-start(f32[40,128]{1,0:T(8,128)S(1)} %select_add_fusion.x_ref), channel_id=1, source_target_pairs={{0,1},{1,0},{2,3},{3,2},{4,5},{5,4},{6,7},{7,6},{8,9},{9,8},{10,11... | collective-permute-start | bytes 61448 | tf_op jit(solution)/shard_map/ppermute | solution.py:330

commit v26 on v18

--- a/solution.py
+++ b/solution.py
@@ -55,12 +55,18 @@
         blocks = [ref[:, j].reshape(ref.shape[0] * 16, LANES) for j in range(first, first + size)]
         return jnp.concatenate(blocks, axis=1)
 
-    totals = [None, None]
+    totals, streamed = [None, None], None
     for i, (_, proj_buf, _, data_buf, (first, size)) in enumerate(plan):
         for copy in copies[i]:
             copy.wait()
         start(i + FLIGHT)
         which = 0 if i < len(g_chunks) else 1
+        if which == 1 and (i - len(g_chunks)) % 5 == 2:
+            part = lax.dot_general(
+                line_up(data_buf, first, size), line_up(proj_buf, first, size), NT, preferred_element_type=jnp.float32
+            )
+            streamed = part if streamed is None else streamed + part
+            continue
         part = lax.dot_general(
             line_up(proj_buf, first, size), line_up(data_buf, first, size), NT, preferred_element_type=jnp.float32
         )
@@ -84,6 +90,14 @@
                 at = i // 2 * LANES
                 out_ref[done:done + 8, at:at + LANES] = jnp.take_along_axis(both, order, axis=1)
             done += 8
+    if streamed is not None:
+        side = lax.broadcasted_iota(jnp.int32, (8, streamed.shape[1]), 1) % 16 < 8
+        lines = [jnp.where(side, streamed[j:j + 8], streamed[j + 8:j + 16]) for j in range(0, streamed.shape[0], 16)]
+        lines = jnp.concatenate(lines, axis=0).T
+        begin = out_ref.shape[0] - lines.shape[0] // 2
+        for g in range(0, lines.shape[0], 16):
+            at = slice(begin + g // 2, begin + g // 2 + 8)
+            out_ref[at, :] = out_ref[at, :] + (lines[g:g + 8] + lines[g + 8:g + 16])
 
 
 def project(hidden, out_grad, pin_t, pout_t):

time: 31.1 us -> 31.4 us (level)
    pallas_call x1, Pallas kernels: 5.59 us -> 5.92 us  [project(): pl.pallas_call(functools.partial(project_kernel, g_chunks, h_chunks), out...]
where the time goes in v26:
time: 31.4 us; the launch traced here: 31.3 us
  Pallas kernels  10.6 us (34%)
  starting transfers between devices  10.5 us (33%)
  waiting for transfers between devices  9.81 us (31%)
    ppermute x4, starting transfers between devices, trade(): got.append(lax.ppermute(x, ('dp', 'tensor'), pairs))  7.09 us
    pallas_call x1, Pallas kernels, project(): pl.pallas_call(functools.partial(project_kernel, g_chunks, h_chunks), out...  5.92 us
    ppermute x2, waiting for transfers between devices, trade_shared(): return lax.ppermute(x, 'dp', [(i, i ^ SHARED) for i in range(dp)])  4.37 us
    ppermute x3, waiting for transfers between devices, swap_cores(): return lax.ppermute(x, 'tensor', [(i, cores - 1 - i) for i in range(cores)])  3.31 us
    ppermute x2, starting transfers between devices, trade_shared(): return lax.ppermute(x, 'dp', [(i, i ^ SHARED) for i in range(dp)])  2.66 us
    pallas_call x1, Pallas kernels, solve(): pl.pallas_call(functools.partial(solve_kernel, docs, queries, scale), out...  2.46 us
    ppermute x4, waiting for transfers between devices, trade(): got.append(lax.ppermute(x, ('dp', 'tensor'), pairs))  2.13 us
    pallas_call x2, Pallas kernels, grads_of(): pl.pallas_call(functools.partial(grads_kernel, rows_a, rows_b, docs, dp,...  1.73 us
  transfers between devices with their start and end apart: 9, of which 7 were waited for; matrix products, arithmetic and copies ran while one was open for 1% of the time, Pallas kernels for 4%

profile of v26, /device:TPU:0, one launch (start us, length us, event | category | flops | bytes accessed | tf_op | source)
XLA Modules:
  0.0 31.3 jit_solution(17486875517962430567)
XLA Ops:
  0.0 0.0 copy-start.1
  0.0 0.0 copy-start
  0.0 5.9 %project.1.part_ref = f32[128,256]{1,0:T(8,128)S(1)} custom-call(bf16[32,56,16,128]{3,2,1,0:T(8,128)(2,1)} %bitcast.32, bf16[32,16,16,128]{3,2,1,0:T(8,128)(2,1)} %bitcast.33, bf16[8,56,16,128]{3,2,1,0:T(8,128)(2,1)} %bitcast.34, bf16[8,16,16,128]{3,2,1,0:T(8,128)(2,1)} %bitcast.35), custom_call_target="tpu_custom_call" | custom-call | flops 603979776 | bytes 11796480 | tf_op jit(solution)/shard_map/project/pallas_call | solution.py:110
  5.9 0.5 %collective-permute-start = (f32[128,256]{1,0:T(8,128)S(1)}, f32[128,256]{1,0:T(8,128)S(1)}, u32[]{:S(2)}, u32[]{:S(2)}) collective-permute-start(f32[128,256]{1,0:T(8,128)S(1)} %project.1.part_ref), channel_id=1, source_target_pairs={{0,1},{1,0},{2,3},{3,2},{4,5},{5,4},{6,7},{7,6},{8,9},{9,8},{10,11... | collective-permute-start | bytes 393224 | tf_op jit(solution)/shard_map/ppermute | solution.py:343
  6.5 0.0 copy-done.1
  6.5 0.0 copy-done
  6.5 0.2 reshape.41
  6.6 0.1 reshape.42
  6.8 0.7 %collective-permute-done.recv_ref = f32[128,256]{1,0:T(8,128)S(1)} collective-permute-done((f32[128,256]{1,0:T(8,128)S(1)}, f32[128,256]{1,0:T(8,128)S(1)}, u32[]{:S(2)}, u32[]{:S(2)}) %collective-permute-start) | collective-permute-done | bytes 131104 | tf_op jit(solution)/shard_map/ppermute | solution.py:343
  7.4 0.1 pack.1
  7.5 4.0 %collective-permute-start.2 = (f32[152,128]{1,0:T(8,128)S(1)}, f32[152,128]{1,0:T(8,128)S(1)}, u32[]{:S(2)}, u32[]{:S(2)}) collective-permute-start(f32[152,128]{1,0:T(8,128)S(1)} %get-tuple-element.11), channel_id=1, source_target_pairs={{0,8},{1,11},{2,10},{3,9},{4,12},{5,15},{6,14},{7,13},{8,0},{9,3},... | collective-permute-start | bytes 233480 | tf_op jit(solution)/shard_map/ppermute | solution.py:351
  11.5 1.6 %collective-permute-start.3 = (f32[152,128]{1,0:T(8,128)S(1)}, f32[152,128]{1,0:T(8,128)S(1)}, u32[]{:S(2)}, u32[]{:S(2)}) collective-permute-start(f32[152,128]{1,0:T(8,128)S(1)} %get-tuple-element.12), channel_id=1, source_target_pairs={{0,4},{1,7},{2,6},{3,5},{4,0},{5,3},{6,2},{7,1},{8,12},{9,15},{10,... | collective-permute-start | bytes 233480 | tf_op jit(solution)/shard_map/ppermute | solution.py:351
  13.1 0.0 collective-permute-start.1
  13.1 1.8 %collective-permute-start.4 = (f32[80,128]{1,0:T(8,128)S(1)}, f32[80,128]{1,0:T(8,128)S(1)}, u32[]{:S(2)}, u32[]{:S(2)}) collective-permute-start(f32[80,128]{1,0:T(8,128)S(1)} %get-tuple-element.13), channel_id=1, source_target_pairs={{0,2},{2,0},{4,6},{6,4},{8,10},{10,8},{12,14},{14,12},{1,3},{3,1},... | collective-permute-start | bytes 122888 | tf_op jit(solution)/shard_map/ppermute | solution.py:357
  14.8 2.9 %collective-permute-done.4.refs_2_ = f32[80,128]{1,0:T(8,128)S(1)} collective-permute-done((f32[80,128]{1,0:T(8,128)S(1)}, f32[80,128]{1,0:T(8,128)S(1)}, u32[]{:S(2)}, u32[]{:S(2)}) %collective-permute-start.4) | collective-permute-done | bytes 40992 | tf_op jit(solution)/shard_map/ppermute | solution.py:357
  17.7 0.0 collective-permute-done.2.refs_0_
  17.8 0.0 collective-permute-done.3.refs_1_
  17.8 1.2 %grads.2.refs_1_ = f32[80,1024]{1,0:T(8,128)S(1)} custom-call(f32[152,128]{1,0:T(8,128)S(1)} %collective-permute-done.2.refs_0_, f32[152,128]{1,0:T(8,128)S(1)} %collective-permute-done.3.refs_1_, f32[80,128]{1,0:T(8,128)S(1)} %collective-permute-done.4.refs_2_, f32[80,128]{1,0:T(8,128)S(1)} %get-tuple-element.14.refs_3_), custom_call_target="tpu_custom_call" | custom-call | flops 201326592 | bytes 196608 | tf_op jit(solution)/shard_map/grads/pallas_call | solution.py:234
  19.0 0.7 %collective-permute-done.1.refs_0_ = f32[152,128]{1,0:T(8,128)S(1)} collective-permute-done((f32[152,128]{1,0:T(8,128)S(1)}, f32[152,128]{1,0:T(8,128)S(1)}, u32[]{:S(2)}, u32[]{:S(2)}) %collective-permute-start.1) | collective-permute-done | bytes 77856 | tf_op jit(solution)/shard_map/ppermute | solution.py:351
  19.7 0.5 %grads.3.part_ref = f32[80,1024]{1,0:T(8,128)S(1)} custom-call(f32[152,128]{1,0:T(8,128)S(1)} %collective-permute-done.1.refs_0_, f32[80,1024]{1,0:T(8,128)S(1)} %grads.2.refs_1_), custom_call_target="tpu_custom_call" | custom-call | flops 67108864 | bytes 65536 | tf_op jit(solution)/shard_map/grads/pallas_call | solution.py:234
  20.2 0.2 collective-permute-start.5
  20.4 1.5 %collective-permute-done.5.recv_ref = f32[80,1024]{1,0:T(8,128)S(1)} collective-permute-done((f32[80,1024]{1,0:T(8,128)S(1)}, f32[80,1024]{1,0:T(8,128)S(1)}, u32[]{:S(2)}, u32[]{:S(2)}) %collective-permute-start.5) | collective-permute-done | bytes 327712 | tf_op jit(solution)/shard_map/ppermute | solution.py:343
  21.9 0.4 %gram.1 = f32[40,128]{1,0:T(8,128)S(1)} custom-call(f32[80,1024]{1,0:T(8,128)S(1)} %grads.3.part_ref, f32[80,1024]{1,0:T(8,128)S(1)} %collective-permute-done.5.recv_ref), custom_call_target="tpu_custom_call" | custom-call | tf_op jit(solution)/shard_map/gram/pallas_call | solution.py:273
  22.3 1.5 %collective-permute-start.6 = (f32[40,128]{1,0:T(8,128)S(1)}, f32[40,128]{1,0:T(8,128)S(1)}, u32[]{:S(2)}, u32[]{:S(2)}) collective-permute-start(f32[40,128]{1,0:T(8,128)S(1)} %gram.1), channel_id=1, source_target_pairs={{0,4},{1,7},{2,6},{3,5},{4,0},{5,3},{6,2},{7,1},{8,12},{9,15},{10,... | collective-permute-start | bytes 61448 | tf_op jit(solution)/shard_map/ppermute | solution.py:351
  23.9 0.9 %collective-permute-start.7 = (f32[40,128]{1,0:T(8,128)S(1)}, f32[40,128]{1,0:T(8,128)S(1)}, u32[]{:S(2)}, u32[]{:S(2)}) collective-permute-start(f32[40,128]{1,0:T(8,128)S(1)} %gram.1), channel_id=1, source_target_pairs={{0,2},{2,0},{4,6},{6,4},{8,10},{10,8},{12,14},{14,12},{1,3},{3,1},... | collective-permute-start | bytes 61448 | tf_op jit(solution)/shard_map/ppermute | solution.py:357
  24.8 1.4 %collective-permute-done.6 = f32[40,128]{1,0:T(8,128)S(1)} collective-permute-done((f32[40,128]{1,0:T(8,128)S(1)}, f32[40,128]{1,0:T(8,128)S(1)}, u32[]{:S(2)}, u32[]{:S(2)}) %collective-permute-start.6) | collective-permute-done | bytes 20512 | tf_op jit(solution)/shard_map/ppermute | solution.py:351
  26.2 1.5 %collective-permute-done.7 = f32[40,128]{1,0:T(8,128)S(1)} collective-permute-done((f32[40,128]{1,0:T(8,128)S(1)}, f32[40,128]{1,0:T(8,128)S(1)}, u32[]{:S(2)}, u32[]{:S(2)}) %collective-permute-start.7) | collective-permute-done | bytes 20512 | tf_op jit(solution)/shard_map/ppermute | solution.py:357
  27.6 0.0 collective-permute-start.8
  27.7 1.2 %collective-permute-done.8.recv_ref = f32[40,128]{1,0:T(8,128)S(1)} collective-permute-done((f32[40,128]{1,0:T(8,128)S(1)}, f32[40,128]{1,0:T(8,128)S(1)}, u32[]{:S(2)}, u32[]{:S(2)}) %collective-permute-start.8) | collective-permute-done | bytes 20512 | tf_op jit(solution)/shard_map/ppermute | solution.py:343
  28.8 2.5 %solve.1 = f32[8,16]{1,0:T(8,128)} custom-call(f32[40,128]{1,0:T(8,128)S(1)} %select_add_fusion.x_ref, f32[40,128]{1,0:T(8,128)S(1)} %collective-permute-done.8.recv_ref), custom_call_target="tpu_custom_call" | custom-call | tf_op jit(solution)/shard_map/solve/pallas_call | solution.py:322
  (5 shorter events, 0.0 us)
Async XLA Ops:
  0.0 6.5 %copy-start.1 = (s32[256]{0:T(256)S(1)}, s32[256]{0:T(256)}, u32[]{:S(2)}) copy-start(s32[256]{0:T(256)} %param.10) | copy-start | bytes 3076
  0.0 6.5 %copy-start = (f32[2,4096]{1,0:T(2,128)S(1)}, f32[2,4096]{1,0:T(2,128)}, u32[]{:S(2)}) copy-start(f32[2,4096]{1,0:T(2,128)} %param.11) | copy-start | bytes 98308
  5.9 1.5 %collective-permute-start = (f32[128,256]{1,0:T(8,128)S(1)}, f32[128,256]{1,0:T(8,128)S(1)}, u32[]{:S(2)}, u32[]{:S(2)}) collective-permute-start(f32[128,256]{1,0:T(8,128)S(1)} %project.1.part_ref), channel_id=1, source_target_pairs={{0,1},{1,0},{2,3},{3,2},{4,5},{5,4},{6,7},{7,6},{8,9},{9,8},{10,11... | collective-permute-start | bytes 393224 | tf_op jit(solution)/shard_map/ppermute | solution.py:343
  7.5 10.2 %collective-permute-start.2 = (f32[152,128]{1,0:T(8,128)S(1)}, f32[152,128]{1,0:T(8,128)S(1)}, u32[]{:S(2)}, u32[]{:S(2)}) collective-permute-start(f32[152,128]{1,0:T(8,128)S(1)} %get-tuple-element.11), channel_id=1, source_target_pairs={{0,8},{1,11},{2,10},{3,9},{4,12},{5,15},{6,14},{7,13},{8,0},{9,3},... | collective-permute-start | bytes 233480 | tf_op jit(solution)/shard_map/ppermute | solution.py:351
  11.5 6.2 %collective-permute-start.3 = (f32[152,128]{1,0:T(8,128)S(1)}, f32[152,128]{1,0:T(8,128)S(1)}, u32[]{:S(2)}, u32[]{:S(2)}) collective-permute-start(f32[152,128]{1,0:T(8,128)S(1)} %get-tuple-element.12), channel_id=1, source_target_pairs={{0,4},{1,7},{2,6},{3,5},{4,0},{5,3},{6,2},{7,1},{8,12},{9,15},{10,... | collective-permute-start | bytes 233480 | tf_op jit(solution)/shard_map/ppermute | solution.py:351
  13.1 6.6 %collective-permute-start.1 = (f32[152,128]{1,0:T(8,128)S(1)}, f32[152,128]{1,0:T(8,128)S(1)}, u32[]{:S(2)}, u32[]{:S(2)}) collective-permute-start(f32[152,128]{1,0:T(8,128)S(1)} %get-tuple-element.10), channel_id=1, source_target_pairs={{0,12},{1,15},{2,14},{3,13},{4,8},{5,11},{6,10},{7,9},{8,4},{9,7},... | collective-permute-start | bytes 233480 | tf_op jit(solution)/shard_map/ppermute | solution.py:351
  13.1 4.7 %collective-permute-start.4 = (f32[80,128]{1,0:T(8,128)S(1)}, f32[80,128]{1,0:T(8,128)S(1)}, u32[]{:S(2)}, u32[]{:S(2)}) collective-permute-start(f32[80,128]{1,0:T(8,128)S(1)} %get-tuple-element.13), channel_id=1, source_target_pairs={{0,2},{2,0},{4,6},{6,4},{8,10},{10,8},{12,14},{14,12},{1,3},{3,1},... | collective-permute-start | bytes 122888 | tf_op jit(solution)/shard_map/ppermute | solution.py:357
  20.2 1.7 %collective-permute-start.5 = (f32[80,1024]{1,0:T(8,128)S(1)}, f32[80,1024]{1,0:T(8,128)S(1)}, u32[]{:S(2)}, u32[]{:S(2)}) collective-permute-start(f32[80,1024]{1,0:T(8,128)S(1)} %grads.3.part_ref), channel_id=1, source_target_pairs={{0,1},{1,0},{2,3},{3,2},{4,5},{5,4},{6,7},{7,6},{8,9},{9,8},{10,11... | collective-permute-start | bytes 983048 | tf_op jit(solution)/shard_map/ppermute | solution.py:343
  22.3 3.8 %collective-permute-start.6 = (f32[40,128]{1,0:T(8,128)S(1)}, f32[40,128]{1,0:T(8,128)S(1)}, u32[]{:S(2)}, u32[]{:S(2)}) collective-permute-start(f32[40,128]{1,0:T(8,128)S(1)} %gram.1), channel_id=1, source_target_pairs={{0,4},{1,7},{2,6},{3,5},{4,0},{5,3},{6,2},{7,1},{8,12},{9,15},{10,... | collective-permute-start | bytes 61448 | tf_op jit(solution)/shard_map/ppermute | solution.py:351
  23.9 3.8 %collective-permute-start.7 = (f32[40,128]{1,0:T(8,128)S(1)}, f32[40,128]{1,0:T(8,128)S(1)}, u32[]{:S(2)}, u32[]{:S(2)}) collective-permute-start(f32[40,128]{1,0:T(8,128)S(1)} %gram.1), channel_id=1, source_target_pairs={{0,2},{2,0},{4,6},{6,4},{8,10},{10,8},{12,14},{14,12},{1,3},{3,1},... | collective-permute-start | bytes 61448 | tf_op jit(solution)/shard_map/ppermute | solution.py:357
  27.6 1.2 %collective-permute-start.8 = (f32[40,128]{1,0:T(8,128)S(1)}, f32[40,128]{1,0:T(8,128)S(1)}, u32[]{:S(2)}, u32[]{:S(2)}) collective-permute-start(f32[40,128]{1,0:T(8,128)S(1)} %select_add_fusion.x_ref), channel_id=1, source_target_pairs={{0,1},{1,0},{2,3},{3,2},{4,5},{5,4},{6,7},{7,6},{8,9},{9,8},{10,11... | collective-permute-start | bytes 61448 | tf_op jit(solution)/shard_map/ppermute | solution.py:343

commit v27 on v18

--- a/solution.py
+++ b/solution.py
@@ -11,7 +11,7 @@
 DOC_DEV = 8
 LANES = 128
 FLIGHT = 7
-SHARED = 1
+SHARED = 2
 NT = (((1,), (1,)), ((), ()))
 VMEM = pl.BlockSpec(memory_space=pltpu.VMEM)
 HBM = pl.BlockSpec(memory_space=pltpu.HBM)

time: 31.1 us -> 31.5 us (1.013)
  starting transfers between devices: 10.4 us -> 11.3 us
  waiting for transfers between devices: 9.88 us -> 9.45 us
    ppermute x4, starting transfers between devices: 7.04 us -> 8.56 us  [trade(): got.append(lax.ppermute(x, ('dp', 'tensor'), pairs))]
    ppermute x2, starting transfers between devices: 2.64 us -> 1.55 us  [trade_shared(): return lax.ppermute(x, 'dp', [(i, i ^ SHARED) for i in range(dp)])]
    ppermute x4, waiting for transfers between devices: 2.29 us -> 1.8 us  [trade(): got.append(lax.ppermute(x, ('dp', 'tensor'), pairs))]
    ppermute x3, starting transfers between devices: 0.74 us -> 1.18 us  [swap_cores(): return lax.ppermute(x, 'tensor', [(i, cores - 1 - i) for i in range(cores)])]
where the time goes in v27:
time: 31.5 us; the launch traced here: 31.4 us
  starting transfers between devices  11.3 us (36%)
  Pallas kernels  10.3 us (33%)
  waiting for transfers between devices  9.45 us (30%)
    ppermute x4, starting transfers between devices, trade(): got.append(lax.ppermute(x, ('dp', 'tensor'), pairs))  8.56 us
    pallas_call x1, Pallas kernels, project(): pl.pallas_call(functools.partial(project_kernel, g_chunks, h_chunks), out...  5.59 us
    ppermute x2, waiting for transfers between devices, trade_shared(): return lax.ppermute(x, 'dp', [(i, i ^ SHARED) for i in range(dp)])  4.55 us
    ppermute x3, waiting for transfers between devices, swap_cores(): return lax.ppermute(x, 'tensor', [(i, cores - 1 - i) for i in range(cores)])  3.11 us
    pallas_call x1, Pallas kernels, solve(): pl.pallas_call(functools.partial(solve_kernel, docs, queries, scale), out...  2.46 us
    ppermute x4, waiting for transfers between devices, trade(): got.append(lax.ppermute(x, ('dp', 'tensor'), pairs))  1.8 us
    pallas_call x2, Pallas kernels, grads_of(): pl.pallas_call(functools.partial(grads_kernel, rows_a, rows_b, docs, dp,...  1.73 us
    ppermute x2, starting transfers between devices, trade_shared(): return lax.ppermute(x, 'dp', [(i, i ^ SHARED) for i in range(dp)])  1.55 us
  transfers between devices with their start and end apart: 9, of which 7 were waited for; matrix products, arithmetic and copies ran while one was open for 1% of the time, Pallas kernels for 4%

profile of v27, /device:TPU:0, one launch (start us, length us, event | category | flops | bytes accessed | tf_op | source)
XLA Modules:
  0.0 31.4 jit_solution(13311486174044504281)
XLA Ops:
  0.0 0.0 copy-start.1
  0.0 0.0 copy-start
  0.0 5.6 %project.1.part_ref = f32[128,256]{1,0:T(8,128)S(1)} custom-call(bf16[32,56,16,128]{3,2,1,0:T(8,128)(2,1)} %bitcast.32, bf16[32,16,16,128]{3,2,1,0:T(8,128)(2,1)} %bitcast.33, bf16[8,56,16,128]{3,2,1,0:T(8,128)(2,1)} %bitcast.34, bf16[8,16,16,128]{3,2,1,0:T(8,128)(2,1)} %bitcast.35), custom_call_target="tpu_custom_call" | custom-call | flops 603979776 | bytes 11796480 | tf_op jit(solution)/shard_map/project/pallas_call | solution.py:96
  5.6 0.5 %collective-permute-start = (f32[128,256]{1,0:T(8,128)S(1)}, f32[128,256]{1,0:T(8,128)S(1)}, u32[]{:S(2)}, u32[]{:S(2)}) collective-permute-start(f32[128,256]{1,0:T(8,128)S(1)} %project.1.part_ref), channel_id=1, source_target_pairs={{0,1},{1,0},{2,3},{3,2},{4,5},{5,4},{6,7},{7,6},{8,9},{9,8},{10,11... | collective-permute-start | bytes 393224 | tf_op jit(solution)/shard_map/ppermute | solution.py:329
  6.1 0.0 copy-done.1
  6.1 0.0 copy-done
  6.1 0.2 reshape.41
  6.3 0.1 reshape.42
  6.4 0.7 %collective-permute-done.recv_ref = f32[128,256]{1,0:T(8,128)S(1)} collective-permute-done((f32[128,256]{1,0:T(8,128)S(1)}, f32[128,256]{1,0:T(8,128)S(1)}, u32[]{:S(2)}, u32[]{:S(2)}) %collective-permute-start) | collective-permute-done | bytes 131104 | tf_op jit(solution)/shard_map/ppermute | solution.py:329
  7.1 0.1 pack.1
  7.2 4.0 %collective-permute-start.2 = (f32[152,128]{1,0:T(8,128)S(1)}, f32[152,128]{1,0:T(8,128)S(1)}, u32[]{:S(2)}, u32[]{:S(2)}) collective-permute-start(f32[152,128]{1,0:T(8,128)S(1)} %get-tuple-element.11), channel_id=1, source_target_pairs={{0,8},{1,11},{2,10},{3,9},{4,12},{5,15},{6,14},{7,13},{8,0},{9,3},... | collective-permute-start | bytes 233480 | tf_op jit(solution)/shard_map/ppermute | solution.py:337
  11.2 1.5 %collective-permute-start.3 = (f32[152,128]{1,0:T(8,128)S(1)}, f32[152,128]{1,0:T(8,128)S(1)}, u32[]{:S(2)}, u32[]{:S(2)}) collective-permute-start(f32[152,128]{1,0:T(8,128)S(1)} %get-tuple-element.12), channel_id=1, source_target_pairs={{0,2},{1,7},{2,0},{3,5},{4,6},{5,3},{6,4},{7,1},{8,10},{9,15},{10,... | collective-permute-start | bytes 233480 | tf_op jit(solution)/shard_map/ppermute | solution.py:337
  12.7 1.3 %collective-permute-start.1 = (f32[152,128]{1,0:T(8,128)S(1)}, f32[152,128]{1,0:T(8,128)S(1)}, u32[]{:S(2)}, u32[]{:S(2)}) collective-permute-start(f32[152,128]{1,0:T(8,128)S(1)} %get-tuple-element.10), channel_id=1, source_target_pairs={{0,12},{1,15},{2,14},{3,13},{4,8},{5,11},{6,10},{7,9},{8,4},{9,7},... | collective-permute-start | bytes 233480 | tf_op jit(solution)/shard_map/ppermute | solution.py:337
  14.1 0.2 collective-permute-start.4
  14.3 3.8 %collective-permute-done.4.refs_2_ = f32[80,128]{1,0:T(8,128)S(1)} collective-permute-done((f32[80,128]{1,0:T(8,128)S(1)}, f32[80,128]{1,0:T(8,128)S(1)}, u32[]{:S(2)}, u32[]{:S(2)}) %collective-permute-start.4) | collective-permute-done | bytes 40992 | tf_op jit(solution)/shard_map/ppermute | solution.py:343
  18.1 0.0 collective-permute-done.2.refs_0_
  18.1 0.0 collective-permute-done.3.refs_1_
  18.1 1.2 %grads.2.refs_1_ = f32[80,1024]{1,0:T(8,128)S(1)} custom-call(f32[152,128]{1,0:T(8,128)S(1)} %collective-permute-done.2.refs_0_, f32[152,128]{1,0:T(8,128)S(1)} %collective-permute-done.3.refs_1_, f32[80,128]{1,0:T(8,128)S(1)} %collective-permute-done.4.refs_2_, f32[80,128]{1,0:T(8,128)S(1)} %get-tuple-element.14.refs_3_), custom_call_target="tpu_custom_call" | custom-call | flops 201326592 | bytes 196608 | tf_op jit(solution)/shard_map/grads/pallas_call | solution.py:220
  19.3 0.1 collective-permute-done.1.refs_0_
  19.4 0.5 %grads.3.part_ref = f32[80,1024]{1,0:T(8,128)S(1)} custom-call(f32[152,128]{1,0:T(8,128)S(1)} %collective-permute-done.1.refs_0_, f32[80,1024]{1,0:T(8,128)S(1)} %grads.2.refs_1_), custom_call_target="tpu_custom_call" | custom-call | flops 67108864 | bytes 65536 | tf_op jit(solution)/shard_map/grads/pallas_call | solution.py:220
  19.9 0.7 %collective-permute-start.5 = (f32[80,1024]{1,0:T(8,128)S(1)}, f32[80,1024]{1,0:T(8,128)S(1)}, u32[]{:S(2)}, u32[]{:S(2)}) collective-permute-start(f32[80,1024]{1,0:T(8,128)S(1)} %grads.3.part_ref), channel_id=1, source_target_pairs={{0,1},{1,0},{2,3},{3,2},{4,5},{5,4},{6,7},{7,6},{8,9},{9,8},{10,11... | collective-permute-start | bytes 983048 | tf_op jit(solution)/shard_map/ppermute | solution.py:329
  20.6 1.3 %collective-permute-done.5.recv_ref = f32[80,1024]{1,0:T(8,128)S(1)} collective-permute-done((f32[80,1024]{1,0:T(8,128)S(1)}, f32[80,1024]{1,0:T(8,128)S(1)}, u32[]{:S(2)}, u32[]{:S(2)}) %collective-permute-start.5) | collective-permute-done | bytes 327712 | tf_op jit(solution)/shard_map/ppermute | solution.py:329
  21.8 0.4 %gram.1 = f32[40,128]{1,0:T(8,128)S(1)} custom-call(f32[80,1024]{1,0:T(8,128)S(1)} %grads.3.part_ref, f32[80,1024]{1,0:T(8,128)S(1)} %collective-permute-done.5.recv_ref), custom_call_target="tpu_custom_call" | custom-call | tf_op jit(solution)/shard_map/gram/pallas_call | solution.py:259
  22.3 1.7 %collective-permute-start.6 = (f32[40,128]{1,0:T(8,128)S(1)}, f32[40,128]{1,0:T(8,128)S(1)}, u32[]{:S(2)}, u32[]{:S(2)}) collective-permute-start(f32[40,128]{1,0:T(8,128)S(1)} %gram.1), channel_id=1, source_target_pairs={{0,6},{1,3},{2,4},{3,1},{4,2},{5,7},{6,0},{7,5},{8,14},{9,11},{10,... | collective-permute-start | bytes 61448 | tf_op jit(solution)/shard_map/ppermute | solution.py:337
  23.9 1.3 %collective-permute-start.7 = (f32[40,128]{1,0:T(8,128)S(1)}, f32[40,128]{1,0:T(8,128)S(1)}, u32[]{:S(2)}, u32[]{:S(2)}) collective-permute-start(f32[40,128]{1,0:T(8,128)S(1)} %gram.1), channel_id=1, source_target_pairs={{0,4},{2,6},{4,0},{6,2},{8,12},{10,14},{12,8},{14,10},{1,5},{3,7},... | collective-permute-start | bytes 61448 | tf_op jit(solution)/shard_map/ppermute | solution.py:343
  25.3 1.7 %collective-permute-done.6 = f32[40,128]{1,0:T(8,128)S(1)} collective-permute-done((f32[40,128]{1,0:T(8,128)S(1)}, f32[40,128]{1,0:T(8,128)S(1)}, u32[]{:S(2)}, u32[]{:S(2)}) %collective-permute-start.6) | collective-permute-done | bytes 20512 | tf_op jit(solution)/shard_map/ppermute | solution.py:337
  27.0 0.8 %collective-permute-done.7 = f32[40,128]{1,0:T(8,128)S(1)} collective-permute-done((f32[40,128]{1,0:T(8,128)S(1)}, f32[40,128]{1,0:T(8,128)S(1)}, u32[]{:S(2)}, u32[]{:S(2)}) %collective-permute-start.7) | collective-permute-done | bytes 20512 | tf_op jit(solution)/shard_map/ppermute | solution.py:343
  27.7 0.0 collective-permute-start.8
  27.7 1.2 %collective-permute-done.8.recv_ref = f32[40,128]{1,0:T(8,128)S(1)} collective-permute-done((f32[40,128]{1,0:T(8,128)S(1)}, f32[40,128]{1,0:T(8,128)S(1)}, u32[]{:S(2)}, u32[]{:S(2)}) %collective-permute-start.8) | collective-permute-done | bytes 20512 | tf_op jit(solution)/shard_map/ppermute | solution.py:329
  28.9 2.5 %solve.1 = f32[8,16]{1,0:T(8,128)} custom-call(f32[40,128]{1,0:T(8,128)S(1)} %select_add_fusion.x_ref, f32[40,128]{1,0:T(8,128)S(1)} %collective-permute-done.8.recv_ref), custom_call_target="tpu_custom_call" | custom-call | tf_op jit(solution)/shard_map/solve/pallas_call | solution.py:308
  (5 shorter events, 0.0 us)
Async XLA Ops:
  0.0 6.1 %copy-start.1 = (s32[256]{0:T(256)S(1)}, s32[256]{0:T(256)}, u32[]{:S(2)}) copy-start(s32[256]{0:T(256)} %param.10) | copy-start | bytes 3076
  0.0 6.1 %copy-start = (f32[2,4096]{1,0:T(2,128)S(1)}, f32[2,4096]{1,0:T(2,128)}, u32[]{:S(2)}) copy-start(f32[2,4096]{1,0:T(2,128)} %param.11) | copy-start | bytes 98308
  5.6 1.5 %collective-permute-start = (f32[128,256]{1,0:T(8,128)S(1)}, f32[128,256]{1,0:T(8,128)S(1)}, u32[]{:S(2)}, u32[]{:S(2)}) collective-permute-start(f32[128,256]{1,0:T(8,128)S(1)} %project.1.part_ref), channel_id=1, source_target_pairs={{0,1},{1,0},{2,3},{3,2},{4,5},{5,4},{6,7},{7,6},{8,9},{9,8},{10,11... | collective-permute-start | bytes 393224 | tf_op jit(solution)/shard_map/ppermute | solution.py:329
  7.2 10.9 %collective-permute-start.2 = (f32[152,128]{1,0:T(8,128)S(1)}, f32[152,128]{1,0:T(8,128)S(1)}, u32[]{:S(2)}, u32[]{:S(2)}) collective-permute-start(f32[152,128]{1,0:T(8,128)S(1)} %get-tuple-element.11), channel_id=1, source_target_pairs={{0,8},{1,11},{2,10},{3,9},{4,12},{5,15},{6,14},{7,13},{8,0},{9,3},... | collective-permute-start | bytes 233480 | tf_op jit(solution)/shard_map/ppermute | solution.py:337
  11.2 6.9 %collective-permute-start.3 = (f32[152,128]{1,0:T(8,128)S(1)}, f32[152,128]{1,0:T(8,128)S(1)}, u32[]{:S(2)}, u32[]{:S(2)}) collective-permute-start(f32[152,128]{1,0:T(8,128)S(1)} %get-tuple-element.12), channel_id=1, source_target_pairs={{0,2},{1,7},{2,0},{3,5},{4,6},{5,3},{6,4},{7,1},{8,10},{9,15},{10,... | collective-permute-start | bytes 233480 | tf_op jit(solution)/shard_map/ppermute | solution.py:337
  12.7 6.7 %collective-permute-start.1 = (f32[152,128]{1,0:T(8,128)S(1)}, f32[152,128]{1,0:T(8,128)S(1)}, u32[]{:S(2)}, u32[]{:S(2)}) collective-permute-start(f32[152,128]{1,0:T(8,128)S(1)} %get-tuple-element.10), channel_id=1, source_target_pairs={{0,12},{1,15},{2,14},{3,13},{4,8},{5,11},{6,10},{7,9},{8,4},{9,7},... | collective-permute-start | bytes 233480 | tf_op jit(solution)/shard_map/ppermute | solution.py:337
  14.1 4.0 %collective-permute-start.4 = (f32[80,128]{1,0:T(8,128)S(1)}, f32[80,128]{1,0:T(8,128)S(1)}, u32[]{:S(2)}, u32[]{:S(2)}) collective-permute-start(f32[80,128]{1,0:T(8,128)S(1)} %get-tuple-element.13), channel_id=1, source_target_pairs={{0,4},{2,6},{4,0},{6,2},{8,12},{10,14},{12,8},{14,10},{1,5},{3,7},... | collective-permute-start | bytes 122888 | tf_op jit(solution)/shard_map/ppermute | solution.py:343
  19.9 1.9 %collective-permute-start.5 = (f32[80,1024]{1,0:T(8,128)S(1)}, f32[80,1024]{1,0:T(8,128)S(1)}, u32[]{:S(2)}, u32[]{:S(2)}) collective-permute-start(f32[80,1024]{1,0:T(8,128)S(1)} %grads.3.part_ref), channel_id=1, source_target_pairs={{0,1},{1,0},{2,3},{3,2},{4,5},{5,4},{6,7},{7,6},{8,9},{9,8},{10,11... | collective-permute-start | bytes 983048 | tf_op jit(solution)/shard_map/ppermute | solution.py:329
  22.3 4.7 %collective-permute-start.6 = (f32[40,128]{1,0:T(8,128)S(1)}, f32[40,128]{1,0:T(8,128)S(1)}, u32[]{:S(2)}, u32[]{:S(2)}) collective-permute-start(f32[40,128]{1,0:T(8,128)S(1)} %gram.1), channel_id=1, source_target_pairs={{0,6},{1,3},{2,4},{3,1},{4,2},{5,7},{6,0},{7,5},{8,14},{9,11},{10,... | collective-permute-start | bytes 61448 | tf_op jit(solution)/shard_map/ppermute | solution.py:337
  23.9 3.8 %collective-permute-start.7 = (f32[40,128]{1,0:T(8,128)S(1)}, f32[40,128]{1,0:T(8,128)S(1)}, u32[]{:S(2)}, u32[]{:S(2)}) collective-permute-start(f32[40,128]{1,0:T(8,128)S(1)} %gram.1), channel_id=1, source_target_pairs={{0,4},{2,6},{4,0},{6,2},{8,12},{10,14},{12,8},{14,10},{1,5},{3,7},... | collective-permute-start | bytes 61448 | tf_op jit(solution)/shard_map/ppermute | solution.py:343
  27.7 1.2 %collective-permute-start.8 = (f32[40,128]{1,0:T(8,128)S(1)}, f32[40,128]{1,0:T(8,128)S(1)}, u32[]{:S(2)}, u32[]{:S(2)}) collective-permute-start(f32[40,128]{1,0:T(8,128)S(1)} %select_add_fusion.x_ref), channel_id=1, source_target_pairs={{0,1},{1,0},{2,3},{3,2},{4,5},{5,4},{6,7},{7,6},{8,9},{9,8},{10,11... | collective-permute-start | bytes 61448 | tf_op jit(solution)/shard_map/ppermute | solution.py:329

commit v28 on v18

--- a/solution.py
+++ b/solution.py
@@ -184,7 +184,7 @@
     me = lax.axis_index("dp")
     core = lax.axis_index("tensor")
     asked = [jnp.zeros((queries, LANES), jnp.float32)] * span
-    start = 0
+    start, tokens = 0, outer_ref.shape[1] // 2
     for x_ref, gap, whole in zip(xs, gaps, wholes):
         parts = 2 if whole else 1
         base = parts * rows
@@ -193,11 +193,14 @@
             start += LANES
             g, b = x_ref[i * rows:i * rows + rows_a, :], x_ref[i * rows + rows_a:(i + 1) * rows, :]
             ids = base + parts * span + i
-            member_ref[:, at] = jnp.where(doc == x_ref[ids:ids + 1, :].astype(jnp.int32), 1.0, 0.0).astype(jnp.bfloat16)
+            member = jnp.where(doc == x_ref[ids:ids + 1, :].astype(jnp.int32), 1.0, 0.0).astype(jnp.bfloat16)
+            later = slice(at.start + tokens, at.stop + tokens)
+            member_ref[:, at] = member
+            member_ref[:, later] = member
             outer = (g[:, None, :] * b[None, :, :]).reshape(wide, LANES)
             high = outer.astype(jnp.bfloat16)
-            outer_ref[0:wide, at] = high
-            outer_ref[wide:, at] = (outer - high.astype(jnp.float32)).astype(jnp.bfloat16)
+            outer_ref[:, at] = high
+            outer_ref[:, later] = (outer - high.astype(jnp.float32)).astype(jnp.bfloat16)
         source = 2 * (me ^ jnp.where(core == 0, gap[0], gap[1]))
         for i in range(parts):
             held = place == source + (i if whole else core)
@@ -205,7 +208,7 @@
                 row = base + i * span + j
                 asked[j] = jnp.where(held, x_ref[row:row + 1, :], asked[j])
     sums = lax.dot_general(member_ref[...], outer_ref[...], NT, preferred_element_type=jnp.float32)
-    sums = (sums[:, wide:] + sums[:, :wide]) * (TOK_DEV ** -0.5)
+    sums = sums * (TOK_DEV ** -0.5)
     asked = jnp.concatenate(asked, axis=1)
     if before:
         sums, asked = sums + before[0][0:docs, :], asked + before[0][docs:, :]
@@ -223,8 +226,8 @@
         in_specs=[VMEM] * len(operands),
         out_specs=VMEM,
         scratch_shapes=[
-            pltpu.VMEM((2 * wide, tokens), jnp.bfloat16),
-            pltpu.VMEM((docs, tokens), jnp.bfloat16),
+            pltpu.VMEM((wide, 2 * tokens), jnp.bfloat16),
+            pltpu.VMEM((docs, 2 * tokens), jnp.bfloat16),
         ],
         compiler_params=vmem_params(40),
         cost_estimate=pl.CostEstimate(

time: 31.1 us -> 31.1 us (level)
  no operation moved by 1% of the time
where the time goes in v28:
time: 31.1 us; the launch traced here: 30.9 us
  starting transfers between devices  10.4 us (33%)
  Pallas kernels  10.3 us (33%)
  waiting for transfers between devices  9.89 us (32%)
    ppermute x4, starting transfers between devices, trade(): got.append(lax.ppermute(x, ('dp', 'tensor'), pairs))  7.04 us
    pallas_call x1, Pallas kernels, project(): pl.pallas_call(functools.partial(project_kernel, g_chunks, h_chunks), out...  5.59 us
    ppermute x2, waiting for transfers between devices, trade_shared(): return lax.ppermute(x, 'dp', [(i, i ^ SHARED) for i in range(dp)])  4.26 us
    ppermute x3, waiting for transfers between devices, swap_cores(): return lax.ppermute(x, 'tensor', [(i, cores - 1 - i) for i in range(cores)])  3.32 us
    ppermute x2, starting transfers between devices, trade_shared(): return lax.ppermute(x, 'dp', [(i, i ^ SHARED) for i in range(dp)])  2.64 us
    pallas_call x1, Pallas kernels, solve(): pl.pallas_call(functools.partial(solve_kernel, docs, queries, scale), out...  2.46 us
    ppermute x4, waiting for transfers between devices, trade(): got.append(lax.ppermute(x, ('dp', 'tensor'), pairs))  2.3 us
    pallas_call x2, Pallas kernels, grads_of(): pl.pallas_call(functools.partial(grads_kernel, rows_a, rows_b, docs, dp,...  1.72 us
  transfers between devices with their start and end apart: 9, of which 7 were waited for; matrix products, arithmetic and copies ran while one was open for 1% of the time, Pallas kernels for 4%

profile of v28, /device:TPU:0, one launch (start us, length us, event | category | flops | bytes accessed | tf_op | source)
XLA Modules:
  0.0 30.9 jit_solution(8877824020733951152)
XLA Ops:
  0.0 0.0 copy-start.1
  0.0 0.0 copy-start
  0.0 5.6 %project.1.part_ref = f32[128,256]{1,0:T(8,128)S(1)} custom-call(bf16[32,56,16,128]{3,2,1,0:T(8,128)(2,1)} %bitcast.32, bf16[32,16,16,128]{3,2,1,0:T(8,128)(2,1)} %bitcast.33, bf16[8,56,16,128]{3,2,1,0:T(8,128)(2,1)} %bitcast.34, bf16[8,16,16,128]{3,2,1,0:T(8,128)(2,1)} %bitcast.35), custom_call_target="tpu_custom_call" | custom-call | flops 603979776 | bytes 11796480 | tf_op jit(solution)/shard_map/project/pallas_call | solution.py:96
  5.6 0.5 %collective-permute-start = (f32[128,256]{1,0:T(8,128)S(1)}, f32[128,256]{1,0:T(8,128)S(1)}, u32[]{:S(2)}, u32[]{:S(2)}) collective-permute-start(f32[128,256]{1,0:T(8,128)S(1)} %project.1.part_ref), channel_id=1, source_target_pairs={{0,1},{1,0},{2,3},{3,2},{4,5},{5,4},{6,7},{7,6},{8,9},{9,8},{10,11... | collective-permute-start | bytes 393224 | tf_op jit(solution)/shard_map/ppermute | solution.py:332
  6.1 0.0 copy-done.1
  6.1 0.0 copy-done
  6.1 0.2 reshape.41
  6.3 0.1 reshape.42
  6.4 0.7 %collective-permute-done.recv_ref = f32[128,256]{1,0:T(8,128)S(1)} collective-permute-done((f32[128,256]{1,0:T(8,128)S(1)}, f32[128,256]{1,0:T(8,128)S(1)}, u32[]{:S(2)}, u32[]{:S(2)}) %collective-permute-start) | collective-permute-done | bytes 131104 | tf_op jit(solution)/shard_map/ppermute | solution.py:332
  7.1 0.1 pack.1
  7.2 4.0 %collective-permute-start.2 = (f32[152,128]{1,0:T(8,128)S(1)}, f32[152,128]{1,0:T(8,128)S(1)}, u32[]{:S(2)}, u32[]{:S(2)}) collective-permute-start(f32[152,128]{1,0:T(8,128)S(1)} %get-tuple-element.11), channel_id=1, source_target_pairs={{0,8},{1,11},{2,10},{3,9},{4,12},{5,15},{6,14},{7,13},{8,0},{9,3},... | collective-permute-start | bytes 233480 | tf_op jit(solution)/shard_map/ppermute | solution.py:340
  11.2 1.6 %collective-permute-start.3 = (f32[152,128]{1,0:T(8,128)S(1)}, f32[152,128]{1,0:T(8,128)S(1)}, u32[]{:S(2)}, u32[]{:S(2)}) collective-permute-start(f32[152,128]{1,0:T(8,128)S(1)} %get-tuple-element.12), channel_id=1, source_target_pairs={{0,4},{1,7},{2,6},{3,5},{4,0},{5,3},{6,2},{7,1},{8,12},{9,15},{10,... | collective-permute-start | bytes 233480 | tf_op jit(solution)/shard_map/ppermute | solution.py:340
  12.8 0.0 collective-permute-start.1
  12.8 1.7 %collective-permute-start.4 = (f32[80,128]{1,0:T(8,128)S(1)}, f32[80,128]{1,0:T(8,128)S(1)}, u32[]{:S(2)}, u32[]{:S(2)}) collective-permute-start(f32[80,128]{1,0:T(8,128)S(1)} %get-tuple-element.13), channel_id=1, source_target_pairs={{0,2},{2,0},{4,6},{6,4},{8,10},{10,8},{12,14},{14,12},{1,3},{3,1},... | collective-permute-start | bytes 122888 | tf_op jit(solution)/shard_map/ppermute | solution.py:346
  14.5 2.9 %collective-permute-done.4.refs_2_ = f32[80,128]{1,0:T(8,128)S(1)} collective-permute-done((f32[80,128]{1,0:T(8,128)S(1)}, f32[80,128]{1,0:T(8,128)S(1)}, u32[]{:S(2)}, u32[]{:S(2)}) %collective-permute-start.4) | collective-permute-done | bytes 40992 | tf_op jit(solution)/shard_map/ppermute | solution.py:346
  17.4 0.0 collective-permute-done.2.refs_0_
  17.4 0.0 collective-permute-done.3.refs_1_
  17.4 1.2 %grads.2.refs_1_ = f32[80,1024]{1,0:T(8,128)S(1)} custom-call(f32[152,128]{1,0:T(8,128)S(1)} %collective-permute-done.2.refs_0_, f32[152,128]{1,0:T(8,128)S(1)} %collective-permute-done.3.refs_1_, f32[80,128]{1,0:T(8,128)S(1)} %collective-permute-done.4.refs_2_, f32[80,128]{1,0:T(8,128)S(1)} %get-tuple-element.14.refs_3_), custom_call_target="tpu_custom_call" | custom-call | flops 201326592 | bytes 196608 | tf_op jit(solution)/shard_map/grads/pallas_call | solution.py:223
  18.6 0.8 %collective-permute-done.1.refs_0_ = f32[152,128]{1,0:T(8,128)S(1)} collective-permute-done((f32[152,128]{1,0:T(8,128)S(1)}, f32[152,128]{1,0:T(8,128)S(1)}, u32[]{:S(2)}, u32[]{:S(2)}) %collective-permute-start.1) | collective-permute-done | bytes 77856 | tf_op jit(solution)/shard_map/ppermute | solution.py:340
  19.4 0.5 %grads.3.part_ref = f32[80,1024]{1,0:T(8,128)S(1)} custom-call(f32[152,128]{1,0:T(8,128)S(1)} %collective-permute-done.1.refs_0_, f32[80,1024]{1,0:T(8,128)S(1)} %grads.2.refs_1_), custom_call_target="tpu_custom_call" | custom-call | flops 67108864 | bytes 65536 | tf_op jit(solution)/shard_map/grads/pallas_call | solution.py:223
  19.9 0.2 collective-permute-start.5
  20.1 1.5 %collective-permute-done.5.recv_ref = f32[80,1024]{1,0:T(8,128)S(1)} collective-permute-done((f32[80,1024]{1,0:T(8,128)S(1)}, f32[80,1024]{1,0:T(8,128)S(1)}, u32[]{:S(2)}, u32[]{:S(2)}) %collective-permute-start.5) | collective-permute-done | bytes 327712 | tf_op jit(solution)/shard_map/ppermute | solution.py:332
  21.6 0.4 %gram.1 = f32[40,128]{1,0:T(8,128)S(1)} custom-call(f32[80,1024]{1,0:T(8,128)S(1)} %grads.3.part_ref, f32[80,1024]{1,0:T(8,128)S(1)} %collective-permute-done.5.recv_ref), custom_call_target="tpu_custom_call" | custom-call | tf_op jit(solution)/shard_map/gram/pallas_call | solution.py:262
  22.0 1.5 %collective-permute-start.6 = (f32[40,128]{1,0:T(8,128)S(1)}, f32[40,128]{1,0:T(8,128)S(1)}, u32[]{:S(2)}, u32[]{:S(2)}) collective-permute-start(f32[40,128]{1,0:T(8,128)S(1)} %gram.1), channel_id=1, source_target_pairs={{0,4},{1,7},{2,6},{3,5},{4,0},{5,3},{6,2},{7,1},{8,12},{9,15},{10,... | collective-permute-start | bytes 61448 | tf_op jit(solution)/shard_map/ppermute | solution.py:340
  23.5 0.9 %collective-permute-start.7 = (f32[40,128]{1,0:T(8,128)S(1)}, f32[40,128]{1,0:T(8,128)S(1)}, u32[]{:S(2)}, u32[]{:S(2)}) collective-permute-start(f32[40,128]{1,0:T(8,128)S(1)} %gram.1), channel_id=1, source_target_pairs={{0,2},{2,0},{4,6},{6,4},{8,10},{10,8},{12,14},{14,12},{1,3},{3,1},... | collective-permute-start | bytes 61448 | tf_op jit(solution)/shard_map/ppermute | solution.py:346
  24.4 1.5 %collective-permute-done.6 = f32[40,128]{1,0:T(8,128)S(1)} collective-permute-done((f32[40,128]{1,0:T(8,128)S(1)}, f32[40,128]{1,0:T(8,128)S(1)}, u32[]{:S(2)}, u32[]{:S(2)}) %collective-permute-start.6) | collective-permute-done | bytes 20512 | tf_op jit(solution)/shard_map/ppermute | solution.py:340
  25.9 1.4 %collective-permute-done.7 = f32[40,128]{1,0:T(8,128)S(1)} collective-permute-done((f32[40,128]{1,0:T(8,128)S(1)}, f32[40,128]{1,0:T(8,128)S(1)}, u32[]{:S(2)}, u32[]{:S(2)}) %collective-permute-start.7) | collective-permute-done | bytes 20512 | tf_op jit(solution)/shard_map/ppermute | solution.py:346
  27.3 0.0 collective-permute-start.8
  27.3 1.2 %collective-permute-done.8.recv_ref = f32[40,128]{1,0:T(8,128)S(1)} collective-permute-done((f32[40,128]{1,0:T(8,128)S(1)}, f32[40,128]{1,0:T(8,128)S(1)}, u32[]{:S(2)}, u32[]{:S(2)}) %collective-permute-start.8) | collective-permute-done | bytes 20512 | tf_op jit(solution)/shard_map/ppermute | solution.py:332
  28.5 2.5 %solve.1 = f32[8,16]{1,0:T(8,128)} custom-call(f32[40,128]{1,0:T(8,128)S(1)} %select_add_fusion.x_ref, f32[40,128]{1,0:T(8,128)S(1)} %collective-permute-done.8.recv_ref), custom_call_target="tpu_custom_call" | custom-call | tf_op jit(solution)/shard_map/solve/pallas_call | solution.py:311
  (5 shorter events, 0.0 us)
Async XLA Ops:
  0.0 6.1 %copy-start.1 = (s32[256]{0:T(256)S(1)}, s32[256]{0:T(256)}, u32[]{:S(2)}) copy-start(s32[256]{0:T(256)} %param.10) | copy-start | bytes 3076
  0.0 6.1 %copy-start = (f32[2,4096]{1,0:T(2,128)S(1)}, f32[2,4096]{1,0:T(2,128)}, u32[]{:S(2)}) copy-start(f32[2,4096]{1,0:T(2,128)} %param.11) | copy-start | bytes 98308
  5.6 1.5 %collective-permute-start = (f32[128,256]{1,0:T(8,128)S(1)}, f32[128,256]{1,0:T(8,128)S(1)}, u32[]{:S(2)}, u32[]{:S(2)}) collective-permute-start(f32[128,256]{1,0:T(8,128)S(1)} %project.1.part_ref), channel_id=1, source_target_pairs={{0,1},{1,0},{2,3},{3,2},{4,5},{5,4},{6,7},{7,6},{8,9},{9,8},{10,11... | collective-permute-start | bytes 393224 | tf_op jit(solution)/shard_map/ppermute | solution.py:332
  7.2 10.2 %collective-permute-start.2 = (f32[152,128]{1,0:T(8,128)S(1)}, f32[152,128]{1,0:T(8,128)S(1)}, u32[]{:S(2)}, u32[]{:S(2)}) collective-permute-start(f32[152,128]{1,0:T(8,128)S(1)} %get-tuple-element.11), channel_id=1, source_target_pairs={{0,8},{1,11},{2,10},{3,9},{4,12},{5,15},{6,14},{7,13},{8,0},{9,3},... | collective-permute-start | bytes 233480 | tf_op jit(solution)/shard_map/ppermute | solution.py:340
  11.2 6.2 %collective-permute-start.3 = (f32[152,128]{1,0:T(8,128)S(1)}, f32[152,128]{1,0:T(8,128)S(1)}, u32[]{:S(2)}, u32[]{:S(2)}) collective-permute-start(f32[152,128]{1,0:T(8,128)S(1)} %get-tuple-element.12), channel_id=1, source_target_pairs={{0,4},{1,7},{2,6},{3,5},{4,0},{5,3},{6,2},{7,1},{8,12},{9,15},{10,... | collective-permute-start | bytes 233480 | tf_op jit(solution)/shard_map/ppermute | solution.py:340
  12.8 6.6 %collective-permute-start.1 = (f32[152,128]{1,0:T(8,128)S(1)}, f32[152,128]{1,0:T(8,128)S(1)}, u32[]{:S(2)}, u32[]{:S(2)}) collective-permute-start(f32[152,128]{1,0:T(8,128)S(1)} %get-tuple-element.10), channel_id=1, source_target_pairs={{0,12},{1,15},{2,14},{3,13},{4,8},{5,11},{6,10},{7,9},{8,4},{9,7},... | collective-permute-start | bytes 233480 | tf_op jit(solution)/shard_map/ppermute | solution.py:340
  12.8 4.6 %collective-permute-start.4 = (f32[80,128]{1,0:T(8,128)S(1)}, f32[80,128]{1,0:T(8,128)S(1)}, u32[]{:S(2)}, u32[]{:S(2)}) collective-permute-start(f32[80,128]{1,0:T(8,128)S(1)} %get-tuple-element.13), channel_id=1, source_target_pairs={{0,2},{2,0},{4,6},{6,4},{8,10},{10,8},{12,14},{14,12},{1,3},{3,1},... | collective-permute-start | bytes 122888 | tf_op jit(solution)/shard_map/ppermute | solution.py:346
  19.9 1.7 %collective-permute-start.5 = (f32[80,1024]{1,0:T(8,128)S(1)}, f32[80,1024]{1,0:T(8,128)S(1)}, u32[]{:S(2)}, u32[]{:S(2)}) collective-permute-start(f32[80,1024]{1,0:T(8,128)S(1)} %grads.3.part_ref), channel_id=1, source_target_pairs={{0,1},{1,0},{2,3},{3,2},{4,5},{5,4},{6,7},{7,6},{8,9},{9,8},{10,11... | collective-permute-start | bytes 983048 | tf_op jit(solution)/shard_map/ppermute | solution.py:332
  22.0 3.9 %collective-permute-start.6 = (f32[40,128]{1,0:T(8,128)S(1)}, f32[40,128]{1,0:T(8,128)S(1)}, u32[]{:S(2)}, u32[]{:S(2)}) collective-permute-start(f32[40,128]{1,0:T(8,128)S(1)} %gram.1), channel_id=1, source_target_pairs={{0,4},{1,7},{2,6},{3,5},{4,0},{5,3},{6,2},{7,1},{8,12},{9,15},{10,... | collective-permute-start | bytes 61448 | tf_op jit(solution)/shard_map/ppermute | solution.py:340
  23.5 3.8 %collective-permute-start.7 = (f32[40,128]{1,0:T(8,128)S(1)}, f32[40,128]{1,0:T(8,128)S(1)}, u32[]{:S(2)}, u32[]{:S(2)}) collective-permute-start(f32[40,128]{1,0:T(8,128)S(1)} %gram.1), channel_id=1, source_target_pairs={{0,2},{2,0},{4,6},{6,4},{8,10},{10,8},{12,14},{14,12},{1,3},{3,1},... | collective-permute-start | bytes 61448 | tf_op jit(solution)/shard_map/ppermute | solution.py:346
  27.3 1.2 %collective-permute-start.8 = (f32[40,128]{1,0:T(8,128)S(1)}, f32[40,128]{1,0:T(8,128)S(1)}, u32[]{:S(2)}, u32[]{:S(2)}) collective-permute-start(f32[40,128]{1,0:T(8,128)S(1)} %select_add_fusion.x_ref), channel_id=1, source_target_pairs={{0,1},{1,0},{2,3},{3,2},{4,5},{5,4},{6,7},{7,6},{8,9},{9,8},{10,11... | collective-permute-start | bytes 61448 | tf_op jit(solution)/shard_map/ppermute | solution.py:332
